TPU v7x, 32 devices: a whole 2x2x4 slice. The times are simulated.
32 devices in a mesh: dp: 8 (over z, x), pipe: 4 (over y, core).
Axes of the slice: x: 2, y: 2, z: 4, core: 2. Of those that a mesh axis runs over, the one named last changes fastest.
Arguments:
- inputs: bfloat16 [2, 9216, 768], P(None, 'dp'), may hold values from -6 to 6
- out_grad: bfloat16 [2, 9216, 768], P(None, 'dp'), may hold values from -6 to 6
- page_side: int32 [2, 8], P(None, 'dp'), may hold values from 14 to 32, as said below
- norm_gain: float32 [4, 768], P('pipe'), may hold values from 0.25 to 1.75
- norm_shift: float32 [4, 768], P('pipe'), may hold values from -3 to 3
- layer_scale: float32 [4, 768], P('pipe'), may hold values from 0.5 to 2
- w_first: bfloat16 [4, 768, 3072], P('pipe'), may hold values from -0.21875 to 0.21875
- w_half: bfloat16 [4, 1536, 768], P('pipe'), may hold values from -0.109375 to 0.109375
- rel_table: float32 [2, 12, 2, 65], replicated, may hold values from -5 to 5
Outputs:
- section_out: bfloat16 [4, 2, 9216, 768], P('pipe', None, 'dp')
- section_in_grad: float32 [4, 2, 9216, 768], P('pipe', None, 'dp')
- g_first: float32 [4, 768, 3072], P('pipe', 'dp')
- g_half: float32 [4, 1536, 768], P('pipe', 'dp')
- g_gain: float32 [4, 768], P('pipe', 'dp')
- g_shift: float32 [4, 768], P('pipe', 'dp')
- g_scale: float32 [4, 768], P('pipe', 'dp')
- g_table: float32 [2, 12, 2, 65], replicated
Inputs may be any that keep to these rules, and one draw needn't show every extreme that they name: `page_side`: each entry is 14, 24 or 32; each value occurs in every draw.
All inputs are finite; a program needn't handle non-finite values.
Results may differ from a plain program's by a relative error of at most 0.018.
Values may be sent and summed in bfloat16 or wider, within the bound.
No kernel may reach another device: no remote copies, remote signals or barrier semaphores. Data moves between devices by JAX's collectives and lax.ppermute only.
A program may use at most 256 MiB of HBM per device.

v0:
```python
from functools import partial

import jax
import jax.numpy as jnp
from jax import lax
from jax.sharding import PartitionSpec as P

LAYERS = 2
SIDE_L = 32


EPSILON = 1e-06
MASKED = -1e30
HIGHEST = lax.Precision.HIGHEST


def shifted(block, axis, distance):
    devices = range(lax.axis_size(axis))
    route = [(i - distance, i) for i in devices if i - distance in devices]
    return lax.ppermute(block, axis, route)


def layer_norm(row_vals, gain_vec, shift_vec):
    row_mean = jnp.mean(row_vals, axis=-1, keepdims=True)
    centered = row_vals - row_mean
    variance = jnp.mean(centered * centered, axis=-1, keepdims=True)
    return centered * lax.rsqrt(variance + EPSILON) * gain_vec + shift_vec


def padded_cells():
    return (SIDE_L + 1 + 127) // 128 * 128


def geometry(grid_side, slot_rows):
    row_ids = jnp.arange(slot_rows, dtype=jnp.int32)
    page_len = grid_side * grid_side + 1
    page_count = slot_rows // page_len
    page_of = jnp.minimum(row_ids // page_len, page_count)
    offset = row_ids - page_of * page_len
    patch_id = jnp.maximum(offset - 1, 0)
    inside = page_of < page_count
    class_row = offset == 0
    coord_y = jnp.where(inside, jnp.where(class_row, SIDE_L, patch_id // grid_side), 0)
    coord_x = jnp.where(inside, jnp.where(class_row, SIDE_L, patch_id % grid_side), 0)
    same_page = page_of[:, None] == page_of[None, :]
    grid_cells = jnp.arange(padded_cells(), dtype=jnp.int32)
    onehot_y = (coord_y[:, None] == grid_cells[None, :]).astype(jnp.float32)
    onehot_x = (coord_x[:, None] == grid_cells[None, :]).astype(jnp.float32)
    both_onehot = jnp.concatenate([onehot_y, onehot_x], axis=1)
    return (same_page, both_onehot, onehot_y, onehot_x)


def offset_tables(layer_table):
    grid_cells = jnp.arange(padded_cells(), dtype=jnp.int32)
    cell_diffs = grid_cells[:, None] - grid_cells[None, :] + SIDE_L
    offset_picks = (
        cell_diffs[:, :, None] == jnp.arange(2 * SIDE_L + 1, dtype=jnp.int32)[None, None, :]
    ).astype(jnp.float32)
    grid_tables = jnp.einsum("abt,hct->hcab", offset_picks, layer_table, precision=HIGHEST)
    return (grid_tables, offset_picks)


def split_heads(flat_rows, head_count):
    return flat_rows.reshape(flat_rows.shape[0], head_count, -1).transpose(1, 0, 2)


def join_heads(stacked):
    return stacked.transpose(1, 0, 2).reshape(stacked.shape[1], -1)


def head_probs(head_q, head_k, grid_pair, layout, score_scale):
    same_page, both_onehot, onehot_y, onehot_x = layout
    along_y = jnp.dot(onehot_y, grid_pair[0], precision=HIGHEST)
    along_x = jnp.dot(onehot_x, grid_pair[1], precision=HIGHEST)
    bias = jnp.dot(jnp.concatenate([along_y, along_x], axis=1), both_onehot.T, precision=HIGHEST)
    raw_scores = jnp.dot(head_q, head_k.T, preferred_element_type=jnp.float32) * score_scale + bias
    raw_scores = jnp.where(same_page, raw_scores, MASKED)
    row_max = jnp.max(raw_scores, axis=-1, keepdims=True)
    exp_scores = jnp.exp(raw_scores - row_max)
    return exp_scores / jnp.sum(exp_scores, axis=-1, keepdims=True)


def attention_forward(section_in, gain_vec, shift_vec, scale_vec, section_w, grid_tables, layout):
    model_width = section_in.shape[1]
    head_count = grid_tables.shape[0]
    score_scale = (model_width // head_count) ** (-0.5)
    in_float = section_in.astype(jnp.float32)
    normed = layer_norm(in_float, gain_vec, shift_vec).astype(jnp.bfloat16)
    project = jnp.dot(
        normed, section_w[:, : 3 * model_width], preferred_element_type=jnp.float32
    ).astype(jnp.bfloat16)
    queries = split_heads(project[:, :model_width], head_count)
    key_rows = split_heads(project[:, model_width : 2 * model_width], head_count)
    values = split_heads(project[:, 2 * model_width :], head_count)

    def one_head(head_item):
        head_q, head_k, head_v, grid_pair = head_item
        probs_low = head_probs(head_q, head_k, grid_pair, layout, score_scale).astype(jnp.bfloat16)
        return jnp.dot(probs_low, head_v, preferred_element_type=jnp.float32).astype(jnp.bfloat16)

    context = join_heads(lax.map(one_head, (queries, key_rows, values, grid_tables)))
    branch = jnp.dot(context, section_w[:, 3 * model_width :], preferred_element_type=jnp.float32)
    return in_float + scale_vec * branch


def attention_backward(
    section_in,
    grad_out,
    gain_vec,
    shift_vec,
    scale_vec,
    section_w,
    grid_tables,
    offset_picks,
    layout,
):
    model_width = section_in.shape[1]
    head_count = grid_tables.shape[0]
    score_scale = (model_width // head_count) ** (-0.5)
    in_float = section_in.astype(jnp.float32)
    normed_f, norm_back = jax.vjp(layer_norm, in_float, gain_vec, shift_vec)
    normed = normed_f.astype(jnp.bfloat16)
    project = jnp.dot(
        normed, section_w[:, : 3 * model_width], preferred_element_type=jnp.float32
    ).astype(jnp.bfloat16)
    queries = split_heads(project[:, :model_width], head_count)
    key_rows = split_heads(project[:, model_width : 2 * model_width], head_count)
    values = split_heads(project[:, 2 * model_width :], head_count)
    d_branch = (grad_out * scale_vec).astype(jnp.bfloat16)
    d_context = jnp.dot(
        d_branch, section_w[:, 3 * model_width :].T, preferred_element_type=jnp.float32
    ).astype(jnp.bfloat16)
    onehot_y = layout[2]
    onehot_x = layout[3]
    onehot_y_low = onehot_y.astype(jnp.bfloat16)
    onehot_x_low = onehot_x.astype(jnp.bfloat16)

    def one_head(head_item):
        head_q, head_k, head_v, head_dout, grid_pair = head_item
        attn_probs = head_probs(head_q, head_k, grid_pair, layout, score_scale)
        probs_low = attn_probs.astype(jnp.bfloat16)
        head_out = jnp.dot(probs_low, head_v, preferred_element_type=jnp.float32).astype(
            jnp.bfloat16
        )
        d_probs = jnp.dot(head_dout, head_v.T, preferred_element_type=jnp.float32)
        row_delta = jnp.sum(attn_probs * d_probs, axis=-1, keepdims=True)
        d_scores = (attn_probs * (d_probs - row_delta)).astype(jnp.bfloat16)
        d_query = (
            jnp.dot(d_scores, head_k, preferred_element_type=jnp.float32) * score_scale
        ).astype(jnp.bfloat16)
        d_key = (
            jnp.dot(d_scores.T, head_q, preferred_element_type=jnp.float32) * score_scale
        ).astype(jnp.bfloat16)
        d_value = jnp.dot(probs_low.T, head_dout, preferred_element_type=jnp.float32).astype(
            jnp.bfloat16
        )
        grid_y = jnp.dot(
            onehot_y.T,
            jnp.dot(d_scores, onehot_y_low, preferred_element_type=jnp.float32),
            precision=HIGHEST,
        )
        grid_x = jnp.dot(
            onehot_x.T,
            jnp.dot(d_scores, onehot_x_low, preferred_element_type=jnp.float32),
            precision=HIGHEST,
        )
        return (head_out, d_query, d_key, d_value, jnp.stack([grid_y, grid_x]))

    head_results = lax.map(
        one_head, (queries, key_rows, values, split_heads(d_context, head_count), grid_tables)
    )
    context = join_heads(head_results[0])
    branch = jnp.dot(context, section_w[:, 3 * model_width :], preferred_element_type=jnp.float32)
    d_project = jnp.concatenate(
        [join_heads(head_results[1]), join_heads(head_results[2]), join_heads(head_results[3])],
        axis=1,
    )
    d_normed = jnp.dot(
        d_project, section_w[:, : 3 * model_width].T, preferred_element_type=jnp.float32
    )
    d_in, d_gain, d_shift = norm_back(d_normed)
    d_scale = jnp.sum(branch * grad_out, axis=0)
    left_rows = jnp.stack([normed, normed, normed, context])
    rights = jnp.concatenate([d_project, d_branch], axis=1)
    d_table = jnp.einsum("hcab,abt->hct", head_results[4], offset_picks, precision=HIGHEST)
    hidden_zero = jnp.zeros((section_in.shape[0], section_w.shape[1]), jnp.bfloat16)
    branch_zero = jnp.zeros(section_in.shape, jnp.bfloat16)
    return (
        grad_out + d_in,
        left_rows,
        rights,
        hidden_zero,
        branch_zero,
        d_gain,
        d_shift,
        d_scale,
        d_table,
    )


def mlp_forward(section_in, gain_vec, shift_vec, scale_vec, section_w, down_w):
    in_float = section_in.astype(jnp.float32)
    normed = layer_norm(in_float, gain_vec, shift_vec).astype(jnp.bfloat16)
    pre_act = jnp.dot(normed, section_w, preferred_element_type=jnp.float32)
    hidden = jax.nn.gelu(pre_act, approximate=True).astype(jnp.bfloat16)
    branch = jnp.dot(hidden, down_w, preferred_element_type=jnp.float32)
    return in_float + scale_vec * branch


def mlp_backward(
    section_in, grad_out, gain_vec, shift_vec, scale_vec, section_w, down_w, table_shape
):
    in_float = section_in.astype(jnp.float32)
    normed_f, norm_back = jax.vjp(layer_norm, in_float, gain_vec, shift_vec)
    normed = normed_f.astype(jnp.bfloat16)
    pre_act = jnp.dot(normed, section_w, preferred_element_type=jnp.float32)
    hidden_f, gelu_back = jax.vjp(partial(jax.nn.gelu, approximate=True), pre_act)
    hidden = hidden_f.astype(jnp.bfloat16)
    branch = jnp.dot(hidden, down_w, preferred_element_type=jnp.float32)
    d_branch = (grad_out * scale_vec).astype(jnp.bfloat16)
    d_hidden = jnp.dot(d_branch, down_w.T, preferred_element_type=jnp.float32)
    d_pre = gelu_back(d_hidden)[0].astype(jnp.bfloat16)
    d_normed = jnp.dot(d_pre, section_w.T, preferred_element_type=jnp.float32)
    d_in, d_gain, d_shift = norm_back(d_normed)
    d_scale = jnp.sum(branch * grad_out, axis=0)
    left_rows = jnp.stack([normed, normed, normed, normed])
    table_zero = jnp.zeros(table_shape, jnp.float32)
    return (
        grad_out + d_in,
        left_rows,
        d_pre,
        hidden,
        d_branch,
        d_gain,
        d_shift,
        d_scale,
        table_zero,
    )


def store_row(stacked, micro_safe, new_row, is_live):
    old_row = lax.dynamic_index_in_dim(stacked, micro_safe, 0, keepdims=False)
    return lax.dynamic_update_index_in_dim(
        stacked, jnp.where(is_live, new_row, old_row), micro_safe, 0
    )


def local(
    inputs, out_grad, page_side, norm_gain, norm_shift, layer_scale, w_first, w_half, rel_table
):
    section_id = lax.axis_index("pipe")
    section_count = lax.axis_size("pipe")
    micro_count = inputs.shape[0]
    slot_rows = inputs.shape[1]
    model_width = inputs.shape[2]
    hidden_width = w_first.shape[2]
    layer_id = section_id // 2
    kind_id = 1 + section_id % 2
    gain_vec = norm_gain[0]
    shift_vec = norm_shift[0]
    scale_vec = layer_scale[0]
    section_w = w_first[0]
    lower_rows = shifted(w_half, "pipe", 1)
    down_w = jnp.concatenate([lower_rows[0], w_half[0]], axis=0)
    layer_table = lax.dynamic_index_in_dim(rel_table, layer_id, 0, keepdims=False)
    grid_tables, offset_picks = offset_tables(layer_table)
    table_shape = layer_table.shape
    steps_total = micro_count + section_count - 1

    def spare_forward(section_in, grid_side):
        return jnp.zeros(section_in.shape, jnp.float32)

    def attention_step(section_in, grid_side):
        return attention_forward(
            section_in,
            gain_vec,
            shift_vec,
            scale_vec,
            section_w,
            grid_tables,
            geometry(grid_side, slot_rows),
        )

    def mlp_step(section_in, grid_side):
        return mlp_forward(section_in, gain_vec, shift_vec, scale_vec, section_w, down_w)

    def forward_step(step_id, loop_state):
        received, kept_in, section_out = loop_state
        micro_id = step_id - section_id
        is_live = (micro_id >= 0) & (micro_id < micro_count)
        micro_safe = jnp.clip(micro_id, 0, micro_count - 1)
        fresh_rows = lax.dynamic_index_in_dim(inputs, micro_safe, 0, keepdims=False)
        section_in = jnp.where(section_id == 0, fresh_rows, received)
        grid_side = lax.dynamic_index_in_dim(page_side, micro_safe, 0, keepdims=False)[0]
        branch_id = jnp.where(is_live, kind_id, 0)
        result = lax.switch(
            branch_id, [spare_forward, attention_step, mlp_step], section_in, grid_side
        ).astype(jnp.bfloat16)
        kept_in = store_row(kept_in, micro_safe, section_in, is_live)
        section_out = store_row(section_out, micro_safe, result, is_live)
        received = shifted(result, "pipe", 1)
        return (received, kept_in, section_out)

    zero_slot = jnp.zeros((slot_rows, model_width), jnp.bfloat16)
    zero_micro = jnp.zeros(inputs.shape, jnp.bfloat16)
    received, kept_in, section_out = lax.fori_loop(
        0, steps_total, forward_step, (zero_slot, zero_micro, zero_micro)
    )

    def spare_back(section_in, grad_out, grid_side):
        return (
            jnp.zeros(grad_out.shape, jnp.float32),
            jnp.zeros((4, slot_rows, model_width), jnp.bfloat16),
            jnp.zeros((slot_rows, hidden_width), jnp.bfloat16),
            jnp.zeros((slot_rows, hidden_width), jnp.bfloat16),
            jnp.zeros((slot_rows, model_width), jnp.bfloat16),
            jnp.zeros((model_width,), jnp.float32),
            jnp.zeros((model_width,), jnp.float32),
            jnp.zeros((model_width,), jnp.float32),
            jnp.zeros(table_shape, jnp.float32),
        )

    def attention_back(section_in, grad_out, grid_side):
        return attention_backward(
            section_in,
            grad_out,
            gain_vec,
            shift_vec,
            scale_vec,
            section_w,
            grid_tables,
            offset_picks,
            geometry(grid_side, slot_rows),
        )

    def mlp_back(section_in, grad_out, grid_side):
        return mlp_backward(
            section_in, grad_out, gain_vec, shift_vec, scale_vec, section_w, down_w, table_shape
        )

    def weight_update(branch_id, totals, weight_parts):
        first_total, down_total = totals
        left_rows, rights, hidden, d_branch = weight_parts

        def first_term():
            blocks = rights.reshape(slot_rows, 4, model_width)
            return jnp.einsum(
                "csd,sce->dce", left_rows, blocks, preferred_element_type=jnp.float32
            ).reshape(model_width, hidden_width)

        def add_none():
            return (first_total, down_total)

        def add_first():
            return (first_total + first_term(), down_total)

        def add_both():
            return (
                first_total + first_term(),
                down_total + jnp.dot(hidden.T, d_branch, preferred_element_type=jnp.float32),
            )

        return lax.switch(branch_id, [add_none, add_first, add_both])

    def backward_step(step_id, loop_state):
        received, in_grads, totals, small_sums, stash_rows = loop_state
        micro_id = micro_count - 1 - step_id + section_count - 1 - section_id
        is_live = (micro_id >= 0) & (micro_id < micro_count)
        micro_safe = jnp.clip(micro_id, 0, micro_count - 1)
        section_in = lax.dynamic_index_in_dim(kept_in, micro_safe, 0, keepdims=False)
        last_grad = lax.dynamic_index_in_dim(out_grad, micro_safe, 0, keepdims=False)
        grad_out = jnp.where(section_id == section_count - 1, last_grad, received).astype(
            jnp.float32
        )
        grid_side = lax.dynamic_index_in_dim(page_side, micro_safe, 0, keepdims=False)[0]
        branch_id = jnp.where(is_live, kind_id, 0)
        step_parts = lax.switch(
            branch_id, [spare_back, attention_back, mlp_back], section_in, grad_out, grid_side
        )
        d_in = step_parts[0]
        in_grads = store_row(in_grads, micro_safe, d_in, is_live)
        small_sums = tuple(
            (old_val + new_val for old_val, new_val in zip(small_sums, step_parts[5:]))
        )
        totals = weight_update(branch_id, totals, step_parts[1:5])
        received = shifted(d_in.astype(jnp.bfloat16), "pipe", -1)
        return (received, in_grads, totals, small_sums, stash_rows)

    totals = (
        jnp.zeros((model_width, hidden_width), jnp.float32),
        jnp.zeros((hidden_width, model_width), jnp.float32),
    )
    small_sums = (
        jnp.zeros((model_width,), jnp.float32),
        jnp.zeros((model_width,), jnp.float32),
        jnp.zeros((model_width,), jnp.float32),
        jnp.zeros(table_shape, jnp.float32),
    )
    stash_rows = ()
    in_grads = jnp.zeros(inputs.shape, jnp.float32)
    received, in_grads, totals, small_sums, stash_rows = lax.fori_loop(
        0, steps_total, backward_step, (zero_slot, in_grads, totals, small_sums, stash_rows)
    )
    first_total, down_total = totals
    gain_total, shift_total, scale_total, table_total = small_sums
    half_rows = hidden_width // 2
    upper_grad = shifted(down_total[:half_rows].astype(jnp.bfloat16), "pipe", -1).astype(
        jnp.float32
    )
    own_down = jnp.where(section_id % 2 == 1, down_total[half_rows:], upper_grad)
    summed = (
        lax.psum_scatter(first_total[None], "dp", scatter_dimension=1, tiled=True),
        lax.psum_scatter(own_down[None], "dp", scatter_dimension=1, tiled=True),
        lax.psum_scatter(gain_total[None], "dp", scatter_dimension=1, tiled=True),
        lax.psum_scatter(shift_total[None], "dp", scatter_dimension=1, tiled=True),
        lax.psum_scatter(scale_total[None], "dp", scatter_dimension=1, tiled=True),
    )
    g_first, g_half, g_gain, g_shift, g_scale = summed
    layer_slots = jnp.arange(LAYERS, dtype=jnp.int32) == layer_id
    table_all = jnp.where(layer_slots[:, None, None, None], table_total[None], 0.0)
    g_table = lax.psum(table_all, ("dp", "pipe"))
    return (section_out[None], in_grads[None], g_first, g_half, g_gain, g_shift, g_scale, g_table)


def solution(mesh):
    in_specs = (
        P(None, "dp", None),
        P(None, "dp", None),
        P(None, "dp"),
        P("pipe", None),
        P("pipe", None),
        P("pipe", None),
        P("pipe", None, None),
        P("pipe", None, None),
        P(),
    )
    out_specs = (
        P("pipe", None, "dp", None),
        P("pipe", None, "dp", None),
        P("pipe", "dp", None),
        P("pipe", "dp", None),
        P("pipe", "dp"),
        P("pipe", "dp"),
        P("pipe", "dp"),
        P(),
    )
    return jax.shard_map(local, mesh=mesh, in_specs=in_specs, out_specs=out_specs, check_vma=False)
```

profile of v0, /device:TPU:0, one launch (start us, length us, event | category | flops | bytes accessed | tf_op | source)
XLA Modules:
  0.0 3412.0 jit_solution(11234868762468201098)
XLA Ops:
  26.6 799.2 %while.91 = (s32[]{:T(128)}, bf16[1152,768]{1,0:T(8,128)(2,1)}, bf16[2,1152,768]{2,1,0:T(8,128)(2,1)}, bf16[2,1152,768]{2,1,0:T(8,128)(2,1)}, s32[]{:T(128)}, /*...) while((s32[]{:T(128)}, bf16[1152,768]{1,0:T(8,128)(2,1)}, ...), condition=%wide.region_12.13_spmd, body=%wide.region_0.12_spmd.sunk | while | flops 10920297472 | bytes 168364032 | solution.py:306
  54.9 211.6 %conditional.8 = (bf16[1152,768]{1,0:T(8,128)(2,1)}) conditional(s32[]{:T(128)} %clamp.25, () %tuple.217, (bf16[1152,768]{1,0:T(8,128)(2,1)S(1)}, f32[1,768]{1,0:T(1,128)S(1)}, f32[1,768]{1,0:T(1,128)S(1)}, f32[1,768]{1,0:T(1,128)S(1)}, bf16[768,3072]{1,0:T(8,128)(2,1)}, /*index=5*/s32[2,1]{0,1:T(1,128)S(1)}, s32[]{:T(128)}, ...), branch_computations={%region_1.1_spmd, %region_2.8_spmd, %region_9.11_spmd} | conditional | flops 10917643264 | bytes 76350920 | solution.py:296
  63.3 7.0 convolution_convert_fusion.2
  84.5 177.3 %while.89 = (s32[]{:T(128)}, bf16[12,1152,64]{1,2,0:T(8,128)(2,1)}, bf16[12,1152,64]{1,2,0:T(8,128)(2,1)}, bf16[12,1152,64]{1,2,0:T(8,128)(2,1)}, f32[12,2,128,1...) while((s32[]{:T(128)}, bf16[12,1152,64]{1,2,0:T(8,128)(2,1)}, ...), condition=%wide.region_8.7_spmd.clone, body=%wide.region_5.6_spmd.clone.sunk | while | flops 4883814400 | bytes 30841996 | solution.py:101
  281.6 211.6 %conditional.8 = (bf16[1152,768]{1,0:T(8,128)(2,1)}) conditional(s32[]{:T(128)} %clamp.25, () %tuple.217, (bf16[1152,768]{1,0:T(8,128)(2,1)S(1)}, f32[1,768]{1,0:T(1,128)S(1)}, f32[1,768]{1,0:T(1,128)S(1)}, f32[1,768]{1,0:T(1,128)S(1)}, bf16[768,3072]{1,0:T(8,128)(2,1)}, /*index=5*/s32[2,1]{0,1:T(1,128)S(1)}, s32[]{:T(128)}, ...), branch_computations={%region_1.1_spmd, %region_2.8_spmd, %region_9.11_spmd} | conditional | flops 10917643264 | bytes 76350920 | solution.py:296
  290.1 7.0 convolution_convert_fusion.2
  311.3 177.3 %while.89 = (s32[]{:T(128)}, bf16[12,1152,64]{1,2,0:T(8,128)(2,1)}, bf16[12,1152,64]{1,2,0:T(8,128)(2,1)}, bf16[12,1152,64]{1,2,0:T(8,128)(2,1)}, f32[12,2,128,1...) while((s32[]{:T(128)}, bf16[12,1152,64]{1,2,0:T(8,128)(2,1)}, ...), condition=%wide.region_8.7_spmd.clone, body=%wide.region_5.6_spmd.clone.sunk | while | flops 4883814400 | bytes 30841996 | solution.py:101
  509.8 17.4 collective-permute-start.1
  540.8 35.3 %collective-permute-start.1 = (bf16[1152,768]{1,0:T(8,128)(2,1)}, bf16[1152,768]{1,0:T(8,128)(2,1)S(1)}, u32[]{:S(2)}, u32[]{:S(2)}) collective-permute-start(bf16[1152,768]{1,0:T(8,128)(2,1)} %get-tuple-element.2632), channel_id=1, source_target_pairs={{0,1},{1,2},{2,3},{4,5},{5,6},{6,7},{8,9},{9,10},{10,11},{12,13},{... | collective-permute-start | bytes 5308424 | tf_op jit(solution)/shard_map/while/body/eval_jaxpr/ppermute | solution.py:20
  589.7 230.6 %collective-permute-start.1 = (bf16[1152,768]{1,0:T(8,128)(2,1)}, bf16[1152,768]{1,0:T(8,128)(2,1)S(1)}, u32[]{:S(2)}, u32[]{:S(2)}) collective-permute-start(bf16[1152,768]{1,0:T(8,128)(2,1)} %get-tuple-element.2632), channel_id=1, source_target_pairs={{0,1},{1,2},{2,3},{4,5},{5,6},{6,7},{8,9},{9,10},{10,11},{12,13},{... | collective-permute-start | bytes 5308424 | tf_op jit(solution)/shard_map/while/body/eval_jaxpr/ppermute | solution.py:20
  838.9 2105.0 %while.92 = (s32[]{:T(128)}, bf16[1152,768]{1,0:T(8,128)(2,1)}, f32[2,1152,768]{2,1,0:T(8,128)}, f32[768,3072]{0,1:T(8,128)}, f32[3072,768]{1,0:T(8,128)}, /*ind...) while((s32[]{:T(128)}, bf16[1152,768]{1,0:T(8,128)(2,1)}, ...), condition=%wide.region_39.40_spmd.clone, body=%wide.region_13.39_spmd.clone.sunk | while | flops 32765095936 | bytes 543123136 | solution.py:401
  855.6 24.7 conditional.9
  891.2 15.5 collective-permute-done
  917.1 24.7 conditional.9
  952.7 17.2 collective-permute-done
  980.3 24.7 conditional.9
  1015.9 641.4 %collective-permute-done = bf16[1152,768]{1,0:T(8,128)(2,1)S(1)} collective-permute-done((bf16[1152,768]{1,0:T(8,128)(2,1)}, bf16[1152,768]{1,0:T(8,128)(2,1)S(1)}, u32[]{:S(2)}, u32[]{:S(2)}) %collective-permute-start) | collective-permute-done | bytes 1769504 | tf_op jit(solution)/shard_map/while/body/eval_jaxpr/ppermute | solution.py:20
  1667.6 581.0 %conditional.9 = (f32[1152,768]{1,0:T(8,128)}, bf16[4,1152,768]{2,1,0:T(8,128)(2,1)}, bf16[1152,3072]{1,0:T(8,128)(2,1)}, bf16[1152,3072]{1,0:T(8,128)(2,1)}, bf...) conditional(s32[]{:T(128)} %clamp.26, () %tuple.222, ...), branch_computations={%region_14.14_spmd, %region_15.27_spmd, %region_28.35_spmd} | conditional | flops 21883064320 | bytes 340409216 | solution.py:377
  1677.3 7.0 convolution_convert_fusion.3
  1710.5 471.1 %while.90 = (s32[]{:T(128)}, bf16[12,1152,64]{1,2,0:T(8,128)(2,1)}, bf16[12,1152,64]{1,2,0:T(8,128)(2,1)}, bf16[12,1152,64]{1,2,0:T(8,128)(2,1)}, bf16[12,1152,6...) while((s32[]{:T(128)}, bf16[12,1152,64]{1,2,0:T(8,128)(2,1)}, ...), condition=%wide.region_22.21_spmd.clone.clone, body=%wide.region_18.20_spmd.clone.clone.sunk | while | flops 6713553920 | bytes 106136848 | solution.py:169
  1834.1 6.0 fusion.319
  1951.8 6.0 fusion.319
  2181.7 7.0 pad_maximum_fusion.2
  2188.6 10.4 copy.100
  2199.1 8.8 fusion.216
  2217.6 6.5 pad_maximum_fusion.1
  2254.0 34.1 conditional.10
  2254.0 10.2 copy.101
  2264.2 12.7 fusion.221
  2277.0 11.1 bitcast_add_fusion
  2309.8 581.0 %conditional.9 = (f32[1152,768]{1,0:T(8,128)}, bf16[4,1152,768]{2,1,0:T(8,128)(2,1)}, bf16[1152,3072]{1,0:T(8,128)(2,1)}, bf16[1152,3072]{1,0:T(8,128)(2,1)}, bf...) conditional(s32[]{:T(128)} %clamp.26, () %tuple.222, ...), branch_computations={%region_14.14_spmd, %region_15.27_spmd, %region_28.35_spmd} | conditional | flops 21883064320 | bytes 340409216 | solution.py:377
  2319.5 7.0 convolution_convert_fusion.3
  2352.7 471.1 %while.90 = (s32[]{:T(128)}, bf16[12,1152,64]{1,2,0:T(8,128)(2,1)}, bf16[12,1152,64]{1,2,0:T(8,128)(2,1)}, bf16[12,1152,64]{1,2,0:T(8,128)(2,1)}, bf16[12,1152,6...) while((s32[]{:T(128)}, bf16[12,1152,64]{1,2,0:T(8,128)(2,1)}, ...), condition=%wide.region_22.21_spmd.clone.clone, body=%wide.region_18.20_spmd.clone.clone.sunk | while | flops 6713553920 | bytes 106136848 | solution.py:169
  2476.1 6.0 fusion.319
  2823.9 7.0 pad_maximum_fusion.2
  2830.8 10.4 copy.100
  2841.3 8.8 fusion.216
  2859.8 6.5 pad_maximum_fusion.1
  2896.2 34.1 conditional.10
  2896.2 10.2 copy.101
  2906.4 12.7 fusion.221
  2919.1 11.1 bitcast_add_fusion
  2959.0 9.7 copy.107
  2969.4 40.9 %psum.7 = f32[2,12,2,65]{3,2,1,0:T(2,128)} all-reduce(f32[2,12,2,65]{3,2,1,0:T(2,128)S(1)} %broadcast_select_fusion), channel_id=1, replica_groups=mesh['dp'=8,'pipe'=4] {'dp','pipe'}, use_global_device_ids=true, to_apply=%region_45.46 | all-reduce | flops 3120 | bytes 24960 | tf_op jit(solution)/shard_map/psum | solution.py:421
  3013.6 62.3 %reduce-scatter.18.cloned.1.call-done = f32[96,1]{1,0:T(8,128)} async-done(((f32[768,1]{1,0:T(8,128)}), f32[96,1]{1,0:T(8,128)}) %reduce-scatter.18.cloned.1.call-update) | async-done | bytes 400
  3077.2 62.3 %reduce-scatter.20.cloned.1.call-done = f32[96,1]{1,0:T(8,128)} async-done(((f32[768,1]{1,0:T(8,128)}), f32[96,1]{1,0:T(8,128)}) %reduce-scatter.20.cloned.1.call-update) | async-done | bytes 400
  3140.9 97.0 %reduce-scatter.14.cloned.1.call-done = f32[1,192,768]{2,1,0:T(8,128)} async-done(((f32[1,1536,768]{2,1,0:T(8,128)}), f32[1,192,768]{2,1,0:T(8,128)}) %reduce-scatter.14.cloned.1.call-update) | async-done | bytes 589840 | tf_op jit(solution)/shard_map/reduce_scatter | solution.py:413
  3237.9 167.3 %reduce-scatter.12.cloned.1.call-done = f32[1,96,3072]{2,1,0:T(8,128)} async-done(((f32[1,768,3072]{2,1,0:T(8,128)}), f32[1,96,3072]{2,1,0:T(8,128)}) %reduce-scatter.12.cloned.1.call-update) | async-done | bytes 1179664 | tf_op jit(solution)/shard_map/reduce_scatter | solution.py:412
  (1281 shorter events, 1725.6 us)
Async XLA Ops:
  7.2 9.8 copy-start.23
  7.2 9.1 copy-start.52
  7.2 3005.0 %reduce-scatter.16.cloned.1.call-start = ((), (), s32[]{:S(2)}) async-start(), calls=%async_computation.7 | async-start | bytes 442368
  7.2 9.7 collective-permute-start.2
  266.5 6.0 collective-permute-start.1
  493.3 6.0 collective-permute-start.1
  509.8 20.8 collective-permute-start.1
  540.8 38.7 %collective-permute-start.1 = (bf16[1152,768]{1,0:T(8,128)(2,1)}, bf16[1152,768]{1,0:T(8,128)(2,1)S(1)}, u32[]{:S(2)}, u32[]{:S(2)}) collective-permute-start(bf16[1152,768]{1,0:T(8,128)(2,1)} %get-tuple-element.2632), channel_id=1, source_target_pairs={{0,1},{1,2},{2,3},{4,5},{5,6},{6,7},{8,9},{9,10},{10,11},{12,13},{... | collective-permute-start | bytes 5308424 | tf_op jit(solution)/shard_map/while/body/eval_jaxpr/ppermute | solution.py:20
  589.7 234.0 %collective-permute-start.1 = (bf16[1152,768]{1,0:T(8,128)(2,1)}, bf16[1152,768]{1,0:T(8,128)(2,1)S(1)}, u32[]{:S(2)}, u32[]{:S(2)}) collective-permute-start(bf16[1152,768]{1,0:T(8,128)(2,1)} %get-tuple-element.2632), channel_id=1, source_target_pairs={{0,1},{1,2},{2,3},{4,5},{5,6},{6,7},{8,9},{9,10},{10,11},{12,13},{... | collective-permute-start | bytes 5308424 | tf_op jit(solution)/shard_map/while/body/eval_jaxpr/ppermute | solution.py:20
  846.4 9.2 copy-start.29
  883.7 23.0 collective-permute-start
  890.5 17.4 copy-start.30
  891.2 15.5 copy-start.15
  907.9 9.2 copy-start.29
  945.2 24.7 collective-permute-start
  952.0 19.1 copy-start.30
  952.7 17.2 copy-start.15
  971.1 9.2 copy-start.29
  1008.4 648.8 %collective-permute-start = (bf16[1152,768]{1,0:T(8,128)(2,1)}, bf16[1152,768]{1,0:T(8,128)(2,1)S(1)}, u32[]{:S(2)}, u32[]{:S(2)}) collective-permute-start(bf16[1152,768]{1,0:T(8,128)(2,1)} %convert_element_type.431), channel_id=1, source_target_pairs={{1,0},{2,1},{3,2},{5,4},{6,5},{7,6},{9,8},{10,9},{11,10},{13,12},{... | collective-permute-start | bytes 5308424 | tf_op jit(solution)/shard_map/while/body/eval_jaxpr/ppermute | solution.py:20
  1015.2 643.2 %copy-start.30 = (f32[1,768]{1,0:T(1,128)S(1)}, f32[1,768]{1,0:T(1,128)}, u32[]{:S(2)}) copy-start(f32[1,768]{1,0:T(1,128)} %copy-done.29) | copy-start | bytes 9220 | tf_op jit(solution)/shard_map/while
  1015.9 641.4 %copy-start.15 = (f32[2,1152,768]{2,1,0:T(8,128)}, f32[2,1152,768]{2,1,0:T(8,128)S(1)}, u32[]{:S(2)}) copy-start(f32[2,1152,768]{2,1,0:T(8,128)S(1)} %bitcast_dynamic-update-slice_fusion.8) | copy-start | bytes 21233668 | tf_op jit(solution)/shard_map/while
  1658.5 9.2 copy-start.29
  1667.6 9.6 copy-start.3
  2188.6 10.4 copy-start.4
  2188.6 10.4 copy-start.22
  2188.6 10.4 copy-start.36
  2213.6 10.5 slice-start
  2252.1 47.0 %collective-permute-start = (bf16[1152,768]{1,0:T(8,128)(2,1)}, bf16[1152,768]{1,0:T(8,128)(2,1)S(1)}, u32[]{:S(2)}, u32[]{:S(2)}) collective-permute-start(bf16[1152,768]{1,0:T(8,128)(2,1)} %convert_element_type.431), channel_id=1, source_target_pairs={{1,0},{2,1},{3,2},{5,4},{6,5},{7,6},{9,8},{10,9},{11,10},{13,12},{... | collective-permute-start | bytes 5308424 | tf_op jit(solution)/shard_map/while/body/eval_jaxpr/ppermute | solution.py:20
  2253.4 34.7 %copy-start.46 = (f32[768]{0:T(1024)S(1)}, f32[768]{0:T(1024)}, u32[]{:S(2)}) copy-start(f32[768]{0:T(1024)} %get-tuple-element.2586) | copy-start | bytes 9220 | tf_op jit(solution)/shard_map/while
  2253.4 34.7 %copy-start.49 = (f32[768]{0:T(1024)S(1)}, f32[768]{0:T(1024)}, u32[]{:S(2)}) copy-start(f32[768]{0:T(1024)} %get-tuple-element.2587) | copy-start | bytes 9220 | tf_op jit(solution)/shard_map/while
  2253.4 35.4 %copy-start.37 = (f32[12,2,65]{2,0,1:T(8,128)S(1)}, f32[12,2,65]{2,0,1:T(8,128)}, u32[]{:S(2)}) copy-start(f32[12,2,65]{2,0,1:T(8,128)} %get-tuple-element.2588) | copy-start | bytes 18724 | tf_op jit(solution)/shard_map/while
  2300.7 9.2 copy-start.29
  2309.8 9.6 copy-start.3
  2830.8 10.4 copy-start.4
  2830.8 10.4 copy-start.22
  2830.8 10.4 copy-start.36
  2841.3 8.9 copy-start.25
  2855.8 10.5 slice-start
  2894.2 43.5 %collective-permute-start = (bf16[1152,768]{1,0:T(8,128)(2,1)}, bf16[1152,768]{1,0:T(8,128)(2,1)S(1)}, u32[]{:S(2)}, u32[]{:S(2)}) collective-permute-start(bf16[1152,768]{1,0:T(8,128)(2,1)} %convert_element_type.431), channel_id=1, source_target_pairs={{1,0},{2,1},{3,2},{5,4},{6,5},{7,6},{9,8},{10,9},{11,10},{13,12},{... | collective-permute-start | bytes 5308424 | tf_op jit(solution)/shard_map/while/body/eval_jaxpr/ppermute | solution.py:20
  2895.6 34.7 %copy-start.46 = (f32[768]{0:T(1024)S(1)}, f32[768]{0:T(1024)}, u32[]{:S(2)}) copy-start(f32[768]{0:T(1024)} %get-tuple-element.2586) | copy-start | bytes 9220 | tf_op jit(solution)/shard_map/while
  2895.6 34.7 %copy-start.49 = (f32[768]{0:T(1024)S(1)}, f32[768]{0:T(1024)}, u32[]{:S(2)}) copy-start(f32[768]{0:T(1024)} %get-tuple-element.2587) | copy-start | bytes 9220 | tf_op jit(solution)/shard_map/while
  2895.6 35.4 %copy-start.37 = (f32[12,2,65]{2,0,1:T(8,128)S(1)}, f32[12,2,65]{2,0,1:T(8,128)}, u32[]{:S(2)}) copy-start(f32[12,2,65]{2,0,1:T(8,128)} %get-tuple-element.2588) | copy-start | bytes 18724 | tf_op jit(solution)/shard_map/while
  2946.6 6.6 collective-permute-start.3
  2948.8 127.0 %reduce-scatter.18.cloned.1.call-start = ((), (), s32[]{:S(2)}) async-start(), calls=%async_computation.8 | async-start | bytes 442368
  2949.9 189.7 %reduce-scatter.20.cloned.1.call-start = ((), (), s32[]{:S(2)}) async-start(), calls=%async_computation.9 | async-start | bytes 442368
  2950.8 287.1 %reduce-scatter.14.cloned.1.call-start = ((), (), s32[]{:S(2)}) async-start(), calls=%async_computation.6 | async-start | bytes 5308416 | tf_op jit(solution)/shard_map/reduce_scatter | solution.py:413
  2958.9 446.3 %reduce-scatter.12.cloned.1.call-start = ((), (), s32[]{:S(2)}) async-start(), calls=%async_computation.5 | async-start | bytes 10616832 | tf_op jit(solution)/shard_map/reduce_scatter | solution.py:412
  2968.6 436.6 %copy-start.1 = (f32[2,12,2,65]{3,2,1,0:T(2,128)S(1)}, f32[2,12,2,65]{3,2,1,0:T(2,128)}, u32[]{:S(2)}) copy-start(f32[2,12,2,65]{3,2,1,0:T(2,128)} %param.34) | copy-start | bytes 37444
  (189 other events, 720.2 us)
Sparse Core Ops, SparseCore 0:
  2949.0 63.1 reduce-scatter.15
  3015.5 60.3 reduce-scatter.17
  3079.1 60.3 reduce-scatter.19
  3143.6 94.2 reduce-scatter.13
  3241.9 163.2 reduce-scatter.11
where the time goes:
time: 3430 us; the launch traced here: 3410 us
  matrix products  1220 us (36%)
  waiting for transfers between devices  1070 us (31%)
  local copies, waits for them, and re-layouts  429 us (13%)
  starting transfers between devices  298 us (9%)
  other arithmetic  244 us (7%)
  loops' own time  99.8 us (3%)
  blocking collectives  40.9 us (1%)
    ppermute x12, waiting for transfers between devices, shifted(): return lax.ppermute(block, axis, route)  681 us
    ppermute x12, starting transfers between devices, shifted(): return lax.ppermute(block, axis, route)  298 us
    dot_general x48, matrix products, head_probs(): jnp.dot(jnp.concatenate([along_y, along_x], axis=1), both_onehot.T, preci...  287 us
    dot_general x48, matrix products, one_head(): jnp.dot(probs_low, head_v, preferred_element_type=jnp.float32)  168 us
    reduce_scatter x1, waiting for transfers between devices, local(): lax.psum_scatter(first_total[None], 'dp', scatter_dimension=1, tiled=True)  167 us
    unnamed x8, waiting for transfers between devices  127 us
    dynamic_update_slice x48, local copies, waits for them, and re-layouts, attention_backward(): lax.map(one_head, (queries, key_rows, values, split_heads(d_context, head...  117 us
    another operation x42, local copies, waits for them, and re-layouts  116 us
  transfers between devices with their start and end apart: 17, of which 13 were waited for; matrix products, arithmetic and copies ran while one was open for 4% of the time, Pallas kernels for 0%

commit v1 on v0

v1 whole, which is shorter than its diff:
```python
from functools import partial

import jax
import jax.numpy as jnp
import numpy as np
from jax import lax
from jax.experimental import pallas as pl
from jax.experimental.pallas import tpu as pltpu
from jax.sharding import PartitionSpec as P

SIDE_L = 32
CELLS = SIDE_L + 1
HEAD = 64
PAIR = 2 * HEAD
PAGES = 8
STATIC = 192
LSE_AT = 4 * CELLS + PAGES
MASKED = 1e30
EPSILON = 1e-06
LOG2E = 1.4426950408889634
LN2 = 0.6931471805599453
BF = jnp.bfloat16
F32 = jnp.float32
NT = (((1,), (1,)), ((), ()))
TN = (((0,), (0,)), ((), ()))


def dot(a, b):
    return jnp.dot(a, b, preferred_element_type=F32)


def dot_nt(a, b):
    return lax.dot_general(a, b, NT, preferred_element_type=F32)


def dot_tn(a, b):
    return lax.dot_general(a, b, TN, preferred_element_type=F32)


def geometry(grid_side, row_ids, slot_rows):
    page_len = grid_side * grid_side + 1
    page_count = slot_rows // page_len
    page_of = jnp.minimum(row_ids // page_len, page_count)
    offset = row_ids - page_of * page_len
    patch_id = jnp.maximum(offset - 1, 0)
    inside = page_of < page_count
    class_row = offset == 0
    coord_y = jnp.where(inside, jnp.where(class_row, SIDE_L, patch_id // grid_side), 0)
    coord_x = jnp.where(inside, jnp.where(class_row, SIDE_L, patch_id % grid_side), 0)
    return page_of, coord_y, coord_x


def doubled(cols):
    return jnp.concatenate([cols[..., :HEAD], cols], axis=-1)


def row_features(page_of, coord_y, coord_x):
    lane = jnp.arange(128, dtype=jnp.int32)[None, :]
    hot = (lane == coord_y[:, None]) | (lane == CELLS + coord_x[:, None])
    hot = hot | (lane == 2 * CELLS + page_of[:, None])
    return hot.astype(BF)


def key_features(page_of, coord_y, coord_x):
    lane = jnp.arange(STATIC, dtype=jnp.int32)[None, :]
    at_y = SIDE_L - coord_y[:, None]
    at_x = SIDE_L - coord_x[:, None] + CELLS
    hot = (lane == at_y) | (lane == at_x)
    hot = hot | (lane == at_y + 2 * CELLS) | (lane == at_x + 2 * CELLS)
    hot = hot | (lane == 4 * CELLS + page_of[:, None])
    hot = hot | ((lane >= LSE_AT) & (lane < LSE_AT + 3))
    return doubled(hot.astype(BF))


def table_maps(rel_table):
    layers, heads = rel_table.shape[:2]
    scaled = rel_table * LOG2E
    hankel = jnp.stack([scaled[..., a : a + CELLS] for a in range(CELLS)], axis=-2)
    high = hankel.astype(BF)
    rest = (hankel - high.astype(F32)).astype(BF)
    none = jnp.zeros((layers, heads, CELLS, CELLS), BF)
    far = np.zeros((PAGES, PAGES), np.float32)
    far[:] = -MASKED
    np.fill_diagonal(far, 0.0)
    y_rows = jnp.concatenate([high[:, :, 0], none, rest[:, :, 0], none], axis=-1)
    x_rows = jnp.concatenate([none, high[:, :, 1], none, rest[:, :, 1]], axis=-1)
    grid_rows = jnp.concatenate([y_rows, x_rows], axis=-2)
    grid_rows = jnp.pad(grid_rows, ((0, 0), (0, 0), (0, 128 - 2 * CELLS), (0, STATIC - 4 * CELLS)))
    page_rows = np.zeros((128, STATIC), np.float32)
    page_rows[2 * CELLS : 2 * CELLS + PAGES, 4 * CELLS : 4 * CELLS + PAGES] = far
    return doubled(grid_rows + jnp.asarray(page_rows, BF))


def split3(value):
    high = value.astype(BF).astype(F32)
    middle = (value - high).astype(BF).astype(F32)
    return high, middle, value - high - middle


def lanes_of(rows):
    return lax.broadcasted_iota(jnp.int32, (rows, PAIR), 1)


def attn_fwd_kernel(hot_ref, map_ref, q_ref, ko_ref, kp_ref, vo_ref, vp_ref, key_ref, o_ref, qx_ref, kx_ref, vx_ref):
    rows = q_ref.shape[0]
    chunk = rows // 3
    kx_ref[:, PAIR:] = key_ref[:, PAIR:]
    lane_k = lanes_of(rows)
    lane_c = lanes_of(chunk)
    outs = []
    for head in range(2):
        mine_k = (lane_k < HEAD) if head == 0 else (lane_k >= HEAD)
        one_at = HEAD if head == 0 else 0
        for part, (k_ref, v_ref) in enumerate(((ko_ref, vo_ref), (kp_ref, vp_ref))):
            at = pl.ds(part * rows, rows)
            kx_ref[at, :PAIR] = jnp.where(mine_k, k_ref[...], key_ref[at, :PAIR])
            vx_ref[at, :] = jnp.where(mine_k, v_ref[...], jnp.where(lane_k == one_at, 1.0, 0.0).astype(BF))
        for c in range(3):
            at = pl.ds(c * chunk, chunk)
            mine = (lane_c < HEAD) if head == 0 else (lane_c >= HEAD)
            feats = dot(hot_ref[at, :], map_ref[head])
            left = jnp.where(mine, q_ref[at, :].astype(F32), feats[:, :PAIR]).astype(BF)
            right = feats[:, PAIR:]
            query = jnp.concatenate([left, right.astype(BF)], axis=1)
            scores = dot_nt(query, kx_ref[...])
            top = jnp.max(scores, axis=1, keepdims=True)
            weights = jnp.exp2(scores - top).astype(BF)
            mixed = dot(weights, vx_ref[...])
            total = mixed[:, one_at : one_at + 1]
            lse = top + jnp.log2(total)
            high, middle, low = split3(lse)
            spot = lane_c - (LSE_AT - HEAD)
            right = jnp.where(spot == 0, -high, jnp.where(spot == 1, -middle, jnp.where(spot == 2, -low, right)))
            qx_ref[head, at, :PAIR] = left
            qx_ref[head, at, PAIR:] = right.astype(BF)
            out = mixed / total
            if head == 0:
                outs.append(out)
            else:
                o_ref[at, :] = jnp.where(mine, out, outs[c]).astype(BF)


def attn_forward(hot, maps, project, partner, keys):
    rows, width = project.shape[0], project.shape[1] // 3
    pairs = width // PAIR
    col = lambda off: pl.BlockSpec((rows, PAIR), lambda g: (0, off + g))
    whole = lambda shape: pl.BlockSpec(shape, lambda g: (0,) * len(shape))
    return pl.pallas_call(
        attn_fwd_kernel,
        grid=(pairs,),
        in_specs=[
            whole((rows, 128)),
            pl.BlockSpec((2, 128, 256), lambda g: (g, 0, 0)),
            col(0),
            col(pairs),
            col(0),
            col(2 * pairs),
            col(pairs),
            whole((2 * rows, 256)),
        ],
        out_specs=[col(0), pl.BlockSpec((2, rows, 256), lambda g: (g, 0, 0))],
        out_shape=[
            jax.ShapeDtypeStruct((rows, width), BF),
            jax.ShapeDtypeStruct((2 * pairs, rows, 256), BF),
        ],
        scratch_shapes=[pltpu.VMEM((2 * rows, 256), BF), pltpu.VMEM((2 * rows, PAIR), BF)],
        compiler_params=pltpu.CompilerParams(vmem_limit_bytes=48 * 2**20),
        cost_estimate=pl.CostEstimate(flops=int(8e9), bytes_accessed=int(1e7), transcendentals=0),
        name="attn_fwd",
    )(hot, maps, project, project, partner, project, partner, keys)


def attn_bwd_kernel(hot_ref, qx_ref, q_ref, ko_ref, kp_ref, vo_ref, vp_ref, key_ref, do_ref, o_ref,
                    dq_ref, dk_ref, dv_ref, gt_ref, kx_ref, vx_ref, ds_ref):
    rows = q_ref.shape[0]
    chunk = rows // 2
    kx_ref[:, PAIR:] = key_ref[:, PAIR:]
    lane = lanes_of(rows)
    lane_c = lanes_of(chunk)
    product = do_ref[...].astype(F32) * o_ref[...].astype(F32)
    dq_halves = []
    for head in range(2):
        mine = (lane < HEAD) if head == 0 else (lane >= HEAD)
        mine_c = (lane_c < HEAD) if head == 0 else (lane_c >= HEAD)
        one_at = HEAD if head == 0 else 0
        spot = lane - one_at
        for part, (k_ref, v_ref) in enumerate(((ko_ref, vo_ref), (kp_ref, vp_ref))):
            at = pl.ds(part * rows, rows)
            kx_ref[at, :PAIR] = jnp.where(mine, k_ref[...], key_ref[at, :PAIR])
            ones = jnp.where((spot >= 0) & (spot < 3), 1.0, 0.0).astype(BF)
            vx_ref[at, :] = jnp.where(mine, v_ref[...], ones)
        delta = jnp.sum(jnp.where(mine, product, 0.0), axis=1, keepdims=True)
        high, middle, low = split3(delta)
        spread = jnp.where(spot == 0, -high, jnp.where(spot == 1, -middle, jnp.where(spot == 2, -low, 0.0)))
        d_out = jnp.where(mine, do_ref[...].astype(F32), spread).astype(BF)
        for c in range(4):
            at = pl.ds(c * chunk, chunk)
            part = c // 2
            inner = pl.ds((c % 2) * chunk, chunk)
            probs = jnp.exp2(dot_nt(kx_ref[at, :], qx_ref[head]))
            d_probs = dot_nt(vx_ref[at, :], d_out)
            d_scores = (probs * d_probs).astype(BF)
            ds_ref[at, :] = d_scores
            d_value = dot(probs.astype(BF), do_ref[...])
            d_key = dot(d_scores, q_ref[...]) * LN2
            if head == 0:
                dv_ref[part, inner, :] = d_value.astype(BF)
                dk_ref[part, inner, :] = d_key.astype(BF)
            else:
                dv_ref[part, inner, :] = jnp.where(mine_c, d_value, dv_ref[part, inner, :].astype(F32)).astype(BF)
                dk_ref[part, inner, :] = jnp.where(mine_c, d_key, dk_ref[part, inner, :].astype(F32)).astype(BF)
        d_query = dot_tn(ds_ref[...], kx_ref[...])
        high_q = d_query.astype(BF)
        low_q = (d_query - high_q.astype(F32)).astype(BF)
        gt_ref[head] = dot_tn(hot_ref[...], high_q) + dot_tn(hot_ref[...], low_q)
        dq_halves.append(d_query[:, :PAIR])
    dq_ref[...] = (jnp.where(lane < HEAD, dq_halves[0], dq_halves[1]) * HEAD**-0.5).astype(BF)


def attn_backward(hot, queries, project, partner, keys, d_context, context):
    rows, width = project.shape[0], project.shape[1] // 3
    pairs = width // PAIR
    col = lambda off: pl.BlockSpec((rows, PAIR), lambda g: (0, off + g))
    both = pl.BlockSpec((2, rows, PAIR), lambda g: (0, 0, g))
    whole = lambda shape: pl.BlockSpec(shape, lambda g: (0,) * len(shape))
    return pl.pallas_call(
        attn_bwd_kernel,
        grid=(pairs,),
        in_specs=[
            whole((rows, 128)),
            pl.BlockSpec((2, rows, 256), lambda g: (g, 0, 0)),
            col(0),
            col(pairs),
            col(0),
            col(2 * pairs),
            col(pairs),
            whole((2 * rows, 256)),
            col(0),
            col(0),
        ],
        out_specs=[col(0), both, both, pl.BlockSpec((2, 128, 256), lambda g: (g, 0, 0))],
        out_shape=[
            jax.ShapeDtypeStruct((rows, width), BF),
            jax.ShapeDtypeStruct((2, rows, width), BF),
            jax.ShapeDtypeStruct((2, rows, width), BF),
            jax.ShapeDtypeStruct((2 * pairs, 128, 256), F32),
        ],
        scratch_shapes=[
            pltpu.VMEM((2 * rows, 256), BF),
            pltpu.VMEM((2 * rows, PAIR), BF),
            pltpu.VMEM((2 * rows, rows), BF),
        ],
        compiler_params=pltpu.CompilerParams(vmem_limit_bytes=48 * 2**20),
        cost_estimate=pl.CostEstimate(flops=int(20e9), bytes_accessed=int(2e7), transcendentals=0),
        name="attn_bwd",
    )(hot, queries, project, project, partner, project, partner, keys, d_context, context)


def layer_norm(row_vals, gain_vec, shift_vec):
    row_mean = jnp.mean(row_vals, axis=-1, keepdims=True)
    centered = row_vals - row_mean
    variance = jnp.mean(centered * centered, axis=-1, keepdims=True)
    return centered * lax.rsqrt(variance + EPSILON) * gain_vec + shift_vec


def layer_norm_back(row_vals, gain_vec, d_normed, grad_out):
    row_mean = jnp.mean(row_vals, axis=-1, keepdims=True)
    centered = row_vals - row_mean
    variance = jnp.mean(centered * centered, axis=-1, keepdims=True)
    scale = lax.rsqrt(variance + EPSILON)
    nhat = centered * scale
    inner = d_normed * gain_vec
    d_in = scale * (
        inner
        - jnp.mean(inner, axis=-1, keepdims=True)
        - nhat * jnp.mean(inner * nhat, axis=-1, keepdims=True)
    )
    return grad_out + d_in, jnp.sum(nhat * d_normed, axis=0), jnp.sum(d_normed, axis=0)


def local(
    inputs, out_grad, page_side, norm_gain, norm_shift, layer_scale, w_first, w_half, rel_table
):
    place = lax.axis_index("pipe")
    sections = lax.axis_size("pipe")
    micro_count, slot_rows, width = inputs.shape
    halves = sections // micro_count
    assert halves == 2
    rows = slot_rows // halves
    micro, half = place // halves, place % halves
    swap = [(i, i ^ 1) for i in range(sections)]
    layers, heads = rel_table.shape[:2]

    first_all = lax.all_gather(w_first[0], "pipe")
    half_all = lax.all_gather(w_half[0], "pipe")
    params = lax.all_gather(jnp.stack([norm_gain[0], norm_shift[0], layer_scale[0]]), "pipe")

    side = lax.dynamic_index_in_dim(page_side, micro, 0, keepdims=False)[0]
    own_rows = lambda x: lax.dynamic_slice(x, (micro, half * rows, 0), (1, rows, width))[0]
    key_ids = (jnp.arange(slot_rows, dtype=jnp.int32) + half * rows) % slot_rows
    layout = geometry(side, key_ids, slot_rows)
    hot = row_features(*(c[:rows] for c in layout))
    keys = key_features(*layout)
    maps = table_maps(rel_table)

    current = own_rows(inputs)
    kept, outs = [], []
    for s in range(sections):
        gain, shift, scale = params[s, 0], params[s, 1], params[s, 2]
        in_float = current.astype(F32)
        normed = layer_norm(in_float, gain, shift).astype(BF)
        if s % 2 == 0:
            q_scale = np.ones((3 * width,), np.float32)
            q_scale[:width] = HEAD**-0.5 * LOG2E
            project = (dot(normed, first_all[s][:, : 3 * width]) * q_scale).astype(BF)
            partner = lax.ppermute(project[:, width:], "pipe", swap)
            context, queries = attn_forward(hot, maps[s // 2], project, partner, keys)
            branch = dot(context, first_all[s][:, 3 * width :])
            kept.append((current, normed, project, partner, context, queries, branch.astype(BF)))
        else:
            down = half_all[s - 1 : s + 1].reshape(-1, width)
            pre = dot(normed, first_all[s])
            hidden = jax.nn.gelu(pre, approximate=True).astype(BF)
            branch = dot(hidden, down)
            kept.append((current, normed, pre.astype(BF), hidden, branch.astype(BF)))
        current = (in_float + scale * branch).astype(BF)
        outs.append(current)

    grad = own_rows(out_grad)
    grads, first_grads, half_grads, vecs, tables = {}, {}, {}, {}, {}
    for s in reversed(range(sections)):
        gain, shift, scale = params[s, 0], params[s, 1], params[s, 2]
        gy = grad.astype(F32)
        d_branch = (gy * scale).astype(BF)
        if s % 2 == 0:
            section_in, normed, project, partner, context, queries, branch = kept[s]
            d_context = dot_nt(d_branch, first_all[s][:, 3 * width :]).astype(BF)
            dq, dk, dv, table = attn_backward(hot, queries, project, partner, keys, d_context, context)
            got_k, got_v = lax.ppermute((dk[1], dv[1]), "pipe", swap)
            d_project = jnp.concatenate([dq, dk[0] + got_k, dv[0] + got_v], axis=1)
            d_normed = dot_nt(d_project, first_all[s][:, : 3 * width])
            first_grads[s] = jnp.concatenate(
                [dot_tn(normed, d_project), dot_tn(context, d_branch)], axis=1
            ).astype(BF)
            tables[s // 2] = table
        else:
            section_in, normed, pre, hidden, branch = kept[s]
            down = half_all[s - 1 : s + 1].reshape(-1, width)
            d_hidden = dot_nt(d_branch, down)
            d_pre = jax.vjp(partial(jax.nn.gelu, approximate=True), pre.astype(F32))[1](d_hidden)[0].astype(BF)
            d_normed = dot_nt(d_pre, first_all[s])
            first_grads[s] = dot_tn(normed, d_pre).astype(BF)
            d_down = dot_tn(hidden, d_branch).astype(BF)
            half_grads[s - 1], half_grads[s] = jnp.split(d_down, 2, axis=0)
        d_in, g_gain, g_shift = layer_norm_back(section_in.astype(F32), gain, d_normed, gy)
        g_scale = jnp.sum(branch.astype(F32) * gy, axis=0)
        vecs[s] = jnp.stack([g_gain, g_shift, g_scale])
        grad = d_in.astype(BF)
        grads[s] = grad

    def spread(parts):
        return lax.all_to_all(jnp.stack([parts[s] for s in range(sections)]), "pipe", 0, 0)

    both = ("pipe", "dp")
    section_out = spread(outs).reshape(1, micro_count, slot_rows, width)
    in_grads = spread(grads).astype(F32).reshape(1, micro_count, slot_rows, width)
    stack = lambda parts: jnp.stack([parts[s] for s in range(sections)])
    g_first = lax.psum_scatter(stack(first_grads), "pipe", scatter_dimension=0, tiled=True)
    g_half = lax.psum_scatter(stack(half_grads), "pipe", scatter_dimension=0, tiled=True)
    g_first = lax.psum_scatter(g_first, "dp", scatter_dimension=1, tiled=True).astype(F32)
    g_half = lax.psum_scatter(g_half, "dp", scatter_dimension=1, tiled=True).astype(F32)
    pairs = np.zeros((CELLS, CELLS, 2 * SIDE_L + 1), np.float32)
    for a in range(CELLS):
        for b in range(CELLS):
            pairs[a, b, a + b] = 1.0
    table_all = []
    for layer in range(layers):
        raw = tables[layer]
        even = jnp.concatenate([raw[0::2, :, HEAD:PAIR], raw[0::2, :, PAIR:]], axis=2)
        odd = jnp.concatenate([raw[1::2, :, :HEAD], raw[1::2, :, PAIR:]], axis=2)
        cols = jnp.stack([even, odd], axis=1).reshape(heads, 128, STATIC)
        grids = jnp.stack([cols[:, :CELLS, :CELLS], cols[:, CELLS : 2 * CELLS, CELLS : 2 * CELLS]], axis=1)
        table_all.append(jnp.einsum("hcab,abt->hct", grids, pairs, precision=lax.Precision.HIGHEST))
    small = jnp.concatenate([stack(vecs).reshape(-1), jnp.stack(table_all).reshape(-1)])
    small = lax.psum(small, ("dp", "pipe"))
    vec_size = sections * 3 * width
    vec_all = small[:vec_size].reshape(sections, 3, width)
    g_table = small[vec_size:].reshape(rel_table.shape)
    share = width // lax.axis_size("dp")
    mine = lax.dynamic_slice(vec_all, (place, 0, lax.axis_index("dp") * share), (1, 3, share))
    return (section_out, in_grads, g_first, g_half, mine[:, 0], mine[:, 1], mine[:, 2], g_table)


def solution(mesh):
    in_specs = (
        P(None, "dp", None),
        P(None, "dp", None),
        P(None, "dp"),
        P("pipe", None),
        P("pipe", None),
        P("pipe", None),
        P("pipe", None, None),
        P("pipe", None, None),
        P(),
    )
    out_specs = (
        P("pipe", None, "dp", None),
        P("pipe", None, "dp", None),
        P("pipe", "dp", None),
        P("pipe", "dp", None),
        P("pipe", "dp"),
        P("pipe", "dp"),
        P("pipe", "dp"),
        P(),
    )
    return jax.shard_map(local, mesh=mesh, in_specs=in_specs, out_specs=out_specs, check_vma=False)
```

time: 3430 us -> 822 us (0.24)
  matrix products: 1220 us -> 116 us
  waiting for transfers between devices: 1070 us -> 351 us
  local copies, waits for them, and re-layouts: 429 us -> 50.4 us
  starting transfers between devices: 298 us -> 11.8 us
  other arithmetic: 244 us -> 52.9 us
  Pallas kernels: 0 us -> 132 us
  loops' own time: 99.8 us -> 0 us
  blocking collectives: 40.9 us -> 78.9 us
    dot_general x449 -> x26, matrix products: 1220 us -> 116 us  [the longest x8 43.5 us: dot_nt(): return lax.dot_general(a, b, NT, preferred_element_type=F32)]
    ppermute x12 -> x6, waiting for transfers between devices: 681 us -> 5.92 us  [the longest x2 3.44 us: local(): partner = lax.ppermute(project[:, width:], 'pipe', swap)]
    ppermute x12 -> x6, starting transfers between devices: 298 us -> 1.81 us  [the longest x4 1.16 us: local(): got_k, got_v = lax.ppermute((dk[1], dv[1]), 'pipe', swap)]
    all_gather x0 -> x2, waiting for transfers between devices: none -> 150 us  [the longest x1 98.4 us: local(): first_all = lax.all_gather(w_first[0], 'pipe')]
    pallas_call x0 -> x4, Pallas kernels: none -> 132 us  [the longest x2 76 us: attn_backward(): pl.pallas_call(attn_bwd_kernel, grid=(pairs,), in_specs=[whole((rows, 128...]
    unnamed x8 -> x6, waiting for transfers between devices: 127 us -> 1.93 us
    dynamic_update_slice x48 -> x0, local copies, waits for them, and re-layouts: 117 us -> none  [attention_backward(): lax.map(one_head, (queries, key_rows, values, split_heads(d_context, head...]
    another operation x42 -> x22, local copies, waits for them, and re-layouts: 116 us -> 9.81 us
  transfers between devices with their start and end apart: 17 -> 14, of which waited for: 13 -> 8; matrix products, arithmetic and copies ran while one was open for 4% -> 17% of each run, Pallas kernels for 0% -> 5%
where the time goes in v1:
time: 822 us; the launch traced here: 813 us
  waiting for transfers between devices  351 us (43%)
  Pallas kernels  132 us (16%)
  matrix products  116 us (14%)
  blocking collectives  78.9 us (10%)
  other arithmetic  52.9 us (6%)
  local copies, waits for them, and re-layouts  50.4 us (6%)
  between operations  20 us (2%)
  starting transfers between devices  11.8 us (1%)
    reduce_scatter x1, waiting for transfers between devices, local(): lax.psum_scatter(stack(first_grads), 'pipe', scatter_dimension=0, tiled=T...  140 us
    all_gather x1, waiting for transfers between devices, local(): first_all = lax.all_gather(w_first[0], 'pipe')  98.4 us
    pallas_call x2, Pallas kernels, attn_backward(): pl.pallas_call(attn_bwd_kernel, grid=(pairs,), in_specs=[whole((rows, 128...  76 us
    psum x1, blocking collectives, local(): small = lax.psum(small, ('dp', 'pipe'))  72.7 us
    pallas_call x2, Pallas kernels, attn_forward(): pl.pallas_call(attn_fwd_kernel, grid=(pairs,), in_specs=[whole((rows, 128...  55.9 us
    all_gather x1, waiting for transfers between devices, local(): half_all = lax.all_gather(w_half[0], 'pipe')  51.5 us
    dot_general x8, matrix products, dot_nt(): return lax.dot_general(a, b, NT, preferred_element_type=F32)  43.5 us
    dot_general x8, matrix products, dot_tn(): return lax.dot_general(a, b, TN, preferred_element_type=F32)  40.8 us
  transfers between devices with their start and end apart: 14, of which 8 were waited for; matrix products, arithmetic and copies ran while one was open for 17% of the time, Pallas kernels for 5%

profile of v1, /device:TPU:0, one launch (start us, length us, event | category | flops | bytes accessed | tf_op | source)
XLA Modules:
  0.0 812.9 jit_solution(4088301971646831974)
XLA Ops:
  25.5 6.2 all-gather.1
  34.2 98.4 %all-gather.5.cloned.1.call-done = bf16[4,768,3072]{2,1,0:T(8,128)(2,1)} async-done(((bf16[1,768,3072]{2,1,0:T(8,128)(2,1)}), bf16[4,768,3072]{2,1,0:T(8,128)(2,1)}) %all-gather.5.cloned.1.call-update) | async-done | bytes 18874384 | tf_op jit(solution)/shard_map/all_gather | solution.py:294
  132.7 6.8 slice_bitcast_fusion.3
  139.5 2.4 multiply_convert_fusion.1.q_ref.ko_ref.vo_ref
  146.9 51.5 %all-gather.7.cloned.1.call-done = bf16[4,1536,768]{2,1,0:T(8,128)(2,1)} async-done(((bf16[1,1536,768]{2,1,0:T(8,128)(2,1)}), bf16[4,1536,768]{2,1,0:T(8,128)(2,1)}) %all-gather.7.cloned.1.call-update) | async-done | bytes 9437200 | tf_op jit(solution)/shard_map/all_gather | solution.py:295
  198.5 6.6 fusion.230
  205.1 28.2 %attn_fwd.2 = (bf16[576,768]{1,0:T(8,128)(2,1)S(1)}, bf16[12,576,256]{2,1,0:T(8,128)(2,1)}) custom-call(bf16[576,128]{1,0:T(8,128)(2,1)S(1)} %fusion.191.hot_ref, bf16[12,128,256]{2,1,0:T(8,128)(2,1)S(1)} %get-tuple-element.84.map_ref, bf16[576,2304]{1,0:T(8,128)(2,1)} %copy-done.39, bf16[576,2304]{1,0:T(8,128)(2,1)} %copy-done.39, ...), custom_call_target="tpu_custom_call" | custom-call | flops 8000000000 | bytes 10000000 | tf_op jit(solution)/shard_map/attn_fwd/pallas_call | solution.py:148
  233.3 3.7 convert_reduce_fusion.2
  237.4 5.1 fusion.39
  242.7 5.1 convert_reduce_fusion.1
  248.3 2.4 multiply_convert_fusion.q_ref.ko_ref.vo_ref
  251.2 3.4 collective-permute-done.1.kp_ref.vp_ref
  254.7 27.7 %attn_fwd.3 = (bf16[576,768]{1,0:T(8,128)(2,1)S(1)}, bf16[12,576,256]{2,1,0:T(8,128)(2,1)}) custom-call(bf16[576,128]{1,0:T(8,128)(2,1)S(1)} %fusion.191.hot_ref, bf16[12,128,256]{2,1,0:T(8,128)(2,1)S(1)} %get-tuple-element.85.map_ref, bf16[576,2304]{1,0:T(8,128)(2,1)} %copy-done.40, bf16[576,2304]{1,0:T(8,128)(2,1)} %copy-done.40, ...), custom_call_target="tpu_custom_call" | custom-call | flops 8000000000 | bytes 10000000 | tf_op jit(solution)/shard_map/attn_fwd/pallas_call | solution.py:148
  283.9 5.3 fusion.41
  289.2 4.2 fusion.219
  293.5 8.1 %fusion.7 = bf16[576,3072]{1,0:T(8,128)(2,1)} fusion(f32[576,3072]{1,0:T(8,128)S(1)} %fusion.41, bf16[3072,768]{1,0:T(8,128)(2,1)S(1)} %bitcast.286, f32[768]{0:T(1024)S(1)} %copy-done.57, bf16[2,1152,768]{2,1,0:T(8,128)(2,1)S(1)} %copy-done.47, s32[]{:T(128)S(6)} %select_n.142, s32[]{:T(128)S(6)} %select_n.144), kind=kOutput, calls=%fused_computation.19 | convolution fusion | flops 2758164480 | bytes 16224264 | tf_op jit(solution)/shard_map/dot_general | solution.py:33
  301.6 5.7 convolution_convert_fusion.2
  307.4 7.4 fusion.91
  314.7 2.8 fusion.124
  318.5 38.1 %attn_bwd.2 = (bf16[576,768]{1,0:T(8,128)(2,1)S(1)}, bf16[2,576,768]{2,1,0:T(8,128)(2,1)}, bf16[2,576,768]{2,1,0:T(8,128)(2,1)}, f32[12,128,256]{2,1,0:T(8,128)S(1)}) custom-call(bf16[576,128]{1,0:T(8,128)(2,1)S(1)} %fusion.191.hot_ref, bf16[12,576,256]{2,1,0:T(8,128)(2,1)} %get-tuple-element.22.qx_ref, bf16[576,2304]{1,0:T(8,128)(2,1)} %copy-done.40, ...), custom_call_target="tpu_custom_call" | custom-call | flops 20000000000 | bytes 20000000 | tf_op jit(solution)/shard_map/attn_bwd/pallas_call | solution.py:226
  362.1 2.7 fusion.98
  365.8 5.6 convolution_convert_fusion.3
  371.8 4.6 pad_maximum_fusion.1
  376.5 3.3 convolution_convert_fusion.6
  379.8 2.6 copy.1866
  382.5 8.0 fusion.35
  390.5 10.4 %fusion.4 = bf16[576,3072]{1,0:T(8,128)(2,1)S(1)} fusion(f32[576,3072]{1,0:T(8,128)} %copy-done.86, bf16[3072,768]{1,0:T(8,128)(2,1)} %bitcast.278, bf16[576,768]{1,0:T(8,128)(2,1)S(1)} %copy-done.21, f32[768]{0:T(1024)S(1)} %copy-done.79), kind=kOutput, calls=%fused_computation.16 | convolution fusion | flops 2758164480 | bytes 16223232 | tf_op jit(solution)/shard_map/dot_general | solution.py:33
  401.0 6.0 fusion.105
  408.0 2.5 convolution_convert_fusion.8.do_ref
  410.6 37.9 %attn_bwd.3 = (bf16[576,768]{1,0:T(8,128)(2,1)S(1)}, bf16[2,576,768]{2,1,0:T(8,128)(2,1)}, bf16[2,576,768]{2,1,0:T(8,128)(2,1)}, f32[12,128,256]{2,1,0:T(8,128)S(1)}) custom-call(bf16[576,128]{1,0:T(8,128)(2,1)S(1)} %fusion.191.hot_ref, bf16[12,576,256]{2,1,0:T(8,128)(2,1)} %get-tuple-element.26.qx_ref, bf16[576,2304]{1,0:T(8,128)(2,1)} %copy-done.39, ...), custom_call_target="tpu_custom_call" | custom-call | flops 20000000000 | bytes 20000000 | tf_op jit(solution)/shard_map/attn_bwd/pallas_call | solution.py:226
  448.5 2.5 slice_bitcast_fusion.12
  451.2 6.0 fusion.34
  458.5 2.2 convolution_convert_fusion.7
  460.6 2.6 copy.1865
  463.3 5.2 fusion.37
  471.9 4.7 fusion.36
  476.8 9.6 %pad_maximum_fusion = bf16[4,768,3072]{2,1,0:T(8,128)(2,1)} fusion(bf16[1,768,3072]{2,1,0:T(8,128)(2,1)S(1)} %bitcast.272, bf16[1,768,768]{2,1,0:T(8,128)(2,1)S(1)} %bitcast.275, bf16[1,768,2304]{2,1,0:T(8,128)(2,1)S(1)} %fusion.37, bf16[1,768,3072]{2,1,0:T(8,128)(2,1)S(1)} %bitcast.274, bf16[1,768,768]{2,1,0:T(8,128)(2,1)S(1)} %bitcast.276, ...), kind=kLoop, calls=%fused_computation | loop fusion | flops 113246208 | bytes 37748736 | tf_op jit(solution)/shard_map/stack | solution.py:367
  487.0 140.0 %reduce-scatter.5.cloned.1.call-done = bf16[1,768,3072]{2,1,0:T(8,128)(2,1)} async-done(((bf16[4,768,3072]{2,1,0:T(8,128)(2,1)}), bf16[1,768,3072]{2,1,0:T(8,128)(2,1)}) %reduce-scatter.5.cloned.1.call-update) | async-done | bytes 4718608 | tf_op jit(solution)/shard_map/reduce_scatter | solution.py:368
  627.0 3.4 pad_maximum_fusion.2
  630.4 5.0 all-to-all-start
  645.1 5.5 fusion.112
  654.8 21.9 %all-to-all-done = bf16[4,576,768]{2,1,0:T(8,128)(2,1)} async-done(((bf16[4,576,768]{2,1,0:T(8,128)(2,1)}), bf16[4,576,768]{2,1,0:T(8,128)(2,1)}, u32[]{:S(2)}, u32[]{:S(2)}) %all-to-all-start) | async-done | bytes 3538976 | tf_op jit(solution)/shard_map/all_to_all | solution.py:362
  676.7 4.7 all-to-all-start.1
  686.9 72.7 %psum.7 = f32[12336]{0:T(1024)S(1)} all-reduce(f32[12336]{0:T(1024)S(1)} %pad_maximum_fusion.14), channel_id=1, replica_groups=mesh['dp'=8,'pipe'=4] {'dp','pipe'}, use_global_device_ids=true, to_apply=%region_32.33 | all-reduce | flops 12336 | bytes 98688 | tf_op jit(solution)/shard_map/psum | solution.py:385
  761.0 5.6 convert.22
  768.4 30.9 %reduce-scatter.7.cloned.1.call-done = bf16[1,96,3072]{2,1,0:T(8,128)(2,1)} async-done(((bf16[1,768,3072]{2,1,0:T(8,128)(2,1)}), bf16[1,96,3072]{2,1,0:T(8,128)(2,1)}) %reduce-scatter.7.cloned.1.call-update) | async-done | bytes 589840 | tf_op jit(solution)/shard_map/reduce_scatter | solution.py:370
  799.3 2.2 convert_element_type.249
  801.5 4.0 copy.1950
  (379 shorter events, 61.1 us)
Async XLA Ops:
  7.2 125.5 %all-gather.5.cloned.1.call-start = ((), (), s32[]{:S(2)}) async-start(), calls=%async_computation.6 | async-start | bytes 23592960 | tf_op jit(solution)/shard_map/all_gather | solution.py:294
  7.9 10.3 %copy-start.53 = (f32[2,12,2,65]{3,2,1,0:T(2,128)S(1)}, f32[2,12,2,65]{3,2,1,0:T(2,128)}, u32[]{:S(2)}) copy-start(f32[2,12,2,65]{3,2,1,0:T(2,128)} %param.22) | copy-start | bytes 37444
  7.9 190.5 %all-gather.7.cloned.1.call-start = ((), (), s32[]{:S(2)}) async-start(), calls=%async_computation.7 | async-start | bytes 11796480 | tf_op jit(solution)/shard_map/all_gather | solution.py:295
  8.7 477.7 %reduce-scatter.9.cloned.1.call-start = ((), (), s32[]{:S(2)}) async-start(), calls=%async_computation.10 | async-start | bytes 11796480 | tf_op jit(solution)/shard_map/reduce_scatter | solution.py:369
  20.8 10.9 %copy-start.33 = (bf16[2,1152,768]{2,1,0:T(8,128)(2,1)S(1)}, bf16[2,1152,768]{2,1,0:T(8,128)(2,1)}, u32[]{:S(2)}) copy-start(bf16[2,1152,768]{2,1,0:T(8,128)(2,1)} %param.14) | copy-start | bytes 10616836
  32.6 106.8 %copy-start.49 = (f32[576]{0:T(1024)}, f32[576]{0:T(1024)S(1)}, u32[]{:S(2)}) copy-start(f32[576]{0:T(1024)S(1)} %broadcast_multiply_fusion.12) | copy-start | bytes 6916
  34.2 105.2 %copy-start.60 = (f32[576]{0:T(1024)S(1)}, f32[576]{0:T(1024)}, u32[]{:S(2)}) copy-start(f32[576]{0:T(1024)} %add_rsqrt_fusion.3) | copy-start | bytes 6916
  34.2 105.2 %copy-start.64 = (f32[768]{0:T(1024)S(1)}, f32[768]{0:T(1024)}, u32[]{:S(2)}) copy-start(f32[768]{0:T(1024)} %get-tuple-element.57) | copy-start | bytes 9220
  132.7 6.8 copy-start.71
  132.7 6.8 copy-start.84
  144.4 60.7 %collective-permute-start = (bf16[576,1536]{1,0:T(8,128)(2,1)}, bf16[576,1536]{1,0:T(8,128)(2,1)}, u32[]{:S(2)}, u32[]{:S(2)}) collective-permute-start(bf16[576,1536]{1,0:T(8,128)(2,1)} %slice.442), channel_id=1, source_target_pairs={{0,1},{1,0},{2,3},{3,2},{4,5},{5,4},{6,7},{7,6},{8,9},{9,8},{10,11... | collective-permute-start | bytes 5308424 | tf_op jit(solution)/shard_map/ppermute | solution.py:316
  146.9 171.6 %copy-start.2 = (bf16[1152,256]{1,0:T(8,128)(2,1)}, bf16[1152,256]{1,0:T(8,128)(2,1)S(1)}, u32[]{:S(2)}) copy-start(bf16[1152,256]{1,0:T(8,128)(2,1)S(1)} %pad_maximum_fusion.13.key_ref) | copy-start | bytes 1769476
  205.0 37.6 %copy-start.28 = (bf16[2,1536,768]{2,1,0:T(8,128)(2,1)}, bf16[2,1536,768]{2,1,0:T(8,128)(2,1)S(1)}, u32[]{:S(2)}) copy-start(bf16[2,1536,768]{2,1,0:T(8,128)(2,1)S(1)} %get-tuple-element.76) | copy-start | bytes 14155780
  205.1 28.2 %copy-start.75 = (f32[768]{0:T(1024)S(1)}, f32[768]{0:T(1024)}, u32[]{:S(2)}) copy-start(f32[768]{0:T(1024)} %get-tuple-element.58) | copy-start | bytes 9220
  237.0 5.7 copy-start.17
  237.0 5.6 copy-start.51
  237.4 10.8 %slice-start.4 = ((s8[4718592]{0:T(1024)(128)(4,1)}), s8[4194304]{0:T(1024)(128)(4,1)S(1)}, s32[]{:S(2)}) async-start(s8[4718592]{0:T(1024)(128)(4,1)} %bitcast.279), calls=%async_computation.16 | async-start | bytes 8388608
  242.7 5.6 slice-start.5
  247.8 117.0 %copy-start.19 = (bf16[576,768]{1,0:T(8,128)(2,1)}, bf16[576,768]{1,0:T(8,128)(2,1)S(1)}, u32[]{:S(2)}) copy-start(bf16[576,768]{1,0:T(8,128)(2,1)S(1)} %get-tuple-element.69) | copy-start | bytes 2654212
  250.8 31.6 %slice-start.6 = ((s8[4718592]{0:T(1024)(128)(4,1)}), s8[4194304]{0:T(1024)(128)(4,1)S(1)}, s32[]{:S(2)}) async-start(s8[4718592]{0:T(1024)(128)(4,1)} %bitcast.281), calls=%async_computation.18 | async-start | bytes 8388608
  250.9 3.8 collective-permute-start.1
  254.7 27.7 %copy-start.4 = (bf16[576,1536]{1,0:T(8,128)(2,1)}, bf16[576,1536]{1,0:T(8,128)(2,1)S(1)}, u32[]{:S(2)}) copy-start(bf16[576,1536]{1,0:T(8,128)(2,1)S(1)} %collective-permute-done.1.kp_ref.vp_ref) | copy-start | bytes 5308420
  254.7 27.7 %slice-start.7 = ((s8[4718592]{0:T(1024)(128)(4,1)}), s8[524288]{0:T(1024)(128)(4,1)S(1)}, s32[]{:S(2)}) async-start(s8[4718592]{0:T(1024)(128)(4,1)} %bitcast.281), calls=%async_computation.19 | async-start | bytes 1048576
  254.7 27.7 %copy-start.81 = (f32[768]{0:T(1024)S(1)}, f32[768]{0:T(1024)}, u32[]{:S(2)}) copy-start(f32[768]{0:T(1024)} %get-tuple-element.52) | copy-start | bytes 9220
  282.4 6.8 slice-start.8
  283.5 31.3 %copy-start.13 = (bf16[576,768]{1,0:T(8,128)(2,1)}, bf16[576,768]{1,0:T(8,128)(2,1)S(1)}, u32[]{:S(2)}) copy-start(bf16[576,768]{1,0:T(8,128)(2,1)S(1)} %get-tuple-element.67) | copy-start | bytes 2654212
  317.6 47.2 %copy-start.15 = (bf16[576,768]{1,0:T(8,128)(2,1)}, bf16[576,768]{1,0:T(8,128)(2,1)S(1)}, u32[]{:S(2)}) copy-start(bf16[576,768]{1,0:T(8,128)(2,1)S(1)} %get-tuple-element.65) | copy-start | bytes 2654212
  358.2 2.5 collective-permute-start.3
  358.7 3.2 collective-permute-start.2
  365.8 5.7 copy-start.20
  376.5 250.5 %reduce-scatter.5.cloned.1.call-start = ((), (), s32[]{:S(2)}) async-start(), calls=%async_computation.8 | async-start | bytes 23592960 | tf_op jit(solution)/shard_map/reduce_scatter | solution.py:368
  382.5 8.0 copy-start.21
  390.5 10.4 %copy-start.18 = (bf16[576,768]{1,0:T(8,128)(2,1)S(1)}, bf16[576,768]{1,0:T(8,128)(2,1)}, u32[]{:S(2)}) copy-start(bf16[576,768]{1,0:T(8,128)(2,1)} %copy-done.17) | copy-start | bytes 2654212
  390.5 10.4 %copy-start.52 = (f32[576]{0:T(1024)S(1)}, f32[576]{0:T(1024)}, u32[]{:S(2)}) copy-start(f32[576]{0:T(1024)} %copy-done.51) | copy-start | bytes 6916
  390.5 10.4 %copy-start.63 = (f32[576]{0:T(1024)S(1)}, f32[576]{0:T(1024)}, u32[]{:S(2)}) copy-start(f32[576]{0:T(1024)} %copy-done.62) | copy-start | bytes 6916
  390.5 10.4 %copy-start.68 = (f32[768]{0:T(1024)S(1)}, f32[768]{0:T(1024)}, u32[]{:S(2)}) copy-start(f32[768]{0:T(1024)} %get-tuple-element.54) | copy-start | bytes 9220
  401.0 6.1 copy-start.45
  408.0 50.5 %copy-start.23 = (bf16[576,768]{1,0:T(8,128)(2,1)}, bf16[576,768]{1,0:T(8,128)(2,1)S(1)}, u32[]{:S(2)}) copy-start(bf16[576,768]{1,0:T(8,128)(2,1)S(1)} %get-tuple-element.61) | copy-start | bytes 2654212
  448.5 8.7 %copy-start.8 = (bf16[576,768]{1,0:T(8,128)(2,1)}, bf16[576,768]{1,0:T(8,128)(2,1)S(1)}, u32[]{:S(2)}) copy-start(bf16[576,768]{1,0:T(8,128)(2,1)S(1)} %get-tuple-element.27) | copy-start | bytes 2654212
  451.0 6.3 copy-start.34
  451.0 17.6 %collective-permute-start.5 = (bf16[576,768]{1,0:T(8,128)(2,1)}, bf16[576,768]{1,0:T(8,128)(2,1)}, u32[]{:S(2)}, u32[]{:S(2)}) collective-permute-start(bf16[576,768]{1,0:T(8,128)(2,1)} %slice_bitcast_fusion.12), channel_id=1, source_target_pairs={{0,1},{1,0},{2,3},{3,2},{4,5},{5,4},{6,7},{7,6},{8,9},{9,8},{10,11... | collective-permute-start | bytes 2654216 | tf_op jit(solution)/shard_map/ppermute | solution.py:339
  458.2 11.8 %collective-permute-start.4 = (bf16[576,768]{1,0:T(8,128)(2,1)}, bf16[576,768]{1,0:T(8,128)(2,1)}, u32[]{:S(2)}, u32[]{:S(2)}) collective-permute-start(bf16[576,768]{1,0:T(8,128)(2,1)} %slice_bitcast_fusion.13), channel_id=1, source_target_pairs={{0,1},{1,0},{2,3},{3,2},{4,5},{5,4},{6,7},{7,6},{8,9},{9,8},{10,11... | collective-permute-start | bytes 2654216 | tf_op jit(solution)/shard_map/ppermute | solution.py:339
  469.9 6.7 copy-start.41
  486.4 280.2 %reduce-scatter.11.cloned.1.call-start = ((), (), s32[]{:S(2)}) async-start(), calls=%async_computation.11 | async-start | bytes 2654208 | tf_op jit(solution)/shard_map/reduce_scatter | solution.py:371
  487.0 312.3 %reduce-scatter.7.cloned.1.call-start = ((), (), s32[]{:S(2)}) async-start(), calls=%async_computation.9 | async-start | bytes 5308416 | tf_op jit(solution)/shard_map/reduce_scatter | solution.py:370
  630.4 46.2 %all-to-all-start = ((bf16[4,576,768]{2,1,0:T(8,128)(2,1)}), bf16[4,576,768]{2,1,0:T(8,128)(2,1)}, u32[]{:S(2)}, u32[]{:S(2)}) async-start(bf16[4,576,768]{2,1,0:T(8,128)(2,1)} %pad_maximum_fusion.2), calls=%async_computation | async-start | bytes 7077888 | tf_op jit(solution)/shard_map/all_to_all | solution.py:362
  638.2 6.9 copy-start.10
  676.7 84.3 %all-to-all-start.1 = ((bf16[4,576,768]{2,1,0:T(8,128)(2,1)}), bf16[4,576,768]{2,1,0:T(8,128)(2,1)}, u32[]{:S(2)}, u32[]{:S(2)}) async-start(bf16[4,576,768]{2,1,0:T(8,128)(2,1)} %pad_maximum_fusion.3), calls=%async_computation.1 | async-start | bytes 7077888 | tf_op jit(solution)/shard_map/all_to_all | solution.py:362
  (66 other events, 211.4 us)
Sparse Core Ops, SparseCore 0:
  9.6 123.0 all-gather.4
  134.2 64.1 all-gather.6
  376.6 78.4 reduce-scatter.8
  486.5 140.4 reduce-scatter.4
  630.7 68.9 reduce-scatter.10
  703.6 95.5 reduce-scatter.6

commit v2 on v1

v2 whole, which is shorter than its diff:
```python
from functools import partial

import jax
import jax.numpy as jnp
import numpy as np
from jax import lax
from jax.experimental import pallas as pl
from jax.experimental.pallas import tpu as pltpu
from jax.sharding import PartitionSpec as P

SIDE_L = 32
CELLS = SIDE_L + 1
HEAD = 64
PAIR = 2 * HEAD
PAGES = 8
BLOCK = 40
PAGE_AT = 3 * CELLS
MASKED = 1e30
EPSILON = 1e-06
LOG2E = 1.4426950408889634
LN2 = 0.6931471805599453
BF = jnp.bfloat16
F32 = jnp.float32
NT = (((1,), (1,)), ((), ()))
TN = (((0,), (0,)), ((), ()))


def dot(a, b):
    return jnp.dot(a, b, preferred_element_type=F32)


def dot_nt(a, b):
    return lax.dot_general(a, b, NT, preferred_element_type=F32)


def dot_tn(a, b):
    return lax.dot_general(a, b, TN, preferred_element_type=F32)


def geometry(grid_side, row_ids, slot_rows):
    page_len = grid_side * grid_side + 1
    page_count = slot_rows // page_len
    page_of = jnp.minimum(row_ids // page_len, page_count)
    offset = row_ids - page_of * page_len
    patch_id = jnp.maximum(offset - 1, 0)
    inside = page_of < page_count
    class_row = offset == 0
    coord_y = jnp.where(inside, jnp.where(class_row, SIDE_L, patch_id // grid_side), 0)
    coord_x = jnp.where(inside, jnp.where(class_row, SIDE_L, patch_id % grid_side), 0)
    return page_of, coord_y, coord_x


def row_features(page_of, coord_y, coord_x, flip):
    lane = jnp.arange(128, dtype=jnp.int32)[None, :]
    at = (lambda c: SIDE_L - c) if flip else (lambda c: c)
    hot = (lane == at(coord_y)[:, None]) | (lane == BLOCK + at(coord_x)[:, None])
    hot = hot | (lane == 2 * BLOCK + page_of[:, None])
    return hot.astype(BF)


def key_features(page_of, coord_y, coord_x):
    lane = jnp.arange(256, dtype=jnp.int32)[None, :]
    at_y = SIDE_L - coord_y[:, None]
    at_x = SIDE_L - coord_x[:, None]
    hot = (lane == at_y) | (lane == HEAD + at_y) | (lane == 128 + at_x)
    hot = hot | (lane == 128 + CELLS + at_y) | (lane == 128 + 2 * CELLS + at_x)
    hot = hot | (lane == 128 + PAGE_AT + page_of[:, None])
    return hot.astype(BF)


def table_rows(rel_table):
    layers, heads = rel_table.shape[:2]
    scaled = rel_table * LOG2E
    gap = jnp.zeros((*scaled.shape[:3], 128 - 2 * SIDE_L - 1), F32)
    scaled = jnp.concatenate([scaled[..., SIDE_L:], gap, scaled[..., :SIDE_L]], axis=-1)
    high = scaled.astype(BF).astype(F32)
    return jnp.concatenate([high, scaled - high], axis=2).reshape(layers, heads // 2, 8, 128)


def table_map(table_ref, head):
    row = lax.broadcasted_iota(jnp.int32, (BLOCK, 128), 0)
    lane = lax.broadcasted_iota(jnp.int32, (BLOCK, 128), 1)

    def grid(i, to):
        values = jnp.broadcast_to(table_ref[0, 4 * head + i : 4 * head + i + 1, :], (BLOCK, 128))
        values = pltpu.roll(values, 0, 1, stride=1, stride_axis=0)
        values = jnp.where((row < CELLS) & (lane < CELLS), values, 0.0)
        return pltpu.roll(values, to, 1) if to else values

    none = jnp.zeros((BLOCK, 128), F32)
    far = jnp.where((lane >= PAGE_AT) & (lane < PAGE_AT + PAGES) & (lane - PAGE_AT != row) & (row < PAGES), -MASKED, 0.0)
    left = [grid(0, HEAD if head == 0 else 0), none, none, none[:8]]
    right = [grid(2, CELLS), grid(1, 0) + grid(3, 2 * CELLS), far, none[:8]]
    return jnp.concatenate([jnp.concatenate(left, axis=0), jnp.concatenate(right, axis=0)], axis=1).astype(BF)


def split3(value):
    high = value.astype(BF).astype(F32)
    middle = (value - high).astype(BF).astype(F32)
    return high, middle, value - high - middle


def lanes_of(rows):
    return lax.broadcasted_iota(jnp.int32, (rows, PAIR), 1)


def attn_fwd_kernel(hot_ref, map_ref, q_ref, ko_ref, kp_ref, vo_ref, vp_ref, key_ref,
                    o_ref, rest_ref, inv_ref, w_ref, kx_ref, vx_ref):
    rows = q_ref.shape[0]
    lane = lanes_of(rows)
    for head in range(2):
        mine = (lane < HEAD) if head == 0 else (lane >= HEAD)
        one_at = HEAD if head == 0 else 0
        table = table_map(map_ref, head)
        kx, vx = kx_ref.at[head], vx_ref.at[head]
        kx[:, PAIR:] = key_ref[:, PAIR:]
        for part, (k_ref, v_ref) in enumerate(((ko_ref, vo_ref), (kp_ref, vp_ref))):
            at = pl.ds(part * rows, rows)
            kx[at, :PAIR] = jnp.where(mine, k_ref[...], key_ref[at, :PAIR])
            vx[at, :] = jnp.where(mine, v_ref[...], jnp.where(lane == one_at, 1.0, 0.0).astype(BF))
        feats = dot(hot_ref[...], table).astype(BF)
        query = jnp.concatenate([jnp.where(mine, q_ref[...], feats[:, :PAIR]), feats[:, PAIR:]], axis=1)
        scores = dot_nt(kx[...], query)
        weights = jnp.exp2(scores - jnp.max(scores, axis=0, keepdims=True)).astype(BF)
        w_ref[head] = weights
        mixed = dot_tn(vx[...], weights).T
        inv = 1.0 / mixed[:, one_at : one_at + 1]
        out = mixed * inv
        high = out.astype(BF)
        rest = (out - high.astype(F32)).astype(BF)
        inv = jnp.broadcast_to(inv, out.shape)
        if head == 0:
            o_ref[...], rest_ref[...], inv_ref[...] = high, rest, inv
        else:
            o_ref[...] = jnp.where(mine, high, o_ref[...])
            rest_ref[...] = jnp.where(mine, rest, rest_ref[...])
            inv_ref[...] = jnp.where(mine, inv, inv_ref[...])


def attn_forward(hot, maps, project, partner, keys):
    rows, width = project.shape[0], project.shape[1] // 3
    pairs = width // PAIR
    col = lambda off: pl.BlockSpec((rows, PAIR), lambda g: (0, off + g))
    return pl.pallas_call(
        attn_fwd_kernel,
        grid=(pairs,),
        in_specs=[
            whole((rows, 128)),
            pl.BlockSpec((1, 8, 128), lambda g: (g, 0, 0)),
            col(0),
            col(pairs),
            col(0),
            col(2 * pairs),
            col(pairs),
            whole((2 * rows, 256)),
        ],
        out_specs=[col(0), col(0), col(0), pl.BlockSpec((2, 2 * rows, rows), lambda g: (g, 0, 0))],
        out_shape=[
            jax.ShapeDtypeStruct((rows, width), BF),
            jax.ShapeDtypeStruct((rows, width), BF),
            jax.ShapeDtypeStruct((rows, width), F32),
            jax.ShapeDtypeStruct((2 * pairs, 2 * rows, rows), BF),
        ],
        scratch_shapes=[pltpu.VMEM((2, 2 * rows, 256), BF), pltpu.VMEM((2, 2 * rows, PAIR), BF)],
        compiler_params=params_for(56),
        cost_estimate=cost(26),
        name="attn_fwd",
    )(hot, maps, project, project, partner, project, partner, keys)


def attn_bwd_kernel(hot_ref, w_ref, q_ref, ko_ref, kp_ref, vo_ref, vp_ref, key_ref, do_ref, o_ref, rest_ref, inv_ref,
                    dq_ref, mine_ref, other_ref, gt_ref, kx_ref, vx_ref, ds_ref):
    rows = q_ref.shape[0]
    lane = lanes_of(rows)
    scaled = (do_ref[...].astype(F32) * inv_ref[...]).astype(BF)
    product = scaled.astype(F32) * (o_ref[...].astype(F32) + rest_ref[...].astype(F32))
    for head in range(2):
        mine = (lane < HEAD) if head == 0 else (lane >= HEAD)
        spot = lane - (HEAD if head == 0 else 0)
        kx, vx, ds = kx_ref.at[head], vx_ref.at[head], ds_ref.at[head]
        kx[:, PAIR:] = key_ref[:, PAIR:]
        ones = jnp.where((spot >= 0) & (spot < 3), 1.0, 0.0).astype(BF)
        for part, (k_ref, v_ref) in enumerate(((ko_ref, vo_ref), (kp_ref, vp_ref))):
            at = pl.ds(part * rows, rows)
            kx[at, :PAIR] = jnp.where(mine, k_ref[...], key_ref[at, :PAIR])
            vx[at, :] = jnp.where(mine, v_ref[...], ones)
        delta = jnp.sum(jnp.where(mine, product, 0.0), axis=1, keepdims=True)
        high, middle, low = split3(delta)
        spread = jnp.where(spot == 0, -high, jnp.where(spot == 1, -middle, jnp.where(spot == 2, -low, 0.0)))
        d_out = jnp.where(mine, scaled, spread.astype(BF))
        for part, out_ref in enumerate((mine_ref, other_ref)):
            at = pl.ds(part * rows, rows)
            weights = w_ref[head, at, :]
            d_scores = (weights.astype(F32) * dot_nt(vx[at, :], d_out)).astype(BF)
            ds[at, :] = d_scores
            d_value = dot(weights, scaled).astype(BF)
            d_key = (dot(d_scores, q_ref[...]) * LN2).astype(BF)
            if head == 0:
                out_ref[1], out_ref[0] = d_value, d_key
            else:
                out_ref[1] = jnp.where(mine, d_value, out_ref[1])
                out_ref[0] = jnp.where(mine, d_key, out_ref[0])
        d_query = dot_tn(ds[...], kx[...])
        high_q = d_query.astype(BF)
        low_q = (d_query - high_q.astype(F32)).astype(BF)
        grid = dot_tn(hot_ref[...], high_q) + dot_tn(hot_ref[...], low_q)
        row = lax.broadcasted_iota(jnp.int32, (BLOCK, 128), 0)
        column = lax.broadcasted_iota(jnp.int32, (BLOCK, 128), 1)
        for axis in range(2):
            part = grid[axis * BLOCK : (axis + 1) * BLOCK, axis * 128 : (axis + 1) * 128]
            part = pltpu.roll(part, HEAD, 1) if axis == 0 and head == 0 else part
            part = jnp.where((row < CELLS) & (column < CELLS), part, 0.0)
            along = pltpu.roll(part, 0, 1, stride=1, stride_axis=0)
            gt_ref[0, 2 * head + axis : 2 * head + axis + 1, :] = jnp.sum(along, axis=0, keepdims=True)
        d_query = (d_query[:, :PAIR] * HEAD**-0.5).astype(BF)
        dq_ref[...] = d_query if head == 0 else jnp.where(mine, d_query, dq_ref[...])
    gt_ref[0, 4:8, :] = jnp.zeros((4, 128), F32)


def attn_backward(hot, weights, project, partner, keys, d_context, outcome, first, count):
    rows, width = project.shape[0], project.shape[1] // 3
    pairs = width // PAIR
    col = lambda off: pl.BlockSpec((rows, PAIR), lambda g: (0, off + first + g))
    out = pl.BlockSpec((rows, PAIR), lambda g: (0, g))
    both = pl.BlockSpec((2, rows, PAIR), lambda g: (0, 0, g))
    return pl.pallas_call(
        attn_bwd_kernel,
        grid=(count,),
        in_specs=[
            whole((rows, 128)),
            pl.BlockSpec((2, 2 * rows, rows), lambda g: (first + g, 0, 0)),
            col(0),
            col(pairs),
            col(0),
            col(2 * pairs),
            col(pairs),
            whole((2 * rows, 256)),
            col(0),
            col(0),
            col(0),
            col(0),
        ],
        out_specs=[out, both, both, pl.BlockSpec((1, 8, 128), lambda g: (g, 0, 0))],
        out_shape=[
            jax.ShapeDtypeStruct((rows, count * PAIR), BF),
            jax.ShapeDtypeStruct((2, rows, count * PAIR), BF),
            jax.ShapeDtypeStruct((2, rows, count * PAIR), BF),
            jax.ShapeDtypeStruct((count, 8, 128), F32),
        ],
        scratch_shapes=[
            pltpu.VMEM((2, 2 * rows, 256), BF),
            pltpu.VMEM((2, 2 * rows, PAIR), BF),
            pltpu.VMEM((2, 2 * rows, rows), BF),
        ],
        compiler_params=params_for(56),
        cost_estimate=cost(6 * count),
        name="attn_bwd",
    )(hot, weights, project, project, partner, project, partner, keys, d_context, *outcome)


def centred(values):
    values = values - jnp.mean(values, axis=-1, keepdims=True)
    inv = lax.rsqrt(jnp.mean(values * values, axis=-1, keepdims=True) + EPSILON)
    return values * inv, inv


def start_first(info_ref, kind, cols, refs, dst, sem):
    own, near, far_own, far_other = refs
    local, core = info_ref[0] == 1, info_ref[1]
    part = far_own.shape[0]

    @pl.when(local & (core == kind))
    def _():
        pltpu.make_async_copy(own.at[:, cols], dst, sem).start()

    @pl.when(local & (core != kind))
    def _():
        pltpu.make_async_copy(near.at[:, cols], dst, sem).start()

    @pl.when(jnp.logical_not(local))
    def _():
        pltpu.make_async_copy(far_own.at[:, cols], dst.at[pl.ds(core * part, part)], sem).start()
        pltpu.make_async_copy(far_other.at[:, cols], dst.at[pl.ds((1 - core) * part, part)], sem).start()


def start_down(info_ref, refs, dst, sem):
    own, near, *far = refs
    local, core = info_ref[0] == 1, info_ref[1]
    part, cut = own.shape[0], far[0].shape[0]
    cuts = part // cut

    @pl.when(local)
    def _():
        pltpu.make_async_copy(own, dst.at[pl.ds(core * part, part)], sem).start()
        pltpu.make_async_copy(near, dst.at[pl.ds((1 - core) * part, part)], sem).start()

    @pl.when(jnp.logical_not(local))
    def _():
        for i in range(2 * cuts):
            at = (core if i < cuts else 1 - core) * part + (i % cuts) * cut
            pltpu.make_async_copy(far[i], dst.at[pl.ds(at, cut)], sem).start()


def wait_for(dst, sem):
    pltpu.make_async_copy(dst, dst, sem).wait()


EARLY = True
SMEM = pl.BlockSpec(memory_space=pltpu.SMEM)
ANY = pl.BlockSpec(memory_space=pl.ANY)


def whole(shape):
    return pl.BlockSpec(shape, lambda *g: (0,) * len(shape))


def params_for(mib):
    return pltpu.CompilerParams(vmem_limit_bytes=mib * 2**20)


def cost(us):
    return pl.CostEstimate(flops=int(us * 2e7), bytes_accessed=1000, transcendentals=0)


def project_kernel(info_ref, x_ref, p_ref, own, near, far_own, far_other, normed_ref, out_ref, w_ref, sem):
    width = x_ref.shape[1]
    start_first(info_ref, 0, pl.ds(0, 3 * width), (own, near, far_own, far_other), w_ref, sem)
    nhat, _ = centred(x_ref[...].astype(F32))
    normed = (nhat * p_ref[0:1, :] + p_ref[1:2, :]).astype(BF)
    normed_ref[...] = normed
    wait_for(w_ref, sem)
    for j in range(3):
        at = pl.ds(j * width, width)
        value = dot(normed, w_ref[:, at])
        if j == 0:
            value = value * (HEAD**-0.5 * LOG2E)
        out_ref[:, at] = value.astype(BF)


def project(info, x, p, first_refs):
    rows, width = x.shape
    return pl.pallas_call(
        project_kernel,
        in_specs=[SMEM, whole(x.shape), whole(p.shape)] + [ANY] * 4,
        out_specs=[whole((rows, width)), whole((rows, 3 * width))],
        out_shape=[jax.ShapeDtypeStruct((rows, width), BF), jax.ShapeDtypeStruct((rows, 3 * width), BF)],
        scratch_shapes=[pltpu.VMEM((width, 3 * width), BF), pltpu.SemaphoreType.DMA],
        compiler_params=params_for(40),
        cost_estimate=cost(5),
        name="project",
    )(info, x, p, *first_refs)


def block_out_kernel(info_ref, x_ref, ctx_ref, p0_ref, p1_ref, *refs):
    att, up, refs = refs[:4], refs[:2] + refs[4:6], refs[6:]
    down, refs = refs[:8], refs[8:]
    b0_ref, x1_ref, n1_ref, slope_ref, hid_ref, b1_ref, x2_ref, wo_ref, wu_ref, wd_ref, slopes, hiddens, sems, out_sems = refs
    width = x_ref.shape[1]
    start_first(info_ref, 0, pl.ds(3 * width, width), att, wo_ref, sems.at[0])
    for j in range(4):
        start_first(info_ref, 1, pl.ds(j * width, width), up, wu_ref.at[j], sems.at[1 + j])
    start_down(info_ref, down, wd_ref, sems.at[5])
    wait_for(wo_ref, sems.at[0])
    branch = dot(ctx_ref[...], wo_ref[...])
    b0_ref[...] = branch.astype(BF)
    x1 = (x_ref[...].astype(F32) + p0_ref[2:3, :] * branch).astype(BF)
    x1_ref[...] = x1
    x1 = x1.astype(F32)
    nhat, _ = centred(x1)
    normed = (nhat * p1_ref[0:1, :] + p1_ref[1:2, :]).astype(BF)
    n1_ref[...] = normed
    for j in range(4):
        wait_for(wu_ref.at[j], sems.at[1 + j])
    wait_for(wd_ref, sems.at[5])
    total = jnp.zeros(x1.shape, F32)
    for j in range(4):
        at = pl.ds(j * width, width)
        v = dot(normed, wu_ref[j])
        square = v * v
        bend = jnp.tanh(v * (0.7978845608028654 + (0.7978845608028654 * 0.044715) * square))
        up_half = 0.5 + 0.5 * bend
        along = v * (2 * 0.7978845608028654 + (6 * 0.7978845608028654 * 0.044715) * square)
        slopes[j] = (up_half + along * (up_half * (1.0 - up_half))).astype(BF)
        hiddens[j] = (v * up_half).astype(BF)
        if EARLY:
            pltpu.make_async_copy(slopes.at[j], slope_ref.at[:, at], out_sems.at[0, j]).start()
            pltpu.make_async_copy(hiddens.at[j], hid_ref.at[:, at], out_sems.at[1, j]).start()
        total = total + dot(hiddens[j], wd_ref[at, :])
    b1_ref[...] = total.astype(BF)
    x2_ref[...] = (x1 + p1_ref[2:3, :] * total).astype(BF)
    if not EARLY:
        for j in range(4):
            at = pl.ds(j * width, width)
            pltpu.make_async_copy(slopes.at[j], slope_ref.at[:, at], out_sems.at[0, j]).start()
            pltpu.make_async_copy(hiddens.at[j], hid_ref.at[:, at], out_sems.at[1, j]).start()
    for j in range(4):
        wait_for(slopes.at[j], out_sems.at[0, j])
        wait_for(hiddens.at[j], out_sems.at[1, j])


def block_out(info, x, context, p0, p1, att_refs, up_refs, down_refs):
    rows, width = x.shape
    one = whole((rows, width))
    shape = lambda n: jax.ShapeDtypeStruct((rows, n), BF)
    widths = [width, width, width, 4 * width, 4 * width, width, width]
    refs = (*att_refs, *up_refs[2:], *down_refs)
    return pl.pallas_call(
        block_out_kernel,
        grid=(1,),
        in_specs=[SMEM, one, one, whole(p0.shape), whole(p1.shape)] + [ANY] * len(refs),
        out_specs=[one if n == width else ANY for n in widths],
        out_shape=[shape(n) for n in widths],
        scratch_shapes=[
            pltpu.VMEM((width, width), BF),
            pltpu.VMEM((4, width, width), BF),
            pltpu.VMEM((4 * width, width), BF),
            pltpu.VMEM((4, rows, width), BF),
            pltpu.VMEM((4, rows, width), BF),
            pltpu.SemaphoreType.DMA((6,)),
            pltpu.SemaphoreType.DMA((2, 4)),
        ],
        compiler_params=params_for(58),
        cost_estimate=cost(12),
        name="block_out",
    )(info, x, context, p0, p1, *refs)


def norm_back(x, gain, d_normed, gy):
    nhat, inv = centred(x)
    inner = d_normed * gain
    shift = jnp.mean(inner, axis=-1, keepdims=True)
    along = jnp.mean(inner * nhat, axis=-1, keepdims=True)
    total = lambda v: jnp.sum(v, axis=0, keepdims=True)
    return gy + inv * (inner - shift - nhat * along), total(nhat * d_normed), total(d_normed)


def block_back_kernel(info_ref, gy_ref, x1_ref, slope_ref, b1_ref, b0_ref, p0_ref, p1_ref, *refs):
    att, up, refs = refs[:4], refs[:2] + refs[4:6], refs[6:]
    down, refs = refs[:8], refs[8:]
    db1_ref, dpre_ref, gx_ref, db0_ref, dctx_ref, vec_ref, wo_ref, wu_ref, wd_ref, slopes, given, sems, more_sems = refs
    width = gy_ref.shape[1]
    start_down(info_ref, down, wd_ref, sems.at[5])
    for j in range(4):
        at = pl.ds(j * width, width)
        start_first(info_ref, 1, at, up, wu_ref.at[j], sems.at[1 + j])
        pltpu.make_async_copy(slope_ref.at[:, at], slopes.at[j], more_sems.at[0, j]).start()
    start_first(info_ref, 0, pl.ds(3 * width, width), att, wo_ref, sems.at[0])
    total = lambda v: jnp.sum(v, axis=0, keepdims=True)
    gy = gy_ref[...].astype(F32)
    d_branch = (gy * p1_ref[2:3, :]).astype(BF)
    db1_ref[...] = d_branch
    vec_ref[2:3, :] = total(b1_ref[...].astype(F32) * gy)
    vec_ref[4:, :] = jnp.zeros((4, width), F32)
    d_normed = jnp.zeros(gy.shape, F32)
    wait_for(wd_ref, sems.at[5])
    for j in range(4):
        wait_for(slopes.at[j], more_sems.at[0, j])
        wait_for(wu_ref.at[j], sems.at[1 + j])
    for j in range(4):
        at = pl.ds(j * width, width)
        d_hidden = dot_nt(d_branch, wd_ref[at, :])
        given[j] = (d_hidden * slopes[j].astype(F32)).astype(BF)
        if EARLY:
            pltpu.make_async_copy(given.at[j], dpre_ref.at[:, at], more_sems.at[1, j]).start()
        d_normed = d_normed + dot_nt(given[j], wu_ref[j])
    if not EARLY:
        for j in range(4):
            pltpu.make_async_copy(given.at[j], dpre_ref.at[:, pl.ds(j * width, width)], more_sems.at[1, j]).start()
    gx, g_gain, g_shift = norm_back(x1_ref[...].astype(F32), p1_ref[0:1, :], d_normed, gy)
    vec_ref[0:1, :] = g_gain
    vec_ref[1:2, :] = g_shift
    gx = gx.astype(BF)
    gx_ref[...] = gx
    gx = gx.astype(F32)
    d_att = (gx * p0_ref[2:3, :]).astype(BF)
    db0_ref[...] = d_att
    vec_ref[3:4, :] = total(b0_ref[...].astype(F32) * gx)
    wait_for(wo_ref, sems.at[0])
    dctx_ref[...] = dot_nt(d_att, wo_ref[...]).astype(BF)
    for j in range(4):
        wait_for(given.at[j], more_sems.at[1, j])


def block_back(info, gy, x1, slope, b1, b0, p0, p1, att_refs, up_refs, down_refs):
    rows, width = gy.shape
    one = whole((rows, width))
    shape = lambda n: jax.ShapeDtypeStruct((rows, n), BF)
    widths = [width, 4 * width, width, width, width]
    refs = (*att_refs, *up_refs[2:], *down_refs)
    return pl.pallas_call(
        block_back_kernel,
        grid=(1,),
        in_specs=[SMEM, one, one, ANY, one, one, whole(p0.shape), whole(p1.shape)] + [ANY] * len(refs),
        out_specs=[one if n == width else ANY for n in widths] + [whole((8, width))],
        out_shape=[shape(n) for n in widths] + [jax.ShapeDtypeStruct((8, width), F32)],
        scratch_shapes=[
            pltpu.VMEM((width, width), BF),
            pltpu.VMEM((4, width, width), BF),
            pltpu.VMEM((4 * width, width), BF),
            pltpu.VMEM((4, rows, width), BF),
            pltpu.VMEM((4, rows, width), BF),
            pltpu.SemaphoreType.DMA((6,)),
            pltpu.SemaphoreType.DMA((2, 4)),
        ],
        compiler_params=params_for(58),
        cost_estimate=cost(14),
        name="block_back",
    )(info, gy, x1, slope, b1, b0, p0, p1, *refs)


def project_back_kernel(info_ref, gy_ref, x_ref, p_ref, dqa, dqb, mya, myb, gota, gotb, own, near, far_own, far_other,
                        dproj_ref, gx_ref, vec_ref, w_ref, sem):
    width = x_ref.shape[1]
    start_first(info_ref, 0, pl.ds(0, 3 * width), (own, near, far_own, far_other), w_ref, sem)
    half = width // 2
    for i, (dq, my, got) in enumerate(((dqa, mya, gota), (dqb, myb, gotb))):
        dproj_ref[:, i * half : (i + 1) * half] = dq[...]
        for j in range(2):
            at = pl.ds((1 + j) * width + i * half, half)
            dproj_ref[:, at] = (my[j].astype(F32) + got[j].astype(F32)).astype(BF)
    wait_for(w_ref, sem)
    d_normed = dot_nt(dproj_ref[:, :width], w_ref[:, :width])
    for j in (1, 2):
        at = pl.ds(j * width, width)
        d_normed = d_normed + dot_nt(dproj_ref[:, at], w_ref[:, at])
    gx, g_gain, g_shift = norm_back(x_ref[...].astype(F32), p_ref[0:1, :], d_normed, gy_ref[...].astype(F32))
    gx_ref[...] = gx.astype(BF)
    vec_ref[0:1, :] = g_gain
    vec_ref[1:2, :] = g_shift
    vec_ref[2:, :] = jnp.zeros((6, width), F32)


def project_back(info, gy, x, p, parts, first_refs):
    rows, width = x.shape
    one = whole((rows, width))
    return pl.pallas_call(
        project_back_kernel,
        in_specs=[SMEM, one, one, whole(p.shape)] + [whole(v.shape) for v in parts] + [ANY] * 4,
        out_specs=[whole((rows, 3 * width)), one, whole((8, width))],
        out_shape=[
            jax.ShapeDtypeStruct((rows, 3 * width), BF),
            jax.ShapeDtypeStruct((rows, width), BF),
            jax.ShapeDtypeStruct((8, width), F32),
        ],
        grid=(1,),
        scratch_shapes=[pltpu.VMEM((width, 3 * width), BF), pltpu.SemaphoreType.DMA],
        compiler_params=params_for(48),
        cost_estimate=cost(7),
        name="project_back",
    )(info, gy, x, p, *parts, *first_refs)


def gather_kernel(info_ref, mine, by_x, by_z, diag_x, diag_z, out_ref, sem):
    quarter = mine.shape[0]
    part = quarter // 2
    q = info_ref[0]
    at = lambda i: pl.multiple_of(i * quarter, part)
    pltpu.make_async_copy(mine, out_ref.at[pl.ds(at(q), quarter)], sem).start()
    pltpu.make_async_copy(by_x, out_ref.at[pl.ds(at(info_ref[1]), quarter)], sem).start()
    pltpu.make_async_copy(by_z, out_ref.at[pl.ds(at(info_ref[2]), quarter)], sem).start()
    pltpu.make_async_copy(diag_x, out_ref.at[pl.ds(at(info_ref[3]), part)], sem).start()
    pltpu.make_async_copy(diag_z, out_ref.at[pl.ds(at(info_ref[3]) + part, part)], sem).start()
    wait_for(out_ref, sem)


def dp_swap(value, bit):
    return lax.ppermute(value, "dp", [(i, i ^ bit) for i in range(lax.axis_size("dp"))])


def tie(value, *deps):
    return lax.optimization_barrier((value, deps))[0]


def hold(values, count):
    state = values[-1]
    if not isinstance(state, list):
        return lax.optimization_barrier(values)
    arrays = [part[:2] for part in state]
    *values, arrays = lax.optimization_barrier((*values[:count], arrays))
    return (*values, [(*part, names) for part, (_, _, names) in zip(arrays, state)])


def together(values):
    return lax.optimization_barrier(values)


def quad_start(mine):
    return (mine, *together((dp_swap(mine, 1), dp_swap(mine, 2))))


def quad_end(mine, by_x, by_z):
    part = mine.shape[0] // 2
    return (mine, by_x, by_z, *together((dp_swap(by_z[:part], 1), dp_swap(by_x[part:], 2))))


def quad_place(mine, *others):
    quarter = mine.shape[0]
    q = lax.axis_index("dp") % 4
    spots = jnp.stack([q, q ^ 1, q ^ 2, q ^ 3]).astype(jnp.int32)
    return pl.pallas_call(
        gather_kernel,
        in_specs=[SMEM] + [ANY] * 5,
        out_specs=whole((4 * quarter, *mine.shape[1:])),
        out_shape=jax.ShapeDtypeStruct((4 * quarter, *mine.shape[1:]), mine.dtype),
        scratch_shapes=[pltpu.SemaphoreType.DMA],
        compiler_params=params_for(16),
        cost_estimate=cost(3),
        name="assemble",
    )(spots, mine, *others)


def put_rows(values, slot, tmp_ref, keep_ref, send_ref, core, for_d, at, sems):
    tmp = tmp_ref.at[slot].reshape(values.shape)
    tmp[...] = values
    pltpu.make_async_copy(tmp.at[:, core], keep_ref.at[for_d, at], sems.at[slot, 0]).start()
    pltpu.make_async_copy(tmp.at[:, 1 - core], send_ref.at[for_d, at], sems.at[slot, 1]).start()


def mlp_grads_kernel(core_ref, n_ref, pre_ref, hid_ref, db_ref, keep_ref, send_ref, tmp_ref, sems):
    core, j = core_ref[0], pl.program_id(0)
    width = n_ref.shape[1]
    size = keep_ref.shape[0]
    short, long = width // (2 * size), 2 * width // (2 * size)

    def finish(slot, long_rows):
        for i, ref in enumerate((keep_ref, send_ref)):
            to = ref.at[pl.ds(0, size // 2), pl.ds(0, long)] if long_rows else ref.at[:, pl.ds(0, short)]
            pltpu.make_async_copy(to, to, sems.at[slot, i]).wait()

    @pl.when(j > 0)
    def _():
        finish(0, False)
    up = dot_tn(n_ref[...], pre_ref[...]).astype(BF).reshape(size, 2, short, width)
    put_rows(up, 0, tmp_ref, keep_ref, send_ref, core, pl.ds(0, size), pl.ds(j * short, short), sems)

    @pl.when(j > 0)
    def _():
        finish(1, True)
    down = dot_tn(hid_ref[...], db_ref[...]).astype(BF).reshape(size // 2, 2, long, width)
    at = pl.ds(4 * short + (j // 2) * long, long)
    put_rows(down, 1, tmp_ref, keep_ref, send_ref, core, pl.ds((j % 2) * (size // 2), size // 2), at, sems)

    @pl.when(j == pl.num_programs(0) - 1)
    def _():
        finish(0, False)
        finish(1, True)


def att_grads_kernel(core_ref, n_ref, dproj_ref, ctx_ref, db_ref, keep_ref, send_ref, tmp_ref, sems):
    core, j = core_ref[0], pl.program_id(0)
    width = n_ref.shape[1]
    size = keep_ref.shape[0]
    short = width // (2 * size)
    slot = lax.rem(j, 2)
    tmp = tmp_ref.at[slot].reshape(size, 2, short, width)

    def finish(at):
        for i, ref in enumerate((keep_ref, send_ref)):
            to = ref.at[:, pl.ds(0, short)]
            pltpu.make_async_copy(to, to, sems.at[at, i]).wait()

    @pl.when(j > 1)
    def _():
        finish(slot)

    @pl.when(j < 3)
    def _():
        tmp[...] = dot_tn(n_ref[...], dproj_ref[...]).astype(BF).reshape(tmp.shape)

    @pl.when(j == 3)
    def _():
        tmp[...] = dot_tn(ctx_ref[...], db_ref[...]).astype(BF).reshape(tmp.shape)

    at = pl.ds(j * short, short)
    pltpu.make_async_copy(tmp.at[:, core], keep_ref.at[:, at], sems.at[slot, 0]).start()
    pltpu.make_async_copy(tmp.at[:, 1 - core], send_ref.at[:, at], sems.at[slot, 1]).start()

    @pl.when(j == 3)
    def _():
        finish(0)
        finish(1)


def plain_grads(att, core, shape, a, b, c, d):
    size, _, width = shape
    cut = lambda grad: [grad[:, j * width : (j + 1) * width].reshape(size, 2, -1, width) for j in range(grad.shape[1] // width)]
    parts = cut(dot_tn(a, b).astype(BF))
    if att:
        parts += cut(dot_tn(c, d).astype(BF))
    else:
        parts += [half.reshape(size, 2, -1, width) for half in jnp.split(dot_tn(c, d).astype(BF), 2, axis=0)]
    both = jnp.concatenate(parts, axis=2)
    at = lambda i: lax.dynamic_index_in_dim(both, i, 1, keepdims=False)
    return at(core), at(1 - core)


def weight_grads(kernel, core, size, us, a, b, c, d):
    rows, width = a.shape
    att = kernel is att_grads_kernel
    shape = (size, (2 * width if att else 4 * width) // size, width)
    if width // (2 * size) % 16:
        return plain_grads(att, core, shape, a, b, c, d)
    col = pl.BlockSpec((rows, width), lambda j: (0, jnp.minimum(j, 2 if att else 3)))
    return pl.pallas_call(
        kernel,
        grid=(4,),
        in_specs=[SMEM, whole(a.shape), col, whole(c.shape) if att else col, whole(d.shape)],
        out_specs=[ANY] * 2,
        out_shape=[jax.ShapeDtypeStruct(shape, BF)] * 2,
        scratch_shapes=[pltpu.VMEM((2, width, width), BF), pltpu.SemaphoreType.DMA((2, 2))],
        compiler_params=params_for(48),
        cost_estimate=cost(us),
        name=kernel.__name__[:-7],
    )(core.astype(jnp.int32).reshape(1), a, b, c, d)


def send(value, pairs):
    return lax.ppermute(value, "pipe", pairs)


def swap(value, bit):
    return send(value, [(i, i ^ bit) for i in range(lax.axis_size("pipe"))])


def to_target(value, target, bit):
    return send(value, [(target ^ bit, target)])


def pick(core, mine_first, mine_second):
    return jnp.where(core == 0, mine_first, mine_second)


ORDERS = (("x", "y", "z2", "z4"), ("y", "z2", "x", "z4"), ("z2", "x", "y", "z4"))
AT = {"x": ("dp", 1), "z2": ("dp", 2), "z4": ("dp", 4), "y": ("pipe", 2)}


def cube_start(parts):
    size, rows, width = parts.shape
    if size != 8:
        return parts
    parts = parts.reshape(2, 2, 2, 2, rows // 2, width)
    share = width // len(ORDERS)
    return [(parts[..., i * share : (i + 1) * share], None, ["z4", "z2", "x", "y"]) for i in range(len(ORDERS))]


def settled(part, got):
    return part if got is None else part + got


def halve(part, names, axis):
    name, bit = AT[axis]
    i = names.index(axis)
    me = (lax.axis_index(name) // bit) % 2
    at = lambda j: lax.dynamic_index_in_dim(part, j, i, keepdims=False)
    give = at(1 - me)
    got = lax.ppermute(give, name, [(k, k ^ bit) for k in range(lax.axis_size(name))])
    return at(me), got, [n for n in names if n != axis], give


def cube_step(state, step):
    if not isinstance(state, list):
        return state, state
    done = [halve(settled(part, got), names, order[step]) for (part, got, names), order in zip(state, ORDERS)]
    gots = together([d[1] for d in done])
    return [(d[0], got, d[2]) for d, got in zip(done, gots)], [d[3] for d in done]


def cube_end(state):
    if not isinstance(state, list):
        plane = lax.axis_index("pipe") // 2
        parts = state.reshape(state.shape[0], 2, -1, state.shape[2])
        at = lambda i: lax.dynamic_index_in_dim(parts, i, 1, keepdims=False)
        return (lax.psum_scatter(at(plane) + swap(at(1 - plane), 2), "dp", scatter_dimension=0), None), state
    whole_part = jnp.concatenate([settled(part, got) for part, got, _ in state], axis=-1)
    mine, got, _, give = halve(whole_part, ["z4"], "z4")
    return (mine, got), give


def line_start(parts):
    return lax.psum_scatter(parts, "dp", scatter_dimension=0)


def line_end(mine):
    plane = lax.axis_index("pipe") // 2
    mine = mine.reshape(2, -1, mine.shape[1])
    at = lambda i: lax.dynamic_index_in_dim(mine, i, 0, keepdims=False)
    return at(plane) + swap(at(1 - plane), 2)


def from_pipe(value, target, sources):
    return [value if i == target else send(value, [(i, target)]) for i in sources]


def att_result(piece, s):
    rows = piece.shape[0] // 2
    got = together(from_pipe(piece, s, range(4)))
    cols = []
    for j in range(4):
        cols.append(jnp.concatenate([got[(j // 2) * 2 + c][(j % 2) * rows : (j % 2 + 1) * rows] for c in range(2)], axis=0))
    return jnp.concatenate(cols, axis=1)


def mlp_result(piece, s):
    rows = piece.shape[0] // 4
    up, low, high = together((from_pipe(piece, s, (0, 1)), from_pipe(piece[: 2 * rows], s - 1, (2, 3)), from_pipe(piece[2 * rows :], s, (2, 3))))
    first = jnp.concatenate(
        [jnp.concatenate([up[c][j * rows : (j + 1) * rows] for c in range(2)], axis=0) for j in range(4)], axis=1
    )
    low, high = jnp.concatenate(low, axis=0), jnp.concatenate(high, axis=0)
    return first, low, high


def choose(place, options):
    result = options[-1]
    for s in range(len(options) - 2, -1, -1):
        result = jnp.where(place == s, options[s], result)
    return result


def small_sum(value, step):
    if lax.axis_size("dp") != 8:
        return lax.psum(value, ("dp", "pipe")) if step == 0 else value
    if step < 2:
        return value + swap(value, step + 1)
    return value + dp_swap(value, 1 << (step - 2))


def local(
    inputs, out_grad, page_side, norm_gain, norm_shift, layer_scale, w_first, w_half, rel_table
):
    place = lax.axis_index("pipe")
    sections = lax.axis_size("pipe")
    dp_size, dp_place = lax.axis_size("dp"), lax.axis_index("dp")
    micro_count, slot_rows, width = inputs.shape
    halves = sections // micro_count
    assert halves == 2 and sections == 4
    rows = slot_rows // halves
    plane, core = place // 2, place % 2
    layers, heads = rel_table.shape[:2]

    own_params = jnp.stack([norm_gain[0], norm_shift[0], layer_scale[0]])
    seen = [own_params] + [swap(own_params, bit) for bit in (1, 2, 3)]
    params = [choose(place, [seen[s ^ p] for p in range(sections)]) for s in range(sections)]

    own_first, own_half = w_first[0], w_half[0]
    count = own_first.shape[0] // 2
    quarter = count // 4
    q = dp_place % 4
    share = [lax.dynamic_slice_in_dim(own_first, c * count + q * quarter, quarter, 0) for c in range(2)]
    mine_att = pick(core, send(share[0], [(0, 2), (2, 0)]), send(share[1], [(0, 3), (2, 1)]))
    some_att = quad_start(mine_att)
    share, own_half_y = tie((share, own_half), mine_att, seen)
    mine_up = pick(core, send(share[0], [(1, 2), (3, 0)]), send(share[1], [(1, 3), (3, 1)]))
    near_first = swap(tie(own_first, mine_att, seen), 1)
    all_att = quad_end(*tie(some_att, mine_up))
    some_up = quad_start(tie(mine_up, some_att))
    cut_half = own_half.shape[0] // 3
    own_half_y = tie(own_half_y, mine_up)
    far_half = [swap(own_half_y[i * cut_half : (i + 1) * cut_half], 2) for i in range(3)]
    far_att = quad_place(*tie(all_att, some_up, far_half[0]))
    far_att_other = swap(far_att, 1)
    near_half = swap(tie(own_half, far_att), 1)
    att_refs = (own_first, near_first, far_att, far_att_other)
    infos = [jnp.stack([(plane == layer).astype(jnp.int32), core.astype(jnp.int32)]) for layer in range(layers)]

    micro, half = plane, core
    side = lax.dynamic_index_in_dim(page_side, micro, 0, keepdims=False)[0]
    own_rows = lambda x: lax.dynamic_slice(x, (micro, half * rows, 0), (1, rows, width))[0]
    key_ids = (jnp.arange(slot_rows, dtype=jnp.int32) + half * rows) % slot_rows
    layout = geometry(side, key_ids, slot_rows)
    own_layout = [c[:rows] for c in layout]
    hot, hot_back = row_features(*own_layout, True), row_features(*own_layout, False)
    keys = key_features(*layout)
    maps = table_rows(rel_table)

    def shared(even, odd, layer):
        mine, other = pick(core, even, odd), pick(core, odd, even)
        inside = [(2 * layer, 2 * layer + 1), (2 * layer + 1, 2 * layer)]
        straight = [(p ^ 2, p) for p in (2 * layer, 2 * layer + 1)]
        across = [(p ^ 3, p) for p in (2 * layer, 2 * layer + 1)]
        return [mine, send(other, inside), send(mine, straight), send(other, across)]

    def to_one(value, s):
        return [value] + [to_target(value, s, bit) for bit in (1, 2, 3)]

    def collected(parts):
        return choose(place, [jnp.stack([parts[s][i ^ s] for i in range(sections)]) for s in range(sections)])

    current = own_rows(inputs)
    kept, outs = [], {}
    for layer in range(layers):
        p0, p1, info = params[2 * layer], params[2 * layer + 1], infos[layer]
        normed, proj = project(info, current, p0, att_refs)
        if layer == 0:
            normed, proj = tie((normed, proj), far_half[1])
        partner = swap(proj[:, width:], 1)
        if layer == 0:
            far_up = quad_place(*quad_end(*tie(some_up, normed)))
            partner = tie(partner, far_up)
        context, rest, inv, queries = attn_forward(hot, maps[layer], proj, partner, keys)
        if layer == 0:
            far_up_other = swap(far_up, 1)
            far_half_other = [swap(part, 1) for part in far_half[:2]]
            context, last_half = tie((context, far_half[2]), far_up_other, near_half, far_half_other)
            up_refs = (own_first, near_first, far_up, far_up_other)
            down_refs = (own_half, near_half, far_half[0], far_half[1], last_half, *far_half_other, swap(last_half, 1))
        else:
            context, rest, inv, queries = tie((context, rest, inv, queries), outs[0][2])
        b0, x1, n1, slope, hidden, b1, x2 = block_out(info, current, context, p0, p1, att_refs, up_refs, down_refs)
        if layer == 1:
            b0, x1, n1, slope, hidden, b1, x2 = tie((b0, x1, n1, slope, hidden, b1, x2), outs[0])
        kept.append((current, normed, proj, partner, (context, rest, inv), queries, b0, x1, n1, slope, hidden, b1))
        outs[2 * layer] = outs[2 * layer + 1] = shared(x1, x2, layer)
        current = x2

    cut = heads // 4
    tables, vecs, grads = {}, {}, {}
    core_id = core.astype(jnp.int32)

    x, normed, proj, partner, outcome, queries, b0, x1, n1, slope, hidden, b1 = kept[1]
    p0, p1, info = params[2], params[3], infos[1]
    grad = tie(own_rows(out_grad), current)
    db1, d_pre, gx1, db0, d_context, vec1 = block_back(info, grad, x1, slope, b1, b0, p0, p1, att_refs, up_refs, down_refs)
    db1, d_pre, gx1, db0, d_context, vec1 = tie((db1, d_pre, gx1, db0, d_context, vec1), outs[2][2])
    keep, other = weight_grads(mlp_grads_kernel, core, dp_size, 15, n1, d_pre, hidden, db1)
    keep, other = tie((keep, other), outs[2])
    got = swap(other, 1)
    back = lambda d_ctx, i: attn_backward(hot_back, queries, proj, partner, keys, d_ctx, outcome, i * cut, cut)
    dqa, mya, oa, ta = back(tie(d_context, keep), 0)
    dqa, mya, oa, ta, got = together((dqa, mya, oa, ta, got))
    mlp_b = keep + got
    gota = swap(oa, 1)
    dqb, myb, ob, tb = back(tie(d_context, mlp_b, oa), 1)
    dqb, myb, ob, tb, gota = together((dqb, myb, ob, tb, gota))
    gotb = swap(ob, 1)
    mlp_b = line_start(mlp_b)
    d_proj, gx0, vec0 = project_back(info, gx1, x, p0, (dqa, dqb, mya, myb, gota, gotb), att_refs)
    keep, other = weight_grads(att_grads_kernel, core, dp_size, 9, normed, d_proj, outcome[0], db0)
    got = swap(other, 1)
    grads[2] = grads[3] = shared(gx0, gx1, 1)
    tables[1] = (ta, tb)
    vecs[3], vecs[2] = vec1[:3], jnp.concatenate([vec0[:2], vec1[3:4]])

    x, normed, proj, partner, outcome, queries, b0, x1, n1, slope, hidden, b1 = kept[0]
    p0, p1, info = params[0], params[1], infos[0]
    db1, d_pre, gx1, db0, d_context, vec1 = block_back(info, tie(gx0, keep), x1, slope, b1, b0, p0, p1, att_refs, up_refs, down_refs)
    db1, d_pre, gx1, db0, d_context, vec1, got = tie((db1, d_pre, gx1, db0, d_context, vec1, got), grads[2][2])
    att_b = keep + got
    d_pre = tie(d_pre, att_b)
    att_b = line_start(att_b)
    keep, other = weight_grads(mlp_grads_kernel, core, dp_size, 15, n1, d_pre, hidden, db1)
    keep, other = tie((keep, other), grads[2])
    got = swap(other, 1)
    grads[1] = to_one(gx1, 1)
    dqa, mya, oa, ta = back(tie(d_context, keep), 0)
    dqa, mya, oa, ta, got, mlp_b = tie((dqa, mya, oa, ta, got, mlp_b), grads[1])
    mlp_a = cube_start(keep + got)
    gota = swap(oa, 1)
    mlp_a, given = cube_step(mlp_a, 0)
    dqb, myb, ob, tb = back(tie(d_context, given, oa), 1)
    dqb, myb, ob, tb, gota, mlp_a = hold((dqb, myb, ob, tb, gota, mlp_a), 5)
    gotb = swap(ob, 1)
    mlp_a, given = cube_step(mlp_a, 1)
    gotb = tie(gotb, given)
    d_proj, gx0, vec0 = project_back(info, gx1, x, p0, (dqa, dqb, mya, myb, gota, gotb), att_refs)
    d_proj, gx0, vec0, mlp_a = hold((d_proj, gx0, vec0, mlp_a), 3)
    mlp_a, given = cube_step(mlp_a, 2)
    keep, other = weight_grads(att_grads_kernel, core, dp_size, 9, tie(normed, given), d_proj, outcome[0], db0)
    keep, other, att_b, mlp_a = hold((keep, other, att_b, mlp_a), 3)
    got = swap(other, 1)
    tables = [(ta, tb), tables[1]]
    vecs[1], vecs[0] = vec1[:3], jnp.concatenate([vec0[:2], vec1[3:4]])
    stack = lambda parts: jnp.stack([parts[s] for s in range(sections)])
    table_all = [jnp.concatenate(tables[layer])[:, :4].reshape(heads, 2, 128)[..., : 2 * SIDE_L + 1] for layer in range(layers)]
    small = jnp.concatenate([stack(vecs).reshape(-1), jnp.stack(table_all).reshape(-1)])
    small = small_sum(small, 0)
    mlp_a, _ = cube_end(mlp_a)
    got, keep, small = together((got, keep, small))
    att_a = cube_start(keep + got)
    att_a, given = cube_step(att_a, 0)
    small = small_sum(small, 1)
    section_out = collected(tie(outs, given)).reshape(1, micro_count, slot_rows, width)
    small, section_out, mlp_a, att_a = hold((small, section_out, mlp_a, att_a), 3)
    att_a, given = cube_step(att_a, 1)
    small = small_sum(small, 2)
    mlp_a, gx0 = tie((settled(*mlp_a), gx0), given)
    grads[0] = to_one(gx0, 0)
    mlp_result_a = mlp_result(mlp_a, 1)
    small, att_a = hold((small, att_a), 1)
    att_a, given = cube_step(att_a, 2)
    small = small_sum(small, 3)
    mlp_b, att_b = tie((mlp_b, att_b), given)
    mlp_b, att_b = line_end(mlp_b), line_end(att_b)
    small, mlp_b, att_b, grads[0], mlp_result_a, att_a = hold((small, mlp_b, att_b, grads[0], mlp_result_a, att_a), 5)
    att_a, given = cube_end(att_a)
    small = small_sum(small, 4)
    mlp_b, att_b, grads = tie((mlp_b, att_b, grads), given)
    mlp_result_b, att_b = mlp_result(mlp_b, 3), att_result(att_b, 2)
    in_grads = collected({s: [part.astype(F32) for part in grads[s]] for s in range(sections)}).reshape(1, micro_count, slot_rows, width)
    small, mlp_result_b, att_b, in_grads, att_a = together((small, mlp_result_b, att_b, in_grads, att_a))
    att_a = settled(*att_a)

    first_grads, half_grads = {}, {}
    first_grads[3], half_grads[2], half_grads[3] = mlp_result_b
    first_grads[2] = att_b
    first_grads[1], half_grads[0], half_grads[1] = mlp_result_a
    first_grads[0] = att_result(att_a, 0)

    g_first = choose(place, [first_grads[s].astype(F32) for s in range(sections)])[None]
    g_half = choose(place, [half_grads[s].astype(F32) for s in range(sections)])[None]
    vec_size = sections * 3 * width
    vec_all = small[:vec_size].reshape(sections, 3, width)
    g_table = small[vec_size:].reshape(rel_table.shape)
    cols = width // dp_size
    mine = lax.dynamic_slice(vec_all, (place, 0, dp_place * cols), (1, 3, cols))
    return (section_out, in_grads, g_first, g_half, mine[:, 0], mine[:, 1], mine[:, 2], g_table)


def solution(mesh):
    in_specs = (
        P(None, "dp", None),
        P(None, "dp", None),
        P(None, "dp"),
        P("pipe", None),
        P("pipe", None),
        P("pipe", None),
        P("pipe", None, None),
        P("pipe", None, None),
        P(),
    )
    out_specs = (
        P("pipe", None, "dp", None),
        P("pipe", None, "dp", None),
        P("pipe", "dp", None),
        P("pipe", "dp", None),
        P("pipe", "dp"),
        P("pipe", "dp"),
        P("pipe", "dp"),
        P(),
    )
    return jax.shard_map(local, mesh=mesh, in_specs=in_specs, out_specs=out_specs, check_vma=False)
```

time: 822 us -> 631 us (0.77)
  waiting for transfers between devices: 351 us -> 120 us
  Pallas kernels: 132 us -> 254 us
  matrix products: 116 us -> 0 us
  starting transfers between devices: 11.8 us -> 109 us
  blocking collectives: 78.9 us -> 0 us
  other arithmetic: 52.9 us -> 62.4 us
    reduce_scatter x4 -> x2, waiting for transfers between devices: 171 us -> 0.04 us  [line_start(): return lax.psum_scatter(parts, 'dp', scatter_dimension=0)]
    all_gather x2 -> x0, waiting for transfers between devices: 150 us -> none  [the longest x1 98.4 us: local(): first_all = lax.all_gather(w_first[0], 'pipe')]
    pallas_call x2 -> x18, Pallas kernels: 76 us -> 209 us  [the longest x4 71.9 us: attn_backward(): pl.pallas_call(attn_bwd_kernel, grid=(count,), in_specs=[whole((rows, 128...]
    dot_general x26 -> x0, matrix products: 116 us -> none  [the longest x8 43.5 us: dot_nt(): return lax.dot_general(a, b, NT, preferred_element_type=F32)]
    ppermute x6 -> x92, waiting for transfers between devices: 5.92 us -> 120 us  [the longest x20 51.5 us: halve(): lax.ppermute(give, name, [(k, k ^ bit) for k in range(lax.axis_size(name))])]
    ppermute x6 -> x92, starting transfers between devices: 1.81 us -> 109 us  [the longest x61 71.9 us: send(): return lax.ppermute(value, 'pipe', pairs)]
    psum x1 -> x0, blocking collectives: 72.7 us -> none  [local(): small = lax.psum(small, ('dp', 'pipe'))]
    unnamed x231, local copies, waits for them, and re-layouts: 8.33 us -> 31.8 us
  transfers between devices with their start and end apart: 14 -> 94, of which waited for: 8 -> 30; matrix products, arithmetic and copies ran while one was open for 17% -> 11% of each run, Pallas kernels for 5% -> 37%
where the time goes in v2:
time: 631 us; the launch traced here: 621 us
  Pallas kernels  254 us (40%)
  waiting for transfers between devices  120 us (19%)
  starting transfers between devices  109 us (17%)
  other arithmetic  62.4 us (10%)
  local copies, waits for them, and re-layouts  55.3 us (9%)
  between operations  20.5 us (3%)
    pallas_call x4, Pallas kernels, attn_backward(): pl.pallas_call(attn_bwd_kernel, grid=(count,), in_specs=[whole((rows, 128...  71.9 us
    ppermute x61, starting transfers between devices, send(): return lax.ppermute(value, 'pipe', pairs)  71.9 us
    ppermute x20, waiting for transfers between devices, halve(): lax.ppermute(give, name, [(k, k ^ bit) for k in range(lax.axis_size(name))])  51.5 us
    pallas_call x2, Pallas kernels, attn_forward(): pl.pallas_call(attn_fwd_kernel, grid=(pairs,), in_specs=[whole((rows, 128...  45.2 us
    pallas_call x4, Pallas kernels, weight_grads(): pl.pallas_call(kernel, grid=(4,), in_specs=[SMEM, whole(a.shape), col, wh...  42.2 us
    ppermute x61, waiting for transfers between devices, send(): return lax.ppermute(value, 'pipe', pairs)  38.6 us
    pallas_call x2, Pallas kernels, block_back(): pl.pallas_call(block_back_kernel, grid=(1,), in_specs=[SMEM, one, one, AN...  34.4 us
    pallas_call x2, Pallas kernels, block_out(): pl.pallas_call(block_out_kernel, grid=(1,), in_specs=[SMEM, one, one, who...  32.5 us
  transfers between devices with their start and end apart: 94, of which 30 were waited for; matrix products, arithmetic and copies ran while one was open for 11% of the time, Pallas kernels for 37%

profile of v2, /device:TPU:0, one launch (start us, length us, event | category | flops | bytes accessed | tf_op | source)
XLA Modules:
  0.0 620.6 jit_solution(15645913152444014686)
XLA Ops:
  9.8 4.9 collective-permute-start.3
  19.3 3.8 collective-permute-done.3
  23.1 5.9 collective-permute-done.4
  32.1 3.8 collective-permute-start.5
  42.4 3.1 fusion.26
  47.0 4.2 collective-permute-done.6.by_x
  56.9 5.5 collective-permute-done.10.diag_x
  64.8 11.8 %collective-permute-done.11.diag_z = bf16[48,3072]{1,0:T(8,128)(2,1)} collective-permute-done((bf16[48,3072]{1,0:T(8,128)(2,1)}, bf16[48,3072]{1,0:T(8,128)(2,1)}, u32[]{:S(2)}, u32[]{:S(2)}) %collective-permute-start.11) | collective-permute-done | bytes 294944 | tf_op jit(solution)/shard_map/ppermute | solution.py:567
  80.8 3.4 assemble.2.far_own.refs_2_
  92.7 3.9 project.2
  96.7 7.9 %collective-permute-done.16.refs_9_ = bf16[512,768]{1,0:T(8,128)(2,1)} collective-permute-done((bf16[512,768]{1,0:T(8,128)(2,1)}, bf16[512,768]{1,0:T(8,128)(2,1)}, u32[]{:S(2)}, u32[]{:S(2)}) %collective-permute-start.16) | collective-permute-done | bytes 786464 | tf_op jit(solution)/shard_map/ppermute | solution.py:718
  111.1 3.1 collective-permute-done.18.diag_x
  124.4 2.8 fusion.5.key_ref
  127.2 22.5 %attn_fwd.2 = (bf16[576,768]{1,0:T(8,128)(2,1)}, bf16[576,768]{1,0:T(8,128)(2,1)}, f32[576,768]{1,0:T(8,128)}, bf16[12,1152,576]{2,1,0:T(8,128)(2,1)}) custom-call(bf16[576,128]{1,0:T(8,128)(2,1)} %get-tuple-element.714.hot_ref, f32[6,8,128]{2,1,0:T(8,128)} %bitcast.247, bf16[576,2304]{1,0:T(8,128)(2,1)} %copy-done.4, bf16[576,2304]{1,0:T(8,128)(2,1)} %copy-done.4, ...), custom_call_target="tpu_custom_call" | custom-call | flops 520000000 | bytes 1000 | tf_op jit(solution)/shard_map/attn_fwd/pallas_call | solution.py:144
  154.4 16.1 %block_out.2 = (bf16[576,768]{1,0:T(8,128)(2,1)}, bf16[576,768]{1,0:T(8,128)(2,1)}, bf16[576,768]{1,0:T(8,128)(2,1)}, bf16[576,3072]{1,0:T(8,128)(2,1)}, bf16[57...) custom-call(s32[2]{0:T(128)} %copy-done.54, bf16[576,768]{1,0:T(8,128)(2,1)} %copy-done.7, ...), custom_call_target="tpu_custom_call" | custom-call | flops 240000000 | bytes 1000 | tf_op jit(solution)/shard_map/block_out/pallas_call | solution.py:407
  174.0 4.9 project.3
  186.9 22.7 %attn_fwd.3 = (bf16[576,768]{1,0:T(8,128)(2,1)}, bf16[576,768]{1,0:T(8,128)(2,1)}, f32[576,768]{1,0:T(8,128)}, bf16[12,1152,576]{2,1,0:T(8,128)(2,1)}) custom-call(bf16[576,128]{1,0:T(8,128)(2,1)} %get-tuple-element.714.hot_ref, f32[6,8,128]{2,1,0:T(8,128)} %bitcast.246, bf16[576,2304]{1,0:T(8,128)(2,1)} %copy-done.5, bf16[576,2304]{1,0:T(8,128)(2,1)} %copy-done.5, ...), custom_call_target="tpu_custom_call" | custom-call | flops 520000000 | bytes 1000 | tf_op jit(solution)/shard_map/attn_fwd/pallas_call | solution.py:144
  209.7 16.4 %block_out.3 = (bf16[576,768]{1,0:T(8,128)(2,1)}, bf16[576,768]{1,0:T(8,128)(2,1)}, bf16[576,768]{1,0:T(8,128)(2,1)}, bf16[576,3072]{1,0:T(8,128)(2,1)}, bf16[57...) custom-call(s32[2]{0:T(128)} %copy-done.56, bf16[576,768]{1,0:T(8,128)(2,1)} %get-tuple-element.343.x_ref, ...), custom_call_target="tpu_custom_call" | custom-call | flops 240000000 | bytes 1000 | tf_op jit(solution)/shard_map/block_out/pallas_call | solution.py:407
  226.2 3.1 broadcast_select_fusion.2
  229.3 4.7 collective-permute-start.30
  239.6 17.0 %block_back.2 = (bf16[576,768]{1,0:T(8,128)(2,1)}, bf16[576,3072]{1,0:T(8,128)(2,1)}, bf16[576,768]{1,0:T(8,128)(2,1)}, bf16[576,768]{1,0:T(8,128)(2,1)}, bf16[576,768]{1,0:T(8,128)(2,1)}, /*index=5*/f32[8,768]{1,0:T(8,128)}) custom-call(s32[2]{0:T(128)} %copy-done.56, bf16[576,768]{1,0:T(8,128)(2,1)} %dynamic-slice_bitcast_fusion.gy_ref, ...), custom_call_target="tpu_custom_call" | custom-call | flops 280000000 | bytes 1000 | tf_op jit(solution)/shard_map/block_back/pallas_call | solution.py:490
  260.8 14.0 %mlp_grads.2 = (bf16[8,384,768]{2,1,0:T(8,128)(2,1)}, bf16[8,384,768]{2,1,0:T(8,128)(2,1)}) custom-call(s32[1]{0:T(128)} %bitcast.core_ref, bf16[576,768]{1,0:T(8,128)(2,1)S(1)} %copy-done.29, bf16[576,3072]{1,0:T(8,128)(2,1)S(1)} %copy-done.15, bf16[576,3072]{1,0:T(8,128)(2,1)} %get-tuple-element.375.hid_ref, bf16[576,768]{1,0:T(8,128)(2,1)S(1)} %copy-done.31), custom_call_target="tpu_custom_call" | custom-call | flops 300000000 | bytes 1000 | tf_op jit(solution)/shard_map/mlp_grads/pallas_call | solution.py:704
  275.9 17.9 %attn_bwd.4 = (bf16[576,384]{1,0:T(8,128)(2,1)}, bf16[2,576,384]{2,1,0:T(8,128)(2,1)}, bf16[2,576,384]{2,1,0:T(8,128)(2,1)}, f32[3,8,128]{2,1,0:T(8,128)}) custom-call(bf16[576,128]{1,0:T(8,128)(2,1)} %get-tuple-element.713.hot_ref, bf16[12,1152,576]{2,1,0:T(8,128)(2,1)} %get-tuple-element.371.w_ref, bf16[576,2304]{1,0:T(8,128)(2,1)} %copy-done.5, ...), custom_call_target="tpu_custom_call" | custom-call | flops 360000000 | bytes 1000 | tf_op jit(solution)/shard_map/attn_bwd/pallas_call | solution.py:226
  293.9 5.7 add.438
  300.1 18.2 %attn_bwd.5 = (bf16[576,384]{1,0:T(8,128)(2,1)}, bf16[2,576,384]{2,1,0:T(8,128)(2,1)}, bf16[2,576,384]{2,1,0:T(8,128)(2,1)}, f32[3,8,128]{2,1,0:T(8,128)}) custom-call(bf16[576,128]{1,0:T(8,128)(2,1)} %get-tuple-element.713.hot_ref, bf16[12,1152,576]{2,1,0:T(8,128)(2,1)} %get-tuple-element.371.w_ref, bf16[576,2304]{1,0:T(8,128)(2,1)} %copy-done.5, ...), custom_call_target="tpu_custom_call" | custom-call | flops 360000000 | bytes 1000 | tf_op jit(solution)/shard_map/attn_bwd/pallas_call | solution.py:226
  324.2 6.7 %project_back.2 = (bf16[576,2304]{1,0:T(8,128)(2,1)}, bf16[576,768]{1,0:T(8,128)(2,1)S(1)}, f32[8,768]{1,0:T(8,128)S(1)}) custom-call(s32[2]{0:T(128)S(1)} %copy-done.57, bf16[576,768]{1,0:T(8,128)(2,1)S(1)} %copy-done.16, bf16[576,768]{1,0:T(8,128)(2,1)S(1)} %copy-done.10, f32[3,768]{1,0:T(4,128)S(1)} %copy-done.51, bf16[576,384]{1,0:T(8,128)(2,1)S(1)} %copy-done.46, ...), custom_call_target="tpu_custom_call" | custom-call | flops 140000000 | bytes 1000 | tf_op jit(solution)/shard_map/project_back/pallas_call | solution.py:536
  331.0 7.4 %att_grads.2 = (bf16[8,192,768]{2,1,0:T(8,128)(2,1)S(1)}, bf16[8,192,768]{2,1,0:T(8,128)(2,1)}) custom-call(s32[1]{0:T(128)} %bitcast.core_ref, bf16[576,768]{1,0:T(8,128)(2,1)S(1)} %copy-done.38, bf16[576,2304]{1,0:T(8,128)(2,1)} %get-tuple-element.403.dproj_ref, bf16[576,768]{1,0:T(8,128)(2,1)S(1)} %copy-done.12, bf16[576,768]{1,0:T(8,128)(2,1)S(1)} %copy-done.40), custom_call_target="tpu_custom_call" | custom-call | flops 180000000 | bytes 1000 | tf_op jit(solution)/shard_map/att_grads/pallas_call | solution.py:704
  343.4 3.0 collective-permute-start.39
  346.4 17.4 %block_back.3 = (bf16[576,768]{1,0:T(8,128)(2,1)}, bf16[576,3072]{1,0:T(8,128)(2,1)}, bf16[576,768]{1,0:T(8,128)(2,1)}, bf16[576,768]{1,0:T(8,128)(2,1)}, bf16[576,768]{1,0:T(8,128)(2,1)}, /*index=5*/f32[8,768]{1,0:T(8,128)}) custom-call(s32[2]{0:T(128)} %copy-done.54, bf16[576,768]{1,0:T(8,128)(2,1)} %copy-done.13, ...), custom_call_target="tpu_custom_call" | custom-call | flops 280000000 | bytes 1000 | tf_op jit(solution)/shard_map/block_back/pallas_call | solution.py:490
  364.8 4.5 add.439
  371.6 13.9 %mlp_grads.3 = (bf16[8,384,768]{2,1,0:T(8,128)(2,1)}, bf16[8,384,768]{2,1,0:T(8,128)(2,1)}) custom-call(s32[1]{0:T(128)} %bitcast.core_ref, bf16[576,768]{1,0:T(8,128)(2,1)S(1)} %copy-done.28, bf16[576,3072]{1,0:T(8,128)(2,1)S(1)} %copy-done.14, bf16[576,3072]{1,0:T(8,128)(2,1)} %get-tuple-element.424.hid_ref, bf16[576,768]{1,0:T(8,128)(2,1)S(1)} %copy-done.30), custom_call_target="tpu_custom_call" | custom-call | flops 300000000 | bytes 1000 | tf_op jit(solution)/shard_map/mlp_grads/pallas_call | solution.py:704
  390.6 17.8 %attn_bwd.6 = (bf16[576,384]{1,0:T(8,128)(2,1)}, bf16[2,576,384]{2,1,0:T(8,128)(2,1)}, bf16[2,576,384]{2,1,0:T(8,128)(2,1)}, f32[3,8,128]{2,1,0:T(8,128)}) custom-call(bf16[576,128]{1,0:T(8,128)(2,1)} %get-tuple-element.713.hot_ref, bf16[12,1152,576]{2,1,0:T(8,128)(2,1)} %get-tuple-element.418.w_ref, bf16[576,2304]{1,0:T(8,128)(2,1)} %copy-done.4, ...), custom_call_target="tpu_custom_call" | custom-call | flops 360000000 | bytes 1000 | tf_op jit(solution)/shard_map/attn_bwd/pallas_call | solution.py:226
  408.6 5.8 add.440
  420.5 18.0 %attn_bwd.7 = (bf16[576,384]{1,0:T(8,128)(2,1)}, bf16[2,576,384]{2,1,0:T(8,128)(2,1)}, bf16[2,576,384]{2,1,0:T(8,128)(2,1)}, f32[3,8,128]{2,1,0:T(8,128)}) custom-call(bf16[576,128]{1,0:T(8,128)(2,1)} %get-tuple-element.713.hot_ref, bf16[12,1152,576]{2,1,0:T(8,128)(2,1)} %get-tuple-element.418.w_ref, bf16[576,2304]{1,0:T(8,128)(2,1)} %copy-done.4, ...), custom_call_target="tpu_custom_call" | custom-call | flops 360000000 | bytes 1000 | tf_op jit(solution)/shard_map/attn_bwd/pallas_call | solution.py:226
  438.5 4.2 collective-permute-done.45
  452.3 5.9 collective-permute-done.49
  458.2 7.5 %collective-permute-done.50 = bf16[2,2,192,256]{3,2,1,0:T(8,128)(2,1)S(1)} collective-permute-done((bf16[2,2,192,256]{3,2,1,0:T(8,128)(2,1)S(1)}, bf16[2,2,192,256]{3,2,1,0:T(8,128)(2,1)S(1)}, u32[]{:S(2)}, u32[]{:S(2)}) %collective-permute-start.50) | collective-permute-done | bytes 393248 | tf_op jit(solution)/shard_map/ppermute | solution.py:756
  466.7 6.5 %project_back.3 = (bf16[576,2304]{1,0:T(8,128)(2,1)}, bf16[576,768]{1,0:T(8,128)(2,1)S(1)}, f32[8,768]{1,0:T(8,128)S(1)}) custom-call(s32[2]{0:T(128)S(1)} %copy-done.55, bf16[576,768]{1,0:T(8,128)(2,1)S(1)} %copy-done.19, bf16[576,768]{1,0:T(8,128)(2,1)S(1)} %copy-done.8, f32[3,768]{1,0:T(4,128)S(1)} %copy-done.49, bf16[576,384]{1,0:T(8,128)(2,1)S(1)} %copy-done.44, ...), custom_call_target="tpu_custom_call" | custom-call | flops 140000000 | bytes 1000 | tf_op jit(solution)/shard_map/project_back/pallas_call | solution.py:536
  478.7 7.0 %att_grads.3 = (bf16[8,192,768]{2,1,0:T(8,128)(2,1)S(1)}, bf16[8,192,768]{2,1,0:T(8,128)(2,1)}) custom-call(s32[1]{0:T(128)} %bitcast.core_ref, bf16[576,768]{1,0:T(8,128)(2,1)S(1)} %copy-done.33, bf16[576,2304]{1,0:T(8,128)(2,1)} %get-tuple-element.473.dproj_ref, bf16[576,768]{1,0:T(8,128)(2,1)S(1)} %copy-done.11, bf16[576,768]{1,0:T(8,128)(2,1)S(1)} %copy-done.36), custom_call_target="tpu_custom_call" | custom-call | flops 180000000 | bytes 1000 | tf_op jit(solution)/shard_map/att_grads/pallas_call | solution.py:704
  503.5 3.6 maximum_select_fusion
  507.2 4.5 collective-permute-done.59
  511.9 5.0 collective-permute-done.61
  546.2 13.4 %collective-permute-done.79 = bf16[2,96,256]{2,1,0:T(8,128)(2,1)S(1)} collective-permute-done((bf16[2,96,256]{2,1,0:T(8,128)(2,1)S(1)}, bf16[2,96,256]{2,1,0:T(8,128)(2,1)S(1)}, u32[]{:S(2)}, u32[]{:S(2)}) %collective-permute-start.79) | collective-permute-done | bytes 98336 | tf_op jit(solution)/shard_map/ppermute | solution.py:756
  562.7 6.8 %collective-permute-done.67 = bf16[192,768]{1,0:T(8,128)(2,1)S(1)} collective-permute-done((bf16[192,768]{1,0:T(8,128)(2,1)S(1)}, bf16[192,768]{1,0:T(8,128)(2,1)S(1)}, u32[]{:S(2)}, u32[]{:S(2)}) %collective-permute-start.67) | collective-permute-done | bytes 294944 | tf_op jit(solution)/shard_map/ppermute | solution.py:718
  574.0 3.0 collective-permute-start.81
  577.1 7.7 %select_select_fusion = f32[4,576,768]{2,1,0:T(8,128)} fusion(bf16[1,576,768]{2,1,0:T(8,128)(2,1)S(1)} %bitcast.233, bf16[1,576,768]{2,1,0:T(8,128)(2,1)S(1)} %bitcast.232, bf16[1,576,768]{2,1,0:T(8,128)(2,1)S(1)} %bitcast.231, bf16[1,576,768]{2,1,0:T(8,128)(2,1)S(1)} %bitcast.195, bf16[1,576,768]{2,1,0:T(8,128)(2,1)S(1)} %bitcast.229, ...), kind=kLoop, calls=%fused_computation | loop fusion | flops 33619968 | bytes 21233668 | tf_op jit(solution)/shard_map/jit(_where)/select_n | solution.py:816
  590.4 5.7 collective-permute-done.88
  603.0 3.3 collective-permute-done.90
  (549 shorter events, 194.4 us)
Async XLA Ops:
  7.2 401.3 %reduce-scatter.3.cloned.1.call-start = ((), (), s32[]{:S(2)}) async-start(), calls=%async_computation.2 | async-start | bytes 5308416 | tf_op jit(solution)/shard_map/reduce_scatter | solution.py:780
  32.1 58.2 %collective-permute-start.5 = (bf16[768,3072]{1,0:T(8,128)(2,1)}, bf16[768,3072]{1,0:T(8,128)(2,1)}, u32[]{:S(2)}, u32[]{:S(2)}) collective-permute-start(bf16[768,3072]{1,0:T(8,128)(2,1)} %bitcast.185), channel_id=1, source_target_pairs={{0,1},{1,0},{2,3},{3,2},{4,5},{5,4},{6,7},{7,6},{8,9},{9,8},{10,11... | collective-permute-start | bytes 14155784 | tf_op jit(solution)/shard_map/ppermute | solution.py:718
  35.9 15.3 %collective-permute-start.6 = (bf16[96,3072]{1,0:T(8,128)(2,1)S(1)}, bf16[96,3072]{1,0:T(8,128)(2,1)S(1)}, u32[]{:S(2)}, u32[]{:S(2)}) collective-permute-start(bf16[96,3072]{1,0:T(8,128)(2,1)S(1)} %broadcast_select_fusion.7.mine), channel_id=1, source_target_pairs={{0,4},{4,0},{8,12},{12,8},{16,20},{20,16},{24,28},{28,24},{1,5},{5... | collective-permute-start | bytes 1769480 | tf_op jit(solution)/shard_map/ppermute | solution.py:567
  37.4 15.0 %collective-permute-start.7 = (bf16[96,3072]{1,0:T(8,128)(2,1)S(1)}, bf16[96,3072]{1,0:T(8,128)(2,1)S(1)}, u32[]{:S(2)}, u32[]{:S(2)}) collective-permute-start(bf16[96,3072]{1,0:T(8,128)(2,1)S(1)} %broadcast_select_fusion.7.mine), channel_id=1, source_target_pairs={{0,8},{4,12},{8,0},{12,4},{16,24},{20,28},{24,16},{28,20},{1,9},{5... | collective-permute-start | bytes 1769480 | tf_op jit(solution)/shard_map/ppermute | solution.py:567
  45.5 31.2 %collective-permute-start.14 = (bf16[512,768]{1,0:T(8,128)(2,1)}, bf16[512,768]{1,0:T(8,128)(2,1)}, u32[]{:S(2)}, u32[]{:S(2)}) collective-permute-start(bf16[512,768]{1,0:T(8,128)(2,1)} %get-tuple-element.620), channel_id=1, source_target_pairs={{0,2},{1,3},{2,0},{3,1},{4,6},{5,7},{6,4},{7,5},{8,10},{9,11},{10,... | collective-permute-start | bytes 2359304 | tf_op jit(solution)/shard_map/ppermute | solution.py:718
  53.0 23.6 %collective-permute-start.12 = (bf16[96,3072]{1,0:T(8,128)(2,1)}, bf16[96,3072]{1,0:T(8,128)(2,1)}, u32[]{:S(2)}, u32[]{:S(2)}) collective-permute-start(bf16[96,3072]{1,0:T(8,128)(2,1)} %broadcast_select_fusion.6.mine), channel_id=1, source_target_pairs={{0,4},{4,0},{8,12},{12,8},{16,20},{20,16},{24,28},{28,24},{1,5},{5... | collective-permute-start | bytes 1769480 | tf_op jit(solution)/shard_map/ppermute | solution.py:567
  54.6 22.1 %collective-permute-start.13 = (bf16[96,3072]{1,0:T(8,128)(2,1)}, bf16[96,3072]{1,0:T(8,128)(2,1)}, u32[]{:S(2)}, u32[]{:S(2)}) collective-permute-start(bf16[96,3072]{1,0:T(8,128)(2,1)} %broadcast_select_fusion.6.mine), channel_id=1, source_target_pairs={{0,8},{4,12},{8,0},{12,4},{16,24},{20,28},{24,16},{28,20},{1,9},{5... | collective-permute-start | bytes 1769480 | tf_op jit(solution)/shard_map/ppermute | solution.py:567
  84.3 20.3 %collective-permute-start.16 = (bf16[512,768]{1,0:T(8,128)(2,1)}, bf16[512,768]{1,0:T(8,128)(2,1)}, u32[]{:S(2)}, u32[]{:S(2)}) collective-permute-start(bf16[512,768]{1,0:T(8,128)(2,1)} %get-tuple-element.619), channel_id=1, source_target_pairs={{0,2},{1,3},{2,0},{3,1},{4,6},{5,7},{6,4},{7,5},{8,10},{9,11},{10,... | collective-permute-start | bytes 2359304 | tf_op jit(solution)/shard_map/ppermute | solution.py:718
  110.6 39.2 %collective-permute-start.22 = (bf16[1536,768]{1,0:T(8,128)(2,1)}, bf16[1536,768]{1,0:T(8,128)(2,1)S(1)}, u32[]{:S(2)}, u32[]{:S(2)}) collective-permute-start(bf16[1536,768]{1,0:T(8,128)(2,1)} %bitcast.10.refs_6_), channel_id=1, source_target_pairs={{0,1},{1,0},{2,3},{3,2},{4,5},{5,4},{6,7},{7,6},{8,9},{9,8},{10,11... | collective-permute-start | bytes 7077896 | tf_op jit(solution)/shard_map/ppermute | solution.py:718
  117.9 31.9 %collective-permute-start.21 = (bf16[384,3072]{1,0:T(8,128)(2,1)S(1)}, bf16[384,3072]{1,0:T(8,128)(2,1)}, u32[]{:S(2)}, u32[]{:S(2)}) collective-permute-start(bf16[384,3072]{1,0:T(8,128)(2,1)S(1)} %assemble.3.refs_4_), channel_id=1, source_target_pairs={{0,1},{1,0},{2,3},{3,2},{4,5},{5,4},{6,7},{7,6},{8,9},{9,8},{10,11... | collective-permute-start | bytes 7077896 | tf_op jit(solution)/shard_map/ppermute | solution.py:718
  120.5 29.2 %collective-permute-start.20 = (bf16[512,768]{1,0:T(8,128)(2,1)}, bf16[512,768]{1,0:T(8,128)(2,1)S(1)}, u32[]{:S(2)}, u32[]{:S(2)}) collective-permute-start(bf16[512,768]{1,0:T(8,128)(2,1)} %get-tuple-element.618), channel_id=1, source_target_pairs={{0,2},{1,3},{2,0},{3,1},{4,6},{5,7},{6,4},{7,5},{8,10},{9,11},{10,... | collective-permute-start | bytes 2359304 | tf_op jit(solution)/shard_map/ppermute | solution.py:718
  121.6 28.1 %collective-permute-start.23 = (bf16[512,768]{1,0:T(8,128)(2,1)}, bf16[512,768]{1,0:T(8,128)(2,1)}, u32[]{:S(2)}, u32[]{:S(2)}) collective-permute-start(bf16[512,768]{1,0:T(8,128)(2,1)} %collective-permute-done.14.refs_8_), channel_id=1, source_target_pairs={{0,1},{1,0},{2,3},{3,2},{4,5},{5,4},{6,7},{7,6},{8,9},{9,8},{10,11... | collective-permute-start | bytes 2359304 | tf_op jit(solution)/shard_map/ppermute | solution.py:718
  121.8 27.9 %collective-permute-start.24 = (bf16[512,768]{1,0:T(8,128)(2,1)}, bf16[512,768]{1,0:T(8,128)(2,1)}, u32[]{:S(2)}, u32[]{:S(2)}) collective-permute-start(bf16[512,768]{1,0:T(8,128)(2,1)} %collective-permute-done.16.refs_9_), channel_id=1, source_target_pairs={{0,1},{1,0},{2,3},{3,2},{4,5},{5,4},{6,7},{7,6},{8,9},{9,8},{10,11... | collective-permute-start | bytes 2359304 | tf_op jit(solution)/shard_map/ppermute | solution.py:718
  181.0 28.7 %collective-permute-start.27 = (bf16[576,768]{1,0:T(8,128)(2,1)S(1)}, bf16[576,768]{1,0:T(8,128)(2,1)S(1)}, u32[]{:S(2)}, u32[]{:S(2)}) collective-permute-start(bf16[576,768]{1,0:T(8,128)(2,1)S(1)} %get-tuple-element.498), channel_id=1, source_target_pairs={{2,0},{3,1},{6,4},{7,5},{10,8},{11,9},{14,12},{15,13},{18,16},{19,... | collective-permute-start | bytes 2654216 | tf_op jit(solution)/shard_map/ppermute | solution.py:718
  182.3 43.9 %collective-permute-start.28 = (bf16[576,768]{1,0:T(8,128)(2,1)S(1)}, bf16[576,768]{1,0:T(8,128)(2,1)S(1)}, u32[]{:S(2)}, u32[]{:S(2)}) collective-permute-start(bf16[576,768]{1,0:T(8,128)(2,1)S(1)} %get-tuple-element.625), channel_id=1, source_target_pairs={{0,1},{1,0},{4,5},{5,4},{8,9},{9,8},{12,13},{13,12},{16,17},{17,16... | collective-permute-start | bytes 2654216 | tf_op jit(solution)/shard_map/ppermute | solution.py:718
  184.4 41.8 %collective-permute-start.29 = (bf16[576,768]{1,0:T(8,128)(2,1)S(1)}, bf16[576,768]{1,0:T(8,128)(2,1)S(1)}, u32[]{:S(2)}, u32[]{:S(2)}) collective-permute-start(bf16[576,768]{1,0:T(8,128)(2,1)S(1)} %get-tuple-element.625), channel_id=1, source_target_pairs={{3,0},{2,1},{7,4},{6,5},{11,8},{10,9},{15,12},{14,13},{19,16},{18,... | collective-permute-start | bytes 2654216 | tf_op jit(solution)/shard_map/ppermute | solution.py:718
  229.3 27.3 %collective-permute-start.30 = (bf16[576,768]{1,0:T(8,128)(2,1)S(1)}, bf16[576,768]{1,0:T(8,128)(2,1)S(1)}, u32[]{:S(2)}, u32[]{:S(2)}) collective-permute-start(bf16[576,768]{1,0:T(8,128)(2,1)S(1)} %get-tuple-element.508), channel_id=1, source_target_pairs={{0,2},{1,3},{4,6},{5,7},{8,10},{9,11},{12,14},{13,15},{16,18},{17,... | collective-permute-start | bytes 2654216 | tf_op jit(solution)/shard_map/ppermute | solution.py:718
  234.0 40.8 %collective-permute-start.31 = (bf16[576,768]{1,0:T(8,128)(2,1)}, bf16[576,768]{1,0:T(8,128)(2,1)S(1)}, u32[]{:S(2)}, u32[]{:S(2)}) collective-permute-start(bf16[576,768]{1,0:T(8,128)(2,1)} %get-tuple-element.623), channel_id=1, source_target_pairs={{2,3},{3,2},{6,7},{7,6},{10,11},{11,10},{14,15},{15,14},{18,19},{1... | collective-permute-start | bytes 2654216 | tf_op jit(solution)/shard_map/ppermute | solution.py:718
  234.7 40.0 %collective-permute-start.32 = (bf16[576,768]{1,0:T(8,128)(2,1)}, bf16[576,768]{1,0:T(8,128)(2,1)S(1)}, u32[]{:S(2)}, u32[]{:S(2)}) collective-permute-start(bf16[576,768]{1,0:T(8,128)(2,1)} %get-tuple-element.623), channel_id=1, source_target_pairs={{1,2},{0,3},{5,6},{4,7},{9,10},{8,11},{13,14},{12,15},{17,18},{16,... | collective-permute-start | bytes 2654216 | tf_op jit(solution)/shard_map/ppermute | solution.py:718
  275.7 18.1 %collective-permute-start.33 = (bf16[8,384,768]{2,1,0:T(8,128)(2,1)}, bf16[8,384,768]{2,1,0:T(8,128)(2,1)}, u32[]{:S(2)}, u32[]{:S(2)}) collective-permute-start(bf16[8,384,768]{2,1,0:T(8,128)(2,1)} %get-tuple-element.387), channel_id=1, source_target_pairs={{0,1},{1,0},{2,3},{3,2},{4,5},{5,4},{6,7},{7,6},{8,9},{9,8},{10,11... | collective-permute-start | bytes 14155784 | tf_op jit(solution)/shard_map/ppermute | solution.py:718
  299.6 186.2 %reduce-scatter.5.cloned.1.call-start = ((), (), s32[]{:S(2)}) async-start(), calls=%async_computation.3 | async-start | bytes 2654208 | tf_op jit(solution)/shard_map/reduce_scatter | solution.py:780
  299.7 18.6 %collective-permute-start.34 = (bf16[2,576,384]{2,1,0:T(8,128)(2,1)}, bf16[2,576,384]{2,1,0:T(8,128)(2,1)S(1)}, u32[]{:S(2)}, u32[]{:S(2)}) collective-permute-start(bf16[2,576,384]{2,1,0:T(8,128)(2,1)} %get-tuple-element.390), channel_id=1, source_target_pairs={{0,1},{1,0},{2,3},{3,2},{4,5},{5,4},{6,7},{7,6},{8,9},{9,8},{10,11... | collective-permute-start | bytes 2654216 | tf_op jit(solution)/shard_map/ppermute | solution.py:718
  338.4 25.5 %collective-permute-start.36 = (bf16[8,192,768]{2,1,0:T(8,128)(2,1)}, bf16[8,192,768]{2,1,0:T(8,128)(2,1)}, u32[]{:S(2)}, u32[]{:S(2)}) collective-permute-start(bf16[8,192,768]{2,1,0:T(8,128)(2,1)} %get-tuple-element.416), channel_id=1, source_target_pairs={{0,1},{1,0},{2,3},{3,2},{4,5},{5,4},{6,7},{7,6},{8,9},{9,8},{10,11... | collective-permute-start | bytes 7077896 | tf_op jit(solution)/shard_map/ppermute | solution.py:718
  340.1 23.8 %collective-permute-start.37 = (bf16[576,768]{1,0:T(8,128)(2,1)S(1)}, bf16[576,768]{1,0:T(8,128)(2,1)S(1)}, u32[]{:S(2)}, u32[]{:S(2)}) collective-permute-start(bf16[576,768]{1,0:T(8,128)(2,1)S(1)} %get-tuple-element.594), channel_id=1, source_target_pairs={{0,2},{1,3},{4,6},{5,7},{8,10},{9,11},{12,14},{13,15},{16,18},{17,... | collective-permute-start | bytes 2654216 | tf_op jit(solution)/shard_map/ppermute | solution.py:718
  341.8 43.7 %collective-permute-start.38 = (bf16[576,768]{1,0:T(8,128)(2,1)}, bf16[576,768]{1,0:T(8,128)(2,1)}, u32[]{:S(2)}, u32[]{:S(2)}) collective-permute-start(bf16[576,768]{1,0:T(8,128)(2,1)} %get-tuple-element.621), channel_id=1, source_target_pairs={{2,3},{3,2},{6,7},{7,6},{10,11},{11,10},{14,15},{15,14},{18,19},{1... | collective-permute-start | bytes 2654216 | tf_op jit(solution)/shard_map/ppermute | solution.py:718
  343.4 42.1 %collective-permute-start.39 = (bf16[576,768]{1,0:T(8,128)(2,1)}, bf16[576,768]{1,0:T(8,128)(2,1)}, u32[]{:S(2)}, u32[]{:S(2)}) collective-permute-start(bf16[576,768]{1,0:T(8,128)(2,1)} %get-tuple-element.621), channel_id=1, source_target_pairs={{1,2},{0,3},{5,6},{4,7},{9,10},{8,11},{13,14},{12,15},{17,18},{16,... | collective-permute-start | bytes 2654216 | tf_op jit(solution)/shard_map/ppermute | solution.py:718
  385.5 23.0 %collective-permute-start.40 = (bf16[8,384,768]{2,1,0:T(8,128)(2,1)}, bf16[8,384,768]{2,1,0:T(8,128)(2,1)}, u32[]{:S(2)}, u32[]{:S(2)}) collective-permute-start(bf16[8,384,768]{2,1,0:T(8,128)(2,1)} %get-tuple-element.436), channel_id=1, source_target_pairs={{0,1},{1,0},{2,3},{3,2},{4,5},{5,4},{6,7},{7,6},{8,9},{9,8},{10,11... | collective-permute-start | bytes 14155784 | tf_op jit(solution)/shard_map/ppermute | solution.py:718
  386.7 21.8 %collective-permute-start.41 = (bf16[576,768]{1,0:T(8,128)(2,1)S(1)}, bf16[576,768]{1,0:T(8,128)(2,1)S(1)}, u32[]{:S(2)}, u32[]{:S(2)}) collective-permute-start(bf16[576,768]{1,0:T(8,128)(2,1)S(1)} %copy-done.18), channel_id=1, source_target_pairs={{0,1},{4,5},{8,9},{12,13},{16,17},{20,21},{24,25},{28,29}} | collective-permute-start | bytes 2654216 | tf_op jit(solution)/shard_map/ppermute | solution.py:718
  388.9 19.6 %collective-permute-start.42 = (bf16[576,768]{1,0:T(8,128)(2,1)S(1)}, bf16[576,768]{1,0:T(8,128)(2,1)S(1)}, u32[]{:S(2)}, u32[]{:S(2)}) collective-permute-start(bf16[576,768]{1,0:T(8,128)(2,1)S(1)} %copy-done.18), channel_id=1, source_target_pairs={{3,1},{7,5},{11,9},{15,13},{19,17},{23,21},{27,25},{31,29}} | collective-permute-start | bytes 2654216 | tf_op jit(solution)/shard_map/ppermute | solution.py:718
  389.6 18.9 %collective-permute-start.43 = (bf16[576,768]{1,0:T(8,128)(2,1)S(1)}, bf16[576,768]{1,0:T(8,128)(2,1)S(1)}, u32[]{:S(2)}, u32[]{:S(2)}) collective-permute-start(bf16[576,768]{1,0:T(8,128)(2,1)S(1)} %copy-done.18), channel_id=1, source_target_pairs={{2,1},{6,5},{10,9},{14,13},{18,17},{22,21},{26,25},{30,29}} | collective-permute-start | bytes 2654216 | tf_op jit(solution)/shard_map/ppermute | solution.py:718
  415.3 29.9 %collective-permute-start.44 = (bf16[2,576,384]{2,1,0:T(8,128)(2,1)}, bf16[2,576,384]{2,1,0:T(8,128)(2,1)S(1)}, u32[]{:S(2)}, u32[]{:S(2)}) collective-permute-start(bf16[2,576,384]{2,1,0:T(8,128)(2,1)} %get-tuple-element.439), channel_id=1, source_target_pairs={{0,1},{1,0},{2,3},{3,2},{4,5},{5,4},{6,7},{7,6},{8,9},{9,8},{10,11... | collective-permute-start | bytes 2654216 | tf_op jit(solution)/shard_map/ppermute | solution.py:718
  418.0 24.8 %collective-permute-start.45 = (bf16[2,2,2,192,256]{4,3,1,0,2:T(8,128)(2,1)S(1)}, bf16[2,2,2,192,256]{4,3,1,0,2:T(8,128)(2,1)}, u32[]{:S(2)}, u32[]{:S(2)}) collective-permute-start(bf16[2,2,2,192,256]{4,3,1,0,2:T(8,128)(2,1)S(1)} %bitcast.234), channel_id=1, source_target_pairs={{0,4},{4,0},{8,12},{12,8},{16,20},{20,16},{24,28},{28,24},{1,5},{5... | collective-permute-start | bytes 2359304 | tf_op jit(solution)/shard_map/ppermute | solution.py:756
  418.6 24.2 %collective-permute-start.46 = (bf16[2,2,2,192,256]{4,3,2,0,1:T(8,128)(2,1)S(1)}, bf16[2,2,2,192,256]{4,3,2,0,1:T(8,128)(2,1)S(1)}, u32[]{:S(2)}, u32[]{:S(2)}) collective-permute-start(bf16[2,2,2,192,256]{4,3,2,0,1:T(8,128)(2,1)S(1)} %bitcast.235), channel_id=1, source_target_pairs={{0,2},{1,3},{2,0},{3,1},{4,6},{5,7},{6,4},{7,5},{8,10},{9,11},{10,... | collective-permute-start | bytes 2359304 | tf_op jit(solution)/shard_map/ppermute | solution.py:756
  418.7 26.6 %collective-permute-start.47 = (bf16[2,2,2,192,256]{4,3,2,0,1:T(8,128)(2,1)S(1)}, bf16[2,2,2,192,256]{4,3,2,0,1:T(8,128)(2,1)}, u32[]{:S(2)}, u32[]{:S(2)}) collective-permute-start(bf16[2,2,2,192,256]{4,3,2,0,1:T(8,128)(2,1)S(1)} %bitcast.236), channel_id=1, source_target_pairs={{0,8},{4,12},{8,0},{12,4},{16,24},{20,28},{24,16},{28,20},{1,9},{5... | collective-permute-start | bytes 2359304 | tf_op jit(solution)/shard_map/ppermute | solution.py:756
  445.2 20.5 %collective-permute-start.48 = (bf16[2,576,384]{2,1,0:T(8,128)(2,1)}, bf16[2,576,384]{2,1,0:T(8,128)(2,1)S(1)}, u32[]{:S(2)}, u32[]{:S(2)}) collective-permute-start(bf16[2,576,384]{2,1,0:T(8,128)(2,1)} %get-tuple-element.452), channel_id=1, source_target_pairs={{0,1},{1,0},{2,3},{3,2},{4,5},{5,4},{6,7},{7,6},{8,9},{9,8},{10,11... | collective-permute-start | bytes 2654216 | tf_op jit(solution)/shard_map/ppermute | solution.py:718
  450.3 15.4 %collective-permute-start.50 = (bf16[2,2,192,256]{3,2,1,0:T(8,128)(2,1)S(1)}, bf16[2,2,192,256]{3,2,1,0:T(8,128)(2,1)S(1)}, u32[]{:S(2)}, u32[]{:S(2)}) collective-permute-start(bf16[2,2,192,256]{3,2,1,0:T(8,128)(2,1)S(1)} %get-tuple-element.642), channel_id=1, source_target_pairs={{0,8},{4,12},{8,0},{12,4},{16,24},{20,28},{24,16},{28,20},{1,9},{5... | collective-permute-start | bytes 1179656 | tf_op jit(solution)/shard_map/ppermute | solution.py:756
  493.8 23.1 %collective-permute-start.58 = (bf16[192,768]{1,0:T(8,128)(2,1)S(1)}, bf16[192,768]{1,0:T(8,128)(2,1)S(1)}, u32[]{:S(2)}, u32[]{:S(2)}) collective-permute-start(bf16[192,768]{1,0:T(8,128)(2,1)S(1)} %get-tuple-element.645), channel_id=1, source_target_pairs={{0,16},{4,20},{8,24},{12,28},{16,0},{20,4},{24,8},{28,12},{1,17},{... | collective-permute-start | bytes 884744 | tf_op jit(solution)/shard_map/ppermute | solution.py:756
  501.5 15.5 %collective-permute-start.61 = (bf16[2,2,2,96,256]{4,3,2,0,1:T(8,128)(2,1)S(1)}, bf16[2,2,2,96,256]{4,3,2,0,1:T(8,128)(2,1)S(1)}, u32[]{:S(2)}, u32[]{:S(2)}) collective-permute-start(bf16[2,2,2,96,256]{4,3,2,0,1:T(8,128)(2,1)S(1)} %bitcast.241), channel_id=1, source_target_pairs={{0,8},{4,12},{8,0},{12,4},{16,24},{20,28},{24,16},{28,20},{1,9},{5... | collective-permute-start | bytes 1179656 | tf_op jit(solution)/shard_map/ppermute | solution.py:756
  521.4 16.8 %collective-permute-start.72 = (bf16[192,768]{1,0:T(8,128)(2,1)S(1)}, bf16[192,768]{1,0:T(8,128)(2,1)S(1)}, u32[]{:S(2)}, u32[]{:S(2)}) collective-permute-start(bf16[192,768]{1,0:T(8,128)(2,1)S(1)} %add.476), channel_id=1, source_target_pairs={{0,1},{4,5},{8,9},{12,13},{16,17},{20,21},{24,25},{28,29}} | collective-permute-start | bytes 884744 | tf_op jit(solution)/shard_map/ppermute | solution.py:718
  532.4 37.1 %collective-permute-start.69 = (bf16[576,768]{1,0:T(8,128)(2,1)S(1)}, bf16[576,768]{1,0:T(8,128)(2,1)S(1)}, u32[]{:S(2)}, u32[]{:S(2)}) collective-permute-start(bf16[576,768]{1,0:T(8,128)(2,1)S(1)} %copy-done.35), channel_id=1, source_target_pairs={{1,0},{5,4},{9,8},{13,12},{17,16},{21,20},{25,24},{29,28}} | collective-permute-start | bytes 2654216 | tf_op jit(solution)/shard_map/ppermute | solution.py:718
  533.7 35.8 %collective-permute-start.70 = (bf16[576,768]{1,0:T(8,128)(2,1)S(1)}, bf16[576,768]{1,0:T(8,128)(2,1)S(1)}, u32[]{:S(2)}, u32[]{:S(2)}) collective-permute-start(bf16[576,768]{1,0:T(8,128)(2,1)S(1)} %copy-done.35), channel_id=1, source_target_pairs={{2,0},{6,4},{10,8},{14,12},{18,16},{22,20},{26,24},{30,28}} | collective-permute-start | bytes 2654216 | tf_op jit(solution)/shard_map/ppermute | solution.py:718
  535.0 34.5 %collective-permute-start.71 = (bf16[576,768]{1,0:T(8,128)(2,1)S(1)}, bf16[576,768]{1,0:T(8,128)(2,1)S(1)}, u32[]{:S(2)}, u32[]{:S(2)}) collective-permute-start(bf16[576,768]{1,0:T(8,128)(2,1)S(1)} %copy-done.35), channel_id=1, source_target_pairs={{3,0},{7,4},{11,8},{15,12},{19,16},{23,20},{27,24},{31,28}} | collective-permute-start | bytes 2654216 | tf_op jit(solution)/shard_map/ppermute | solution.py:718
  541.8 17.7 %collective-permute-start.79 = (bf16[2,96,256]{2,1,0:T(8,128)(2,1)S(1)}, bf16[2,96,256]{2,1,0:T(8,128)(2,1)S(1)}, u32[]{:S(2)}, u32[]{:S(2)}) collective-permute-start(bf16[2,96,256]{2,1,0:T(8,128)(2,1)S(1)} %get-tuple-element.682), channel_id=1, source_target_pairs={{0,2},{1,3},{2,0},{3,1},{4,6},{5,7},{6,4},{7,5},{8,10},{9,11},{10,... | collective-permute-start | bytes 294920 | tf_op jit(solution)/shard_map/ppermute | solution.py:756
  544.2 18.5 %collective-permute-start.68 = (bf16[96,768]{1,0:T(8,128)(2,1)S(1)}, bf16[96,768]{1,0:T(8,128)(2,1)S(1)}, u32[]{:S(2)}, u32[]{:S(2)}) collective-permute-start(bf16[96,768]{1,0:T(8,128)(2,1)S(1)} %dynamic-slice_bitcast_fusion.27), channel_id=1, source_target_pairs={{0,2},{1,3},{2,0},{3,1},{4,6},{5,7},{6,4},{7,5},{8,10},{9,11},{10,... | collective-permute-start | bytes 442376 | tf_op jit(solution)/shard_map/ppermute | solution.py:718
  569.7 15.8 %collective-permute-start.85 = (bf16[96,768]{1,0:T(8,128)(2,1)S(1)}, bf16[96,768]{1,0:T(8,128)(2,1)S(1)}, u32[]{:S(2)}, u32[]{:S(2)}) collective-permute-start(bf16[96,768]{1,0:T(8,128)(2,1)S(1)} %bitcast_add_fusion.1), channel_id=1, source_target_pairs={{0,2},{4,6},{8,10},{12,14},{16,18},{20,22},{24,26},{28,30}} | collective-permute-start | bytes 442376 | tf_op jit(solution)/shard_map/ppermute | solution.py:718
  571.2 15.9 %collective-permute-start.86 = (bf16[96,768]{1,0:T(8,128)(2,1)S(1)}, bf16[96,768]{1,0:T(8,128)(2,1)S(1)}, u32[]{:S(2)}, u32[]{:S(2)}) collective-permute-start(bf16[96,768]{1,0:T(8,128)(2,1)S(1)} %bitcast_add_fusion.1), channel_id=1, source_target_pairs={{1,2},{5,6},{9,10},{13,14},{17,18},{21,22},{25,26},{29,30}} | collective-permute-start | bytes 442376 | tf_op jit(solution)/shard_map/ppermute | solution.py:718
  571.8 15.9 %collective-permute-start.87 = (bf16[96,768]{1,0:T(8,128)(2,1)S(1)}, bf16[96,768]{1,0:T(8,128)(2,1)S(1)}, u32[]{:S(2)}, u32[]{:S(2)}) collective-permute-start(bf16[96,768]{1,0:T(8,128)(2,1)S(1)} %bitcast_add_fusion.1), channel_id=1, source_target_pairs={{3,2},{7,6},{11,10},{15,14},{19,18},{23,22},{27,26},{31,30}} | collective-permute-start | bytes 442376 | tf_op jit(solution)/shard_map/ppermute | solution.py:718
  574.0 15.4 %collective-permute-start.81 = (bf16[192,768]{1,0:T(8,128)(2,1)S(1)}, bf16[192,768]{1,0:T(8,128)(2,1)S(1)}, u32[]{:S(2)}, u32[]{:S(2)}) collective-permute-start(bf16[192,768]{1,0:T(8,128)(2,1)S(1)} %bitcast_add_fusion), channel_id=1, source_target_pairs={{0,3},{4,7},{8,11},{12,15},{16,19},{20,23},{24,27},{28,31}} | collective-permute-start | bytes 884744 | tf_op jit(solution)/shard_map/ppermute | solution.py:718
  (161 other events, 1718.3 us)
Sparse Core Ops, SparseCore 0:
  299.7 94.6 reduce-scatter.2
  397.9 75.1 reduce-scatter.4

commit v3 on v2

--- a/solution.py
+++ b/solution.py
@@ -137,16 +137,17 @@
             inv_ref[...] = jnp.where(mine, inv, inv_ref[...])
 
 
-def attn_forward(hot, maps, project, partner, keys):
+def attn_forward(hot, maps, project, partner, keys, first, count):
     rows, width = project.shape[0], project.shape[1] // 3
     pairs = width // PAIR
-    col = lambda off: pl.BlockSpec((rows, PAIR), lambda g: (0, off + g))
+    col = lambda off: pl.BlockSpec((rows, PAIR), lambda g: (0, off + first + g))
+    out = pl.BlockSpec((rows, PAIR), lambda g: (0, g))
     return pl.pallas_call(
         attn_fwd_kernel,
-        grid=(pairs,),
+        grid=(count,),
         in_specs=[
             whole((rows, 128)),
-            pl.BlockSpec((1, 8, 128), lambda g: (g, 0, 0)),
+            pl.BlockSpec((1, 8, 128), lambda g: (first + g, 0, 0)),
             col(0),
             col(pairs),
             col(0),
@@ -154,12 +155,12 @@
             col(pairs),
             whole((2 * rows, 256)),
         ],
-        out_specs=[col(0), col(0), col(0), pl.BlockSpec((2, 2 * rows, rows), lambda g: (g, 0, 0))],
+        out_specs=[out, out, out, pl.BlockSpec((2, 2 * rows, rows), lambda g: (g, 0, 0))],
         out_shape=[
-            jax.ShapeDtypeStruct((rows, width), BF),
-            jax.ShapeDtypeStruct((rows, width), BF),
-            jax.ShapeDtypeStruct((rows, width), F32),
-            jax.ShapeDtypeStruct((2 * pairs, 2 * rows, rows), BF),
+            jax.ShapeDtypeStruct((rows, count * PAIR), BF),
+            jax.ShapeDtypeStruct((rows, count * PAIR), BF),
+            jax.ShapeDtypeStruct((rows, count * PAIR), F32),
+            jax.ShapeDtypeStruct((2 * count, 2 * rows, rows), BF),
         ],
         scratch_shapes=[pltpu.VMEM((2, 2 * rows, 256), BF), pltpu.VMEM((2, 2 * rows, PAIR), BF)],
         compiler_params=params_for(56),
@@ -228,7 +229,7 @@
         grid=(count,),
         in_specs=[
             whole((rows, 128)),
-            pl.BlockSpec((2, 2 * rows, rows), lambda g: (first + g, 0, 0)),
+            pl.BlockSpec((2, 2 * rows, rows), lambda g: (g, 0, 0)),
             col(0),
             col(pairs),
             col(0),
@@ -236,9 +237,9 @@
             col(pairs),
             whole((2 * rows, 256)),
             col(0),
-            col(0),
-            col(0),
-            col(0),
+            out,
+            out,
+            out,
         ],
         out_specs=[out, both, both, pl.BlockSpec((1, 8, 128), lambda g: (g, 0, 0))],
         out_shape=[
@@ -264,7 +265,7 @@
     return values * inv, inv
 
 
-def start_first(info_ref, kind, cols, refs, dst, sem):
+def start_first(info_ref, kind, cols, far_cols, refs, dst, sem):
     own, near, far_own, far_other = refs
     local, core = info_ref[0] == 1, info_ref[1]
     part = far_own.shape[0]
@@ -279,26 +280,23 @@
 
     @pl.when(jnp.logical_not(local))
     def _():
-        pltpu.make_async_copy(far_own.at[:, cols], dst.at[pl.ds(core * part, part)], sem).start()
-        pltpu.make_async_copy(far_other.at[:, cols], dst.at[pl.ds((1 - core) * part, part)], sem).start()
+        if part == dst.shape[0]:
+            pltpu.make_async_copy(far_own, dst, sem).start()
+            return
+        pltpu.make_async_copy(far_own.at[:, far_cols], dst.at[pl.ds(core * part, part)], sem).start()
+        pltpu.make_async_copy(far_other.at[:, far_cols], dst.at[pl.ds((1 - core) * part, part)], sem).start()
 
 
 def start_down(info_ref, refs, dst, sem):
-    own, near, *far = refs
+    own, near, far_own, far_other = refs
     local, core = info_ref[0] == 1, info_ref[1]
-    part, cut = own.shape[0], far[0].shape[0]
-    cuts = part // cut
-
-    @pl.when(local)
-    def _():
-        pltpu.make_async_copy(own, dst.at[pl.ds(core * part, part)], sem).start()
-        pltpu.make_async_copy(near, dst.at[pl.ds((1 - core) * part, part)], sem).start()
-
-    @pl.when(jnp.logical_not(local))
-    def _():
-        for i in range(2 * cuts):
-            at = (core if i < cuts else 1 - core) * part + (i % cuts) * cut
-            pltpu.make_async_copy(far[i], dst.at[pl.ds(at, cut)], sem).start()
+    part = own.shape[0]
+    for here, mine, other in ((local, own, near), (jnp.logical_not(local), far_own, far_other)):
+
+        @pl.when(here)
+        def _(mine=mine, other=other):
+            pltpu.make_async_copy(mine, dst.at[pl.ds(core * part, part)], sem).start()
+            pltpu.make_async_copy(other, dst.at[pl.ds((1 - core) * part, part)], sem).start()
 
 
 def wait_for(dst, sem):
@@ -324,7 +322,7 @@
 
 def project_kernel(info_ref, x_ref, p_ref, own, near, far_own, far_other, normed_ref, out_ref, w_ref, sem):
     width = x_ref.shape[1]
-    start_first(info_ref, 0, pl.ds(0, 3 * width), (own, near, far_own, far_other), w_ref, sem)
+    start_first(info_ref, 0, pl.ds(0, 3 * width), pl.ds(0, 3 * width), (own, near, far_own, far_other), w_ref, sem)
     nhat, _ = centred(x_ref[...].astype(F32))
     normed = (nhat * p_ref[0:1, :] + p_ref[1:2, :]).astype(BF)
     normed_ref[...] = normed
@@ -351,17 +349,18 @@
     )(info, x, p, *first_refs)
 
 
-def block_out_kernel(info_ref, x_ref, ctx_ref, p0_ref, p1_ref, *refs):
+def block_out_kernel(info_ref, x_ref, ctx_a, ctx_b, p0_ref, p1_ref, *refs):
     att, up, refs = refs[:4], refs[:2] + refs[4:6], refs[6:]
-    down, refs = refs[:8], refs[8:]
+    down, refs = refs[:4], refs[4:]
     b0_ref, x1_ref, n1_ref, slope_ref, hid_ref, b1_ref, x2_ref, wo_ref, wu_ref, wd_ref, slopes, hiddens, sems, out_sems = refs
     width = x_ref.shape[1]
-    start_first(info_ref, 0, pl.ds(3 * width, width), att, wo_ref, sems.at[0])
+    start_first(info_ref, 0, pl.ds(3 * width, width), pl.ds(0, width), att, wo_ref, sems.at[0])
     for j in range(4):
-        start_first(info_ref, 1, pl.ds(j * width, width), up, wu_ref.at[j], sems.at[1 + j])
+        start_first(info_ref, 1, pl.ds(j * width, width), pl.ds(j * width, width), up, wu_ref.at[j], sems.at[1 + j])
     start_down(info_ref, down, wd_ref, sems.at[5])
     wait_for(wo_ref, sems.at[0])
-    branch = dot(ctx_ref[...], wo_ref[...])
+    half = width // 2
+    branch = dot(ctx_a[...], wo_ref[:half]) + dot(ctx_b[...], wo_ref[half:])
     b0_ref[...] = branch.astype(BF)
     x1 = (x_ref[...].astype(F32) + p0_ref[2:3, :] * branch).astype(BF)
     x1_ref[...] = x1
@@ -398,16 +397,16 @@
         wait_for(hiddens.at[j], out_sems.at[1, j])
 
 
-def block_out(info, x, context, p0, p1, att_refs, up_refs, down_refs):
+def block_out(info, x, context, p0, p1, more_refs, up_refs, down_refs):
     rows, width = x.shape
     one = whole((rows, width))
     shape = lambda n: jax.ShapeDtypeStruct((rows, n), BF)
     widths = [width, width, width, 4 * width, 4 * width, width, width]
-    refs = (*att_refs, *up_refs[2:], *down_refs)
+    refs = (*more_refs, *up_refs[2:], *down_refs)
     return pl.pallas_call(
         block_out_kernel,
         grid=(1,),
-        in_specs=[SMEM, one, one, whole(p0.shape), whole(p1.shape)] + [ANY] * len(refs),
+        in_specs=[SMEM, one, *[whole(c.shape) for c in context], whole(p0.shape), whole(p1.shape)] + [ANY] * len(refs),
         out_specs=[one if n == width else ANY for n in widths],
         out_shape=[shape(n) for n in widths],
         scratch_shapes=[
@@ -422,7 +421,7 @@
         compiler_params=params_for(58),
         cost_estimate=cost(12),
         name="block_out",
-    )(info, x, context, p0, p1, *refs)
+    )(info, x, *context, p0, p1, *refs)
 
 
 def norm_back(x, gain, d_normed, gy):
@@ -436,15 +435,15 @@
 
 def block_back_kernel(info_ref, gy_ref, x1_ref, slope_ref, b1_ref, b0_ref, p0_ref, p1_ref, *refs):
     att, up, refs = refs[:4], refs[:2] + refs[4:6], refs[6:]
-    down, refs = refs[:8], refs[8:]
+    down, refs = refs[:4], refs[4:]
     db1_ref, dpre_ref, gx_ref, db0_ref, dctx_ref, vec_ref, wo_ref, wu_ref, wd_ref, slopes, given, sems, more_sems = refs
     width = gy_ref.shape[1]
     start_down(info_ref, down, wd_ref, sems.at[5])
     for j in range(4):
         at = pl.ds(j * width, width)
-        start_first(info_ref, 1, at, up, wu_ref.at[j], sems.at[1 + j])
+        start_first(info_ref, 1, at, at, up, wu_ref.at[j], sems.at[1 + j])
         pltpu.make_async_copy(slope_ref.at[:, at], slopes.at[j], more_sems.at[0, j]).start()
-    start_first(info_ref, 0, pl.ds(3 * width, width), att, wo_ref, sems.at[0])
+    start_first(info_ref, 0, pl.ds(3 * width, width), pl.ds(0, width), att, wo_ref, sems.at[0])
     total = lambda v: jnp.sum(v, axis=0, keepdims=True)
     gy = gy_ref[...].astype(F32)
     d_branch = (gy * p1_ref[2:3, :]).astype(BF)
@@ -481,12 +480,12 @@
         wait_for(given.at[j], more_sems.at[1, j])
 
 
-def block_back(info, gy, x1, slope, b1, b0, p0, p1, att_refs, up_refs, down_refs):
+def block_back(info, gy, x1, slope, b1, b0, p0, p1, more_refs, up_refs, down_refs):
     rows, width = gy.shape
     one = whole((rows, width))
     shape = lambda n: jax.ShapeDtypeStruct((rows, n), BF)
     widths = [width, 4 * width, width, width, width]
-    refs = (*att_refs, *up_refs[2:], *down_refs)
+    refs = (*more_refs, *up_refs[2:], *down_refs)
     return pl.pallas_call(
         block_back_kernel,
         grid=(1,),
@@ -511,7 +510,7 @@
 def project_back_kernel(info_ref, gy_ref, x_ref, p_ref, dqa, dqb, mya, myb, gota, gotb, own, near, far_own, far_other,
                         dproj_ref, gx_ref, vec_ref, w_ref, sem):
     width = x_ref.shape[1]
-    start_first(info_ref, 0, pl.ds(0, 3 * width), (own, near, far_own, far_other), w_ref, sem)
+    start_first(info_ref, 0, pl.ds(0, 3 * width), pl.ds(0, 3 * width), (own, near, far_own, far_other), w_ref, sem)
     half = width // 2
     for i, (dq, my, got) in enumerate(((dqa, mya, gota), (dqb, myb, gotb))):
         dproj_ref[:, i * half : (i + 1) * half] = dq[...]
@@ -585,12 +584,12 @@
 
 
 def quad_start(mine):
-    return (mine, *together((dp_swap(mine, 1), dp_swap(mine, 2))))
+    return mine, dp_swap(mine, 1), dp_swap(mine, 2)
 
 
 def quad_end(mine, by_x, by_z):
     part = mine.shape[0] // 2
-    return (mine, by_x, by_z, *together((dp_swap(by_z[:part], 1), dp_swap(by_x[part:], 2))))
+    return mine, by_x, by_z, dp_swap(by_z[:part], 1), dp_swap(by_x[part:], 2)
 
 
 def quad_place(mine, *others):
@@ -646,7 +645,7 @@
         finish(1, True)
 
 
-def att_grads_kernel(core_ref, n_ref, dproj_ref, ctx_ref, db_ref, keep_ref, send_ref, tmp_ref, sems):
+def att_grads_kernel(core_ref, n_ref, dproj_ref, ctx_a, ctx_b, db_ref, keep_ref, send_ref, tmp_ref, sems):
     core, j = core_ref[0], pl.program_id(0)
     width = n_ref.shape[1]
     size = keep_ref.shape[0]
@@ -669,7 +668,9 @@
 
     @pl.when(j == 3)
     def _():
-        tmp[...] = dot_tn(ctx_ref[...], db_ref[...]).astype(BF).reshape(tmp.shape)
+        for i, ctx_ref in enumerate((ctx_a, ctx_b)):
+            grad = dot_tn(ctx_ref[...], db_ref[...]).astype(BF)
+            tmp[pl.ds(i * (size // 2), size // 2)] = grad.reshape(size // 2, 2, short, width)
 
     at = pl.ds(j * short, short)
     pltpu.make_async_copy(tmp.at[:, core], keep_ref.at[:, at], sems.at[slot, 0]).start()
@@ -699,19 +700,19 @@
     att = kernel is att_grads_kernel
     shape = (size, (2 * width if att else 4 * width) // size, width)
     if width // (2 * size) % 16:
-        return plain_grads(att, core, shape, a, b, c, d)
+        return plain_grads(att, core, shape, a, b, jnp.concatenate(c, axis=1), d)
     col = pl.BlockSpec((rows, width), lambda j: (0, jnp.minimum(j, 2 if att else 3)))
     return pl.pallas_call(
         kernel,
         grid=(4,),
-        in_specs=[SMEM, whole(a.shape), col, whole(c.shape) if att else col, whole(d.shape)],
+        in_specs=[SMEM, whole(a.shape), col, *([whole(v.shape) for v in c] if att else [col]), whole(d.shape)],
         out_specs=[ANY] * 2,
         out_shape=[jax.ShapeDtypeStruct(shape, BF)] * 2,
         scratch_shapes=[pltpu.VMEM((2, width, width), BF), pltpu.SemaphoreType.DMA((2, 2))],
         compiler_params=params_for(48),
         cost_estimate=cost(us),
         name=kernel.__name__[:-7],
-    )(core.astype(jnp.int32).reshape(1), a, b, c, d)
+    )(core.astype(jnp.int32).reshape(1), a, b, *c, d)
 
 
 def send(value, pairs):
@@ -761,8 +762,7 @@
     if not isinstance(state, list):
         return state, state
     done = [halve(settled(part, got), names, order[step]) for (part, got, names), order in zip(state, ORDERS)]
-    gots = together([d[1] for d in done])
-    return [(d[0], got, d[2]) for d, got in zip(done, gots)], [d[3] for d in done]
+    return [d[:3] for d in done], [d[3] for d in done]
 
 
 def cube_end(state):
@@ -780,34 +780,35 @@
     return lax.psum_scatter(parts, "dp", scatter_dimension=0)
 
 
-def line_end(mine):
+def line_end(mlp, att):
     plane = lax.axis_index("pipe") // 2
-    mine = mine.reshape(2, -1, mine.shape[1])
-    at = lambda i: lax.dynamic_index_in_dim(mine, i, 0, keepdims=False)
-    return at(plane) + swap(at(1 - plane), 2)
+    cut = lambda v, i: lax.dynamic_index_in_dim(v.reshape(2, -1, v.shape[1]), i, 0, keepdims=False)
+    got = swap(jnp.concatenate([cut(mlp, 1 - plane), cut(att, 1 - plane)], axis=0), 2)
+    rows = mlp.shape[0] // 2
+    return cut(mlp, plane) + got[:rows], cut(att, plane) + got[rows:]
+
+
+def by_sender(layer, even, odd, core, bits):
+    targets = (2 * layer, 2 * layer + 1)
+    mine, other = pick(core, even, odd), pick(core, odd, even)
+    return [send(mine if bit == 2 else other, [(t ^ bit, t) for t in targets]) for bit in bits]
 
 
 def from_pipe(value, target, sources):
     return [value if i == target else send(value, [(i, target)]) for i in sources]
 
 
-def att_result(piece, s):
-    rows = piece.shape[0] // 2
-    got = together(from_pipe(piece, s, range(4)))
+def att_result(got):
+    rows = got[0].shape[0] // 2
     cols = []
     for j in range(4):
         cols.append(jnp.concatenate([got[(j // 2) * 2 + c][(j % 2) * rows : (j % 2 + 1) * rows] for c in range(2)], axis=0))
     return jnp.concatenate(cols, axis=1)
 
 
-def mlp_result(piece, s):
-    rows = piece.shape[0] // 4
-    up, low, high = together((from_pipe(piece, s, (0, 1)), from_pipe(piece[: 2 * rows], s - 1, (2, 3)), from_pipe(piece[2 * rows :], s, (2, 3))))
-    first = jnp.concatenate(
-        [jnp.concatenate([up[c][j * rows : (j + 1) * rows] for c in range(2)], axis=0) for j in range(4)], axis=1
-    )
-    low, high = jnp.concatenate(low, axis=0), jnp.concatenate(high, axis=0)
-    return first, low, high
+def up_result(up):
+    rows = up[0].shape[0] // 4
+    return jnp.concatenate([jnp.concatenate([v[j * rows : (j + 1) * rows] for v in up], axis=0) for j in range(4)], axis=1)
 
 
 def choose(place, options):
@@ -846,21 +847,6 @@
     count = own_first.shape[0] // 2
     quarter = count // 4
     q = dp_place % 4
-    share = [lax.dynamic_slice_in_dim(own_first, c * count + q * quarter, quarter, 0) for c in range(2)]
-    mine_att = pick(core, send(share[0], [(0, 2), (2, 0)]), send(share[1], [(0, 3), (2, 1)]))
-    some_att = quad_start(mine_att)
-    share, own_half_y = tie((share, own_half), mine_att, seen)
-    mine_up = pick(core, send(share[0], [(1, 2), (3, 0)]), send(share[1], [(1, 3), (3, 1)]))
-    near_first = swap(tie(own_first, mine_att, seen), 1)
-    all_att = quad_end(*tie(some_att, mine_up))
-    some_up = quad_start(tie(mine_up, some_att))
-    cut_half = own_half.shape[0] // 3
-    own_half_y = tie(own_half_y, mine_up)
-    far_half = [swap(own_half_y[i * cut_half : (i + 1) * cut_half], 2) for i in range(3)]
-    far_att = quad_place(*tie(all_att, some_up, far_half[0]))
-    far_att_other = swap(far_att, 1)
-    near_half = swap(tie(own_half, far_att), 1)
-    att_refs = (own_first, near_first, far_att, far_att_other)
     infos = [jnp.stack([(plane == layer).astype(jnp.int32), core.astype(jnp.int32)]) for layer in range(layers)]
 
     micro, half = plane, core
@@ -873,6 +859,20 @@
     keys = key_features(*layout)
     maps = table_rows(rel_table)
 
+    current = own_rows(inputs)
+    qkv = own_first[:, : 3 * width]
+    far_qkv = (send(qkv[:count], [(0, 2), (2, 0)]), send(qkv[count:], [(0, 3), (2, 1)]))
+    share = [lax.dynamic_slice_in_dim(own_first, c * count + q * quarter, quarter, 0) for c in range(2)]
+    half_rows = own_half.shape[0] // 4
+    share_half = lax.dynamic_slice_in_dim(own_half, q * half_rows, half_rows, 0)
+    own_out = own_first[:, 3 * width :]
+    ready = (far_qkv, params, infos, current, hot, hot_back, keys, maps, share, share_half, own_out)
+    far_qkv, params, infos, current, hot, hot_back, keys, maps, share, share_half, own_out = together(ready)
+    far_qkv = pick(core, *far_qkv)
+    qkv_refs = (own_first, swap(own_first, 1), far_qkv, swap(far_qkv, 1))
+    mine_up = (send(share[0], [(1, 2), (3, 0)]), send(share[1], [(1, 3), (3, 1)]))
+    mine_half = swap(share_half, 2)
+
     def shared(even, odd, layer):
         mine, other = pick(core, even, odd), pick(core, odd, even)
         inside = [(2 * layer, 2 * layer + 1), (2 * layer + 1, 2 * layer)]
@@ -886,46 +886,55 @@
     def collected(parts):
         return choose(place, [jnp.stack([parts[s][i ^ s] for i in range(sections)]) for s in range(sections)])
 
-    current = own_rows(inputs)
     kept, outs = [], {}
+    cut = heads // 4
     for layer in range(layers):
         p0, p1, info = params[2 * layer], params[2 * layer + 1], infos[layer]
-        normed, proj = project(info, current, p0, att_refs)
+        normed, proj = project(info, current, p0, qkv_refs)
         if layer == 0:
-            normed, proj = tie((normed, proj), far_half[1])
+            normed, proj, mine_up, mine_half = together((normed, proj, mine_up, mine_half))
+            some_up = quad_start(pick(core, *mine_up))
         partner = swap(proj[:, width:], 1)
+        front = lambda keys, i: attn_forward(hot, maps[layer], proj, partner, keys, i * cut, cut)
         if layer == 0:
-            far_up = quad_place(*quad_end(*tie(some_up, normed)))
-            partner = tie(partner, far_up)
-        context, rest, inv, queries = attn_forward(hot, maps[layer], proj, partner, keys)
+            partner, own_out = together((partner, own_out))
+            some_half = quad_start(mine_half)
+            far_out = send(own_out, [(0, 2), (2, 0)])
+        part_a = front(keys, 0)
         if layer == 0:
-            far_up_other = swap(far_up, 1)
-            far_half_other = [swap(part, 1) for part in far_half[:2]]
-            context, last_half = tie((context, far_half[2]), far_up_other, near_half, far_half_other)
-            up_refs = (own_first, near_first, far_up, far_up_other)
-            down_refs = (own_half, near_half, far_half[0], far_half[1], last_half, *far_half_other, swap(last_half, 1))
+            part_a, some_up, some_half = together((part_a, some_up, some_half))
+            all_up, all_half = quad_end(*some_up), quad_end(*some_half)
+        part_b = front(tie(keys, part_a[0]), 1)
+        if layer == 0:
+            part_b, all_up, all_half, far_out = together((part_b, all_up, all_half, far_out))
+            far_up, far_half = quad_place(*all_up), quad_place(*all_half)
+            far_out = pick(core, far_out, swap(far_out, 1))
+            near_half = swap(tie(own_half, far_qkv), 1)
+            more_refs = (qkv_refs[0], qkv_refs[1], far_out, far_out)
+            up_refs = (qkv_refs[0], qkv_refs[1], far_up, swap(far_up, 1))
+            down_refs = (own_half, near_half, far_half, swap(far_half, 1))
         else:
-            context, rest, inv, queries = tie((context, rest, inv, queries), outs[0][2])
-        b0, x1, n1, slope, hidden, b1, x2 = block_out(info, current, context, p0, p1, att_refs, up_refs, down_refs)
+            part_b = tie(part_b, outs[0][2])
+        context = (part_a[0], part_b[0])
+        b0, x1, n1, slope, hidden, b1, x2 = block_out(info, current, context, p0, p1, more_refs, up_refs, down_refs)
         if layer == 1:
             b0, x1, n1, slope, hidden, b1, x2 = tie((b0, x1, n1, slope, hidden, b1, x2), outs[0])
-        kept.append((current, normed, proj, partner, (context, rest, inv), queries, b0, x1, n1, slope, hidden, b1))
+        kept.append((current, normed, proj, partner, (part_a, part_b), b0, x1, n1, slope, hidden, b1))
         outs[2 * layer] = outs[2 * layer + 1] = shared(x1, x2, layer)
         current = x2
 
-    cut = heads // 4
     tables, vecs, grads = {}, {}, {}
     core_id = core.astype(jnp.int32)
 
-    x, normed, proj, partner, outcome, queries, b0, x1, n1, slope, hidden, b1 = kept[1]
+    x, normed, proj, partner, outcome, b0, x1, n1, slope, hidden, b1 = kept[1]
     p0, p1, info = params[2], params[3], infos[1]
     grad = tie(own_rows(out_grad), current)
-    db1, d_pre, gx1, db0, d_context, vec1 = block_back(info, grad, x1, slope, b1, b0, p0, p1, att_refs, up_refs, down_refs)
+    db1, d_pre, gx1, db0, d_context, vec1 = block_back(info, grad, x1, slope, b1, b0, p0, p1, more_refs, up_refs, down_refs)
     db1, d_pre, gx1, db0, d_context, vec1 = tie((db1, d_pre, gx1, db0, d_context, vec1), outs[2][2])
-    keep, other = weight_grads(mlp_grads_kernel, core, dp_size, 15, n1, d_pre, hidden, db1)
+    keep, other = weight_grads(mlp_grads_kernel, core, dp_size, 15, n1, d_pre, (hidden,), db1)
     keep, other = tie((keep, other), outs[2])
     got = swap(other, 1)
-    back = lambda d_ctx, i: attn_backward(hot_back, queries, proj, partner, keys, d_ctx, outcome, i * cut, cut)
+    back = lambda d_ctx, i: attn_backward(hot_back, outcome[i][3], proj, partner, keys, d_ctx, outcome[i][:3], i * cut, cut)
     dqa, mya, oa, ta = back(tie(d_context, keep), 0)
     dqa, mya, oa, ta, got = together((dqa, mya, oa, ta, got))
     mlp_b = keep + got
@@ -934,21 +943,21 @@
     dqb, myb, ob, tb, gota = together((dqb, myb, ob, tb, gota))
     gotb = swap(ob, 1)
     mlp_b = line_start(mlp_b)
-    d_proj, gx0, vec0 = project_back(info, gx1, x, p0, (dqa, dqb, mya, myb, gota, gotb), att_refs)
-    keep, other = weight_grads(att_grads_kernel, core, dp_size, 9, normed, d_proj, outcome[0], db0)
+    d_proj, gx0, vec0 = project_back(info, gx1, x, p0, (dqa, dqb, mya, myb, gota, gotb), qkv_refs)
+    keep, other = weight_grads(att_grads_kernel, core, dp_size, 9, normed, d_proj, [part[0] for part in outcome], db0)
     got = swap(other, 1)
     grads[2] = grads[3] = shared(gx0, gx1, 1)
     tables[1] = (ta, tb)
     vecs[3], vecs[2] = vec1[:3], jnp.concatenate([vec0[:2], vec1[3:4]])
 
-    x, normed, proj, partner, outcome, queries, b0, x1, n1, slope, hidden, b1 = kept[0]
+    x, normed, proj, partner, outcome, b0, x1, n1, slope, hidden, b1 = kept[0]
     p0, p1, info = params[0], params[1], infos[0]
-    db1, d_pre, gx1, db0, d_context, vec1 = block_back(info, tie(gx0, keep), x1, slope, b1, b0, p0, p1, att_refs, up_refs, down_refs)
+    db1, d_pre, gx1, db0, d_context, vec1 = block_back(info, tie(gx0, keep), x1, slope, b1, b0, p0, p1, more_refs, up_refs, down_refs)
     db1, d_pre, gx1, db0, d_context, vec1, got = tie((db1, d_pre, gx1, db0, d_context, vec1, got), grads[2][2])
     att_b = keep + got
     d_pre = tie(d_pre, att_b)
     att_b = line_start(att_b)
-    keep, other = weight_grads(mlp_grads_kernel, core, dp_size, 15, n1, d_pre, hidden, db1)
+    keep, other = weight_grads(mlp_grads_kernel, core, dp_size, 15, n1, d_pre, (hidden,), db1)
     keep, other = tie((keep, other), grads[2])
     got = swap(other, 1)
     grads[1] = to_one(gx1, 1)
@@ -962,11 +971,12 @@
     gotb = swap(ob, 1)
     mlp_a, given = cube_step(mlp_a, 1)
     gotb = tie(gotb, given)
-    d_proj, gx0, vec0 = project_back(info, gx1, x, p0, (dqa, dqb, mya, myb, gota, gotb), att_refs)
+    d_proj, gx0, vec0 = project_back(info, gx1, x, p0, (dqa, dqb, mya, myb, gota, gotb), qkv_refs)
     d_proj, gx0, vec0, mlp_a = hold((d_proj, gx0, vec0, mlp_a), 3)
     mlp_a, given = cube_step(mlp_a, 2)
-    keep, other = weight_grads(att_grads_kernel, core, dp_size, 9, tie(normed, given), d_proj, outcome[0], db0)
-    keep, other, att_b, mlp_a = hold((keep, other, att_b, mlp_a), 3)
+    grads[0] = to_one(tie(gx0, given), 0)
+    keep, other = weight_grads(att_grads_kernel, core, dp_size, 9, tie(normed, given), d_proj, [part[0] for part in outcome], db0)
+    keep, other, att_b, grads[0][1], mlp_a = hold((keep, other, att_b, grads[0][1], mlp_a), 4)
     got = swap(other, 1)
     tables = [(ta, tb), tables[1]]
     vecs[1], vecs[0] = vec1[:3], jnp.concatenate([vec0[:2], vec1[3:4]])
@@ -976,35 +986,42 @@
     small = small_sum(small, 0)
     mlp_a, _ = cube_end(mlp_a)
     got, keep, small = together((got, keep, small))
-    att_a = cube_start(keep + got)
-    att_a, given = cube_step(att_a, 0)
+    att_sum = keep + got
+    att_a = line_start(att_sum)
+    mlp_b, att_b, small, outs = tie((mlp_b, att_b, small, outs), att_sum)
+    mlp_b, att_b = line_end(mlp_b, att_b)
     small = small_sum(small, 1)
-    section_out = collected(tie(outs, given)).reshape(1, micro_count, slot_rows, width)
-    small, section_out, mlp_a, att_a = hold((small, section_out, mlp_a, att_a), 3)
-    att_a, given = cube_step(att_a, 1)
+    section_out = collected(outs).reshape(1, micro_count, slot_rows, width)
+    small, section_out, mlp_b, att_b, mlp_a, grads[0] = together((small, section_out, mlp_b, att_b, mlp_a, grads[0]))
+    mlp_a = settled(*mlp_a)
+    low, high = jnp.split(mlp_a, 2, axis=0)
     small = small_sum(small, 2)
-    mlp_a, gx0 = tie((settled(*mlp_a), gx0), given)
-    grads[0] = to_one(gx0, 0)
-    mlp_result_a = mlp_result(mlp_a, 1)
-    small, att_a = hold((small, att_a), 1)
-    att_a, given = cube_step(att_a, 2)
+    ups = [mlp_a, send(mlp_a, [(0, 1)])]
+    downs = by_sender(0, low, high, core, (2, 3))
+    small, ups, downs, mlp_b, att_b = together((small, ups, downs, mlp_b, att_b))
     small = small_sum(small, 3)
-    mlp_b, att_b = tie((mlp_b, att_b), given)
-    mlp_b, att_b = line_end(mlp_b), line_end(att_b)
-    small, mlp_b, att_b, grads[0], mlp_result_a, att_a = hold((small, mlp_b, att_b, grads[0], mlp_result_a, att_a), 5)
-    att_a, given = cube_end(att_a)
+    even = jnp.concatenate([att_b, mlp_b[: att_b.shape[0]]], axis=0)
+    own_b = pick(core, even, mlp_b)
+    got_b = by_sender(1, even, mlp_b, core, (1, 2, 3))
+    grads = tie(grads, own_b)
+    in_grads = collected({s: [part.astype(F32) for part in grads[s]] for s in range(sections)}).reshape(1, micro_count, slot_rows, width)
+    small, got_b, in_grads, att_a = together((small, got_b, in_grads, att_a))
     small = small_sum(small, 4)
-    mlp_b, att_b, grads = tie((mlp_b, att_b, grads), given)
-    mlp_result_b, att_b = mlp_result(mlp_b, 3), att_result(att_b, 2)
-    in_grads = collected({s: [part.astype(F32) for part in grads[s]] for s in range(sections)}).reshape(1, micro_count, slot_rows, width)
-    small, mlp_result_b, att_b, in_grads, att_a = together((small, mlp_result_b, att_b, in_grads, att_a))
-    att_a = settled(*att_a)
+    got_a = from_pipe(att_a, 0, range(4))
 
     first_grads, half_grads = {}, {}
-    first_grads[3], half_grads[2], half_grads[3] = mlp_result_b
-    first_grads[2] = att_b
-    first_grads[1], half_grads[0], half_grads[1] = mlp_result_a
-    first_grads[0] = att_result(att_a, 0)
+    rows_a = [(got_a[c].astype(F32) + got_a[2 + c].astype(F32)).reshape(4, -1, width) for c in range(2)]
+    first_grads[0] = jnp.concatenate([jnp.concatenate([v[j] for v in rows_a], axis=0) for j in range(4)], axis=1)
+    first_grads[1] = up_result([ups[1], ups[0]])
+    half_grads[0] = jnp.concatenate(downs, axis=0)
+    half_grads[1] = jnp.concatenate(downs[::-1], axis=0)
+    by_bit = [own_b, *got_b]
+    on = lambda target: [by_bit[p ^ target] for p in range(sections)]
+    piece = att_b.shape[0]
+    first_grads[2] = att_result([v[:piece] for v in on(2)])
+    half_grads[2] = jnp.concatenate([v[piece:] for v in on(2)[2:]], axis=0)
+    first_grads[3] = up_result(on(3)[:2])
+    half_grads[3] = jnp.concatenate([v[piece:] for v in on(3)[2:]], axis=0)
 
     g_first = choose(place, [first_grads[s].astype(F32) for s in range(sections)])[None]
     g_half = choose(place, [half_grads[s].astype(F32) for s in range(sections)])[None]

time: 631 us -> 612 us (0.970)
  waiting for transfers between devices: 120 us -> 67 us
  other arithmetic: 62.4 us -> 83 us
  local copies, waits for them, and re-layouts: 55.3 us -> 70.2 us
    ppermute x20 -> x10, waiting for transfers between devices: 51.5 us -> 8.79 us  [halve(): lax.ppermute(give, name, [(k, k ^ bit) for k in range(lax.axis_size(name))])]
    ppermute x11, waiting for transfers between devices: 30 us -> 14.8 us  [dp_swap(): lax.ppermute(value, 'dp', [(i, i ^ bit) for i in range(lax.axis_size('dp'...]
    ppermute x61 -> x52, starting transfers between devices: 71.9 us -> 85.8 us  [send(): return lax.ppermute(value, 'pipe', pairs)]
    ppermute x20 -> x10, starting transfers between devices: 20.3 us -> 11.2 us  [halve(): lax.ppermute(give, name, [(k, k ^ bit) for k in range(lax.axis_size(name))])]
    reduce_scatter x2 -> x3, waiting for transfers between devices: 0.04 us -> 8.9 us  [line_start(): return lax.psum_scatter(parts, 'dp', scatter_dimension=0)]
    select_n x3 -> x5, other arithmetic: 12.8 us -> 20.8 us  [choose(): result = jnp.where(place == s, options[s], result)]
    pallas_call x8 -> x10, Pallas kernels: 120 us -> 125 us  [the longest x4 51.1 us: attn_forward(): pl.pallas_call(attn_fwd_kernel, grid=(count,), in_specs=[whole((rows, 128...]
    unnamed x231 -> x273, local copies, waits for them, and re-layouts: 31.8 us -> 36.4 us
  transfers between devices with their start and end apart: 94 -> 76, of which waited for: 30 -> 18; matrix products, arithmetic and copies ran while one was open for 11% -> 17% of each run, Pallas kernels for 37% -> 39%
where the time goes in v3:
time: 612 us; the launch traced here: 604 us
  Pallas kernels  256 us (42%)
  starting transfers between devices  108 us (18%)
  other arithmetic  83 us (14%)
  local copies, waits for them, and re-layouts  70.2 us (11%)
  waiting for transfers between devices  67 us (11%)
  between operations  19.7 us (3%)
    ppermute x52, starting transfers between devices, send(): return lax.ppermute(value, 'pipe', pairs)  85.8 us
    pallas_call x4, Pallas kernels, attn_backward(): pl.pallas_call(attn_bwd_kernel, grid=(count,), in_specs=[whole((rows, 128...  71.5 us
    pallas_call x4, Pallas kernels, attn_forward(): pl.pallas_call(attn_fwd_kernel, grid=(count,), in_specs=[whole((rows, 128...  51.1 us
    pallas_call x4, Pallas kernels, weight_grads(): pl.pallas_call(kernel, grid=(4,), in_specs=[SMEM, whole(a.shape), col, *(...  42.2 us
    unnamed x273, local copies, waits for them, and re-layouts  36.4 us
    ppermute x52, waiting for transfers between devices, send(): return lax.ppermute(value, 'pipe', pairs)  34.5 us
    pallas_call x2, Pallas kernels, block_back(): pl.pallas_call(block_back_kernel, grid=(1,), in_specs=[SMEM, one, one, AN...  34.3 us
    pallas_call x2, Pallas kernels, block_out(): pl.pallas_call(block_out_kernel, grid=(1,), in_specs=[SMEM, one, *[whole(...  32 us
  transfers between devices with their start and end apart: 76, of which 18 were waited for; matrix products, arithmetic and copies ran while one was open for 17% of the time, Pallas kernels for 39%

profile of v3, /device:TPU:0, one launch (start us, length us, event | category | flops | bytes accessed | tf_op | source)
XLA Modules:
  0.0 603.8 jit_solution(216742844389125557)
XLA Ops:
  11.8 4.0 fusion.24
  15.8 3.6 collective-permute-start
  43.0 2.8 fusion.5.key_ref
  50.9 7.8 %collective-permute-done.1 = bf16[384,2304]{1,0:T(8,128)(2,1)} collective-permute-done((bf16[384,2304]{1,0:T(8,128)(2,1)}, bf16[384,2304]{1,0:T(8,128)(2,1)}, u32[]{:S(2)}, u32[]{:S(2)}) %collective-permute-start.1) | collective-permute-done | bytes 1769504 | tf_op jit(solution)/shard_map/ppermute | solution.py:719
  65.0 2.9 copy-done.4
  68.0 3.9 project.2
  71.9 6.5 %collective-permute-done.7 = bf16[96,3072]{1,0:T(8,128)(2,1)S(1)} collective-permute-done((bf16[96,3072]{1,0:T(8,128)(2,1)}, bf16[96,3072]{1,0:T(8,128)(2,1)S(1)}, u32[]{:S(2)}, u32[]{:S(2)}) %collective-permute-start.7) | collective-permute-done | bytes 589856 | tf_op jit(solution)/shard_map/ppermute | solution.py:719
  79.5 12.1 %collective-permute-start.10 = (bf16[576,1536]{1,0:T(8,128)(2,1)S(1)}, bf16[576,1536]{1,0:T(8,128)(2,1)S(1)}, u32[]{:S(2)}, u32[]{:S(2)}) collective-permute-start(bf16[576,1536]{1,0:T(8,128)(2,1)S(1)} %slice.241), channel_id=1, source_target_pairs={{0,1},{1,0},{2,3},{3,2},{4,5},{5,4},{6,7},{7,6},{8,9},{9,8},{10,11... | collective-permute-start | bytes 5308424 | tf_op jit(solution)/shard_map/ppermute | solution.py:719
  91.5 3.3 collective-permute-done.10.kp_ref.vp_ref
  94.9 3.8 collective-permute-start.19
  103.5 12.6 %attn_fwd.4 = (bf16[576,384]{1,0:T(8,128)(2,1)}, bf16[576,384]{1,0:T(8,128)(2,1)}, f32[576,384]{1,0:T(8,128)}, bf16[6,1152,576]{2,1,0:T(8,128)(2,1)}) custom-call(bf16[576,128]{1,0:T(8,128)(2,1)} %get-tuple-element.282.hot_ref, f32[6,8,128]{2,1,0:T(8,128)} %get-tuple-element.624.map_ref, bf16[576,2304]{1,0:T(8,128)(2,1)} %copy-done.2, ...), custom_call_target="tpu_custom_call" | custom-call | flops 520000000 | bytes 1000 | tf_op jit(solution)/shard_map/attn_fwd/pallas_call | solution.py:145
  116.6 8.5 %collective-permute-done.13.by_x = bf16[384,768]{1,0:T(8,128)(2,1)S(1)} collective-permute-done((bf16[384,768]{1,0:T(8,128)(2,1)S(1)}, bf16[384,768]{1,0:T(8,128)(2,1)S(1)}, u32[]{:S(2)}, u32[]{:S(2)}) %collective-permute-start.13) | collective-permute-done | bytes 589856 | tf_op jit(solution)/shard_map/ppermute | solution.py:566
  133.1 12.7 %attn_fwd.5 = (bf16[576,384]{1,0:T(8,128)(2,1)}, bf16[576,384]{1,0:T(8,128)(2,1)}, f32[576,384]{1,0:T(8,128)}, bf16[6,1152,576]{2,1,0:T(8,128)(2,1)}) custom-call(bf16[576,128]{1,0:T(8,128)(2,1)} %get-tuple-element.282.hot_ref, f32[6,8,128]{2,1,0:T(8,128)} %get-tuple-element.624.map_ref, bf16[576,2304]{1,0:T(8,128)(2,1)} %copy-done.2, ...), custom_call_target="tpu_custom_call" | custom-call | flops 520000000 | bytes 1000 | tf_op jit(solution)/shard_map/attn_fwd/pallas_call | solution.py:145
  153.1 4.7 collective-permute-done.20
  163.1 15.9 %block_out.2 = (bf16[576,768]{1,0:T(8,128)(2,1)}, bf16[576,768]{1,0:T(8,128)(2,1)}, bf16[576,768]{1,0:T(8,128)(2,1)}, bf16[576,3072]{1,0:T(8,128)(2,1)}, bf16[57...) custom-call(s32[2]{0:T(128)} %copy-done.67, ...), custom_call_target="tpu_custom_call" | custom-call | flops 240000000 | bytes 1000 | tf_op jit(solution)/shard_map/block_out/pallas_call | solution.py:406
  185.4 4.2 project.3
  197.5 13.0 %attn_fwd.6 = (bf16[576,384]{1,0:T(8,128)(2,1)}, bf16[576,384]{1,0:T(8,128)(2,1)}, f32[576,384]{1,0:T(8,128)}, bf16[6,1152,576]{2,1,0:T(8,128)(2,1)}) custom-call(bf16[576,128]{1,0:T(8,128)(2,1)} %get-tuple-element.282.hot_ref, f32[6,8,128]{2,1,0:T(8,128)} %get-tuple-element.623.map_ref, bf16[576,2304]{1,0:T(8,128)(2,1)} %copy-done.3, ...), custom_call_target="tpu_custom_call" | custom-call | flops 520000000 | bytes 1000 | tf_op jit(solution)/shard_map/attn_fwd/pallas_call | solution.py:145
  210.5 12.7 %attn_fwd.7 = (bf16[576,384]{1,0:T(8,128)(2,1)}, bf16[576,384]{1,0:T(8,128)(2,1)}, f32[576,384]{1,0:T(8,128)}, bf16[6,1152,576]{2,1,0:T(8,128)(2,1)}) custom-call(bf16[576,128]{1,0:T(8,128)(2,1)} %get-tuple-element.282.hot_ref, f32[6,8,128]{2,1,0:T(8,128)} %get-tuple-element.623.map_ref, bf16[576,2304]{1,0:T(8,128)(2,1)} %copy-done.3, ...), custom_call_target="tpu_custom_call" | custom-call | flops 520000000 | bytes 1000 | tf_op jit(solution)/shard_map/attn_fwd/pallas_call | solution.py:145
  223.2 16.1 %block_out.3 = (bf16[576,768]{1,0:T(8,128)(2,1)}, bf16[576,768]{1,0:T(8,128)(2,1)}, bf16[576,768]{1,0:T(8,128)(2,1)}, bf16[576,3072]{1,0:T(8,128)(2,1)}, bf16[57...) custom-call(s32[2]{0:T(128)} %get-tuple-element.306.info_ref, ...), custom_call_target="tpu_custom_call" | custom-call | flops 240000000 | bytes 1000 | tf_op jit(solution)/shard_map/block_out/pallas_call | solution.py:406
  239.3 3.1 broadcast_select_fusion.4
  242.5 4.8 collective-permute-start.28
  252.9 16.9 %block_back.2 = (bf16[576,768]{1,0:T(8,128)(2,1)}, bf16[576,3072]{1,0:T(8,128)(2,1)}, bf16[576,768]{1,0:T(8,128)(2,1)}, bf16[576,768]{1,0:T(8,128)(2,1)}, bf16[576,768]{1,0:T(8,128)(2,1)}, /*index=5*/f32[8,768]{1,0:T(8,128)}) custom-call(s32[2]{0:T(128)} %get-tuple-element.306.info_ref, bf16[576,768]{1,0:T(8,128)(2,1)} %dynamic-slice_bitcast_fusion.gy_ref, ...), custom_call_target="tpu_custom_call" | custom-call | flops 280000000 | bytes 1000 | tf_op jit(solution)/shard_map/block_back/pallas_call | solution.py:489
  273.4 14.0 %mlp_grads.2 = (bf16[8,384,768]{2,1,0:T(8,128)(2,1)}, bf16[8,384,768]{2,1,0:T(8,128)(2,1)}) custom-call(s32[1]{0:T(128)} %bitcast.2.core_ref, bf16[576,768]{1,0:T(8,128)(2,1)S(1)} %copy-done.38, bf16[576,3072]{1,0:T(8,128)(2,1)S(1)} %copy-done.22, bf16[576,3072]{1,0:T(8,128)(2,1)} %get-tuple-element.370.hid_ref, bf16[576,768]{1,0:T(8,128)(2,1)S(1)} %copy-done.40), custom_call_target="tpu_custom_call" | custom-call | flops 300000000 | bytes 1000 | tf_op jit(solution)/shard_map/mlp_grads/pallas_call | solution.py:705
  288.7 17.9 %attn_bwd.4 = (bf16[576,384]{1,0:T(8,128)(2,1)}, bf16[2,576,384]{2,1,0:T(8,128)(2,1)}, bf16[2,576,384]{2,1,0:T(8,128)(2,1)}, f32[3,8,128]{2,1,0:T(8,128)}) custom-call(bf16[576,128]{1,0:T(8,128)(2,1)} %get-tuple-element.281.hot_ref, bf16[6,1152,576]{2,1,0:T(8,128)(2,1)} %get-tuple-element.366.w_ref, bf16[576,2304]{1,0:T(8,128)(2,1)} %copy-done.3, ...), custom_call_target="tpu_custom_call" | custom-call | flops 360000000 | bytes 1000 | tf_op jit(solution)/shard_map/attn_bwd/pallas_call | solution.py:227
  306.6 5.6 add.388
  312.4 18.1 %attn_bwd.5 = (bf16[576,384]{1,0:T(8,128)(2,1)}, bf16[2,576,384]{2,1,0:T(8,128)(2,1)}, bf16[2,576,384]{2,1,0:T(8,128)(2,1)}, f32[3,8,128]{2,1,0:T(8,128)}) custom-call(bf16[576,128]{1,0:T(8,128)(2,1)} %get-tuple-element.281.hot_ref, bf16[6,1152,576]{2,1,0:T(8,128)(2,1)} %get-tuple-element.384.w_ref, bf16[576,2304]{1,0:T(8,128)(2,1)} %copy-done.3, ...), custom_call_target="tpu_custom_call" | custom-call | flops 360000000 | bytes 1000 | tf_op jit(solution)/shard_map/attn_bwd/pallas_call | solution.py:227
  336.4 6.7 %project_back.2 = (bf16[576,2304]{1,0:T(8,128)(2,1)}, bf16[576,768]{1,0:T(8,128)(2,1)S(1)}, f32[8,768]{1,0:T(8,128)S(1)}) custom-call(s32[2]{0:T(128)S(1)} %copy-done.70, bf16[576,768]{1,0:T(8,128)(2,1)S(1)} %copy-done.23, bf16[576,768]{1,0:T(8,128)(2,1)S(1)} %copy-done.15, f32[3,768]{1,0:T(4,128)S(1)} %copy-done.60, bf16[576,384]{1,0:T(8,128)(2,1)S(1)} %copy-done.55, ...), custom_call_target="tpu_custom_call" | custom-call | flops 140000000 | bytes 1000 | tf_op jit(solution)/shard_map/project_back/pallas_call | solution.py:535
  343.8 7.4 %att_grads.2 = (bf16[8,192,768]{2,1,0:T(8,128)(2,1)S(1)}, bf16[8,192,768]{2,1,0:T(8,128)(2,1)}) custom-call(s32[1]{0:T(128)} %bitcast.2.core_ref, bf16[576,768]{1,0:T(8,128)(2,1)S(1)} %copy-done.45, bf16[576,2304]{1,0:T(8,128)(2,1)} %get-tuple-element.401.dproj_ref, bf16[576,384]{1,0:T(8,128)(2,1)S(1)} %copy-done.18, bf16[576,384]{1,0:T(8,128)(2,1)S(1)} %copy-done.19, ...), custom_call_target="tpu_custom_call" | custom-call | flops 180000000 | bytes 1000 | tf_op jit(solution)/shard_map/att_grads/pallas_call | solution.py:705
  356.3 3.0 collective-permute-start.37
  359.3 17.4 %block_back.3 = (bf16[576,768]{1,0:T(8,128)(2,1)}, bf16[576,3072]{1,0:T(8,128)(2,1)}, bf16[576,768]{1,0:T(8,128)(2,1)}, bf16[576,768]{1,0:T(8,128)(2,1)}, bf16[576,768]{1,0:T(8,128)(2,1)}, /*index=5*/f32[8,768]{1,0:T(8,128)}) custom-call(s32[2]{0:T(128)} %copy-done.67, bf16[576,768]{1,0:T(8,128)(2,1)} %copy-done.20, ...), custom_call_target="tpu_custom_call" | custom-call | flops 280000000 | bytes 1000 | tf_op jit(solution)/shard_map/block_back/pallas_call | solution.py:489
  377.7 4.5 add.389
  384.5 13.8 %mlp_grads.3 = (bf16[8,384,768]{2,1,0:T(8,128)(2,1)}, bf16[8,384,768]{2,1,0:T(8,128)(2,1)}) custom-call(s32[1]{0:T(128)} %bitcast.2.core_ref, bf16[576,768]{1,0:T(8,128)(2,1)S(1)} %copy-done.37, bf16[576,3072]{1,0:T(8,128)(2,1)S(1)} %copy-done.21, bf16[576,3072]{1,0:T(8,128)(2,1)} %get-tuple-element.420.hid_ref, bf16[576,768]{1,0:T(8,128)(2,1)S(1)} %copy-done.39), custom_call_target="tpu_custom_call" | custom-call | flops 300000000 | bytes 1000 | tf_op jit(solution)/shard_map/mlp_grads/pallas_call | solution.py:705
  403.5 17.8 %attn_bwd.6 = (bf16[576,384]{1,0:T(8,128)(2,1)}, bf16[2,576,384]{2,1,0:T(8,128)(2,1)}, bf16[2,576,384]{2,1,0:T(8,128)(2,1)}, f32[3,8,128]{2,1,0:T(8,128)}) custom-call(bf16[576,128]{1,0:T(8,128)(2,1)} %get-tuple-element.281.hot_ref, bf16[6,1152,576]{2,1,0:T(8,128)(2,1)} %get-tuple-element.305.w_ref, bf16[576,2304]{1,0:T(8,128)(2,1)} %copy-done.2, ...), custom_call_target="tpu_custom_call" | custom-call | flops 360000000 | bytes 1000 | tf_op jit(solution)/shard_map/attn_bwd/pallas_call | solution.py:227
  421.3 5.8 add.390
  427.2 3.0 collective-permute-start.42
  435.1 17.8 %attn_bwd.7 = (bf16[576,384]{1,0:T(8,128)(2,1)}, bf16[2,576,384]{2,1,0:T(8,128)(2,1)}, bf16[2,576,384]{2,1,0:T(8,128)(2,1)}, f32[3,8,128]{2,1,0:T(8,128)}) custom-call(bf16[576,128]{1,0:T(8,128)(2,1)} %get-tuple-element.281.hot_ref, bf16[6,1152,576]{2,1,0:T(8,128)(2,1)} %get-tuple-element.437.w_ref, bf16[576,2304]{1,0:T(8,128)(2,1)} %copy-done.2, ...), custom_call_target="tpu_custom_call" | custom-call | flops 360000000 | bytes 1000 | tf_op jit(solution)/shard_map/attn_bwd/pallas_call | solution.py:227
  452.9 4.1 collective-permute-done.43
  464.7 7.4 %project_back.3 = (bf16[576,2304]{1,0:T(8,128)(2,1)}, bf16[576,768]{1,0:T(8,128)(2,1)}, f32[8,768]{1,0:T(8,128)S(1)}) custom-call(s32[2]{0:T(128)S(1)} %copy-done.68, bf16[576,768]{1,0:T(8,128)(2,1)S(1)} %copy-done.26, bf16[576,768]{1,0:T(8,128)(2,1)S(1)} %copy-done.13, f32[3,768]{1,0:T(4,128)S(1)} %copy-done.58, bf16[576,384]{1,0:T(8,128)(2,1)S(1)} %copy-done.53, ...), custom_call_target="tpu_custom_call" | custom-call | flops 140000000 | bytes 1000 | tf_op jit(solution)/shard_map/project_back/pallas_call | solution.py:535
  482.3 7.0 %att_grads.3 = (bf16[8,192,768]{2,1,0:T(8,128)(2,1)S(1)}, bf16[8,192,768]{2,1,0:T(8,128)(2,1)}) custom-call(s32[1]{0:T(128)} %bitcast.2.core_ref, bf16[576,768]{1,0:T(8,128)(2,1)S(1)} %copy-done.42, bf16[576,2304]{1,0:T(8,128)(2,1)} %get-tuple-element.469.dproj_ref, bf16[576,384]{1,0:T(8,128)(2,1)S(1)} %copy-done.16, bf16[576,384]{1,0:T(8,128)(2,1)S(1)} %copy-done.17, ...), custom_call_target="tpu_custom_call" | custom-call | flops 180000000 | bytes 1000 | tf_op jit(solution)/shard_map/att_grads/pallas_call | solution.py:705
  502.1 3.7 add.407
  505.8 3.9 collective-permute-start.56
  512.0 7.2 %maximum_select_fusion = bf16[4,576,768]{2,1,0:T(8,128)(2,1)} fusion(bf16[1,576,768]{2,1,0:T(8,128)(2,1)} %bitcast.207, bf16[1,576,768]{2,1,0:T(8,128)(2,1)S(1)} %bitcast.203, bf16[1,576,768]{2,1,0:T(8,128)(2,1)S(1)} %bitcast.205, bf16[1,576,768]{2,1,0:T(8,128)(2,1)S(1)} %bitcast.193, bf16[1,576,768]{2,1,0:T(8,128)(2,1)S(1)} %bitcast.204, ...), kind=kLoop, calls=%fused_computation.1 | loop fusion | flops 26542080 | bytes 17694724 | tf_op jit(solution)/shard_map/jit(_where)/select_n | solution.py:817
  519.8 7.4 %collective-permute-done.57 = bf16[288,768]{1,0:T(8,128)(2,1)S(1)} collective-permute-done((bf16[288,768]{1,0:T(8,128)(2,1)S(1)}, bf16[288,768]{1,0:T(8,128)(2,1)S(1)}, u32[]{:S(2)}, u32[]{:S(2)}) %collective-permute-start.57) | collective-permute-done | bytes 442400 | tf_op jit(solution)/shard_map/ppermute | solution.py:719
  529.1 3.1 collective-permute-start.62
  535.9 4.4 collective-permute-done.61
  545.0 6.8 %collective-permute-start.68 = (bf16[192,768]{1,0:T(8,128)(2,1)S(1)}, bf16[192,768]{1,0:T(8,128)(2,1)}, u32[]{:S(2)}, u32[]{:S(2)}) collective-permute-start(bf16[192,768]{1,0:T(8,128)(2,1)S(1)} %get-tuple-element.588), channel_id=1, source_target_pairs={{1,2},{0,3},{5,6},{4,7},{9,10},{8,11},{13,14},{12,15},{17,18},{16,... | collective-permute-start | bytes 884744 | tf_op jit(solution)/shard_map/ppermute | solution.py:719
  557.5 8.9 %select_select_fusion = f32[4,576,768]{2,1,0:T(8,128)} fusion(bf16[1,576,768]{2,1,0:T(8,128)(2,1)} %bitcast.75, bf16[1,576,768]{2,1,0:T(8,128)(2,1)} %bitcast.74, bf16[1,576,768]{2,1,0:T(8,128)(2,1)} %bitcast.73, bf16[1,576,768]{2,1,0:T(8,128)(2,1)} %bitcast.72, bf16[1,576,768]{2,1,0:T(8,128)(2,1)S(1)} %bitcast.219, bf16[1,576,768]{2,1,0:T(8,128)(2,1)} %bitcast.220, ...), kind=kLoop, calls=%fused_computation | loop fusion | flops 33619968 | bytes 21233668 | tf_op jit(solution)/shard_map/jit(_where)/select_n | solution.py:817
  568.5 8.9 %reduce-scatter.8.cloned.1.call-done = bf16[1,192,768]{2,1,0:T(8,128)(2,1)} async-done(((bf16[8,192,768]{2,1,0:T(8,128)(2,1)}), bf16[1,192,768]{2,1,0:T(8,128)(2,1)}) %reduce-scatter.8.cloned.1.call-update) | async-done | bytes 294928 | tf_op jit(solution)/shard_map/reduce_scatter | solution.py:780
  (542 shorter events, 182.5 us)
Async XLA Ops:
  7.2 414.1 %reduce-scatter.4.cloned.1.call-start = ((), (), s32[]{:S(2)}) async-start(), calls=%async_computation.3 | async-start | bytes 5308416 | tf_op jit(solution)/shard_map/reduce_scatter | solution.py:780
  8.7 37.8 %collective-permute-start.4 = (f32[3,768]{1,0:T(4,128)}, f32[3,768]{1,0:T(4,128)}, u32[]{:S(2)}, u32[]{:S(2)}) collective-permute-start(f32[3,768]{1,0:T(4,128)} %pad_maximum_fusion.9), channel_id=1, source_target_pairs={{0,3},{1,2},{2,1},{3,0},{4,7},{5,6},{6,5},{7,4},{8,11},{9,10},{10,... | collective-permute-start | bytes 27656 | tf_op jit(solution)/shard_map/ppermute | solution.py:719
  11.1 38.4 %collective-permute-start.3 = (f32[3,768]{1,0:T(4,128)}, f32[3,768]{1,0:T(4,128)}, u32[]{:S(2)}, u32[]{:S(2)}) collective-permute-start(f32[3,768]{1,0:T(4,128)} %pad_maximum_fusion.9), channel_id=1, source_target_pairs={{0,2},{1,3},{2,0},{3,1},{4,6},{5,7},{6,4},{7,5},{8,10},{9,11},{10,... | collective-permute-start | bytes 27656 | tf_op jit(solution)/shard_map/ppermute | solution.py:719
  11.7 53.2 %collective-permute-start.5 = (bf16[768,3072]{1,0:T(8,128)(2,1)}, bf16[768,3072]{1,0:T(8,128)(2,1)}, u32[]{:S(2)}, u32[]{:S(2)}) collective-permute-start(bf16[768,3072]{1,0:T(8,128)(2,1)} %bitcast.178), channel_id=1, source_target_pairs={{0,1},{1,0},{2,3},{3,2},{4,5},{5,4},{6,7},{7,6},{8,9},{9,8},{10,11... | collective-permute-start | bytes 14155784 | tf_op jit(solution)/shard_map/ppermute | solution.py:719
  15.8 35.1 %collective-permute-start = (bf16[384,2304]{1,0:T(8,128)(2,1)}, bf16[384,2304]{1,0:T(8,128)(2,1)}, u32[]{:S(2)}, u32[]{:S(2)}) collective-permute-start(bf16[384,2304]{1,0:T(8,128)(2,1)} %get-tuple-element.560), channel_id=1, source_target_pairs={{0,2},{2,0},{4,6},{6,4},{8,10},{10,8},{12,14},{14,12},{16,18},{18,... | collective-permute-start | bytes 5308424 | tf_op jit(solution)/shard_map/ppermute | solution.py:719
  19.5 39.3 %collective-permute-start.1 = (bf16[384,2304]{1,0:T(8,128)(2,1)}, bf16[384,2304]{1,0:T(8,128)(2,1)}, u32[]{:S(2)}, u32[]{:S(2)}) collective-permute-start(bf16[384,2304]{1,0:T(8,128)(2,1)} %get-tuple-element.559), channel_id=1, source_target_pairs={{0,3},{2,1},{4,7},{6,5},{8,11},{10,9},{12,15},{14,13},{16,19},{18,... | collective-permute-start | bytes 5308424 | tf_op jit(solution)/shard_map/ppermute | solution.py:719
  61.1 17.2 %collective-permute-start.7 = (bf16[96,3072]{1,0:T(8,128)(2,1)}, bf16[96,3072]{1,0:T(8,128)(2,1)S(1)}, u32[]{:S(2)}, u32[]{:S(2)}) collective-permute-start(bf16[96,3072]{1,0:T(8,128)(2,1)} %get-tuple-element.291), channel_id=1, source_target_pairs={{1,2},{3,0},{5,6},{7,4},{9,10},{11,8},{13,14},{15,12},{17,18},{19,... | collective-permute-start | bytes 1769480 | tf_op jit(solution)/shard_map/ppermute | solution.py:719
  62.4 16.0 %collective-permute-start.8 = (bf16[96,3072]{1,0:T(8,128)(2,1)}, bf16[96,3072]{1,0:T(8,128)(2,1)S(1)}, u32[]{:S(2)}, u32[]{:S(2)}) collective-permute-start(bf16[96,3072]{1,0:T(8,128)(2,1)} %get-tuple-element.292), channel_id=1, source_target_pairs={{1,3},{3,1},{5,7},{7,5},{9,11},{11,9},{13,15},{15,13},{17,19},{19,... | collective-permute-start | bytes 1769480 | tf_op jit(solution)/shard_map/ppermute | solution.py:719
  63.1 16.2 %collective-permute-start.9 = (bf16[384,768]{1,0:T(8,128)(2,1)S(1)}, bf16[384,768]{1,0:T(8,128)(2,1)S(1)}, u32[]{:S(2)}, u32[]{:S(2)}) collective-permute-start(bf16[384,768]{1,0:T(8,128)(2,1)S(1)} %dynamic-slice_bitcast_fusion.8), channel_id=1, source_target_pairs={{0,2},{1,3},{2,0},{3,1},{4,6},{5,7},{6,4},{7,5},{8,10},{9,11},{10,... | collective-permute-start | bytes 1769480 | tf_op jit(solution)/shard_map/ppermute | solution.py:719
  79.5 15.4 %collective-permute-start.10 = (bf16[576,1536]{1,0:T(8,128)(2,1)S(1)}, bf16[576,1536]{1,0:T(8,128)(2,1)S(1)}, u32[]{:S(2)}, u32[]{:S(2)}) collective-permute-start(bf16[576,1536]{1,0:T(8,128)(2,1)S(1)} %slice.241), channel_id=1, source_target_pairs={{0,1},{1,0},{2,3},{3,2},{4,5},{5,4},{6,7},{7,6},{8,9},{9,8},{10,11... | collective-permute-start | bytes 5308424 | tf_op jit(solution)/shard_map/ppermute | solution.py:719
  94.9 52.6 %collective-permute-start.19 = (bf16[768,768]{1,0:T(8,128)(2,1)}, bf16[768,768]{1,0:T(8,128)(2,1)}, u32[]{:S(2)}, u32[]{:S(2)}) collective-permute-start(bf16[768,768]{1,0:T(8,128)(2,1)} %slice.306), channel_id=1, source_target_pairs={{0,2},{2,0},{4,6},{6,4},{8,10},{10,8},{12,14},{14,12},{16,18},{18,... | collective-permute-start | bytes 3538952 | tf_op jit(solution)/shard_map/ppermute | solution.py:719
  98.8 17.4 %collective-permute-start.11 = (bf16[96,3072]{1,0:T(8,128)(2,1)S(1)}, bf16[96,3072]{1,0:T(8,128)(2,1)S(1)}, u32[]{:S(2)}, u32[]{:S(2)}) collective-permute-start(bf16[96,3072]{1,0:T(8,128)(2,1)S(1)} %broadcast_select_fusion.8.mine), channel_id=1, source_target_pairs={{0,4},{4,0},{8,12},{12,8},{16,20},{20,16},{24,28},{28,24},{1,5},{5... | collective-permute-start | bytes 1769480 | tf_op jit(solution)/shard_map/ppermute | solution.py:566
  100.3 16.3 %collective-permute-start.12 = (bf16[96,3072]{1,0:T(8,128)(2,1)S(1)}, bf16[96,3072]{1,0:T(8,128)(2,1)S(1)}, u32[]{:S(2)}, u32[]{:S(2)}) collective-permute-start(bf16[96,3072]{1,0:T(8,128)(2,1)S(1)} %broadcast_select_fusion.8.mine), channel_id=1, source_target_pairs={{0,8},{4,12},{8,0},{12,4},{16,24},{20,28},{24,16},{28,20},{1,9},{5... | collective-permute-start | bytes 1769480 | tf_op jit(solution)/shard_map/ppermute | solution.py:566
  101.9 23.2 %collective-permute-start.13 = (bf16[384,768]{1,0:T(8,128)(2,1)S(1)}, bf16[384,768]{1,0:T(8,128)(2,1)S(1)}, u32[]{:S(2)}, u32[]{:S(2)}) collective-permute-start(bf16[384,768]{1,0:T(8,128)(2,1)S(1)} %collective-permute-done.9.mine), channel_id=1, source_target_pairs={{0,4},{4,0},{8,12},{12,8},{16,20},{20,16},{24,28},{28,24},{1,5},{5... | collective-permute-start | bytes 1769480 | tf_op jit(solution)/shard_map/ppermute | solution.py:566
  102.5 24.1 %collective-permute-start.14 = (bf16[384,768]{1,0:T(8,128)(2,1)S(1)}, bf16[384,768]{1,0:T(8,128)(2,1)S(1)}, u32[]{:S(2)}, u32[]{:S(2)}) collective-permute-start(bf16[384,768]{1,0:T(8,128)(2,1)S(1)} %collective-permute-done.9.mine), channel_id=1, source_target_pairs={{0,8},{4,12},{8,0},{12,4},{16,24},{20,28},{24,16},{28,20},{1,9},{5... | collective-permute-start | bytes 1769480 | tf_op jit(solution)/shard_map/ppermute | solution.py:566
  127.4 18.5 %collective-permute-start.15 = (bf16[48,3072]{1,0:T(8,128)(2,1)}, bf16[48,3072]{1,0:T(8,128)(2,1)S(1)}, u32[]{:S(2)}, u32[]{:S(2)}) collective-permute-start(bf16[48,3072]{1,0:T(8,128)(2,1)} %slice.242), channel_id=1, source_target_pairs={{0,4},{4,0},{8,12},{12,8},{16,20},{20,16},{24,28},{28,24},{1,5},{5... | collective-permute-start | bytes 884744 | tf_op jit(solution)/shard_map/ppermute | solution.py:566
  127.8 18.1 %collective-permute-start.16 = (bf16[48,3072]{1,0:T(8,128)(2,1)S(1)}, bf16[48,3072]{1,0:T(8,128)(2,1)S(1)}, u32[]{:S(2)}, u32[]{:S(2)}) collective-permute-start(bf16[48,3072]{1,0:T(8,128)(2,1)S(1)} %slice.243), channel_id=1, source_target_pairs={{0,8},{4,12},{8,0},{12,4},{16,24},{20,28},{24,16},{28,20},{1,9},{5... | collective-permute-start | bytes 884744 | tf_op jit(solution)/shard_map/ppermute | solution.py:566
  130.3 16.4 %collective-permute-start.17 = (bf16[192,768]{1,0:T(8,128)(2,1)}, bf16[192,768]{1,0:T(8,128)(2,1)S(1)}, u32[]{:S(2)}, u32[]{:S(2)}) collective-permute-start(bf16[192,768]{1,0:T(8,128)(2,1)} %slice.244), channel_id=1, source_target_pairs={{0,4},{4,0},{8,12},{12,8},{16,20},{20,16},{24,28},{28,24},{1,5},{5... | collective-permute-start | bytes 884744 | tf_op jit(solution)/shard_map/ppermute | solution.py:566
  191.6 31.5 %collective-permute-start.25 = (bf16[576,768]{1,0:T(8,128)(2,1)S(1)}, bf16[576,768]{1,0:T(8,128)(2,1)S(1)}, u32[]{:S(2)}, u32[]{:S(2)}) collective-permute-start(bf16[576,768]{1,0:T(8,128)(2,1)S(1)} %get-tuple-element.495), channel_id=1, source_target_pairs={{2,0},{3,1},{6,4},{7,5},{10,8},{11,9},{14,12},{15,13},{18,16},{19,... | collective-permute-start | bytes 2654216 | tf_op jit(solution)/shard_map/ppermute | solution.py:719
  192.9 46.4 %collective-permute-start.26 = (bf16[576,768]{1,0:T(8,128)(2,1)S(1)}, bf16[576,768]{1,0:T(8,128)(2,1)S(1)}, u32[]{:S(2)}, u32[]{:S(2)}) collective-permute-start(bf16[576,768]{1,0:T(8,128)(2,1)S(1)} %get-tuple-element.565), channel_id=1, source_target_pairs={{0,1},{1,0},{4,5},{5,4},{8,9},{9,8},{12,13},{13,12},{16,17},{17,16... | collective-permute-start | bytes 2654216 | tf_op jit(solution)/shard_map/ppermute | solution.py:719
  194.9 44.4 %collective-permute-start.27 = (bf16[576,768]{1,0:T(8,128)(2,1)S(1)}, bf16[576,768]{1,0:T(8,128)(2,1)S(1)}, u32[]{:S(2)}, u32[]{:S(2)}) collective-permute-start(bf16[576,768]{1,0:T(8,128)(2,1)S(1)} %get-tuple-element.565), channel_id=1, source_target_pairs={{3,0},{2,1},{7,4},{6,5},{11,8},{10,9},{15,12},{14,13},{19,16},{18,... | collective-permute-start | bytes 2654216 | tf_op jit(solution)/shard_map/ppermute | solution.py:719
  242.5 27.4 %collective-permute-start.28 = (bf16[576,768]{1,0:T(8,128)(2,1)S(1)}, bf16[576,768]{1,0:T(8,128)(2,1)S(1)}, u32[]{:S(2)}, u32[]{:S(2)}) collective-permute-start(bf16[576,768]{1,0:T(8,128)(2,1)S(1)} %get-tuple-element.505), channel_id=1, source_target_pairs={{0,2},{1,3},{4,6},{5,7},{8,10},{9,11},{12,14},{13,15},{16,18},{17,... | collective-permute-start | bytes 2654216 | tf_op jit(solution)/shard_map/ppermute | solution.py:719
  247.2 40.2 %collective-permute-start.29 = (bf16[576,768]{1,0:T(8,128)(2,1)}, bf16[576,768]{1,0:T(8,128)(2,1)S(1)}, u32[]{:S(2)}, u32[]{:S(2)}) collective-permute-start(bf16[576,768]{1,0:T(8,128)(2,1)} %get-tuple-element.563), channel_id=1, source_target_pairs={{2,3},{3,2},{6,7},{7,6},{10,11},{11,10},{14,15},{15,14},{18,19},{1... | collective-permute-start | bytes 2654216 | tf_op jit(solution)/shard_map/ppermute | solution.py:719
  247.9 39.5 %collective-permute-start.30 = (bf16[576,768]{1,0:T(8,128)(2,1)}, bf16[576,768]{1,0:T(8,128)(2,1)S(1)}, u32[]{:S(2)}, u32[]{:S(2)}) collective-permute-start(bf16[576,768]{1,0:T(8,128)(2,1)} %get-tuple-element.563), channel_id=1, source_target_pairs={{1,2},{0,3},{5,6},{4,7},{9,10},{8,11},{13,14},{12,15},{17,18},{16,... | collective-permute-start | bytes 2654216 | tf_op jit(solution)/shard_map/ppermute | solution.py:719
  287.5 19.0 %collective-permute-start.31 = (bf16[8,384,768]{2,1,0:T(8,128)(2,1)}, bf16[8,384,768]{2,1,0:T(8,128)(2,1)}, u32[]{:S(2)}, u32[]{:S(2)}) collective-permute-start(bf16[8,384,768]{2,1,0:T(8,128)(2,1)} %get-tuple-element.382), channel_id=1, source_target_pairs={{0,1},{1,0},{2,3},{3,2},{4,5},{5,4},{6,7},{7,6},{8,9},{9,8},{10,11... | collective-permute-start | bytes 14155784 | tf_op jit(solution)/shard_map/ppermute | solution.py:719
  312.2 177.1 %reduce-scatter.6.cloned.1.call-start = ((), (), s32[]{:S(2)}) async-start(), calls=%async_computation.4 | async-start | bytes 2654208 | tf_op jit(solution)/shard_map/reduce_scatter | solution.py:780
  312.3 18.1 %collective-permute-start.32 = (bf16[2,576,384]{2,1,0:T(8,128)(2,1)}, bf16[2,576,384]{2,1,0:T(8,128)(2,1)S(1)}, u32[]{:S(2)}, u32[]{:S(2)}) collective-permute-start(bf16[2,576,384]{2,1,0:T(8,128)(2,1)} %get-tuple-element.386), channel_id=1, source_target_pairs={{0,1},{1,0},{2,3},{3,2},{4,5},{5,4},{6,7},{7,6},{8,9},{9,8},{10,11... | collective-permute-start | bytes 2654216 | tf_op jit(solution)/shard_map/ppermute | solution.py:719
  351.1 25.6 %collective-permute-start.34 = (bf16[8,192,768]{2,1,0:T(8,128)(2,1)}, bf16[8,192,768]{2,1,0:T(8,128)(2,1)}, u32[]{:S(2)}, u32[]{:S(2)}) collective-permute-start(bf16[8,192,768]{2,1,0:T(8,128)(2,1)} %get-tuple-element.414), channel_id=1, source_target_pairs={{0,1},{1,0},{2,3},{3,2},{4,5},{5,4},{6,7},{7,6},{8,9},{9,8},{10,11... | collective-permute-start | bytes 7077896 | tf_op jit(solution)/shard_map/ppermute | solution.py:719
  352.8 23.9 %collective-permute-start.35 = (bf16[576,768]{1,0:T(8,128)(2,1)S(1)}, bf16[576,768]{1,0:T(8,128)(2,1)S(1)}, u32[]{:S(2)}, u32[]{:S(2)}) collective-permute-start(bf16[576,768]{1,0:T(8,128)(2,1)S(1)} %get-tuple-element.543), channel_id=1, source_target_pairs={{0,2},{1,3},{4,6},{5,7},{8,10},{9,11},{12,14},{13,15},{16,18},{17,... | collective-permute-start | bytes 2654216 | tf_op jit(solution)/shard_map/ppermute | solution.py:719
  354.7 43.7 %collective-permute-start.36 = (bf16[576,768]{1,0:T(8,128)(2,1)}, bf16[576,768]{1,0:T(8,128)(2,1)}, u32[]{:S(2)}, u32[]{:S(2)}) collective-permute-start(bf16[576,768]{1,0:T(8,128)(2,1)} %get-tuple-element.561), channel_id=1, source_target_pairs={{2,3},{3,2},{6,7},{7,6},{10,11},{11,10},{14,15},{15,14},{18,19},{1... | collective-permute-start | bytes 2654216 | tf_op jit(solution)/shard_map/ppermute | solution.py:719
  356.3 42.1 %collective-permute-start.37 = (bf16[576,768]{1,0:T(8,128)(2,1)}, bf16[576,768]{1,0:T(8,128)(2,1)}, u32[]{:S(2)}, u32[]{:S(2)}) collective-permute-start(bf16[576,768]{1,0:T(8,128)(2,1)} %get-tuple-element.561), channel_id=1, source_target_pairs={{1,2},{0,3},{5,6},{4,7},{9,10},{8,11},{13,14},{12,15},{17,18},{16,... | collective-permute-start | bytes 2654216 | tf_op jit(solution)/shard_map/ppermute | solution.py:719
  398.4 22.9 %collective-permute-start.38 = (bf16[8,384,768]{2,1,0:T(8,128)(2,1)}, bf16[8,384,768]{2,1,0:T(8,128)(2,1)}, u32[]{:S(2)}, u32[]{:S(2)}) collective-permute-start(bf16[8,384,768]{2,1,0:T(8,128)(2,1)} %get-tuple-element.432), channel_id=1, source_target_pairs={{0,1},{1,0},{2,3},{3,2},{4,5},{5,4},{6,7},{7,6},{8,9},{9,8},{10,11... | collective-permute-start | bytes 14155784 | tf_op jit(solution)/shard_map/ppermute | solution.py:719
  398.7 178.7 %reduce-scatter.8.cloned.1.call-start = ((), (), s32[]{:S(2)}) async-start(), calls=%async_computation.5 | async-start | bytes 2654208 | tf_op jit(solution)/shard_map/reduce_scatter | solution.py:780
  399.5 21.7 %collective-permute-start.39 = (bf16[576,768]{1,0:T(8,128)(2,1)S(1)}, bf16[576,768]{1,0:T(8,128)(2,1)S(1)}, u32[]{:S(2)}, u32[]{:S(2)}) collective-permute-start(bf16[576,768]{1,0:T(8,128)(2,1)S(1)} %copy-done.25), channel_id=1, source_target_pairs={{0,1},{4,5},{8,9},{12,13},{16,17},{20,21},{24,25},{28,29}} | collective-permute-start | bytes 2654216 | tf_op jit(solution)/shard_map/ppermute | solution.py:719
  401.7 19.5 %collective-permute-start.40 = (bf16[576,768]{1,0:T(8,128)(2,1)S(1)}, bf16[576,768]{1,0:T(8,128)(2,1)S(1)}, u32[]{:S(2)}, u32[]{:S(2)}) collective-permute-start(bf16[576,768]{1,0:T(8,128)(2,1)S(1)} %copy-done.25), channel_id=1, source_target_pairs={{3,1},{7,5},{11,9},{15,13},{19,17},{23,21},{27,25},{31,29}} | collective-permute-start | bytes 2654216 | tf_op jit(solution)/shard_map/ppermute | solution.py:719
  402.5 18.8 %collective-permute-start.41 = (bf16[576,768]{1,0:T(8,128)(2,1)S(1)}, bf16[576,768]{1,0:T(8,128)(2,1)S(1)}, u32[]{:S(2)}, u32[]{:S(2)}) collective-permute-start(bf16[576,768]{1,0:T(8,128)(2,1)S(1)} %copy-done.25), channel_id=1, source_target_pairs={{2,1},{6,5},{10,9},{14,13},{18,17},{22,21},{26,25},{30,29}} | collective-permute-start | bytes 2654216 | tf_op jit(solution)/shard_map/ppermute | solution.py:719
  427.2 30.6 %collective-permute-start.42 = (bf16[2,576,384]{2,1,0:T(8,128)(2,1)}, bf16[2,576,384]{2,1,0:T(8,128)(2,1)S(1)}, u32[]{:S(2)}, u32[]{:S(2)}) collective-permute-start(bf16[2,576,384]{2,1,0:T(8,128)(2,1)} %get-tuple-element.439), channel_id=1, source_target_pairs={{0,1},{1,0},{2,3},{3,2},{4,5},{5,4},{6,7},{7,6},{8,9},{9,8},{10,11... | collective-permute-start | bytes 2654216 | tf_op jit(solution)/shard_map/ppermute | solution.py:719
  431.7 25.3 %collective-permute-start.43 = (bf16[2,2,2,192,256]{4,3,2,1,0:T(8,128)(2,1)}, bf16[2,2,2,192,256]{4,3,2,1,0:T(8,128)(2,1)S(1)}, u32[]{:S(2)}, u32[]{:S(2)}) collective-permute-start(bf16[2,2,2,192,256]{4,3,2,1,0:T(8,128)(2,1)} %get-tuple-element.572), channel_id=1, source_target_pairs={{0,4},{4,0},{8,12},{12,8},{16,20},{20,16},{24,28},{28,24},{1,5},{5... | collective-permute-start | bytes 2359304 | tf_op jit(solution)/shard_map/ppermute | solution.py:757
  432.7 24.3 %collective-permute-start.44 = (bf16[2,2,2,192,256]{4,3,2,1,0:T(8,128)(2,1)}, bf16[2,2,2,192,256]{4,3,2,1,0:T(8,128)(2,1)S(1)}, u32[]{:S(2)}, u32[]{:S(2)}) collective-permute-start(bf16[2,2,2,192,256]{4,3,2,1,0:T(8,128)(2,1)} %get-tuple-element.570), channel_id=1, source_target_pairs={{0,2},{1,3},{2,0},{3,1},{4,6},{5,7},{6,4},{7,5},{8,10},{9,11},{10,... | collective-permute-start | bytes 2359304 | tf_op jit(solution)/shard_map/ppermute | solution.py:757
  433.0 24.8 %collective-permute-start.45 = (bf16[2,2,2,192,256]{4,3,2,1,0:T(8,128)(2,1)S(1)}, bf16[2,2,2,192,256]{4,3,2,1,0:T(8,128)(2,1)S(1)}, u32[]{:S(2)}, u32[]{:S(2)}) collective-permute-start(bf16[2,2,2,192,256]{4,3,2,1,0:T(8,128)(2,1)S(1)} %get-tuple-element.568), channel_id=1, source_target_pairs={{0,8},{4,12},{8,0},{12,4},{16,24},{20,28},{24,16},{28,20},{1,9},{5... | collective-permute-start | bytes 2359304 | tf_op jit(solution)/shard_map/ppermute | solution.py:757
  492.7 35.3 %collective-permute-start.59 = (bf16[576,768]{1,0:T(8,128)(2,1)}, bf16[576,768]{1,0:T(8,128)(2,1)}, u32[]{:S(2)}, u32[]{:S(2)}) collective-permute-start(bf16[576,768]{1,0:T(8,128)(2,1)} %get-tuple-element.528), channel_id=1, source_target_pairs={{2,0},{6,4},{10,8},{14,12},{18,16},{22,20},{26,24},{30,28}} | collective-permute-start | bytes 2654216 | tf_op jit(solution)/shard_map/ppermute | solution.py:719
  494.0 34.0 %collective-permute-start.60 = (bf16[576,768]{1,0:T(8,128)(2,1)}, bf16[576,768]{1,0:T(8,128)(2,1)}, u32[]{:S(2)}, u32[]{:S(2)}) collective-permute-start(bf16[576,768]{1,0:T(8,128)(2,1)} %get-tuple-element.528), channel_id=1, source_target_pairs={{3,0},{7,4},{11,8},{15,12},{19,16},{23,20},{27,24},{31,28}} | collective-permute-start | bytes 2654216 | tf_op jit(solution)/shard_map/ppermute | solution.py:719
  499.9 28.0 %collective-permute-start.58 = (bf16[192,768]{1,0:T(8,128)(2,1)}, bf16[192,768]{1,0:T(8,128)(2,1)}, u32[]{:S(2)}, u32[]{:S(2)}) collective-permute-start(bf16[192,768]{1,0:T(8,128)(2,1)} %get-tuple-element.589), channel_id=1, source_target_pairs={{0,16},{4,20},{8,24},{12,28},{16,0},{20,4},{24,8},{28,12},{1,17},{... | collective-permute-start | bytes 884744 | tf_op jit(solution)/shard_map/ppermute | solution.py:757
  511.7 15.5 %collective-permute-start.57 = (bf16[288,768]{1,0:T(8,128)(2,1)S(1)}, bf16[288,768]{1,0:T(8,128)(2,1)S(1)}, u32[]{:S(2)}, u32[]{:S(2)}) collective-permute-start(bf16[288,768]{1,0:T(8,128)(2,1)S(1)} %pad_maximum_fusion.1), channel_id=1, source_target_pairs={{0,2},{1,3},{2,0},{3,1},{4,6},{5,7},{6,4},{7,5},{8,10},{9,11},{10,... | collective-permute-start | bytes 1327112 | tf_op jit(solution)/shard_map/ppermute | solution.py:719
  544.3 22.8 %collective-permute-start.66 = (bf16[192,768]{1,0:T(8,128)(2,1)S(1)}, bf16[192,768]{1,0:T(8,128)(2,1)S(1)}, u32[]{:S(2)}, u32[]{:S(2)}) collective-permute-start(bf16[192,768]{1,0:T(8,128)(2,1)S(1)} %get-tuple-element.588), channel_id=1, source_target_pairs={{3,2},{2,3},{7,6},{6,7},{11,10},{10,11},{15,14},{14,15},{19,18},{1... | collective-permute-start | bytes 884744 | tf_op jit(solution)/shard_map/ppermute | solution.py:719
  545.0 23.6 %collective-permute-start.68 = (bf16[192,768]{1,0:T(8,128)(2,1)S(1)}, bf16[192,768]{1,0:T(8,128)(2,1)}, u32[]{:S(2)}, u32[]{:S(2)}) collective-permute-start(bf16[192,768]{1,0:T(8,128)(2,1)S(1)} %get-tuple-element.588), channel_id=1, source_target_pairs={{1,2},{0,3},{5,6},{4,7},{9,10},{8,11},{13,14},{12,15},{17,18},{16,... | collective-permute-start | bytes 884744 | tf_op jit(solution)/shard_map/ppermute | solution.py:719
  577.4 16.8 %collective-permute-start.71 = (bf16[192,768]{1,0:T(8,128)(2,1)}, bf16[192,768]{1,0:T(8,128)(2,1)S(1)}, u32[]{:S(2)}, u32[]{:S(2)}) collective-permute-start(bf16[192,768]{1,0:T(8,128)(2,1)} %bitcast.230), channel_id=1, source_target_pairs={{3,0},{7,4},{11,8},{15,12},{19,16},{23,20},{27,24},{31,28}} | collective-permute-start | bytes 884744 | tf_op jit(solution)/shard_map/ppermute | solution.py:719
  578.7 15.5 %collective-permute-start.70 = (bf16[192,768]{1,0:T(8,128)(2,1)}, bf16[192,768]{1,0:T(8,128)(2,1)S(1)}, u32[]{:S(2)}, u32[]{:S(2)}) collective-permute-start(bf16[192,768]{1,0:T(8,128)(2,1)} %bitcast.231), channel_id=1, source_target_pairs={{1,0},{5,4},{9,8},{13,12},{17,16},{21,20},{25,24},{29,28}} | collective-permute-start | bytes 884744 | tf_op jit(solution)/shard_map/ppermute | solution.py:719
  (164 other events, 1525.3 us)
Sparse Core Ops, SparseCore 0:
  312.3 94.6 reduce-scatter.3
  410.5 73.3 reduce-scatter.5
  506.0 71.3 reduce-scatter.7

commit v4 on v3

--- a/solution.py
+++ b/solution.py
@@ -821,9 +821,10 @@
 def small_sum(value, step):
     if lax.axis_size("dp") != 8:
         return lax.psum(value, ("dp", "pipe")) if step == 0 else value
-    if step < 2:
-        return value + swap(value, step + 1)
-    return value + dp_swap(value, 1 << (step - 2))
+    if step == 2:
+        return value + dp_swap(value, 4)
+    move = swap if step == 0 else dp_swap
+    return (value + move(value, 1)) + (move(value, 2) + move(value, 3))
 
 
 def local(
@@ -866,8 +867,9 @@
     half_rows = own_half.shape[0] // 4
     share_half = lax.dynamic_slice_in_dim(own_half, q * half_rows, half_rows, 0)
     own_out = own_first[:, 3 * width :]
-    ready = (far_qkv, params, infos, current, hot, hot_back, keys, maps, share, share_half, own_out)
-    far_qkv, params, infos, current, hot, hot_back, keys, maps, share, share_half, own_out = together(ready)
+    last_grad = own_rows(out_grad)
+    ready = (far_qkv, params, infos, current, last_grad, hot, hot_back, keys, maps, share, share_half, own_out)
+    far_qkv, params, infos, current, last_grad, hot, hot_back, keys, maps, share, share_half, own_out = together(ready)
     far_qkv = pick(core, *far_qkv)
     qkv_refs = (own_first, swap(own_first, 1), far_qkv, swap(far_qkv, 1))
     mine_up = (send(share[0], [(1, 2), (3, 0)]), send(share[1], [(1, 3), (3, 1)]))
@@ -892,23 +894,24 @@
         p0, p1, info = params[2 * layer], params[2 * layer + 1], infos[layer]
         normed, proj = project(info, current, p0, qkv_refs)
         if layer == 0:
-            normed, proj, mine_up, mine_half = together((normed, proj, mine_up, mine_half))
-            some_up = quad_start(pick(core, *mine_up))
+            own_out = tie(own_out, normed)
         partner = swap(proj[:, width:], 1)
         front = lambda keys, i: attn_forward(hot, maps[layer], proj, partner, keys, i * cut, cut)
         if layer == 0:
-            partner, own_out = together((partner, own_out))
-            some_half = quad_start(mine_half)
+            partner, own_out, mine_up = together((partner, own_out, mine_up))
+            some_up = quad_start(pick(core, *mine_up))
             far_out = send(own_out, [(0, 2), (2, 0)])
         part_a = front(keys, 0)
         if layer == 0:
-            part_a, some_up, some_half = together((part_a, some_up, some_half))
-            all_up, all_half = quad_end(*some_up), quad_end(*some_half)
+            part_a, some_up, mine_half = together((part_a, some_up, mine_half))
+            some_half = quad_start(mine_half)
+            all_up = quad_end(*some_up)
         part_b = front(tie(keys, part_a[0]), 1)
         if layer == 0:
-            part_b, all_up, all_half, far_out = together((part_b, all_up, all_half, far_out))
+            part_b, all_up, some_half, far_out = together((part_b, all_up, some_half, far_out))
+            near_out, all_half = swap(far_out, 1), quad_end(*some_half)
             far_up, far_half = quad_place(*all_up), quad_place(*all_half)
-            far_out = pick(core, far_out, swap(far_out, 1))
+            far_out = pick(core, far_out, near_out)
             near_half = swap(tie(own_half, far_qkv), 1)
             more_refs = (qkv_refs[0], qkv_refs[1], far_out, far_out)
             up_refs = (qkv_refs[0], qkv_refs[1], far_up, swap(far_up, 1))
@@ -928,7 +931,7 @@
 
     x, normed, proj, partner, outcome, b0, x1, n1, slope, hidden, b1 = kept[1]
     p0, p1, info = params[2], params[3], infos[1]
-    grad = tie(own_rows(out_grad), current)
+    grad = tie(last_grad, current)
     db1, d_pre, gx1, db0, d_context, vec1 = block_back(info, grad, x1, slope, b1, b0, p0, p1, more_refs, up_refs, down_refs)
     db1, d_pre, gx1, db0, d_context, vec1 = tie((db1, d_pre, gx1, db0, d_context, vec1), outs[2][2])
     keep, other = weight_grads(mlp_grads_kernel, core, dp_size, 15, n1, d_pre, (hidden,), db1)
@@ -978,35 +981,32 @@
     keep, other = weight_grads(att_grads_kernel, core, dp_size, 9, tie(normed, given), d_proj, [part[0] for part in outcome], db0)
     keep, other, att_b, grads[0][1], mlp_a = hold((keep, other, att_b, grads[0][1], mlp_a), 4)
     got = swap(other, 1)
+    att_sum = keep + got
+    att_a = line_start(att_sum)
     tables = [(ta, tb), tables[1]]
+    att_sum, tables, vec0, mlp_b, att_b, outs, mlp_a = hold((att_sum, tables, vec0, mlp_b, att_b, outs, mlp_a), 6)
     vecs[1], vecs[0] = vec1[:3], jnp.concatenate([vec0[:2], vec1[3:4]])
     stack = lambda parts: jnp.stack([parts[s] for s in range(sections)])
     table_all = [jnp.concatenate(tables[layer])[:, :4].reshape(heads, 2, 128)[..., : 2 * SIDE_L + 1] for layer in range(layers)]
     small = jnp.concatenate([stack(vecs).reshape(-1), jnp.stack(table_all).reshape(-1)])
+    mlp_a, _ = cube_end(mlp_a)
+    mlp_b, att_b = line_end(mlp_b, att_b)
     small = small_sum(small, 0)
-    mlp_a, _ = cube_end(mlp_a)
-    got, keep, small = together((got, keep, small))
-    att_sum = keep + got
-    att_a = line_start(att_sum)
-    mlp_b, att_b, small, outs = tie((mlp_b, att_b, small, outs), att_sum)
-    mlp_b, att_b = line_end(mlp_b, att_b)
-    small = small_sum(small, 1)
     section_out = collected(outs).reshape(1, micro_count, slot_rows, width)
     small, section_out, mlp_b, att_b, mlp_a, grads[0] = together((small, section_out, mlp_b, att_b, mlp_a, grads[0]))
     mlp_a = settled(*mlp_a)
     low, high = jnp.split(mlp_a, 2, axis=0)
-    small = small_sum(small, 2)
+    small = small_sum(small, 1)
     ups = [mlp_a, send(mlp_a, [(0, 1)])]
     downs = by_sender(0, low, high, core, (2, 3))
     small, ups, downs, mlp_b, att_b = together((small, ups, downs, mlp_b, att_b))
-    small = small_sum(small, 3)
+    small = small_sum(small, 2)
     even = jnp.concatenate([att_b, mlp_b[: att_b.shape[0]]], axis=0)
     own_b = pick(core, even, mlp_b)
     got_b = by_sender(1, even, mlp_b, core, (1, 2, 3))
     grads = tie(grads, own_b)
     in_grads = collected({s: [part.astype(F32) for part in grads[s]] for s in range(sections)}).reshape(1, micro_count, slot_rows, width)
     small, got_b, in_grads, att_a = together((small, got_b, in_grads, att_a))
-    small = small_sum(small, 4)
     got_a = from_pipe(att_a, 0, range(4))
 
     first_grads, half_grads = {}, {}

time: 612 us -> 604 us (0.987)
  waiting for transfers between devices: 67 us -> 104 us
  other arithmetic: 83 us -> 61.5 us
  local copies, waits for them, and re-layouts: 70.2 us -> 57.9 us
  starting transfers between devices: 108 us -> 96.3 us
    ppermute x52 -> x53, waiting for transfers between devices: 34.5 us -> 65.1 us  [send(): return lax.ppermute(value, 'pipe', pairs)]
    ppermute x10, waiting for transfers between devices: 8.79 us -> 29.2 us  [halve(): lax.ppermute(give, name, [(k, k ^ bit) for k in range(lax.axis_size(name))])]
    ppermute x52 -> x53, starting transfers between devices: 85.8 us -> 74 us  [send(): return lax.ppermute(value, 'pipe', pairs)]
    ppermute x11 -> x12, waiting for transfers between devices: 14.8 us -> 5.03 us  [dp_swap(): lax.ppermute(value, 'dp', [(i, i ^ bit) for i in range(lax.axis_size('dp'...]
    unnamed x273 -> x227, local copies, waits for them, and re-layouts: 36.4 us -> 32 us
    ppermute x11 -> x12, starting transfers between devices: 11.2 us -> 13.4 us  [dp_swap(): lax.ppermute(value, 'dp', [(i, i ^ bit) for i in range(lax.axis_size('dp'...]
  transfers between devices with their start and end apart: 76 -> 78, of which waited for: 18 -> 25; matrix products, arithmetic and copies ran while one was open for 17% -> 13% of each run, Pallas kernels for 39% -> 39%
where the time goes in v4:
time: 604 us; the launch traced here: 596 us
  Pallas kernels  257 us (43%)
  waiting for transfers between devices  104 us (17%)
  starting transfers between devices  96.3 us (16%)
  other arithmetic  61.5 us (10%)
  local copies, waits for them, and re-layouts  57.9 us (10%)
  between operations  19.8 us (3%)
    ppermute x53, starting transfers between devices, send(): return lax.ppermute(value, 'pipe', pairs)  74 us
    pallas_call x4, Pallas kernels, attn_backward(): pl.pallas_call(attn_bwd_kernel, grid=(count,), in_specs=[whole((rows, 128...  71.9 us
    ppermute x53, waiting for transfers between devices, send(): return lax.ppermute(value, 'pipe', pairs)  65.1 us
    pallas_call x4, Pallas kernels, attn_forward(): pl.pallas_call(attn_fwd_kernel, grid=(count,), in_specs=[whole((rows, 128...  51 us
    pallas_call x4, Pallas kernels, weight_grads(): pl.pallas_call(kernel, grid=(4,), in_specs=[SMEM, whole(a.shape), col, *(...  42.1 us
    pallas_call x2, Pallas kernels, block_back(): pl.pallas_call(block_back_kernel, grid=(1,), in_specs=[SMEM, one, one, AN...  34.4 us
    unnamed x227, local copies, waits for them, and re-layouts  32 us
    pallas_call x2, Pallas kernels, block_out(): pl.pallas_call(block_out_kernel, grid=(1,), in_specs=[SMEM, one, *[whole(...  31.9 us
  transfers between devices with their start and end apart: 78, of which 25 were waited for; matrix products, arithmetic and copies ran while one was open for 13% of the time, Pallas kernels for 39%

profile of v4, /device:TPU:0, one launch (start us, length us, event | category | flops | bytes accessed | tf_op | source)
XLA Modules:
  0.0 596.0 jit_solution(1991486949733741223)
XLA Ops:
  11.1 3.4 fusion.24
  14.6 3.6 collective-permute-start
  18.2 2.8 collective-permute-start.1
  43.4 14.0 %collective-permute-done.1 = bf16[384,2304]{1,0:T(8,128)(2,1)} collective-permute-done((bf16[384,2304]{1,0:T(8,128)(2,1)S(1)}, bf16[384,2304]{1,0:T(8,128)(2,1)}, u32[]{:S(2)}, u32[]{:S(2)}) %collective-permute-start.1) | collective-permute-done | bytes 1769504 | tf_op jit(solution)/shard_map/ppermute | solution.py:719
  59.8 3.3 collective-permute-done.6.far_other
  63.2 3.0 copy-done.4
  66.1 3.9 project.2
  74.9 13.9 %collective-permute-done.8 = bf16[96,3072]{1,0:T(8,128)(2,1)S(1)} collective-permute-done((bf16[96,3072]{1,0:T(8,128)(2,1)}, bf16[96,3072]{1,0:T(8,128)(2,1)S(1)}, u32[]{:S(2)}, u32[]{:S(2)}) %collective-permute-start.8) | collective-permute-done | bytes 589856 | tf_op jit(solution)/shard_map/ppermute | solution.py:719
  92.2 3.1 collective-permute-start.17
  96.0 12.6 %attn_fwd.4 = (bf16[576,384]{1,0:T(8,128)(2,1)}, bf16[576,384]{1,0:T(8,128)(2,1)}, f32[576,384]{1,0:T(8,128)}, bf16[6,1152,576]{2,1,0:T(8,128)(2,1)}) custom-call(bf16[576,128]{1,0:T(8,128)(2,1)} %get-tuple-element.291.hot_ref, f32[6,8,128]{2,1,0:T(8,128)} %get-tuple-element.628.map_ref, bf16[576,2304]{1,0:T(8,128)(2,1)} %copy-done.2, ...), custom_call_target="tpu_custom_call" | custom-call | flops 520000000 | bytes 1000 | tf_op jit(solution)/shard_map/attn_fwd/pallas_call | solution.py:145
  112.9 12.6 %attn_fwd.5 = (bf16[576,384]{1,0:T(8,128)(2,1)}, bf16[576,384]{1,0:T(8,128)(2,1)}, f32[576,384]{1,0:T(8,128)}, bf16[6,1152,576]{2,1,0:T(8,128)(2,1)}) custom-call(bf16[576,128]{1,0:T(8,128)(2,1)} %get-tuple-element.291.hot_ref, f32[6,8,128]{2,1,0:T(8,128)} %get-tuple-element.628.map_ref, bf16[576,2304]{1,0:T(8,128)(2,1)} %copy-done.2, ...), custom_call_target="tpu_custom_call" | custom-call | flops 520000000 | bytes 1000 | tf_op jit(solution)/shard_map/attn_fwd/pallas_call | solution.py:145
  145.8 5.6 collective-permute-done.18
  155.4 15.8 %block_out.2 = (bf16[576,768]{1,0:T(8,128)(2,1)}, bf16[576,768]{1,0:T(8,128)(2,1)}, bf16[576,768]{1,0:T(8,128)(2,1)}, bf16[576,3072]{1,0:T(8,128)(2,1)}, bf16[57...) custom-call(s32[2]{0:T(128)} %copy-done.50, bf16[576,768]{1,0:T(8,128)(2,1)} %copy-done.11, ...), custom_call_target="tpu_custom_call" | custom-call | flops 240000000 | bytes 1000 | tf_op jit(solution)/shard_map/block_out/pallas_call | solution.py:406
  175.4 4.2 project.3
  188.4 13.0 %attn_fwd.6 = (bf16[576,384]{1,0:T(8,128)(2,1)}, bf16[576,384]{1,0:T(8,128)(2,1)}, f32[576,384]{1,0:T(8,128)}, bf16[6,1152,576]{2,1,0:T(8,128)(2,1)}) custom-call(bf16[576,128]{1,0:T(8,128)(2,1)} %get-tuple-element.291.hot_ref, f32[6,8,128]{2,1,0:T(8,128)} %get-tuple-element.627.map_ref, bf16[576,2304]{1,0:T(8,128)(2,1)} %copy-done.3, ...), custom_call_target="tpu_custom_call" | custom-call | flops 520000000 | bytes 1000 | tf_op jit(solution)/shard_map/attn_fwd/pallas_call | solution.py:145
  201.4 12.7 %attn_fwd.7 = (bf16[576,384]{1,0:T(8,128)(2,1)}, bf16[576,384]{1,0:T(8,128)(2,1)}, f32[576,384]{1,0:T(8,128)}, bf16[6,1152,576]{2,1,0:T(8,128)(2,1)}) custom-call(bf16[576,128]{1,0:T(8,128)(2,1)} %get-tuple-element.291.hot_ref, f32[6,8,128]{2,1,0:T(8,128)} %get-tuple-element.627.map_ref, bf16[576,2304]{1,0:T(8,128)(2,1)} %copy-done.3, ...), custom_call_target="tpu_custom_call" | custom-call | flops 520000000 | bytes 1000 | tf_op jit(solution)/shard_map/attn_fwd/pallas_call | solution.py:145
  214.1 16.1 %block_out.3 = (bf16[576,768]{1,0:T(8,128)(2,1)}, bf16[576,768]{1,0:T(8,128)(2,1)}, bf16[576,768]{1,0:T(8,128)(2,1)}, bf16[576,3072]{1,0:T(8,128)(2,1)}, bf16[57...) custom-call(s32[2]{0:T(128)} %get-tuple-element.289.info_ref, ...), custom_call_target="tpu_custom_call" | custom-call | flops 240000000 | bytes 1000 | tf_op jit(solution)/shard_map/block_out/pallas_call | solution.py:406
  233.1 5.5 collective-permute-start.28
  242.2 16.9 %block_back.2 = (bf16[576,768]{1,0:T(8,128)(2,1)}, bf16[576,3072]{1,0:T(8,128)(2,1)}, bf16[576,768]{1,0:T(8,128)(2,1)}, bf16[576,768]{1,0:T(8,128)(2,1)}, bf16[576,768]{1,0:T(8,128)(2,1)}, /*index=5*/f32[8,768]{1,0:T(8,128)}) custom-call(s32[2]{0:T(128)} %get-tuple-element.289.info_ref, bf16[576,768]{1,0:T(8,128)(2,1)} %get-tuple-element.350.gy_ref, ...), custom_call_target="tpu_custom_call" | custom-call | flops 280000000 | bytes 1000 | tf_op jit(solution)/shard_map/block_back/pallas_call | solution.py:489
  262.6 14.0 %mlp_grads.2 = (bf16[8,384,768]{2,1,0:T(8,128)(2,1)}, bf16[8,384,768]{2,1,0:T(8,128)(2,1)}) custom-call(s32[1]{0:T(128)} %bitcast.core_ref, bf16[576,768]{1,0:T(8,128)(2,1)S(1)} %copy-done.27, bf16[576,3072]{1,0:T(8,128)(2,1)S(1)} %copy-done.21, bf16[576,3072]{1,0:T(8,128)(2,1)} %get-tuple-element.367.hid_ref, bf16[576,768]{1,0:T(8,128)(2,1)S(1)} %copy-done.29), custom_call_target="tpu_custom_call" | custom-call | flops 300000000 | bytes 1000 | tf_op jit(solution)/shard_map/mlp_grads/pallas_call | solution.py:705
  276.9 18.2 %attn_bwd.4 = (bf16[576,384]{1,0:T(8,128)(2,1)}, bf16[2,576,384]{2,1,0:T(8,128)(2,1)}, bf16[2,576,384]{2,1,0:T(8,128)(2,1)}, f32[3,8,128]{2,1,0:T(8,128)}) custom-call(bf16[576,128]{1,0:T(8,128)(2,1)} %get-tuple-element.362.hot_ref, bf16[6,1152,576]{2,1,0:T(8,128)(2,1)} %get-tuple-element.363.w_ref, bf16[576,2304]{1,0:T(8,128)(2,1)} %copy-done.3, ...), custom_call_target="tpu_custom_call" | custom-call | flops 360000000 | bytes 1000 | tf_op jit(solution)/shard_map/attn_bwd/pallas_call | solution.py:227
  295.2 5.7 add.394
  301.2 18.2 %attn_bwd.5 = (bf16[576,384]{1,0:T(8,128)(2,1)}, bf16[2,576,384]{2,1,0:T(8,128)(2,1)}, bf16[2,576,384]{2,1,0:T(8,128)(2,1)}, f32[3,8,128]{2,1,0:T(8,128)}) custom-call(bf16[576,128]{1,0:T(8,128)(2,1)} %get-tuple-element.362.hot_ref, bf16[6,1152,576]{2,1,0:T(8,128)(2,1)} %get-tuple-element.381.w_ref, bf16[576,2304]{1,0:T(8,128)(2,1)} %copy-done.3, ...), custom_call_target="tpu_custom_call" | custom-call | flops 360000000 | bytes 1000 | tf_op jit(solution)/shard_map/attn_bwd/pallas_call | solution.py:227
  325.3 6.7 %project_back.2 = (bf16[576,2304]{1,0:T(8,128)(2,1)}, bf16[576,768]{1,0:T(8,128)(2,1)S(1)}, f32[8,768]{1,0:T(8,128)S(1)}) custom-call(s32[2]{0:T(128)S(1)} %copy-done.53, bf16[576,768]{1,0:T(8,128)(2,1)S(1)} %copy-done.22, bf16[576,768]{1,0:T(8,128)(2,1)S(1)} %copy-done.14, f32[3,768]{1,0:T(4,128)S(1)} %copy-done.45, bf16[576,384]{1,0:T(8,128)(2,1)S(1)} %copy-done.40, ...), custom_call_target="tpu_custom_call" | custom-call | flops 140000000 | bytes 1000 | tf_op jit(solution)/shard_map/project_back/pallas_call | solution.py:535
  332.0 7.3 %att_grads.2 = (bf16[8,192,768]{2,1,0:T(8,128)(2,1)S(1)}, bf16[8,192,768]{2,1,0:T(8,128)(2,1)}) custom-call(s32[1]{0:T(128)} %bitcast.core_ref, bf16[576,768]{1,0:T(8,128)(2,1)S(1)} %get-tuple-element.397.n_ref, bf16[576,2304]{1,0:T(8,128)(2,1)} %get-tuple-element.398.dproj_ref, bf16[576,384]{1,0:T(8,128)(2,1)S(1)} %copy-done.17, ...), custom_call_target="tpu_custom_call" | custom-call | flops 180000000 | bytes 1000 | tf_op jit(solution)/shard_map/att_grads/pallas_call | solution.py:705
  341.1 3.8 collective-permute-start.35
  346.5 3.1 collective-permute-start.37
  349.6 17.5 %block_back.3 = (bf16[576,768]{1,0:T(8,128)(2,1)}, bf16[576,3072]{1,0:T(8,128)(2,1)}, bf16[576,768]{1,0:T(8,128)(2,1)}, bf16[576,768]{1,0:T(8,128)(2,1)}, bf16[576,768]{1,0:T(8,128)(2,1)}, /*index=5*/f32[8,768]{1,0:T(8,128)}) custom-call(s32[2]{0:T(128)} %copy-done.50, bf16[576,768]{1,0:T(8,128)(2,1)} %copy-done.19, ...), custom_call_target="tpu_custom_call" | custom-call | flops 280000000 | bytes 1000 | tf_op jit(solution)/shard_map/block_back/pallas_call | solution.py:489
  368.0 3.8 add.395
  374.5 13.8 %mlp_grads.3 = (bf16[8,384,768]{2,1,0:T(8,128)(2,1)}, bf16[8,384,768]{2,1,0:T(8,128)(2,1)}) custom-call(s32[1]{0:T(128)} %bitcast.core_ref, bf16[576,768]{1,0:T(8,128)(2,1)S(1)} %copy-done.26, bf16[576,3072]{1,0:T(8,128)(2,1)S(1)} %copy-done.20, bf16[576,3072]{1,0:T(8,128)(2,1)} %get-tuple-element.419.hid_ref, bf16[576,768]{1,0:T(8,128)(2,1)S(1)} %copy-done.28), custom_call_target="tpu_custom_call" | custom-call | flops 300000000 | bytes 1000 | tf_op jit(solution)/shard_map/mlp_grads/pallas_call | solution.py:705
  393.2 17.8 %attn_bwd.6 = (bf16[576,384]{1,0:T(8,128)(2,1)}, bf16[2,576,384]{2,1,0:T(8,128)(2,1)}, bf16[2,576,384]{2,1,0:T(8,128)(2,1)}, f32[3,8,128]{2,1,0:T(8,128)}) custom-call(bf16[576,128]{1,0:T(8,128)(2,1)} %get-tuple-element.362.hot_ref, bf16[6,1152,576]{2,1,0:T(8,128)(2,1)} %get-tuple-element.413.w_ref, bf16[576,2304]{1,0:T(8,128)(2,1)} %copy-done.2, ...), custom_call_target="tpu_custom_call" | custom-call | flops 360000000 | bytes 1000 | tf_op jit(solution)/shard_map/attn_bwd/pallas_call | solution.py:227
  411.1 5.8 add.396
  417.0 3.0 collective-permute-start.42
  423.9 17.8 %attn_bwd.7 = (bf16[576,384]{1,0:T(8,128)(2,1)}, bf16[2,576,384]{2,1,0:T(8,128)(2,1)}, bf16[2,576,384]{2,1,0:T(8,128)(2,1)}, f32[3,8,128]{2,1,0:T(8,128)}) custom-call(bf16[576,128]{1,0:T(8,128)(2,1)} %get-tuple-element.362.hot_ref, bf16[6,1152,576]{2,1,0:T(8,128)(2,1)} %get-tuple-element.433.w_ref, bf16[576,2304]{1,0:T(8,128)(2,1)} %copy-done.2, ...), custom_call_target="tpu_custom_call" | custom-call | flops 360000000 | bytes 1000 | tf_op jit(solution)/shard_map/attn_bwd/pallas_call | solution.py:227
  441.8 4.2 collective-permute-done.43
  456.2 7.6 %project_back.3 = (bf16[576,2304]{1,0:T(8,128)(2,1)}, bf16[576,768]{1,0:T(8,128)(2,1)}, f32[8,768]{1,0:T(8,128)S(1)}) custom-call(s32[2]{0:T(128)S(1)} %copy-done.51, bf16[576,768]{1,0:T(8,128)(2,1)S(1)} %copy-done.23, bf16[576,768]{1,0:T(8,128)(2,1)S(1)} %copy-done.12, f32[3,768]{1,0:T(4,128)S(1)} %copy-done.43, bf16[576,384]{1,0:T(8,128)(2,1)S(1)} %copy-done.38, ...), custom_call_target="tpu_custom_call" | custom-call | flops 140000000 | bytes 1000 | tf_op jit(solution)/shard_map/project_back/pallas_call | solution.py:535
  463.8 7.2 %collective-permute-done.48 = bf16[2,2,192,256]{3,2,0,1:T(8,128)(2,1)S(1)} collective-permute-done((bf16[2,2,192,256]{3,2,0,1:T(8,128)(2,1)S(1)}, bf16[2,2,192,256]{3,2,0,1:T(8,128)(2,1)S(1)}, u32[]{:S(2)}, u32[]{:S(2)}) %collective-permute-start.48) | collective-permute-done | bytes 393248 | tf_op jit(solution)/shard_map/ppermute | solution.py:757
  476.2 7.0 %att_grads.3 = (bf16[8,192,768]{2,1,0:T(8,128)(2,1)S(1)}, bf16[8,192,768]{2,1,0:T(8,128)(2,1)}) custom-call(s32[1]{0:T(128)} %bitcast.core_ref, bf16[576,768]{1,0:T(8,128)(2,1)S(1)} %copy-done.31, bf16[576,2304]{1,0:T(8,128)(2,1)} %get-tuple-element.465.dproj_ref, bf16[576,384]{1,0:T(8,128)(2,1)S(1)} %copy-done.15, bf16[576,384]{1,0:T(8,128)(2,1)S(1)} %copy-done.16, ...), custom_call_target="tpu_custom_call" | custom-call | flops 180000000 | bytes 1000 | tf_op jit(solution)/shard_map/att_grads/pallas_call | solution.py:705
  489.3 3.7 add.412
  493.3 3.0 collective-permute-start.56
  502.1 5.9 maximum_select_fusion
  516.2 7.3 %collective-permute-done.58 = bf16[288,768]{1,0:T(8,128)(2,1)S(1)} collective-permute-done((bf16[288,768]{1,0:T(8,128)(2,1)S(1)}, bf16[288,768]{1,0:T(8,128)(2,1)S(1)}, u32[]{:S(2)}, u32[]{:S(2)}) %collective-permute-start.58) | collective-permute-done | bytes 442400 | tf_op jit(solution)/shard_map/ppermute | solution.py:719
  523.5 15.9 %collective-permute-done.59 = bf16[192,768]{1,0:T(8,128)(2,1)S(1)} collective-permute-done((bf16[192,768]{1,0:T(8,128)(2,1)S(1)}, bf16[192,768]{1,0:T(8,128)(2,1)S(1)}, u32[]{:S(2)}, u32[]{:S(2)}) %collective-permute-start.59) | collective-permute-done | bytes 294944 | tf_op jit(solution)/shard_map/ppermute | solution.py:757
  547.4 5.3 collective-permute-done.66
  555.5 3.7 collective-permute-start.71
  561.1 8.8 %select_select_fusion = f32[4,576,768]{2,1,0:T(8,128)} fusion(bf16[1,576,768]{2,1,0:T(8,128)(2,1)} %bitcast.75, bf16[1,576,768]{2,1,0:T(8,128)(2,1)} %bitcast.74, bf16[1,576,768]{2,1,0:T(8,128)(2,1)} %bitcast.73, bf16[1,576,768]{2,1,0:T(8,128)(2,1)} %bitcast.72, bf16[1,576,768]{2,1,0:T(8,128)(2,1)S(1)} %bitcast.224, bf16[1,576,768]{2,1,0:T(8,128)(2,1)S(1)} %bitcast.225, ...), kind=kLoop, calls=%fused_computation | loop fusion | flops 33619968 | bytes 21233668 | tf_op jit(solution)/shard_map/jit(_where)/select_n | solution.py:817
  572.2 4.1 reduce-scatter.8.cloned.1.call-done
  584.7 3.1 collective-permute-done.72
  (498 shorter events, 166.7 us)
Async XLA Ops:
  7.2 403.9 %reduce-scatter.4.cloned.1.call-start = ((), (), s32[]{:S(2)}) async-start(), calls=%async_computation.3 | async-start | bytes 5308416 | tf_op jit(solution)/shard_map/reduce_scatter | solution.py:780
  8.0 31.7 %collective-permute-start.4 = (f32[3,768]{1,0:T(4,128)S(1)}, f32[3,768]{1,0:T(4,128)S(1)}, u32[]{:S(2)}, u32[]{:S(2)}) collective-permute-start(f32[3,768]{1,0:T(4,128)S(1)} %pad_maximum_fusion.9), channel_id=1, source_target_pairs={{0,3},{1,2},{2,1},{3,0},{4,7},{5,6},{6,5},{7,4},{8,11},{9,10},{10,... | collective-permute-start | bytes 27656 | tf_op jit(solution)/shard_map/ppermute | solution.py:719
  10.4 32.3 %collective-permute-start.3 = (f32[3,768]{1,0:T(4,128)S(1)}, f32[3,768]{1,0:T(4,128)S(1)}, u32[]{:S(2)}, u32[]{:S(2)}) collective-permute-start(f32[3,768]{1,0:T(4,128)S(1)} %pad_maximum_fusion.9), channel_id=1, source_target_pairs={{0,2},{1,3},{2,0},{3,1},{4,6},{5,7},{6,4},{7,5},{8,10},{9,11},{10,... | collective-permute-start | bytes 27656 | tf_op jit(solution)/shard_map/ppermute | solution.py:719
  11.1 52.1 %collective-permute-start.5 = (bf16[768,3072]{1,0:T(8,128)(2,1)}, bf16[768,3072]{1,0:T(8,128)(2,1)}, u32[]{:S(2)}, u32[]{:S(2)}) collective-permute-start(bf16[768,3072]{1,0:T(8,128)(2,1)} %bitcast.178), channel_id=1, source_target_pairs={{0,1},{1,0},{2,3},{3,2},{4,5},{5,4},{6,7},{7,6},{8,9},{9,8},{10,11... | collective-permute-start | bytes 14155784 | tf_op jit(solution)/shard_map/ppermute | solution.py:719
  14.6 28.9 %collective-permute-start = (bf16[384,2304]{1,0:T(8,128)(2,1)}, bf16[384,2304]{1,0:T(8,128)(2,1)}, u32[]{:S(2)}, u32[]{:S(2)}) collective-permute-start(bf16[384,2304]{1,0:T(8,128)(2,1)} %get-tuple-element.564), channel_id=1, source_target_pairs={{0,2},{2,0},{4,6},{6,4},{8,10},{10,8},{12,14},{14,12},{16,18},{18,... | collective-permute-start | bytes 5308424 | tf_op jit(solution)/shard_map/ppermute | solution.py:719
  18.2 39.2 %collective-permute-start.1 = (bf16[384,2304]{1,0:T(8,128)(2,1)S(1)}, bf16[384,2304]{1,0:T(8,128)(2,1)}, u32[]{:S(2)}, u32[]{:S(2)}) collective-permute-start(bf16[384,2304]{1,0:T(8,128)(2,1)S(1)} %get-tuple-element.563), channel_id=1, source_target_pairs={{0,3},{2,1},{4,7},{6,5},{8,11},{10,9},{12,15},{14,13},{16,19},{18,... | collective-permute-start | bytes 5308424 | tf_op jit(solution)/shard_map/ppermute | solution.py:719
  70.2 18.5 %collective-permute-start.7 = (bf16[576,1536]{1,0:T(8,128)(2,1)S(1)}, bf16[576,1536]{1,0:T(8,128)(2,1)S(1)}, u32[]{:S(2)}, u32[]{:S(2)}) collective-permute-start(bf16[576,1536]{1,0:T(8,128)(2,1)S(1)} %slice.241), channel_id=1, source_target_pairs={{0,1},{1,0},{2,3},{3,2},{4,5},{5,4},{6,7},{7,6},{8,9},{9,8},{10,11... | collective-permute-start | bytes 5308424 | tf_op jit(solution)/shard_map/ppermute | solution.py:719
  71.5 17.2 %collective-permute-start.8 = (bf16[96,3072]{1,0:T(8,128)(2,1)}, bf16[96,3072]{1,0:T(8,128)(2,1)S(1)}, u32[]{:S(2)}, u32[]{:S(2)}) collective-permute-start(bf16[96,3072]{1,0:T(8,128)(2,1)} %get-tuple-element.296), channel_id=1, source_target_pairs={{1,2},{3,0},{5,6},{7,4},{9,10},{11,8},{13,14},{15,12},{17,18},{19,... | collective-permute-start | bytes 1769480 | tf_op jit(solution)/shard_map/ppermute | solution.py:719
  73.5 35.1 %collective-permute-start.12 = (bf16[384,768]{1,0:T(8,128)(2,1)S(1)}, bf16[384,768]{1,0:T(8,128)(2,1)S(1)}, u32[]{:S(2)}, u32[]{:S(2)}) collective-permute-start(bf16[384,768]{1,0:T(8,128)(2,1)S(1)} %copy-done.95), channel_id=1, source_target_pairs={{0,2},{1,3},{2,0},{3,1},{4,6},{5,7},{6,4},{7,5},{8,10},{9,11},{10,... | collective-permute-start | bytes 1769480 | tf_op jit(solution)/shard_map/ppermute | solution.py:719
  88.9 19.8 %collective-permute-start.10 = (bf16[96,3072]{1,0:T(8,128)(2,1)S(1)}, bf16[96,3072]{1,0:T(8,128)(2,1)S(1)}, u32[]{:S(2)}, u32[]{:S(2)}) collective-permute-start(bf16[96,3072]{1,0:T(8,128)(2,1)S(1)} %broadcast_select_fusion.8.mine), channel_id=1, source_target_pairs={{0,4},{4,0},{8,12},{12,8},{16,20},{20,16},{24,28},{28,24},{1,5},{5... | collective-permute-start | bytes 1769480 | tf_op jit(solution)/shard_map/ppermute | solution.py:566
  90.7 18.0 %collective-permute-start.11 = (bf16[96,3072]{1,0:T(8,128)(2,1)S(1)}, bf16[96,3072]{1,0:T(8,128)(2,1)S(1)}, u32[]{:S(2)}, u32[]{:S(2)}) collective-permute-start(bf16[96,3072]{1,0:T(8,128)(2,1)S(1)} %broadcast_select_fusion.8.mine), channel_id=1, source_target_pairs={{0,8},{4,12},{8,0},{12,4},{16,24},{20,28},{24,16},{28,20},{1,9},{5... | collective-permute-start | bytes 1769480 | tf_op jit(solution)/shard_map/ppermute | solution.py:566
  92.2 37.3 %collective-permute-start.17 = (bf16[768,768]{1,0:T(8,128)(2,1)}, bf16[768,768]{1,0:T(8,128)(2,1)S(1)}, u32[]{:S(2)}, u32[]{:S(2)}) collective-permute-start(bf16[768,768]{1,0:T(8,128)(2,1)} %slice.306), channel_id=1, source_target_pairs={{0,2},{2,0},{4,6},{6,4},{8,10},{10,8},{12,14},{14,12},{16,18},{18,... | collective-permute-start | bytes 3538952 | tf_op jit(solution)/shard_map/ppermute | solution.py:719
  108.6 20.9 %collective-permute-start.15 = (bf16[384,768]{1,0:T(8,128)(2,1)S(1)}, bf16[384,768]{1,0:T(8,128)(2,1)S(1)}, u32[]{:S(2)}, u32[]{:S(2)}) collective-permute-start(bf16[384,768]{1,0:T(8,128)(2,1)S(1)} %collective-permute-done.12.mine), channel_id=1, source_target_pairs={{0,4},{4,0},{8,12},{12,8},{16,20},{20,16},{24,28},{28,24},{1,5},{5... | collective-permute-start | bytes 1769480 | tf_op jit(solution)/shard_map/ppermute | solution.py:566
  109.2 20.3 %collective-permute-start.16 = (bf16[384,768]{1,0:T(8,128)(2,1)S(1)}, bf16[384,768]{1,0:T(8,128)(2,1)S(1)}, u32[]{:S(2)}, u32[]{:S(2)}) collective-permute-start(bf16[384,768]{1,0:T(8,128)(2,1)S(1)} %collective-permute-done.12.mine), channel_id=1, source_target_pairs={{0,8},{4,12},{8,0},{12,4},{16,24},{20,28},{24,16},{28,20},{1,9},{5... | collective-permute-start | bytes 1769480 | tf_op jit(solution)/shard_map/ppermute | solution.py:566
  109.7 18.1 %collective-permute-start.13 = (bf16[48,3072]{1,0:T(8,128)(2,1)S(1)}, bf16[48,3072]{1,0:T(8,128)(2,1)S(1)}, u32[]{:S(2)}, u32[]{:S(2)}) collective-permute-start(bf16[48,3072]{1,0:T(8,128)(2,1)S(1)} %slice.242), channel_id=1, source_target_pairs={{0,4},{4,0},{8,12},{12,8},{16,20},{20,16},{24,28},{28,24},{1,5},{5... | collective-permute-start | bytes 884744 | tf_op jit(solution)/shard_map/ppermute | solution.py:566
  111.3 17.5 %collective-permute-start.14 = (bf16[48,3072]{1,0:T(8,128)(2,1)S(1)}, bf16[48,3072]{1,0:T(8,128)(2,1)S(1)}, u32[]{:S(2)}, u32[]{:S(2)}) collective-permute-start(bf16[48,3072]{1,0:T(8,128)(2,1)S(1)} %slice.243), channel_id=1, source_target_pairs={{0,8},{4,12},{8,0},{12,4},{16,24},{20,28},{24,16},{28,20},{1,9},{5... | collective-permute-start | bytes 884744 | tf_op jit(solution)/shard_map/ppermute | solution.py:566
  134.1 18.5 %collective-permute-start.20 = (bf16[1536,768]{1,0:T(8,128)(2,1)}, bf16[1536,768]{1,0:T(8,128)(2,1)S(1)}, u32[]{:S(2)}, u32[]{:S(2)}) collective-permute-start(bf16[1536,768]{1,0:T(8,128)(2,1)} %bitcast.192), channel_id=1, source_target_pairs={{0,1},{1,0},{2,3},{3,2},{4,5},{5,4},{6,7},{7,6},{8,9},{9,8},{10,11... | collective-permute-start | bytes 7077896 | tf_op jit(solution)/shard_map/ppermute | solution.py:719
  182.4 31.7 %collective-permute-start.25 = (bf16[576,768]{1,0:T(8,128)(2,1)S(1)}, bf16[576,768]{1,0:T(8,128)(2,1)S(1)}, u32[]{:S(2)}, u32[]{:S(2)}) collective-permute-start(bf16[576,768]{1,0:T(8,128)(2,1)S(1)} %get-tuple-element.499), channel_id=1, source_target_pairs={{2,0},{3,1},{6,4},{7,5},{10,8},{11,9},{14,12},{15,13},{18,16},{19,... | collective-permute-start | bytes 2654216 | tf_op jit(solution)/shard_map/ppermute | solution.py:719
  183.7 46.5 %collective-permute-start.26 = (bf16[576,768]{1,0:T(8,128)(2,1)}, bf16[576,768]{1,0:T(8,128)(2,1)S(1)}, u32[]{:S(2)}, u32[]{:S(2)}) collective-permute-start(bf16[576,768]{1,0:T(8,128)(2,1)} %get-tuple-element.569), channel_id=1, source_target_pairs={{0,1},{1,0},{4,5},{5,4},{8,9},{9,8},{12,13},{13,12},{16,17},{17,16... | collective-permute-start | bytes 2654216 | tf_op jit(solution)/shard_map/ppermute | solution.py:719
  185.8 44.5 %collective-permute-start.27 = (bf16[576,768]{1,0:T(8,128)(2,1)}, bf16[576,768]{1,0:T(8,128)(2,1)}, u32[]{:S(2)}, u32[]{:S(2)}) collective-permute-start(bf16[576,768]{1,0:T(8,128)(2,1)} %get-tuple-element.569), channel_id=1, source_target_pairs={{3,0},{2,1},{7,4},{6,5},{11,8},{10,9},{15,12},{14,13},{19,16},{18,... | collective-permute-start | bytes 2654216 | tf_op jit(solution)/shard_map/ppermute | solution.py:719
  233.1 26.1 %collective-permute-start.28 = (bf16[576,768]{1,0:T(8,128)(2,1)S(1)}, bf16[576,768]{1,0:T(8,128)(2,1)S(1)}, u32[]{:S(2)}, u32[]{:S(2)}) collective-permute-start(bf16[576,768]{1,0:T(8,128)(2,1)S(1)} %get-tuple-element.509), channel_id=1, source_target_pairs={{0,2},{1,3},{4,6},{5,7},{8,10},{9,11},{12,14},{13,15},{16,18},{17,... | collective-permute-start | bytes 2654216 | tf_op jit(solution)/shard_map/ppermute | solution.py:719
  238.6 38.1 %collective-permute-start.29 = (bf16[576,768]{1,0:T(8,128)(2,1)}, bf16[576,768]{1,0:T(8,128)(2,1)S(1)}, u32[]{:S(2)}, u32[]{:S(2)}) collective-permute-start(bf16[576,768]{1,0:T(8,128)(2,1)} %get-tuple-element.567), channel_id=1, source_target_pairs={{2,3},{3,2},{6,7},{7,6},{10,11},{11,10},{14,15},{15,14},{18,19},{1... | collective-permute-start | bytes 2654216 | tf_op jit(solution)/shard_map/ppermute | solution.py:719
  239.4 37.3 %collective-permute-start.30 = (bf16[576,768]{1,0:T(8,128)(2,1)}, bf16[576,768]{1,0:T(8,128)(2,1)S(1)}, u32[]{:S(2)}, u32[]{:S(2)}) collective-permute-start(bf16[576,768]{1,0:T(8,128)(2,1)} %get-tuple-element.567), channel_id=1, source_target_pairs={{1,2},{0,3},{5,6},{4,7},{9,10},{8,11},{13,14},{12,15},{17,18},{16,... | collective-permute-start | bytes 2654216 | tf_op jit(solution)/shard_map/ppermute | solution.py:719
  276.8 18.3 %collective-permute-start.31 = (bf16[8,384,768]{2,1,0:T(8,128)(2,1)}, bf16[8,384,768]{2,1,0:T(8,128)(2,1)}, u32[]{:S(2)}, u32[]{:S(2)}) collective-permute-start(bf16[8,384,768]{2,1,0:T(8,128)(2,1)} %get-tuple-element.379), channel_id=1, source_target_pairs={{0,1},{1,0},{2,3},{3,2},{4,5},{5,4},{6,7},{7,6},{8,9},{9,8},{10,11... | collective-permute-start | bytes 14155784 | tf_op jit(solution)/shard_map/ppermute | solution.py:719
  300.9 182.3 %reduce-scatter.6.cloned.1.call-start = ((), (), s32[]{:S(2)}) async-start(), calls=%async_computation.4 | async-start | bytes 2654208 | tf_op jit(solution)/shard_map/reduce_scatter | solution.py:780
  301.0 18.4 %collective-permute-start.32 = (bf16[2,576,384]{2,1,0:T(8,128)(2,1)}, bf16[2,576,384]{2,1,0:T(8,128)(2,1)S(1)}, u32[]{:S(2)}, u32[]{:S(2)}) collective-permute-start(bf16[2,576,384]{2,1,0:T(8,128)(2,1)} %get-tuple-element.383), channel_id=1, source_target_pairs={{0,1},{1,0},{2,3},{3,2},{4,5},{5,4},{6,7},{7,6},{8,9},{9,8},{10,11... | collective-permute-start | bytes 2654216 | tf_op jit(solution)/shard_map/ppermute | solution.py:719
  339.3 27.8 %collective-permute-start.34 = (bf16[8,192,768]{2,1,0:T(8,128)(2,1)}, bf16[8,192,768]{2,1,0:T(8,128)(2,1)}, u32[]{:S(2)}, u32[]{:S(2)}) collective-permute-start(bf16[8,192,768]{2,1,0:T(8,128)(2,1)} %get-tuple-element.411), channel_id=1, source_target_pairs={{0,1},{1,0},{2,3},{3,2},{4,5},{5,4},{6,7},{7,6},{8,9},{9,8},{10,11... | collective-permute-start | bytes 7077896 | tf_op jit(solution)/shard_map/ppermute | solution.py:719
  341.1 26.1 %collective-permute-start.35 = (bf16[576,768]{1,0:T(8,128)(2,1)S(1)}, bf16[576,768]{1,0:T(8,128)(2,1)S(1)}, u32[]{:S(2)}, u32[]{:S(2)}) collective-permute-start(bf16[576,768]{1,0:T(8,128)(2,1)S(1)} %get-tuple-element.547), channel_id=1, source_target_pairs={{0,2},{1,3},{4,6},{5,7},{8,10},{9,11},{12,14},{13,15},{16,18},{17,... | collective-permute-start | bytes 2654216 | tf_op jit(solution)/shard_map/ppermute | solution.py:719
  344.9 43.4 %collective-permute-start.36 = (bf16[576,768]{1,0:T(8,128)(2,1)}, bf16[576,768]{1,0:T(8,128)(2,1)}, u32[]{:S(2)}, u32[]{:S(2)}) collective-permute-start(bf16[576,768]{1,0:T(8,128)(2,1)} %get-tuple-element.565), channel_id=1, source_target_pairs={{2,3},{3,2},{6,7},{7,6},{10,11},{11,10},{14,15},{15,14},{18,19},{1... | collective-permute-start | bytes 2654216 | tf_op jit(solution)/shard_map/ppermute | solution.py:719
  346.5 41.8 %collective-permute-start.37 = (bf16[576,768]{1,0:T(8,128)(2,1)}, bf16[576,768]{1,0:T(8,128)(2,1)}, u32[]{:S(2)}, u32[]{:S(2)}) collective-permute-start(bf16[576,768]{1,0:T(8,128)(2,1)} %get-tuple-element.565), channel_id=1, source_target_pairs={{1,2},{0,3},{5,6},{4,7},{9,10},{8,11},{13,14},{12,15},{17,18},{16,... | collective-permute-start | bytes 2654216 | tf_op jit(solution)/shard_map/ppermute | solution.py:719
  388.3 22.7 %collective-permute-start.38 = (bf16[8,384,768]{2,1,0:T(8,128)(2,1)}, bf16[8,384,768]{2,1,0:T(8,128)(2,1)}, u32[]{:S(2)}, u32[]{:S(2)}) collective-permute-start(bf16[8,384,768]{2,1,0:T(8,128)(2,1)} %get-tuple-element.431), channel_id=1, source_target_pairs={{0,1},{1,0},{2,3},{3,2},{4,5},{5,4},{6,7},{7,6},{8,9},{9,8},{10,11... | collective-permute-start | bytes 14155784 | tf_op jit(solution)/shard_map/ppermute | solution.py:719
  388.5 187.8 %reduce-scatter.8.cloned.1.call-start = ((), (), s32[]{:S(2)}) async-start(), calls=%async_computation.5 | async-start | bytes 2654208 | tf_op jit(solution)/shard_map/reduce_scatter | solution.py:780
  389.5 21.5 %collective-permute-start.39 = (bf16[576,768]{1,0:T(8,128)(2,1)S(1)}, bf16[576,768]{1,0:T(8,128)(2,1)S(1)}, u32[]{:S(2)}, u32[]{:S(2)}) collective-permute-start(bf16[576,768]{1,0:T(8,128)(2,1)S(1)} %copy-done.23), channel_id=1, source_target_pairs={{0,1},{4,5},{8,9},{12,13},{16,17},{20,21},{24,25},{28,29}} | collective-permute-start | bytes 2654216 | tf_op jit(solution)/shard_map/ppermute | solution.py:719
  391.5 19.5 %collective-permute-start.40 = (bf16[576,768]{1,0:T(8,128)(2,1)S(1)}, bf16[576,768]{1,0:T(8,128)(2,1)S(1)}, u32[]{:S(2)}, u32[]{:S(2)}) collective-permute-start(bf16[576,768]{1,0:T(8,128)(2,1)S(1)} %copy-done.23), channel_id=1, source_target_pairs={{3,1},{7,5},{11,9},{15,13},{19,17},{23,21},{27,25},{31,29}} | collective-permute-start | bytes 2654216 | tf_op jit(solution)/shard_map/ppermute | solution.py:719
  392.2 18.8 %collective-permute-start.41 = (bf16[576,768]{1,0:T(8,128)(2,1)S(1)}, bf16[576,768]{1,0:T(8,128)(2,1)S(1)}, u32[]{:S(2)}, u32[]{:S(2)}) collective-permute-start(bf16[576,768]{1,0:T(8,128)(2,1)S(1)} %copy-done.23), channel_id=1, source_target_pairs={{2,1},{6,5},{10,9},{14,13},{18,17},{22,21},{26,25},{30,29}} | collective-permute-start | bytes 2654216 | tf_op jit(solution)/shard_map/ppermute | solution.py:719
  417.0 30.2 %collective-permute-start.42 = (bf16[2,576,384]{2,1,0:T(8,128)(2,1)}, bf16[2,576,384]{2,1,0:T(8,128)(2,1)S(1)}, u32[]{:S(2)}, u32[]{:S(2)}) collective-permute-start(bf16[2,576,384]{2,1,0:T(8,128)(2,1)} %get-tuple-element.435), channel_id=1, source_target_pairs={{0,1},{1,0},{2,3},{3,2},{4,5},{5,4},{6,7},{7,6},{8,9},{9,8},{10,11... | collective-permute-start | bytes 2654216 | tf_op jit(solution)/shard_map/ppermute | solution.py:719
  420.7 25.3 %collective-permute-start.43 = (bf16[2,2,2,192,256]{4,3,2,1,0:T(8,128)(2,1)S(1)}, bf16[2,2,2,192,256]{4,3,2,1,0:T(8,128)(2,1)}, u32[]{:S(2)}, u32[]{:S(2)}) collective-permute-start(bf16[2,2,2,192,256]{4,3,2,1,0:T(8,128)(2,1)S(1)} %get-tuple-element.576), channel_id=1, source_target_pairs={{0,4},{4,0},{8,12},{12,8},{16,20},{20,16},{24,28},{28,24},{1,5},{5... | collective-permute-start | bytes 2359304 | tf_op jit(solution)/shard_map/ppermute | solution.py:757
  422.5 23.5 %collective-permute-start.44 = (bf16[2,2,2,192,256]{4,3,2,1,0:T(8,128)(2,1)}, bf16[2,2,2,192,256]{4,3,2,1,0:T(8,128)(2,1)S(1)}, u32[]{:S(2)}, u32[]{:S(2)}) collective-permute-start(bf16[2,2,2,192,256]{4,3,2,1,0:T(8,128)(2,1)} %get-tuple-element.574), channel_id=1, source_target_pairs={{0,2},{1,3},{2,0},{3,1},{4,6},{5,7},{6,4},{7,5},{8,10},{9,11},{10,... | collective-permute-start | bytes 2359304 | tf_op jit(solution)/shard_map/ppermute | solution.py:757
  423.5 23.6 %collective-permute-start.45 = (bf16[2,2,2,192,256]{4,3,2,1,0:T(8,128)(2,1)}, bf16[2,2,2,192,256]{4,3,2,1,0:T(8,128)(2,1)S(1)}, u32[]{:S(2)}, u32[]{:S(2)}) collective-permute-start(bf16[2,2,2,192,256]{4,3,2,1,0:T(8,128)(2,1)} %get-tuple-element.572), channel_id=1, source_target_pairs={{0,8},{4,12},{8,0},{12,4},{16,24},{20,28},{24,16},{28,20},{1,9},{5... | collective-permute-start | bytes 2359304 | tf_op jit(solution)/shard_map/ppermute | solution.py:757
  452.8 18.2 %collective-permute-start.48 = (bf16[2,2,192,256]{3,2,0,1:T(8,128)(2,1)S(1)}, bf16[2,2,192,256]{3,2,0,1:T(8,128)(2,1)S(1)}, u32[]{:S(2)}, u32[]{:S(2)}) collective-permute-start(bf16[2,2,192,256]{3,2,0,1:T(8,128)(2,1)S(1)} %bitcast.229), channel_id=1, source_target_pairs={{0,8},{4,12},{8,0},{12,4},{16,24},{20,28},{24,16},{28,20},{1,9},{5... | collective-permute-start | bytes 1179656 | tf_op jit(solution)/shard_map/ppermute | solution.py:757
  453.7 17.4 %collective-permute-start.49 = (bf16[2,2,192,256]{3,2,0,1:T(8,128)(2,1)S(1)}, bf16[2,2,192,256]{3,2,0,1:T(8,128)(2,1)S(1)}, u32[]{:S(2)}, u32[]{:S(2)}) collective-permute-start(bf16[2,2,192,256]{3,2,0,1:T(8,128)(2,1)S(1)} %bitcast.230), channel_id=1, source_target_pairs={{0,4},{4,0},{8,12},{12,8},{16,20},{20,16},{24,28},{28,24},{1,5},{5... | collective-permute-start | bytes 1179656 | tf_op jit(solution)/shard_map/ppermute | solution.py:757
  485.6 37.9 %collective-permute-start.60 = (bf16[576,768]{1,0:T(8,128)(2,1)}, bf16[576,768]{1,0:T(8,128)(2,1)}, u32[]{:S(2)}, u32[]{:S(2)}) collective-permute-start(bf16[576,768]{1,0:T(8,128)(2,1)} %get-tuple-element.532), channel_id=1, source_target_pairs={{2,0},{6,4},{10,8},{14,12},{18,16},{22,20},{26,24},{30,28}} | collective-permute-start | bytes 2654216 | tf_op jit(solution)/shard_map/ppermute | solution.py:719
  487.0 36.5 %collective-permute-start.61 = (bf16[576,768]{1,0:T(8,128)(2,1)}, bf16[576,768]{1,0:T(8,128)(2,1)}, u32[]{:S(2)}, u32[]{:S(2)}) collective-permute-start(bf16[576,768]{1,0:T(8,128)(2,1)} %get-tuple-element.532), channel_id=1, source_target_pairs={{3,0},{7,4},{11,8},{15,12},{19,16},{23,20},{27,24},{31,28}} | collective-permute-start | bytes 2654216 | tf_op jit(solution)/shard_map/ppermute | solution.py:719
  493.3 17.5 %collective-permute-start.56 = (f32[12336]{0:T(1024)S(1)}, f32[12336]{0:T(1024)S(1)}, u32[]{:S(2)}, u32[]{:S(2)}) collective-permute-start(f32[12336]{0:T(1024)S(1)} %constant_dynamic-update-slice_fusion), channel_id=1, source_target_pairs={{0,2},{1,3},{2,0},{3,1},{4,6},{5,7},{6,4},{7,5},{8,10},{9,11},{10,... | collective-permute-start | bytes 148040 | tf_op jit(solution)/shard_map/ppermute | solution.py:719
  496.3 16.5 %collective-permute-start.57 = (f32[12336]{0:T(1024)S(1)}, f32[12336]{0:T(1024)}, u32[]{:S(2)}, u32[]{:S(2)}) collective-permute-start(f32[12336]{0:T(1024)S(1)} %constant_dynamic-update-slice_fusion), channel_id=1, source_target_pairs={{0,3},{1,2},{2,1},{3,0},{4,7},{5,6},{6,5},{7,4},{8,11},{9,10},{10,... | collective-permute-start | bytes 148040 | tf_op jit(solution)/shard_map/ppermute | solution.py:719
  496.3 19.0 %collective-permute-start.55 = (f32[12336]{0:T(1024)S(1)}, f32[12336]{0:T(1024)}, u32[]{:S(2)}, u32[]{:S(2)}) collective-permute-start(f32[12336]{0:T(1024)S(1)} %constant_dynamic-update-slice_fusion), channel_id=1, source_target_pairs={{0,1},{1,0},{2,3},{3,2},{4,5},{5,4},{6,7},{7,6},{8,9},{9,8},{10,11... | collective-permute-start | bytes 148040 | tf_op jit(solution)/shard_map/ppermute | solution.py:719
  512.8 26.7 %collective-permute-start.59 = (bf16[192,768]{1,0:T(8,128)(2,1)S(1)}, bf16[192,768]{1,0:T(8,128)(2,1)S(1)}, u32[]{:S(2)}, u32[]{:S(2)}) collective-permute-start(bf16[192,768]{1,0:T(8,128)(2,1)S(1)} %get-tuple-element.593), channel_id=1, source_target_pairs={{0,16},{4,20},{8,24},{12,28},{16,0},{20,4},{24,8},{28,12},{1,17},{... | collective-permute-start | bytes 884744 | tf_op jit(solution)/shard_map/ppermute | solution.py:757
  555.5 16.7 %collective-permute-start.71 = (bf16[192,768]{1,0:T(8,128)(2,1)S(1)}, bf16[192,768]{1,0:T(8,128)(2,1)S(1)}, u32[]{:S(2)}, u32[]{:S(2)}) collective-permute-start(bf16[192,768]{1,0:T(8,128)(2,1)S(1)} %get-tuple-element.592), channel_id=1, source_target_pairs={{1,2},{0,3},{5,6},{4,7},{9,10},{8,11},{13,14},{12,15},{17,18},{16,... | collective-permute-start | bytes 884744 | tf_op jit(solution)/shard_map/ppermute | solution.py:719
  (143 other events, 1335.2 us)
Sparse Core Ops, SparseCore 0:
  301.0 94.9 reduce-scatter.3
  399.5 75.5 reduce-scatter.5
  496.6 79.6 reduce-scatter.7

commit v5 on v4

--- a/solution.py
+++ b/solution.py
@@ -352,7 +352,7 @@
 def block_out_kernel(info_ref, x_ref, ctx_a, ctx_b, p0_ref, p1_ref, *refs):
     att, up, refs = refs[:4], refs[:2] + refs[4:6], refs[6:]
     down, refs = refs[:4], refs[4:]
-    b0_ref, x1_ref, n1_ref, slope_ref, hid_ref, b1_ref, x2_ref, wo_ref, wu_ref, wd_ref, slopes, hiddens, sems, out_sems = refs
+    b0_ref, x1_ref, n1_ref, slope_ref, hid_ref, b1_ref, x2_ref, mine_ref, other_ref, wo_ref, wu_ref, wd_ref, slopes, hiddens, sems, out_sems = refs
     width = x_ref.shape[1]
     start_first(info_ref, 0, pl.ds(3 * width, width), pl.ds(0, width), att, wo_ref, sems.at[0])
     for j in range(4):
@@ -386,7 +386,11 @@
             pltpu.make_async_copy(hiddens.at[j], hid_ref.at[:, at], out_sems.at[1, j]).start()
         total = total + dot(hiddens[j], wd_ref[at, :])
     b1_ref[...] = total.astype(BF)
-    x2_ref[...] = (x1 + p1_ref[2:3, :] * total).astype(BF)
+    x2 = (x1 + p1_ref[2:3, :] * total).astype(BF)
+    x2_ref[...] = x2
+    first = info_ref[1] == 0
+    mine_ref[...] = jnp.where(first, x1_ref[...], x2)
+    other_ref[...] = jnp.where(first, x2, x1_ref[...])
     if not EARLY:
         for j in range(4):
             at = pl.ds(j * width, width)
@@ -401,7 +405,7 @@
     rows, width = x.shape
     one = whole((rows, width))
     shape = lambda n: jax.ShapeDtypeStruct((rows, n), BF)
-    widths = [width, width, width, 4 * width, 4 * width, width, width]
+    widths = [width, width, width, 4 * width, 4 * width, width, width, width, width]
     refs = (*more_refs, *up_refs[2:], *down_refs)
     return pl.pallas_call(
         block_out_kernel,
@@ -875,8 +879,7 @@
     mine_up = (send(share[0], [(1, 2), (3, 0)]), send(share[1], [(1, 3), (3, 1)]))
     mine_half = swap(share_half, 2)
 
-    def shared(even, odd, layer):
-        mine, other = pick(core, even, odd), pick(core, odd, even)
+    def shared(mine, other, layer):
         inside = [(2 * layer, 2 * layer + 1), (2 * layer + 1, 2 * layer)]
         straight = [(p ^ 2, p) for p in (2 * layer, 2 * layer + 1)]
         across = [(p ^ 3, p) for p in (2 * layer, 2 * layer + 1)]
@@ -919,11 +922,11 @@
         else:
             part_b = tie(part_b, outs[0][2])
         context = (part_a[0], part_b[0])
-        b0, x1, n1, slope, hidden, b1, x2 = block_out(info, current, context, p0, p1, more_refs, up_refs, down_refs)
+        b0, x1, n1, slope, hidden, b1, x2, mine, other = block_out(info, current, context, p0, p1, more_refs, up_refs, down_refs)
         if layer == 1:
-            b0, x1, n1, slope, hidden, b1, x2 = tie((b0, x1, n1, slope, hidden, b1, x2), outs[0])
+            b0, x1, n1, slope, hidden, b1, x2, mine, other = tie((b0, x1, n1, slope, hidden, b1, x2, mine, other), outs[0])
         kept.append((current, normed, proj, partner, (part_a, part_b), b0, x1, n1, slope, hidden, b1))
-        outs[2 * layer] = outs[2 * layer + 1] = shared(x1, x2, layer)
+        outs[2 * layer] = outs[2 * layer + 1] = shared(mine, other, layer)
         current = x2
 
     tables, vecs, grads = {}, {}, {}
@@ -949,7 +952,7 @@
     d_proj, gx0, vec0 = project_back(info, gx1, x, p0, (dqa, dqb, mya, myb, gota, gotb), qkv_refs)
     keep, other = weight_grads(att_grads_kernel, core, dp_size, 9, normed, d_proj, [part[0] for part in outcome], db0)
     got = swap(other, 1)
-    grads[2] = grads[3] = shared(gx0, gx1, 1)
+    grads[2] = grads[3] = shared(pick(core, gx0, gx1), pick(core, gx1, gx0), 1)
     tables[1] = (ta, tb)
     vecs[3], vecs[2] = vec1[:3], jnp.concatenate([vec0[:2], vec1[3:4]])
 
@@ -976,10 +979,9 @@
     gotb = tie(gotb, given)
     d_proj, gx0, vec0 = project_back(info, gx1, x, p0, (dqa, dqb, mya, myb, gota, gotb), qkv_refs)
     d_proj, gx0, vec0, mlp_a = hold((d_proj, gx0, vec0, mlp_a), 3)
-    mlp_a, given = cube_step(mlp_a, 2)
-    grads[0] = to_one(tie(gx0, given), 0)
-    keep, other = weight_grads(att_grads_kernel, core, dp_size, 9, tie(normed, given), d_proj, [part[0] for part in outcome], db0)
-    keep, other, att_b, grads[0][1], mlp_a = hold((keep, other, att_b, grads[0][1], mlp_a), 4)
+    grads[0] = to_one(gx0, 0)
+    keep, other = weight_grads(att_grads_kernel, core, dp_size, 9, normed, d_proj, [part[0] for part in outcome], db0)
+    keep, other, att_b, grads[0][1] = together((keep, other, att_b, grads[0][1]))
     got = swap(other, 1)
     att_sum = keep + got
     att_a = line_start(att_sum)
@@ -989,24 +991,25 @@
     stack = lambda parts: jnp.stack([parts[s] for s in range(sections)])
     table_all = [jnp.concatenate(tables[layer])[:, :4].reshape(heads, 2, 128)[..., : 2 * SIDE_L + 1] for layer in range(layers)]
     small = jnp.concatenate([stack(vecs).reshape(-1), jnp.stack(table_all).reshape(-1)])
+    mlp_a, _ = cube_step(mlp_a, 2)
+    mlp_b, att_b = line_end(mlp_b, att_b)
+    section_out = collected(outs).reshape(1, micro_count, slot_rows, width)
+    small, section_out, mlp_b, att_b, grads[0], mlp_a = hold((small, section_out, mlp_b, att_b, grads[0], mlp_a), 5)
     mlp_a, _ = cube_end(mlp_a)
-    mlp_b, att_b = line_end(mlp_b, att_b)
     small = small_sum(small, 0)
-    section_out = collected(outs).reshape(1, micro_count, slot_rows, width)
-    small, section_out, mlp_b, att_b, mlp_a, grads[0] = together((small, section_out, mlp_b, att_b, mlp_a, grads[0]))
+    even = jnp.concatenate([att_b, mlp_b[: att_b.shape[0]]], axis=0)
+    own_b = pick(core, even, mlp_b)
+    got_b = by_sender(1, even, mlp_b, core, (1, 2, 3))
+    small, got_b, own_b, mlp_a = together((small, got_b, own_b, mlp_a))
     mlp_a = settled(*mlp_a)
     low, high = jnp.split(mlp_a, 2, axis=0)
     small = small_sum(small, 1)
     ups = [mlp_a, send(mlp_a, [(0, 1)])]
     downs = by_sender(0, low, high, core, (2, 3))
-    small, ups, downs, mlp_b, att_b = together((small, ups, downs, mlp_b, att_b))
-    small = small_sum(small, 2)
-    even = jnp.concatenate([att_b, mlp_b[: att_b.shape[0]]], axis=0)
-    own_b = pick(core, even, mlp_b)
-    got_b = by_sender(1, even, mlp_b, core, (1, 2, 3))
     grads = tie(grads, own_b)
     in_grads = collected({s: [part.astype(F32) for part in grads[s]] for s in range(sections)}).reshape(1, micro_count, slot_rows, width)
-    small, got_b, in_grads, att_a = together((small, got_b, in_grads, att_a))
+    small, ups, downs, in_grads, att_a = together((small, ups, downs, in_grads, att_a))
+    small = small_sum(small, 2)
     got_a = from_pipe(att_a, 0, range(4))
 
     first_grads, half_grads = {}, {}

time: 604 us -> 600 us (level)
  waiting for transfers between devices: 104 us -> 91.7 us
    unnamed x227 -> x234, local copies, waits for them, and re-layouts: 32 us -> 32.1 us
  transfers between devices with their start and end apart: 78 -> 78, of which waited for: 25 -> 20; matrix products, arithmetic and copies ran while one was open for 13% -> 13% of each run, Pallas kernels for 39% -> 39%
where the time goes in v5:
time: 600 us; the launch traced here: 592 us
  Pallas kernels  258 us (43%)
  starting transfers between devices  102 us (17%)
  waiting for transfers between devices  91.7 us (15%)
  other arithmetic  60.7 us (10%)
  local copies, waits for them, and re-layouts  59 us (10%)
  between operations  19.7 us (3%)
    ppermute x53, starting transfers between devices, send(): return lax.ppermute(value, 'pipe', pairs)  79.2 us
    pallas_call x4, Pallas kernels, attn_backward(): pl.pallas_call(attn_bwd_kernel, grid=(count,), in_specs=[whole((rows, 128...  71.6 us
    ppermute x53, waiting for transfers between devices, send(): return lax.ppermute(value, 'pipe', pairs)  60 us
    pallas_call x4, Pallas kernels, attn_forward(): pl.pallas_call(attn_fwd_kernel, grid=(count,), in_specs=[whole((rows, 128...  51.2 us
    pallas_call x4, Pallas kernels, weight_grads(): pl.pallas_call(kernel, grid=(4,), in_specs=[SMEM, whole(a.shape), col, *(...  42.2 us
    pallas_call x2, Pallas kernels, block_back(): pl.pallas_call(block_back_kernel, grid=(1,), in_specs=[SMEM, one, one, AN...  34.3 us
    pallas_call x2, Pallas kernels, block_out(): pl.pallas_call(block_out_kernel, grid=(1,), in_specs=[SMEM, one, *[whole(...  33.2 us
    unnamed x234, local copies, waits for them, and re-layouts  32.1 us
  transfers between devices with their start and end apart: 78, of which 20 were waited for; matrix products, arithmetic and copies ran while one was open for 13% of the time, Pallas kernels for 39%

profile of v5, /device:TPU:0, one launch (start us, length us, event | category | flops | bytes accessed | tf_op | source)
XLA Modules:
  0.0 591.6 jit_solution(1008642837028721560)
XLA Ops:
  11.1 3.4 fusion.24
  14.6 3.6 collective-permute-start
  18.2 2.9 collective-permute-start.1
  36.0 2.8 fusion.5.key_ref
  43.1 14.3 %collective-permute-done.1 = bf16[384,2304]{1,0:T(8,128)(2,1)} collective-permute-done((bf16[384,2304]{1,0:T(8,128)(2,1)S(1)}, bf16[384,2304]{1,0:T(8,128)(2,1)}, u32[]{:S(2)}, u32[]{:S(2)}) %collective-permute-start.1) | collective-permute-done | bytes 1769504 | tf_op jit(solution)/shard_map/ppermute | solution.py:723
  59.8 3.3 collective-permute-done.6.far_other
  63.2 3.0 copy-done.4
  66.1 3.9 project.2
  75.7 12.7 %collective-permute-done.8 = bf16[96,3072]{1,0:T(8,128)(2,1)S(1)} collective-permute-done((bf16[96,3072]{1,0:T(8,128)(2,1)S(1)}, bf16[96,3072]{1,0:T(8,128)(2,1)S(1)}, u32[]{:S(2)}, u32[]{:S(2)}) %collective-permute-start.8) | collective-permute-done | bytes 589856 | tf_op jit(solution)/shard_map/ppermute | solution.py:723
  91.8 3.9 collective-permute-start.17
  96.3 12.7 %attn_fwd.4 = (bf16[576,384]{1,0:T(8,128)(2,1)}, bf16[576,384]{1,0:T(8,128)(2,1)}, f32[576,384]{1,0:T(8,128)}, bf16[6,1152,576]{2,1,0:T(8,128)(2,1)}) custom-call(bf16[576,128]{1,0:T(8,128)(2,1)} %get-tuple-element.291.hot_ref, f32[6,8,128]{2,1,0:T(8,128)} %get-tuple-element.624.map_ref, bf16[576,2304]{1,0:T(8,128)(2,1)} %copy-done.2, ...), custom_call_target="tpu_custom_call" | custom-call | flops 520000000 | bytes 1000 | tf_op jit(solution)/shard_map/attn_fwd/pallas_call | solution.py:145
  113.3 12.6 %attn_fwd.5 = (bf16[576,384]{1,0:T(8,128)(2,1)}, bf16[576,384]{1,0:T(8,128)(2,1)}, f32[576,384]{1,0:T(8,128)}, bf16[6,1152,576]{2,1,0:T(8,128)(2,1)}) custom-call(bf16[576,128]{1,0:T(8,128)(2,1)} %get-tuple-element.291.hot_ref, f32[6,8,128]{2,1,0:T(8,128)} %get-tuple-element.624.map_ref, bf16[576,2304]{1,0:T(8,128)(2,1)} %copy-done.2, ...), custom_call_target="tpu_custom_call" | custom-call | flops 520000000 | bytes 1000 | tf_op jit(solution)/shard_map/attn_fwd/pallas_call | solution.py:145
  146.4 5.6 collective-permute-done.18
  156.1 16.4 %block_out.2 = (bf16[576,768]{1,0:T(8,128)(2,1)}, bf16[576,768]{1,0:T(8,128)(2,1)}, bf16[576,768]{1,0:T(8,128)(2,1)}, bf16[576,3072]{1,0:T(8,128)(2,1)}, bf16[57...) custom-call(s32[2]{0:T(128)} %copy-done.50, ...), custom_call_target="tpu_custom_call" | custom-call | flops 240000000 | bytes 1000 | tf_op jit(solution)/shard_map/block_out/pallas_call | solution.py:410
  176.7 4.2 project.3
  188.6 13.1 %attn_fwd.6 = (bf16[576,384]{1,0:T(8,128)(2,1)}, bf16[576,384]{1,0:T(8,128)(2,1)}, f32[576,384]{1,0:T(8,128)}, bf16[6,1152,576]{2,1,0:T(8,128)(2,1)}) custom-call(bf16[576,128]{1,0:T(8,128)(2,1)} %get-tuple-element.291.hot_ref, f32[6,8,128]{2,1,0:T(8,128)} %get-tuple-element.623.map_ref, bf16[576,2304]{1,0:T(8,128)(2,1)} %copy-done.3, ...), custom_call_target="tpu_custom_call" | custom-call | flops 520000000 | bytes 1000 | tf_op jit(solution)/shard_map/attn_fwd/pallas_call | solution.py:145
  201.7 12.8 %attn_fwd.7 = (bf16[576,384]{1,0:T(8,128)(2,1)}, bf16[576,384]{1,0:T(8,128)(2,1)}, f32[576,384]{1,0:T(8,128)}, bf16[6,1152,576]{2,1,0:T(8,128)(2,1)}) custom-call(bf16[576,128]{1,0:T(8,128)(2,1)} %get-tuple-element.291.hot_ref, f32[6,8,128]{2,1,0:T(8,128)} %get-tuple-element.623.map_ref, bf16[576,2304]{1,0:T(8,128)(2,1)} %copy-done.3, ...), custom_call_target="tpu_custom_call" | custom-call | flops 520000000 | bytes 1000 | tf_op jit(solution)/shard_map/attn_fwd/pallas_call | solution.py:145
  214.5 16.7 %block_out.3 = (bf16[576,768]{1,0:T(8,128)(2,1)}, bf16[576,768]{1,0:T(8,128)(2,1)}, bf16[576,768]{1,0:T(8,128)(2,1)}, bf16[576,3072]{1,0:T(8,128)(2,1)}, bf16[57...) custom-call(s32[2]{0:T(128)} %get-tuple-element.289.info_ref, ...), custom_call_target="tpu_custom_call" | custom-call | flops 240000000 | bytes 1000 | tf_op jit(solution)/shard_map/block_out/pallas_call | solution.py:410
  231.3 5.6 collective-permute-start.28
  240.5 16.9 %block_back.2 = (bf16[576,768]{1,0:T(8,128)(2,1)}, bf16[576,3072]{1,0:T(8,128)(2,1)}, bf16[576,768]{1,0:T(8,128)(2,1)}, bf16[576,768]{1,0:T(8,128)(2,1)}, bf16[576,768]{1,0:T(8,128)(2,1)}, /*index=5*/f32[8,768]{1,0:T(8,128)}) custom-call(s32[2]{0:T(128)} %get-tuple-element.289.info_ref, bf16[576,768]{1,0:T(8,128)(2,1)} %get-tuple-element.290.gy_ref, ...), custom_call_target="tpu_custom_call" | custom-call | flops 280000000 | bytes 1000 | tf_op jit(solution)/shard_map/block_back/pallas_call | solution.py:493
  260.9 14.0 %mlp_grads.2 = (bf16[8,384,768]{2,1,0:T(8,128)(2,1)}, bf16[8,384,768]{2,1,0:T(8,128)(2,1)}) custom-call(s32[1]{0:T(128)} %bitcast.core_ref, bf16[576,768]{1,0:T(8,128)(2,1)S(1)} %copy-done.27, bf16[576,3072]{1,0:T(8,128)(2,1)S(1)} %copy-done.21, bf16[576,3072]{1,0:T(8,128)(2,1)} %get-tuple-element.368.hid_ref, bf16[576,768]{1,0:T(8,128)(2,1)S(1)} %copy-done.29), custom_call_target="tpu_custom_call" | custom-call | flops 300000000 | bytes 1000 | tf_op jit(solution)/shard_map/mlp_grads/pallas_call | solution.py:709
  275.9 17.9 %attn_bwd.4 = (bf16[576,384]{1,0:T(8,128)(2,1)}, bf16[2,576,384]{2,1,0:T(8,128)(2,1)}, bf16[2,576,384]{2,1,0:T(8,128)(2,1)}, f32[3,8,128]{2,1,0:T(8,128)}) custom-call(bf16[576,128]{1,0:T(8,128)(2,1)} %get-tuple-element.363.hot_ref, bf16[6,1152,576]{2,1,0:T(8,128)(2,1)} %get-tuple-element.364.w_ref, bf16[576,2304]{1,0:T(8,128)(2,1)} %copy-done.3, ...), custom_call_target="tpu_custom_call" | custom-call | flops 360000000 | bytes 1000 | tf_op jit(solution)/shard_map/attn_bwd/pallas_call | solution.py:227
  293.9 5.7 add.394
  299.9 18.1 %attn_bwd.5 = (bf16[576,384]{1,0:T(8,128)(2,1)}, bf16[2,576,384]{2,1,0:T(8,128)(2,1)}, bf16[2,576,384]{2,1,0:T(8,128)(2,1)}, f32[3,8,128]{2,1,0:T(8,128)}) custom-call(bf16[576,128]{1,0:T(8,128)(2,1)} %get-tuple-element.363.hot_ref, bf16[6,1152,576]{2,1,0:T(8,128)(2,1)} %get-tuple-element.383.w_ref, bf16[576,2304]{1,0:T(8,128)(2,1)} %copy-done.3, ...), custom_call_target="tpu_custom_call" | custom-call | flops 360000000 | bytes 1000 | tf_op jit(solution)/shard_map/attn_bwd/pallas_call | solution.py:227
  324.0 6.6 %project_back.2 = (bf16[576,2304]{1,0:T(8,128)(2,1)}, bf16[576,768]{1,0:T(8,128)(2,1)S(1)}, f32[8,768]{1,0:T(8,128)S(1)}) custom-call(s32[2]{0:T(128)S(1)} %copy-done.53, bf16[576,768]{1,0:T(8,128)(2,1)S(1)} %copy-done.22, bf16[576,768]{1,0:T(8,128)(2,1)S(1)} %copy-done.14, f32[3,768]{1,0:T(4,128)S(1)} %copy-done.45, bf16[576,384]{1,0:T(8,128)(2,1)S(1)} %copy-done.40, ...), custom_call_target="tpu_custom_call" | custom-call | flops 140000000 | bytes 1000 | tf_op jit(solution)/shard_map/project_back/pallas_call | solution.py:539
  330.6 7.3 %att_grads.2 = (bf16[8,192,768]{2,1,0:T(8,128)(2,1)S(1)}, bf16[8,192,768]{2,1,0:T(8,128)(2,1)}) custom-call(s32[1]{0:T(128)} %bitcast.core_ref, bf16[576,768]{1,0:T(8,128)(2,1)S(1)} %get-tuple-element.399.n_ref, bf16[576,2304]{1,0:T(8,128)(2,1)} %get-tuple-element.400.dproj_ref, bf16[576,384]{1,0:T(8,128)(2,1)S(1)} %copy-done.17, ...), custom_call_target="tpu_custom_call" | custom-call | flops 180000000 | bytes 1000 | tf_op jit(solution)/shard_map/att_grads/pallas_call | solution.py:709
  339.7 4.0 collective-permute-start.35
  345.3 3.1 collective-permute-start.37
  348.4 17.4 %block_back.3 = (bf16[576,768]{1,0:T(8,128)(2,1)}, bf16[576,3072]{1,0:T(8,128)(2,1)}, bf16[576,768]{1,0:T(8,128)(2,1)}, bf16[576,768]{1,0:T(8,128)(2,1)}, bf16[576,768]{1,0:T(8,128)(2,1)}, /*index=5*/f32[8,768]{1,0:T(8,128)}) custom-call(s32[2]{0:T(128)} %copy-done.50, bf16[576,768]{1,0:T(8,128)(2,1)} %copy-done.19, ...), custom_call_target="tpu_custom_call" | custom-call | flops 280000000 | bytes 1000 | tf_op jit(solution)/shard_map/block_back/pallas_call | solution.py:493
  366.8 3.8 add.395
  373.0 13.8 %mlp_grads.3 = (bf16[8,384,768]{2,1,0:T(8,128)(2,1)}, bf16[8,384,768]{2,1,0:T(8,128)(2,1)}) custom-call(s32[1]{0:T(128)} %bitcast.core_ref, bf16[576,768]{1,0:T(8,128)(2,1)S(1)} %copy-done.26, bf16[576,3072]{1,0:T(8,128)(2,1)S(1)} %copy-done.20, bf16[576,3072]{1,0:T(8,128)(2,1)} %get-tuple-element.422.hid_ref, bf16[576,768]{1,0:T(8,128)(2,1)S(1)} %copy-done.28), custom_call_target="tpu_custom_call" | custom-call | flops 300000000 | bytes 1000 | tf_op jit(solution)/shard_map/mlp_grads/pallas_call | solution.py:709
  391.8 17.8 %attn_bwd.6 = (bf16[576,384]{1,0:T(8,128)(2,1)}, bf16[2,576,384]{2,1,0:T(8,128)(2,1)}, bf16[2,576,384]{2,1,0:T(8,128)(2,1)}, f32[3,8,128]{2,1,0:T(8,128)}) custom-call(bf16[576,128]{1,0:T(8,128)(2,1)} %get-tuple-element.363.hot_ref, bf16[6,1152,576]{2,1,0:T(8,128)(2,1)} %get-tuple-element.416.w_ref, bf16[576,2304]{1,0:T(8,128)(2,1)} %copy-done.2, ...), custom_call_target="tpu_custom_call" | custom-call | flops 360000000 | bytes 1000 | tf_op jit(solution)/shard_map/attn_bwd/pallas_call | solution.py:227
  409.7 5.8 add.396
  415.6 3.0 collective-permute-start.42
  422.7 17.8 %attn_bwd.7 = (bf16[576,384]{1,0:T(8,128)(2,1)}, bf16[2,576,384]{2,1,0:T(8,128)(2,1)}, bf16[2,576,384]{2,1,0:T(8,128)(2,1)}, f32[3,8,128]{2,1,0:T(8,128)}) custom-call(bf16[576,128]{1,0:T(8,128)(2,1)} %get-tuple-element.363.hot_ref, bf16[6,1152,576]{2,1,0:T(8,128)(2,1)} %get-tuple-element.436.w_ref, bf16[576,2304]{1,0:T(8,128)(2,1)} %copy-done.2, ...), custom_call_target="tpu_custom_call" | custom-call | flops 360000000 | bytes 1000 | tf_op jit(solution)/shard_map/attn_bwd/pallas_call | solution.py:227
  440.5 4.1 collective-permute-done.43
  455.3 7.6 %project_back.3 = (bf16[576,2304]{1,0:T(8,128)(2,1)}, bf16[576,768]{1,0:T(8,128)(2,1)}, f32[8,768]{1,0:T(8,128)S(1)}) custom-call(s32[2]{0:T(128)S(1)} %copy-done.51, bf16[576,768]{1,0:T(8,128)(2,1)S(1)} %copy-done.23, bf16[576,768]{1,0:T(8,128)(2,1)S(1)} %copy-done.12, f32[3,768]{1,0:T(4,128)S(1)} %copy-done.43, bf16[576,384]{1,0:T(8,128)(2,1)S(1)} %copy-done.38, ...), custom_call_target="tpu_custom_call" | custom-call | flops 140000000 | bytes 1000 | tf_op jit(solution)/shard_map/project_back/pallas_call | solution.py:539
  466.5 7.0 %att_grads.3 = (bf16[8,192,768]{2,1,0:T(8,128)(2,1)S(1)}, bf16[8,192,768]{2,1,0:T(8,128)(2,1)}) custom-call(s32[1]{0:T(128)} %bitcast.core_ref, bf16[576,768]{1,0:T(8,128)(2,1)S(1)} %copy-done.31, bf16[576,2304]{1,0:T(8,128)(2,1)} %get-tuple-element.461.dproj_ref, bf16[576,384]{1,0:T(8,128)(2,1)S(1)} %copy-done.15, bf16[576,384]{1,0:T(8,128)(2,1)S(1)} %copy-done.16, ...), custom_call_target="tpu_custom_call" | custom-call | flops 180000000 | bytes 1000 | tf_op jit(solution)/shard_map/att_grads/pallas_call | solution.py:709
  480.2 3.7 add.409
  485.6 3.9 collective-permute-start.52
  495.4 6.4 %maximum_select_fusion = bf16[4,576,768]{2,1,0:T(8,128)(2,1)} fusion(bf16[1,576,768]{2,1,0:T(8,128)(2,1)} %bitcast.44, bf16[1,576,768]{2,1,0:T(8,128)(2,1)S(1)} %bitcast.208, bf16[1,576,768]{2,1,0:T(8,128)(2,1)} %bitcast.42, bf16[1,576,768]{2,1,0:T(8,128)(2,1)S(1)} %bitcast.206, bf16[1,576,768]{2,1,0:T(8,128)(2,1)S(1)} %bitcast.209, ...), kind=kLoop, calls=%fused_computation.1 | loop fusion | flops 26542080 | bytes 17694724 | tf_op jit(solution)/shard_map/jit(_where)/select_n | solution.py:821
  504.8 6.2 %collective-permute-done.52 = bf16[288,768]{1,0:T(8,128)(2,1)S(1)} collective-permute-done((bf16[288,768]{1,0:T(8,128)(2,1)S(1)}, bf16[288,768]{1,0:T(8,128)(2,1)S(1)}, u32[]{:S(2)}, u32[]{:S(2)}) %collective-permute-start.52) | collective-permute-done | bytes 442400 | tf_op jit(solution)/shard_map/ppermute | solution.py:723
  511.1 7.6 %collective-permute-done.57 = bf16[2,192,256]{2,1,0:T(8,128)(2,1)S(1)} collective-permute-done((bf16[2,192,256]{2,1,0:T(8,128)(2,1)S(1)}, bf16[2,192,256]{2,1,0:T(8,128)(2,1)S(1)}, u32[]{:S(2)}, u32[]{:S(2)}) %collective-permute-start.57) | collective-permute-done | bytes 196640 | tf_op jit(solution)/shard_map/ppermute | solution.py:761
  521.7 3.3 collective-permute-start.63
  529.6 8.7 %collective-permute-done.62 = bf16[192,768]{1,0:T(8,128)(2,1)S(1)} collective-permute-done((bf16[192,768]{1,0:T(8,128)(2,1)S(1)}, bf16[192,768]{1,0:T(8,128)(2,1)S(1)}, u32[]{:S(2)}, u32[]{:S(2)}) %collective-permute-start.62) | collective-permute-done | bytes 294944 | tf_op jit(solution)/shard_map/ppermute | solution.py:723
  538.3 8.6 %collective-permute-done.64 = bf16[192,768]{1,0:T(8,128)(2,1)S(1)} collective-permute-done((bf16[192,768]{1,0:T(8,128)(2,1)S(1)}, bf16[192,768]{1,0:T(8,128)(2,1)S(1)}, u32[]{:S(2)}, u32[]{:S(2)}) %collective-permute-start.64) | collective-permute-done | bytes 294944 | tf_op jit(solution)/shard_map/ppermute | solution.py:761
  553.7 8.6 %select_select_fusion = f32[4,576,768]{2,1,0:T(8,128)} fusion(bf16[1,576,768]{2,1,0:T(8,128)(2,1)} %bitcast.75, bf16[1,576,768]{2,1,0:T(8,128)(2,1)} %bitcast.74, bf16[1,576,768]{2,1,0:T(8,128)(2,1)} %bitcast.73, bf16[1,576,768]{2,1,0:T(8,128)(2,1)} %bitcast.72, bf16[1,576,768]{2,1,0:T(8,128)(2,1)S(1)} %bitcast.222, bf16[1,576,768]{2,1,0:T(8,128)(2,1)S(1)} %bitcast.223, ...), kind=kLoop, calls=%fused_computation | loop fusion | flops 33619968 | bytes 21233668 | tf_op jit(solution)/shard_map/jit(_where)/select_n | solution.py:821
  563.8 6.2 %collective-permute-done.70 = bf16[96,768]{1,0:T(8,128)(2,1)S(1)} collective-permute-done((bf16[96,768]{1,0:T(8,128)(2,1)S(1)}, bf16[96,768]{1,0:T(8,128)(2,1)S(1)}, u32[]{:S(2)}, u32[]{:S(2)}) %collective-permute-start.70) | collective-permute-done | bytes 147488 | tf_op jit(solution)/shard_map/ppermute | solution.py:723
  (503 shorter events, 163.4 us)
Async XLA Ops:
  7.2 402.5 %reduce-scatter.4.cloned.1.call-start = ((), (), s32[]{:S(2)}) async-start(), calls=%async_computation.3 | async-start | bytes 5308416 | tf_op jit(solution)/shard_map/reduce_scatter | solution.py:784
  8.0 31.5 %collective-permute-start.4 = (f32[3,768]{1,0:T(4,128)S(1)}, f32[3,768]{1,0:T(4,128)S(1)}, u32[]{:S(2)}, u32[]{:S(2)}) collective-permute-start(f32[3,768]{1,0:T(4,128)S(1)} %pad_maximum_fusion.10), channel_id=1, source_target_pairs={{0,3},{1,2},{2,1},{3,0},{4,7},{5,6},{6,5},{7,4},{8,11},{9,10},{10,... | collective-permute-start | bytes 27656 | tf_op jit(solution)/shard_map/ppermute | solution.py:723
  10.4 32.0 %collective-permute-start.3 = (f32[3,768]{1,0:T(4,128)S(1)}, f32[3,768]{1,0:T(4,128)S(1)}, u32[]{:S(2)}, u32[]{:S(2)}) collective-permute-start(f32[3,768]{1,0:T(4,128)S(1)} %pad_maximum_fusion.10), channel_id=1, source_target_pairs={{0,2},{1,3},{2,0},{3,1},{4,6},{5,7},{6,4},{7,5},{8,10},{9,11},{10,... | collective-permute-start | bytes 27656 | tf_op jit(solution)/shard_map/ppermute | solution.py:723
  11.1 52.1 %collective-permute-start.5 = (bf16[768,3072]{1,0:T(8,128)(2,1)}, bf16[768,3072]{1,0:T(8,128)(2,1)}, u32[]{:S(2)}, u32[]{:S(2)}) collective-permute-start(bf16[768,3072]{1,0:T(8,128)(2,1)} %bitcast.178), channel_id=1, source_target_pairs={{0,1},{1,0},{2,3},{3,2},{4,5},{5,4},{6,7},{7,6},{8,9},{9,8},{10,11... | collective-permute-start | bytes 14155784 | tf_op jit(solution)/shard_map/ppermute | solution.py:723
  14.6 28.5 %collective-permute-start = (bf16[384,2304]{1,0:T(8,128)(2,1)}, bf16[384,2304]{1,0:T(8,128)(2,1)}, u32[]{:S(2)}, u32[]{:S(2)}) collective-permute-start(bf16[384,2304]{1,0:T(8,128)(2,1)} %get-tuple-element.564), channel_id=1, source_target_pairs={{0,2},{2,0},{4,6},{6,4},{8,10},{10,8},{12,14},{14,12},{16,18},{18,... | collective-permute-start | bytes 5308424 | tf_op jit(solution)/shard_map/ppermute | solution.py:723
  18.2 39.2 %collective-permute-start.1 = (bf16[384,2304]{1,0:T(8,128)(2,1)S(1)}, bf16[384,2304]{1,0:T(8,128)(2,1)}, u32[]{:S(2)}, u32[]{:S(2)}) collective-permute-start(bf16[384,2304]{1,0:T(8,128)(2,1)S(1)} %get-tuple-element.563), channel_id=1, source_target_pairs={{0,3},{2,1},{4,7},{6,5},{8,11},{10,9},{12,15},{14,13},{16,19},{18,... | collective-permute-start | bytes 5308424 | tf_op jit(solution)/shard_map/ppermute | solution.py:723
  70.3 18.1 %collective-permute-start.7 = (bf16[576,1536]{1,0:T(8,128)(2,1)S(1)}, bf16[576,1536]{1,0:T(8,128)(2,1)S(1)}, u32[]{:S(2)}, u32[]{:S(2)}) collective-permute-start(bf16[576,1536]{1,0:T(8,128)(2,1)S(1)} %slice.241), channel_id=1, source_target_pairs={{0,1},{1,0},{2,3},{3,2},{4,5},{5,4},{6,7},{7,6},{8,9},{9,8},{10,11... | collective-permute-start | bytes 5308424 | tf_op jit(solution)/shard_map/ppermute | solution.py:723
  71.6 16.8 %collective-permute-start.8 = (bf16[96,3072]{1,0:T(8,128)(2,1)S(1)}, bf16[96,3072]{1,0:T(8,128)(2,1)S(1)}, u32[]{:S(2)}, u32[]{:S(2)}) collective-permute-start(bf16[96,3072]{1,0:T(8,128)(2,1)S(1)} %copy-done.91), channel_id=1, source_target_pairs={{1,2},{3,0},{5,6},{7,4},{9,10},{11,8},{13,14},{15,12},{17,18},{19,... | collective-permute-start | bytes 1769480 | tf_op jit(solution)/shard_map/ppermute | solution.py:723
  73.6 35.4 %collective-permute-start.12 = (bf16[384,768]{1,0:T(8,128)(2,1)S(1)}, bf16[384,768]{1,0:T(8,128)(2,1)S(1)}, u32[]{:S(2)}, u32[]{:S(2)}) collective-permute-start(bf16[384,768]{1,0:T(8,128)(2,1)S(1)} %dynamic-slice_bitcast_fusion.8), channel_id=1, source_target_pairs={{0,2},{1,3},{2,0},{3,1},{4,6},{5,7},{6,4},{7,5},{8,10},{9,11},{10,... | collective-permute-start | bytes 1769480 | tf_op jit(solution)/shard_map/ppermute | solution.py:723
  88.5 20.5 %collective-permute-start.10 = (bf16[96,3072]{1,0:T(8,128)(2,1)S(1)}, bf16[96,3072]{1,0:T(8,128)(2,1)S(1)}, u32[]{:S(2)}, u32[]{:S(2)}) collective-permute-start(bf16[96,3072]{1,0:T(8,128)(2,1)S(1)} %broadcast_select_fusion.4.mine), channel_id=1, source_target_pairs={{0,4},{4,0},{8,12},{12,8},{16,20},{20,16},{24,28},{28,24},{1,5},{5... | collective-permute-start | bytes 1769480 | tf_op jit(solution)/shard_map/ppermute | solution.py:570
  90.3 18.8 %collective-permute-start.11 = (bf16[96,3072]{1,0:T(8,128)(2,1)S(1)}, bf16[96,3072]{1,0:T(8,128)(2,1)S(1)}, u32[]{:S(2)}, u32[]{:S(2)}) collective-permute-start(bf16[96,3072]{1,0:T(8,128)(2,1)S(1)} %broadcast_select_fusion.4.mine), channel_id=1, source_target_pairs={{0,8},{4,12},{8,0},{12,4},{16,24},{20,28},{24,16},{28,20},{1,9},{5... | collective-permute-start | bytes 1769480 | tf_op jit(solution)/shard_map/ppermute | solution.py:570
  91.8 38.4 %collective-permute-start.17 = (bf16[768,768]{1,0:T(8,128)(2,1)}, bf16[768,768]{1,0:T(8,128)(2,1)S(1)}, u32[]{:S(2)}, u32[]{:S(2)}) collective-permute-start(bf16[768,768]{1,0:T(8,128)(2,1)} %slice.306), channel_id=1, source_target_pairs={{0,2},{2,0},{4,6},{6,4},{8,10},{10,8},{12,14},{14,12},{16,18},{18,... | collective-permute-start | bytes 3538952 | tf_op jit(solution)/shard_map/ppermute | solution.py:723
  109.0 21.2 %collective-permute-start.15 = (bf16[384,768]{1,0:T(8,128)(2,1)S(1)}, bf16[384,768]{1,0:T(8,128)(2,1)S(1)}, u32[]{:S(2)}, u32[]{:S(2)}) collective-permute-start(bf16[384,768]{1,0:T(8,128)(2,1)S(1)} %collective-permute-done.12.mine), channel_id=1, source_target_pairs={{0,4},{4,0},{8,12},{12,8},{16,20},{20,16},{24,28},{28,24},{1,5},{5... | collective-permute-start | bytes 1769480 | tf_op jit(solution)/shard_map/ppermute | solution.py:570
  109.6 20.6 %collective-permute-start.16 = (bf16[384,768]{1,0:T(8,128)(2,1)S(1)}, bf16[384,768]{1,0:T(8,128)(2,1)S(1)}, u32[]{:S(2)}, u32[]{:S(2)}) collective-permute-start(bf16[384,768]{1,0:T(8,128)(2,1)S(1)} %collective-permute-done.12.mine), channel_id=1, source_target_pairs={{0,8},{4,12},{8,0},{12,4},{16,24},{20,28},{24,16},{28,20},{1,9},{5... | collective-permute-start | bytes 1769480 | tf_op jit(solution)/shard_map/ppermute | solution.py:570
  110.1 18.4 %collective-permute-start.13 = (bf16[48,3072]{1,0:T(8,128)(2,1)S(1)}, bf16[48,3072]{1,0:T(8,128)(2,1)S(1)}, u32[]{:S(2)}, u32[]{:S(2)}) collective-permute-start(bf16[48,3072]{1,0:T(8,128)(2,1)S(1)} %slice.242), channel_id=1, source_target_pairs={{0,4},{4,0},{8,12},{12,8},{16,20},{20,16},{24,28},{28,24},{1,5},{5... | collective-permute-start | bytes 884744 | tf_op jit(solution)/shard_map/ppermute | solution.py:570
  111.7 17.8 %collective-permute-start.14 = (bf16[48,3072]{1,0:T(8,128)(2,1)S(1)}, bf16[48,3072]{1,0:T(8,128)(2,1)S(1)}, u32[]{:S(2)}, u32[]{:S(2)}) collective-permute-start(bf16[48,3072]{1,0:T(8,128)(2,1)S(1)} %slice.243), channel_id=1, source_target_pairs={{0,8},{4,12},{8,0},{12,4},{16,24},{20,28},{24,16},{28,20},{1,9},{5... | collective-permute-start | bytes 884744 | tf_op jit(solution)/shard_map/ppermute | solution.py:570
  134.7 18.5 %collective-permute-start.20 = (bf16[1536,768]{1,0:T(8,128)(2,1)}, bf16[1536,768]{1,0:T(8,128)(2,1)S(1)}, u32[]{:S(2)}, u32[]{:S(2)}) collective-permute-start(bf16[1536,768]{1,0:T(8,128)(2,1)} %bitcast.192), channel_id=1, source_target_pairs={{0,1},{1,0},{2,3},{3,2},{4,5},{5,4},{6,7},{7,6},{8,9},{9,8},{10,11... | collective-permute-start | bytes 7077896 | tf_op jit(solution)/shard_map/ppermute | solution.py:723
  182.7 31.8 %collective-permute-start.25 = (bf16[576,768]{1,0:T(8,128)(2,1)S(1)}, bf16[576,768]{1,0:T(8,128)(2,1)S(1)}, u32[]{:S(2)}, u32[]{:S(2)}) collective-permute-start(bf16[576,768]{1,0:T(8,128)(2,1)S(1)} %copy-done.63), channel_id=1, source_target_pairs={{2,0},{3,1},{6,4},{7,5},{10,8},{11,9},{14,12},{15,13},{18,16},{19,... | collective-permute-start | bytes 2654216 | tf_op jit(solution)/shard_map/ppermute | solution.py:723
  184.0 47.3 %collective-permute-start.26 = (bf16[576,768]{1,0:T(8,128)(2,1)}, bf16[576,768]{1,0:T(8,128)(2,1)}, u32[]{:S(2)}, u32[]{:S(2)}) collective-permute-start(bf16[576,768]{1,0:T(8,128)(2,1)} %get-tuple-element.350), channel_id=1, source_target_pairs={{0,1},{1,0},{4,5},{5,4},{8,9},{9,8},{12,13},{13,12},{16,17},{17,16... | collective-permute-start | bytes 2654216 | tf_op jit(solution)/shard_map/ppermute | solution.py:723
  186.0 45.3 %collective-permute-start.27 = (bf16[576,768]{1,0:T(8,128)(2,1)}, bf16[576,768]{1,0:T(8,128)(2,1)}, u32[]{:S(2)}, u32[]{:S(2)}) collective-permute-start(bf16[576,768]{1,0:T(8,128)(2,1)} %get-tuple-element.350), channel_id=1, source_target_pairs={{3,0},{2,1},{7,4},{6,5},{11,8},{10,9},{15,12},{14,13},{19,16},{18,... | collective-permute-start | bytes 2654216 | tf_op jit(solution)/shard_map/ppermute | solution.py:723
  231.3 26.1 %collective-permute-start.28 = (bf16[576,768]{1,0:T(8,128)(2,1)}, bf16[576,768]{1,0:T(8,128)(2,1)S(1)}, u32[]{:S(2)}, u32[]{:S(2)}) collective-permute-start(bf16[576,768]{1,0:T(8,128)(2,1)} %get-tuple-element.504), channel_id=1, source_target_pairs={{0,2},{1,3},{4,6},{5,7},{8,10},{9,11},{12,14},{13,15},{16,18},{17,... | collective-permute-start | bytes 2654216 | tf_op jit(solution)/shard_map/ppermute | solution.py:723
  237.0 38.0 %collective-permute-start.29 = (bf16[576,768]{1,0:T(8,128)(2,1)}, bf16[576,768]{1,0:T(8,128)(2,1)S(1)}, u32[]{:S(2)}, u32[]{:S(2)}) collective-permute-start(bf16[576,768]{1,0:T(8,128)(2,1)} %get-tuple-element.372), channel_id=1, source_target_pairs={{2,3},{3,2},{6,7},{7,6},{10,11},{11,10},{14,15},{15,14},{18,19},{1... | collective-permute-start | bytes 2654216 | tf_op jit(solution)/shard_map/ppermute | solution.py:723
  237.7 37.7 %collective-permute-start.30 = (bf16[576,768]{1,0:T(8,128)(2,1)}, bf16[576,768]{1,0:T(8,128)(2,1)S(1)}, u32[]{:S(2)}, u32[]{:S(2)}) collective-permute-start(bf16[576,768]{1,0:T(8,128)(2,1)} %get-tuple-element.372), channel_id=1, source_target_pairs={{1,2},{0,3},{5,6},{4,7},{9,10},{8,11},{13,14},{12,15},{17,18},{16,... | collective-permute-start | bytes 2654216 | tf_op jit(solution)/shard_map/ppermute | solution.py:723
  275.4 18.4 %collective-permute-start.31 = (bf16[8,384,768]{2,1,0:T(8,128)(2,1)}, bf16[8,384,768]{2,1,0:T(8,128)(2,1)}, u32[]{:S(2)}, u32[]{:S(2)}) collective-permute-start(bf16[8,384,768]{2,1,0:T(8,128)(2,1)} %get-tuple-element.381), channel_id=1, source_target_pairs={{0,1},{1,0},{2,3},{3,2},{4,5},{5,4},{6,7},{7,6},{8,9},{9,8},{10,11... | collective-permute-start | bytes 14155784 | tf_op jit(solution)/shard_map/ppermute | solution.py:723
  299.6 173.9 %reduce-scatter.6.cloned.1.call-start = ((), (), s32[]{:S(2)}) async-start(), calls=%async_computation.4 | async-start | bytes 2654208 | tf_op jit(solution)/shard_map/reduce_scatter | solution.py:784
  299.7 18.4 %collective-permute-start.32 = (bf16[2,576,384]{2,1,0:T(8,128)(2,1)}, bf16[2,576,384]{2,1,0:T(8,128)(2,1)S(1)}, u32[]{:S(2)}, u32[]{:S(2)}) collective-permute-start(bf16[2,576,384]{2,1,0:T(8,128)(2,1)} %get-tuple-element.385), channel_id=1, source_target_pairs={{0,1},{1,0},{2,3},{3,2},{4,5},{5,4},{6,7},{7,6},{8,9},{9,8},{10,11... | collective-permute-start | bytes 2654216 | tf_op jit(solution)/shard_map/ppermute | solution.py:723
  338.0 27.9 %collective-permute-start.34 = (bf16[8,192,768]{2,1,0:T(8,128)(2,1)}, bf16[8,192,768]{2,1,0:T(8,128)(2,1)}, u32[]{:S(2)}, u32[]{:S(2)}) collective-permute-start(bf16[8,192,768]{2,1,0:T(8,128)(2,1)} %get-tuple-element.414), channel_id=1, source_target_pairs={{0,1},{1,0},{2,3},{3,2},{4,5},{5,4},{6,7},{7,6},{8,9},{9,8},{10,11... | collective-permute-start | bytes 7077896 | tf_op jit(solution)/shard_map/ppermute | solution.py:723
  339.7 26.2 %collective-permute-start.35 = (bf16[576,768]{1,0:T(8,128)(2,1)S(1)}, bf16[576,768]{1,0:T(8,128)(2,1)S(1)}, u32[]{:S(2)}, u32[]{:S(2)}) collective-permute-start(bf16[576,768]{1,0:T(8,128)(2,1)S(1)} %get-tuple-element.547), channel_id=1, source_target_pairs={{0,2},{1,3},{4,6},{5,7},{8,10},{9,11},{12,14},{13,15},{16,18},{17,... | collective-permute-start | bytes 2654216 | tf_op jit(solution)/shard_map/ppermute | solution.py:723
  343.7 43.1 %collective-permute-start.36 = (bf16[576,768]{1,0:T(8,128)(2,1)}, bf16[576,768]{1,0:T(8,128)(2,1)}, u32[]{:S(2)}, u32[]{:S(2)}) collective-permute-start(bf16[576,768]{1,0:T(8,128)(2,1)} %get-tuple-element.565), channel_id=1, source_target_pairs={{2,3},{3,2},{6,7},{7,6},{10,11},{11,10},{14,15},{15,14},{18,19},{1... | collective-permute-start | bytes 2654216 | tf_op jit(solution)/shard_map/ppermute | solution.py:723
  345.3 41.5 %collective-permute-start.37 = (bf16[576,768]{1,0:T(8,128)(2,1)}, bf16[576,768]{1,0:T(8,128)(2,1)}, u32[]{:S(2)}, u32[]{:S(2)}) collective-permute-start(bf16[576,768]{1,0:T(8,128)(2,1)} %get-tuple-element.565), channel_id=1, source_target_pairs={{1,2},{0,3},{5,6},{4,7},{9,10},{8,11},{13,14},{12,15},{17,18},{16,... | collective-permute-start | bytes 2654216 | tf_op jit(solution)/shard_map/ppermute | solution.py:723
  386.8 22.8 %collective-permute-start.38 = (bf16[8,384,768]{2,1,0:T(8,128)(2,1)}, bf16[8,384,768]{2,1,0:T(8,128)(2,1)}, u32[]{:S(2)}, u32[]{:S(2)}) collective-permute-start(bf16[8,384,768]{2,1,0:T(8,128)(2,1)} %get-tuple-element.434), channel_id=1, source_target_pairs={{0,1},{1,0},{2,3},{3,2},{4,5},{5,4},{6,7},{7,6},{8,9},{9,8},{10,11... | collective-permute-start | bytes 14155784 | tf_op jit(solution)/shard_map/ppermute | solution.py:723
  387.1 182.8 %reduce-scatter.8.cloned.1.call-start = ((), (), s32[]{:S(2)}) async-start(), calls=%async_computation.5 | async-start | bytes 2654208 | tf_op jit(solution)/shard_map/reduce_scatter | solution.py:784
  388.0 21.6 %collective-permute-start.39 = (bf16[576,768]{1,0:T(8,128)(2,1)S(1)}, bf16[576,768]{1,0:T(8,128)(2,1)S(1)}, u32[]{:S(2)}, u32[]{:S(2)}) collective-permute-start(bf16[576,768]{1,0:T(8,128)(2,1)S(1)} %copy-done.23), channel_id=1, source_target_pairs={{0,1},{4,5},{8,9},{12,13},{16,17},{20,21},{24,25},{28,29}} | collective-permute-start | bytes 2654216 | tf_op jit(solution)/shard_map/ppermute | solution.py:723
  390.1 19.5 %collective-permute-start.40 = (bf16[576,768]{1,0:T(8,128)(2,1)S(1)}, bf16[576,768]{1,0:T(8,128)(2,1)S(1)}, u32[]{:S(2)}, u32[]{:S(2)}) collective-permute-start(bf16[576,768]{1,0:T(8,128)(2,1)S(1)} %copy-done.23), channel_id=1, source_target_pairs={{3,1},{7,5},{11,9},{15,13},{19,17},{23,21},{27,25},{31,29}} | collective-permute-start | bytes 2654216 | tf_op jit(solution)/shard_map/ppermute | solution.py:723
  390.9 18.8 %collective-permute-start.41 = (bf16[576,768]{1,0:T(8,128)(2,1)S(1)}, bf16[576,768]{1,0:T(8,128)(2,1)S(1)}, u32[]{:S(2)}, u32[]{:S(2)}) collective-permute-start(bf16[576,768]{1,0:T(8,128)(2,1)S(1)} %copy-done.23), channel_id=1, source_target_pairs={{2,1},{6,5},{10,9},{14,13},{18,17},{22,21},{26,25},{30,29}} | collective-permute-start | bytes 2654216 | tf_op jit(solution)/shard_map/ppermute | solution.py:723
  415.6 30.7 %collective-permute-start.42 = (bf16[2,576,384]{2,1,0:T(8,128)(2,1)}, bf16[2,576,384]{2,1,0:T(8,128)(2,1)S(1)}, u32[]{:S(2)}, u32[]{:S(2)}) collective-permute-start(bf16[2,576,384]{2,1,0:T(8,128)(2,1)} %get-tuple-element.438), channel_id=1, source_target_pairs={{0,1},{1,0},{2,3},{3,2},{4,5},{5,4},{6,7},{7,6},{8,9},{9,8},{10,11... | collective-permute-start | bytes 2654216 | tf_op jit(solution)/shard_map/ppermute | solution.py:723
  419.3 25.4 %collective-permute-start.43 = (bf16[2,2,2,192,256]{4,3,2,1,0:T(8,128)(2,1)S(1)}, bf16[2,2,2,192,256]{4,3,2,1,0:T(8,128)(2,1)S(1)}, u32[]{:S(2)}, u32[]{:S(2)}) collective-permute-start(bf16[2,2,2,192,256]{4,3,2,1,0:T(8,128)(2,1)S(1)} %get-tuple-element.572), channel_id=1, source_target_pairs={{0,4},{4,0},{8,12},{12,8},{16,20},{20,16},{24,28},{28,24},{1,5},{5... | collective-permute-start | bytes 2359304 | tf_op jit(solution)/shard_map/ppermute | solution.py:761
  421.1 23.5 %collective-permute-start.44 = (bf16[2,2,2,192,256]{4,3,2,1,0:T(8,128)(2,1)}, bf16[2,2,2,192,256]{4,3,2,1,0:T(8,128)(2,1)S(1)}, u32[]{:S(2)}, u32[]{:S(2)}) collective-permute-start(bf16[2,2,2,192,256]{4,3,2,1,0:T(8,128)(2,1)} %get-tuple-element.570), channel_id=1, source_target_pairs={{0,2},{1,3},{2,0},{3,1},{4,6},{5,7},{6,4},{7,5},{8,10},{9,11},{10,... | collective-permute-start | bytes 2359304 | tf_op jit(solution)/shard_map/ppermute | solution.py:761
  422.4 23.9 %collective-permute-start.45 = (bf16[2,2,2,192,256]{4,3,2,1,0:T(8,128)(2,1)}, bf16[2,2,2,192,256]{4,3,2,1,0:T(8,128)(2,1)S(1)}, u32[]{:S(2)}, u32[]{:S(2)}) collective-permute-start(bf16[2,2,2,192,256]{4,3,2,1,0:T(8,128)(2,1)} %get-tuple-element.568), channel_id=1, source_target_pairs={{0,8},{4,12},{8,0},{12,4},{16,24},{20,28},{24,16},{28,20},{1,9},{5... | collective-permute-start | bytes 2359304 | tf_op jit(solution)/shard_map/ppermute | solution.py:761
  477.6 33.5 %collective-permute-start.53 = (bf16[576,768]{1,0:T(8,128)(2,1)}, bf16[576,768]{1,0:T(8,128)(2,1)}, u32[]{:S(2)}, u32[]{:S(2)}) collective-permute-start(bf16[576,768]{1,0:T(8,128)(2,1)} %get-tuple-element.532), channel_id=1, source_target_pairs={{2,0},{6,4},{10,8},{14,12},{18,16},{22,20},{26,24},{30,28}} | collective-permute-start | bytes 2654216 | tf_op jit(solution)/shard_map/ppermute | solution.py:723
  478.9 32.2 %collective-permute-start.54 = (bf16[576,768]{1,0:T(8,128)(2,1)}, bf16[576,768]{1,0:T(8,128)(2,1)}, u32[]{:S(2)}, u32[]{:S(2)}) collective-permute-start(bf16[576,768]{1,0:T(8,128)(2,1)} %get-tuple-element.532), channel_id=1, source_target_pairs={{3,0},{7,4},{11,8},{15,12},{19,16},{23,20},{27,24},{31,28}} | collective-permute-start | bytes 2654216 | tf_op jit(solution)/shard_map/ppermute | solution.py:723
  485.6 25.4 %collective-permute-start.52 = (bf16[288,768]{1,0:T(8,128)(2,1)S(1)}, bf16[288,768]{1,0:T(8,128)(2,1)S(1)}, u32[]{:S(2)}, u32[]{:S(2)}) collective-permute-start(bf16[288,768]{1,0:T(8,128)(2,1)S(1)} %pad_maximum_fusion.1), channel_id=1, source_target_pairs={{0,2},{1,3},{2,0},{3,1},{4,6},{5,7},{6,4},{7,5},{8,10},{9,11},{10,... | collective-permute-start | bytes 1327112 | tf_op jit(solution)/shard_map/ppermute | solution.py:723
  491.3 19.8 %collective-permute-start.55 = (bf16[2,192,256]{2,1,0:T(8,128)(2,1)}, bf16[2,192,256]{2,1,0:T(8,128)(2,1)}, u32[]{:S(2)}, u32[]{:S(2)}) collective-permute-start(bf16[2,192,256]{2,1,0:T(8,128)(2,1)} %get-tuple-element.595), channel_id=1, source_target_pairs={{0,8},{4,12},{8,0},{12,4},{16,24},{20,28},{24,16},{28,20},{1,9},{5... | collective-permute-start | bytes 589832 | tf_op jit(solution)/shard_map/ppermute | solution.py:761
  494.4 16.8 %collective-permute-start.56 = (bf16[2,192,256]{2,1,0:T(8,128)(2,1)}, bf16[2,192,256]{2,1,0:T(8,128)(2,1)}, u32[]{:S(2)}, u32[]{:S(2)}) collective-permute-start(bf16[2,192,256]{2,1,0:T(8,128)(2,1)} %get-tuple-element.593), channel_id=1, source_target_pairs={{0,4},{4,0},{8,12},{12,8},{16,20},{20,16},{24,28},{28,24},{1,5},{5... | collective-permute-start | bytes 589832 | tf_op jit(solution)/shard_map/ppermute | solution.py:761
  521.7 16.7 %collective-permute-start.63 = (bf16[192,768]{1,0:T(8,128)(2,1)S(1)}, bf16[192,768]{1,0:T(8,128)(2,1)S(1)}, u32[]{:S(2)}, u32[]{:S(2)}) collective-permute-start(bf16[192,768]{1,0:T(8,128)(2,1)S(1)} %get-tuple-element.590), channel_id=1, source_target_pairs={{1,2},{0,3},{5,6},{4,7},{9,10},{8,11},{13,14},{12,15},{17,18},{16,... | collective-permute-start | bytes 884744 | tf_op jit(solution)/shard_map/ppermute | solution.py:723
  528.7 18.2 %collective-permute-start.64 = (bf16[192,768]{1,0:T(8,128)(2,1)S(1)}, bf16[192,768]{1,0:T(8,128)(2,1)S(1)}, u32[]{:S(2)}, u32[]{:S(2)}) collective-permute-start(bf16[192,768]{1,0:T(8,128)(2,1)S(1)} %get-tuple-element.587), channel_id=1, source_target_pairs={{0,16},{4,20},{8,24},{12,28},{16,0},{20,4},{24,8},{28,12},{1,17},{... | collective-permute-start | bytes 884744 | tf_op jit(solution)/shard_map/ppermute | solution.py:761
  546.9 16.8 %collective-permute-start.67 = (f32[12336]{0:T(1024)S(1)}, f32[12336]{0:T(1024)S(1)}, u32[]{:S(2)}, u32[]{:S(2)}) collective-permute-start(f32[12336]{0:T(1024)S(1)} %add_add_fusion.1), channel_id=1, source_target_pairs={{0,12},{4,8},{8,4},{12,0},{16,28},{20,24},{24,20},{28,16},{1,13},{... | collective-permute-start | bytes 148040 | tf_op jit(solution)/shard_map/ppermute | solution.py:570
  550.5 19.4 %collective-permute-start.68 = (bf16[192,768]{1,0:T(8,128)(2,1)S(1)}, bf16[192,768]{1,0:T(8,128)(2,1)S(1)}, u32[]{:S(2)}, u32[]{:S(2)}) collective-permute-start(bf16[192,768]{1,0:T(8,128)(2,1)S(1)} %add.428), channel_id=1, source_target_pairs={{0,1},{4,5},{8,9},{12,13},{16,17},{20,21},{24,25},{28,29}} | collective-permute-start | bytes 884744 | tf_op jit(solution)/shard_map/ppermute | solution.py:723
  (147 other events, 1296.1 us)
Sparse Core Ops, SparseCore 0:
  299.7 95.5 reduce-scatter.3
  398.8 73.4 reduce-scatter.5
  484.1 74.0 reduce-scatter.7

commit v6 on v5

--- a/solution.py
+++ b/solution.py
@@ -995,7 +995,8 @@
     mlp_b, att_b = line_end(mlp_b, att_b)
     section_out = collected(outs).reshape(1, micro_count, slot_rows, width)
     small, section_out, mlp_b, att_b, grads[0], mlp_a = hold((small, section_out, mlp_b, att_b, grads[0], mlp_a), 5)
-    mlp_a, _ = cube_end(mlp_a)
+    mlp_a, given = cube_end(mlp_a)
+    mlp_b, att_b, small = tie((mlp_b, att_b, small), given)
     small = small_sum(small, 0)
     even = jnp.concatenate([att_b, mlp_b[: att_b.shape[0]]], axis=0)
     own_b = pick(core, even, mlp_b)

time: 600 us -> 597 us (level)
  transfers between devices with their start and end apart: 78 -> 78, of which waited for: 20 -> 20; matrix products, arithmetic and copies ran while one was open for 13% -> 13% of each run, Pallas kernels for 39% -> 40%
where the time goes in v6:
time: 597 us; the launch traced here: 588 us
  Pallas kernels  258 us (43%)
  starting transfers between devices  102 us (17%)
  waiting for transfers between devices  89.3 us (15%)
  other arithmetic  60.8 us (10%)
  local copies, waits for them, and re-layouts  59 us (10%)
  between operations  19.7 us (3%)
    ppermute x53, starting transfers between devices, send(): return lax.ppermute(value, 'pipe', pairs)  79.3 us
    pallas_call x4, Pallas kernels, attn_backward(): pl.pallas_call(attn_bwd_kernel, grid=(count,), in_specs=[whole((rows, 128...  71.6 us
    ppermute x53, waiting for transfers between devices, send(): return lax.ppermute(value, 'pipe', pairs)  62.1 us
    pallas_call x4, Pallas kernels, attn_forward(): pl.pallas_call(attn_fwd_kernel, grid=(count,), in_specs=[whole((rows, 128...  51.2 us
    pallas_call x4, Pallas kernels, weight_grads(): pl.pallas_call(kernel, grid=(4,), in_specs=[SMEM, whole(a.shape), col, *(...  42.2 us
    pallas_call x2, Pallas kernels, block_back(): pl.pallas_call(block_back_kernel, grid=(1,), in_specs=[SMEM, one, one, AN...  34.3 us
    pallas_call x2, Pallas kernels, block_out(): pl.pallas_call(block_out_kernel, grid=(1,), in_specs=[SMEM, one, *[whole(...  33.2 us
    unnamed x234, local copies, waits for them, and re-layouts  32.1 us
  transfers between devices with their start and end apart: 78, of which 20 were waited for; matrix products, arithmetic and copies ran while one was open for 13% of the time, Pallas kernels for 40%

profile of v6, /device:TPU:0, one launch (start us, length us, event | category | flops | bytes accessed | tf_op | source)
XLA Modules:
  0.0 588.4 jit_solution(2929834077228447103)
XLA Ops:
  11.1 3.4 fusion.24
  14.6 3.6 collective-permute-start
  18.2 2.9 collective-permute-start.1
  43.1 14.3 %collective-permute-done.1 = bf16[384,2304]{1,0:T(8,128)(2,1)} collective-permute-done((bf16[384,2304]{1,0:T(8,128)(2,1)S(1)}, bf16[384,2304]{1,0:T(8,128)(2,1)}, u32[]{:S(2)}, u32[]{:S(2)}) %collective-permute-start.1) | collective-permute-done | bytes 1769504 | tf_op jit(solution)/shard_map/ppermute | solution.py:723
  59.8 3.3 collective-permute-done.6.far_other
  63.2 3.0 copy-done.4
  66.1 3.9 project.2
  75.7 12.7 %collective-permute-done.8 = bf16[96,3072]{1,0:T(8,128)(2,1)S(1)} collective-permute-done((bf16[96,3072]{1,0:T(8,128)(2,1)S(1)}, bf16[96,3072]{1,0:T(8,128)(2,1)S(1)}, u32[]{:S(2)}, u32[]{:S(2)}) %collective-permute-start.8) | collective-permute-done | bytes 589856 | tf_op jit(solution)/shard_map/ppermute | solution.py:723
  91.8 3.9 collective-permute-start.17
  96.3 12.7 %attn_fwd.4 = (bf16[576,384]{1,0:T(8,128)(2,1)}, bf16[576,384]{1,0:T(8,128)(2,1)}, f32[576,384]{1,0:T(8,128)}, bf16[6,1152,576]{2,1,0:T(8,128)(2,1)}) custom-call(bf16[576,128]{1,0:T(8,128)(2,1)} %get-tuple-element.294.hot_ref, f32[6,8,128]{2,1,0:T(8,128)} %get-tuple-element.630.map_ref, bf16[576,2304]{1,0:T(8,128)(2,1)} %copy-done.2, ...), custom_call_target="tpu_custom_call" | custom-call | flops 520000000 | bytes 1000 | tf_op jit(solution)/shard_map/attn_fwd/pallas_call | solution.py:145
  113.3 12.6 %attn_fwd.5 = (bf16[576,384]{1,0:T(8,128)(2,1)}, bf16[576,384]{1,0:T(8,128)(2,1)}, f32[576,384]{1,0:T(8,128)}, bf16[6,1152,576]{2,1,0:T(8,128)(2,1)}) custom-call(bf16[576,128]{1,0:T(8,128)(2,1)} %get-tuple-element.294.hot_ref, f32[6,8,128]{2,1,0:T(8,128)} %get-tuple-element.630.map_ref, bf16[576,2304]{1,0:T(8,128)(2,1)} %copy-done.2, ...), custom_call_target="tpu_custom_call" | custom-call | flops 520000000 | bytes 1000 | tf_op jit(solution)/shard_map/attn_fwd/pallas_call | solution.py:145
  146.4 5.6 collective-permute-done.18
  156.1 16.4 %block_out.2 = (bf16[576,768]{1,0:T(8,128)(2,1)}, bf16[576,768]{1,0:T(8,128)(2,1)}, bf16[576,768]{1,0:T(8,128)(2,1)}, bf16[576,3072]{1,0:T(8,128)(2,1)}, bf16[57...) custom-call(s32[2]{0:T(128)} %copy-done.50, ...), custom_call_target="tpu_custom_call" | custom-call | flops 240000000 | bytes 1000 | tf_op jit(solution)/shard_map/block_out/pallas_call | solution.py:410
  176.7 4.2 project.3
  188.6 13.1 %attn_fwd.6 = (bf16[576,384]{1,0:T(8,128)(2,1)}, bf16[576,384]{1,0:T(8,128)(2,1)}, f32[576,384]{1,0:T(8,128)}, bf16[6,1152,576]{2,1,0:T(8,128)(2,1)}) custom-call(bf16[576,128]{1,0:T(8,128)(2,1)} %get-tuple-element.294.hot_ref, f32[6,8,128]{2,1,0:T(8,128)} %get-tuple-element.629.map_ref, bf16[576,2304]{1,0:T(8,128)(2,1)} %copy-done.3, ...), custom_call_target="tpu_custom_call" | custom-call | flops 520000000 | bytes 1000 | tf_op jit(solution)/shard_map/attn_fwd/pallas_call | solution.py:145
  201.7 12.8 %attn_fwd.7 = (bf16[576,384]{1,0:T(8,128)(2,1)}, bf16[576,384]{1,0:T(8,128)(2,1)}, f32[576,384]{1,0:T(8,128)}, bf16[6,1152,576]{2,1,0:T(8,128)(2,1)}) custom-call(bf16[576,128]{1,0:T(8,128)(2,1)} %get-tuple-element.294.hot_ref, f32[6,8,128]{2,1,0:T(8,128)} %get-tuple-element.629.map_ref, bf16[576,2304]{1,0:T(8,128)(2,1)} %copy-done.3, ...), custom_call_target="tpu_custom_call" | custom-call | flops 520000000 | bytes 1000 | tf_op jit(solution)/shard_map/attn_fwd/pallas_call | solution.py:145
  214.5 16.7 %block_out.3 = (bf16[576,768]{1,0:T(8,128)(2,1)}, bf16[576,768]{1,0:T(8,128)(2,1)}, bf16[576,768]{1,0:T(8,128)(2,1)}, bf16[576,3072]{1,0:T(8,128)(2,1)}, bf16[57...) custom-call(s32[2]{0:T(128)} %get-tuple-element.292.info_ref, ...), custom_call_target="tpu_custom_call" | custom-call | flops 240000000 | bytes 1000 | tf_op jit(solution)/shard_map/block_out/pallas_call | solution.py:410
  231.3 5.6 collective-permute-start.28
  240.5 16.9 %block_back.2 = (bf16[576,768]{1,0:T(8,128)(2,1)}, bf16[576,3072]{1,0:T(8,128)(2,1)}, bf16[576,768]{1,0:T(8,128)(2,1)}, bf16[576,768]{1,0:T(8,128)(2,1)}, bf16[576,768]{1,0:T(8,128)(2,1)}, /*index=5*/f32[8,768]{1,0:T(8,128)}) custom-call(s32[2]{0:T(128)} %get-tuple-element.292.info_ref, bf16[576,768]{1,0:T(8,128)(2,1)} %get-tuple-element.293.gy_ref, ...), custom_call_target="tpu_custom_call" | custom-call | flops 280000000 | bytes 1000 | tf_op jit(solution)/shard_map/block_back/pallas_call | solution.py:493
  260.9 14.0 %mlp_grads.2 = (bf16[8,384,768]{2,1,0:T(8,128)(2,1)}, bf16[8,384,768]{2,1,0:T(8,128)(2,1)}) custom-call(s32[1]{0:T(128)} %bitcast.core_ref, bf16[576,768]{1,0:T(8,128)(2,1)S(1)} %copy-done.27, bf16[576,3072]{1,0:T(8,128)(2,1)S(1)} %copy-done.21, bf16[576,3072]{1,0:T(8,128)(2,1)} %get-tuple-element.371.hid_ref, bf16[576,768]{1,0:T(8,128)(2,1)S(1)} %copy-done.29), custom_call_target="tpu_custom_call" | custom-call | flops 300000000 | bytes 1000 | tf_op jit(solution)/shard_map/mlp_grads/pallas_call | solution.py:709
  275.9 17.9 %attn_bwd.4 = (bf16[576,384]{1,0:T(8,128)(2,1)}, bf16[2,576,384]{2,1,0:T(8,128)(2,1)}, bf16[2,576,384]{2,1,0:T(8,128)(2,1)}, f32[3,8,128]{2,1,0:T(8,128)}) custom-call(bf16[576,128]{1,0:T(8,128)(2,1)} %get-tuple-element.366.hot_ref, bf16[6,1152,576]{2,1,0:T(8,128)(2,1)} %get-tuple-element.367.w_ref, bf16[576,2304]{1,0:T(8,128)(2,1)} %copy-done.3, ...), custom_call_target="tpu_custom_call" | custom-call | flops 360000000 | bytes 1000 | tf_op jit(solution)/shard_map/attn_bwd/pallas_call | solution.py:227
  293.9 5.7 add.394
  299.9 18.1 %attn_bwd.5 = (bf16[576,384]{1,0:T(8,128)(2,1)}, bf16[2,576,384]{2,1,0:T(8,128)(2,1)}, bf16[2,576,384]{2,1,0:T(8,128)(2,1)}, f32[3,8,128]{2,1,0:T(8,128)}) custom-call(bf16[576,128]{1,0:T(8,128)(2,1)} %get-tuple-element.366.hot_ref, bf16[6,1152,576]{2,1,0:T(8,128)(2,1)} %get-tuple-element.386.w_ref, bf16[576,2304]{1,0:T(8,128)(2,1)} %copy-done.3, ...), custom_call_target="tpu_custom_call" | custom-call | flops 360000000 | bytes 1000 | tf_op jit(solution)/shard_map/attn_bwd/pallas_call | solution.py:227
  324.0 6.6 %project_back.2 = (bf16[576,2304]{1,0:T(8,128)(2,1)}, bf16[576,768]{1,0:T(8,128)(2,1)S(1)}, f32[8,768]{1,0:T(8,128)S(1)}) custom-call(s32[2]{0:T(128)S(1)} %copy-done.53, bf16[576,768]{1,0:T(8,128)(2,1)S(1)} %copy-done.22, bf16[576,768]{1,0:T(8,128)(2,1)S(1)} %copy-done.14, f32[3,768]{1,0:T(4,128)S(1)} %copy-done.45, bf16[576,384]{1,0:T(8,128)(2,1)S(1)} %copy-done.40, ...), custom_call_target="tpu_custom_call" | custom-call | flops 140000000 | bytes 1000 | tf_op jit(solution)/shard_map/project_back/pallas_call | solution.py:539
  330.6 7.3 %att_grads.2 = (bf16[8,192,768]{2,1,0:T(8,128)(2,1)S(1)}, bf16[8,192,768]{2,1,0:T(8,128)(2,1)}) custom-call(s32[1]{0:T(128)} %bitcast.core_ref, bf16[576,768]{1,0:T(8,128)(2,1)S(1)} %get-tuple-element.402.n_ref, bf16[576,2304]{1,0:T(8,128)(2,1)} %get-tuple-element.403.dproj_ref, bf16[576,384]{1,0:T(8,128)(2,1)S(1)} %copy-done.17, ...), custom_call_target="tpu_custom_call" | custom-call | flops 180000000 | bytes 1000 | tf_op jit(solution)/shard_map/att_grads/pallas_call | solution.py:709
  339.7 4.0 collective-permute-start.35
  345.3 3.1 collective-permute-start.37
  348.4 17.4 %block_back.3 = (bf16[576,768]{1,0:T(8,128)(2,1)}, bf16[576,3072]{1,0:T(8,128)(2,1)}, bf16[576,768]{1,0:T(8,128)(2,1)}, bf16[576,768]{1,0:T(8,128)(2,1)}, bf16[576,768]{1,0:T(8,128)(2,1)}, /*index=5*/f32[8,768]{1,0:T(8,128)}) custom-call(s32[2]{0:T(128)} %copy-done.50, bf16[576,768]{1,0:T(8,128)(2,1)} %copy-done.19, ...), custom_call_target="tpu_custom_call" | custom-call | flops 280000000 | bytes 1000 | tf_op jit(solution)/shard_map/block_back/pallas_call | solution.py:493
  366.8 3.8 add.395
  373.0 13.8 %mlp_grads.3 = (bf16[8,384,768]{2,1,0:T(8,128)(2,1)}, bf16[8,384,768]{2,1,0:T(8,128)(2,1)}) custom-call(s32[1]{0:T(128)} %bitcast.core_ref, bf16[576,768]{1,0:T(8,128)(2,1)S(1)} %copy-done.26, bf16[576,3072]{1,0:T(8,128)(2,1)S(1)} %copy-done.20, bf16[576,3072]{1,0:T(8,128)(2,1)} %get-tuple-element.425.hid_ref, bf16[576,768]{1,0:T(8,128)(2,1)S(1)} %copy-done.28), custom_call_target="tpu_custom_call" | custom-call | flops 300000000 | bytes 1000 | tf_op jit(solution)/shard_map/mlp_grads/pallas_call | solution.py:709
  391.8 17.8 %attn_bwd.6 = (bf16[576,384]{1,0:T(8,128)(2,1)}, bf16[2,576,384]{2,1,0:T(8,128)(2,1)}, bf16[2,576,384]{2,1,0:T(8,128)(2,1)}, f32[3,8,128]{2,1,0:T(8,128)}) custom-call(bf16[576,128]{1,0:T(8,128)(2,1)} %get-tuple-element.366.hot_ref, bf16[6,1152,576]{2,1,0:T(8,128)(2,1)} %get-tuple-element.419.w_ref, bf16[576,2304]{1,0:T(8,128)(2,1)} %copy-done.2, ...), custom_call_target="tpu_custom_call" | custom-call | flops 360000000 | bytes 1000 | tf_op jit(solution)/shard_map/attn_bwd/pallas_call | solution.py:227
  409.7 5.8 add.396
  415.6 3.0 collective-permute-start.42
  422.7 17.8 %attn_bwd.7 = (bf16[576,384]{1,0:T(8,128)(2,1)}, bf16[2,576,384]{2,1,0:T(8,128)(2,1)}, bf16[2,576,384]{2,1,0:T(8,128)(2,1)}, f32[3,8,128]{2,1,0:T(8,128)}) custom-call(bf16[576,128]{1,0:T(8,128)(2,1)} %get-tuple-element.366.hot_ref, bf16[6,1152,576]{2,1,0:T(8,128)(2,1)} %get-tuple-element.439.w_ref, bf16[576,2304]{1,0:T(8,128)(2,1)} %copy-done.2, ...), custom_call_target="tpu_custom_call" | custom-call | flops 360000000 | bytes 1000 | tf_op jit(solution)/shard_map/attn_bwd/pallas_call | solution.py:227
  440.5 4.1 collective-permute-done.43
  455.3 7.6 %project_back.3 = (bf16[576,2304]{1,0:T(8,128)(2,1)}, bf16[576,768]{1,0:T(8,128)(2,1)}, f32[8,768]{1,0:T(8,128)S(1)}) custom-call(s32[2]{0:T(128)S(1)} %copy-done.51, bf16[576,768]{1,0:T(8,128)(2,1)S(1)} %copy-done.23, bf16[576,768]{1,0:T(8,128)(2,1)S(1)} %copy-done.12, f32[3,768]{1,0:T(4,128)S(1)} %copy-done.43, bf16[576,384]{1,0:T(8,128)(2,1)S(1)} %copy-done.38, ...), custom_call_target="tpu_custom_call" | custom-call | flops 140000000 | bytes 1000 | tf_op jit(solution)/shard_map/project_back/pallas_call | solution.py:539
  466.5 7.0 %att_grads.3 = (bf16[8,192,768]{2,1,0:T(8,128)(2,1)S(1)}, bf16[8,192,768]{2,1,0:T(8,128)(2,1)}) custom-call(s32[1]{0:T(128)} %bitcast.core_ref, bf16[576,768]{1,0:T(8,128)(2,1)S(1)} %copy-done.31, bf16[576,2304]{1,0:T(8,128)(2,1)} %get-tuple-element.464.dproj_ref, bf16[576,384]{1,0:T(8,128)(2,1)S(1)} %copy-done.15, bf16[576,384]{1,0:T(8,128)(2,1)S(1)} %copy-done.16, ...), custom_call_target="tpu_custom_call" | custom-call | flops 180000000 | bytes 1000 | tf_op jit(solution)/shard_map/att_grads/pallas_call | solution.py:709
  480.2 3.7 add.409
  485.6 3.9 collective-permute-start.52
  495.4 6.4 %maximum_select_fusion = bf16[4,576,768]{2,1,0:T(8,128)(2,1)} fusion(bf16[1,576,768]{2,1,0:T(8,128)(2,1)} %bitcast.44, bf16[1,576,768]{2,1,0:T(8,128)(2,1)S(1)} %bitcast.208, bf16[1,576,768]{2,1,0:T(8,128)(2,1)} %bitcast.42, bf16[1,576,768]{2,1,0:T(8,128)(2,1)S(1)} %bitcast.206, bf16[1,576,768]{2,1,0:T(8,128)(2,1)S(1)} %bitcast.209, ...), kind=kLoop, calls=%fused_computation.1 | loop fusion | flops 26542080 | bytes 17694724 | tf_op jit(solution)/shard_map/jit(_where)/select_n | solution.py:821
  504.8 6.2 %collective-permute-done.52 = bf16[288,768]{1,0:T(8,128)(2,1)S(1)} collective-permute-done((bf16[288,768]{1,0:T(8,128)(2,1)S(1)}, bf16[288,768]{1,0:T(8,128)(2,1)S(1)}, u32[]{:S(2)}, u32[]{:S(2)}) %collective-permute-start.52) | collective-permute-done | bytes 442400 | tf_op jit(solution)/shard_map/ppermute | solution.py:723
  511.1 7.6 %collective-permute-done.57 = bf16[2,192,256]{2,1,0:T(8,128)(2,1)S(1)} collective-permute-done((bf16[2,192,256]{2,1,0:T(8,128)(2,1)S(1)}, bf16[2,192,256]{2,1,0:T(8,128)(2,1)S(1)}, u32[]{:S(2)}, u32[]{:S(2)}) %collective-permute-start.57) | collective-permute-done | bytes 196640 | tf_op jit(solution)/shard_map/ppermute | solution.py:761
  523.9 3.3 collective-permute-start.63
  529.7 10.8 %collective-permute-done.62 = bf16[192,768]{1,0:T(8,128)(2,1)S(1)} collective-permute-done((bf16[192,768]{1,0:T(8,128)(2,1)S(1)}, bf16[192,768]{1,0:T(8,128)(2,1)S(1)}, u32[]{:S(2)}, u32[]{:S(2)}) %collective-permute-start.62) | collective-permute-done | bytes 294944 | tf_op jit(solution)/shard_map/ppermute | solution.py:723
  540.5 3.2 collective-permute-done.64
  550.6 8.6 %select_select_fusion = f32[4,576,768]{2,1,0:T(8,128)} fusion(bf16[1,576,768]{2,1,0:T(8,128)(2,1)} %bitcast.75, bf16[1,576,768]{2,1,0:T(8,128)(2,1)} %bitcast.74, bf16[1,576,768]{2,1,0:T(8,128)(2,1)} %bitcast.73, bf16[1,576,768]{2,1,0:T(8,128)(2,1)} %bitcast.72, bf16[1,576,768]{2,1,0:T(8,128)(2,1)S(1)} %bitcast.222, bf16[1,576,768]{2,1,0:T(8,128)(2,1)S(1)} %bitcast.223, ...), kind=kLoop, calls=%fused_computation | loop fusion | flops 33619968 | bytes 21233668 | tf_op jit(solution)/shard_map/jit(_where)/select_n | solution.py:821
  560.6 6.2 %collective-permute-done.70 = bf16[96,768]{1,0:T(8,128)(2,1)S(1)} collective-permute-done((bf16[96,768]{1,0:T(8,128)(2,1)S(1)}, bf16[96,768]{1,0:T(8,128)(2,1)S(1)}, u32[]{:S(2)}, u32[]{:S(2)}) %collective-permute-start.70) | collective-permute-done | bytes 147488 | tf_op jit(solution)/shard_map/ppermute | solution.py:723
  574.4 3.3 collective-permute-done.74
  (503 shorter events, 162.8 us)
Async XLA Ops:
  7.2 402.5 %reduce-scatter.4.cloned.1.call-start = ((), (), s32[]{:S(2)}) async-start(), calls=%async_computation.3 | async-start | bytes 5308416 | tf_op jit(solution)/shard_map/reduce_scatter | solution.py:784
  8.0 31.5 %collective-permute-start.4 = (f32[3,768]{1,0:T(4,128)S(1)}, f32[3,768]{1,0:T(4,128)S(1)}, u32[]{:S(2)}, u32[]{:S(2)}) collective-permute-start(f32[3,768]{1,0:T(4,128)S(1)} %pad_maximum_fusion.10), channel_id=1, source_target_pairs={{0,3},{1,2},{2,1},{3,0},{4,7},{5,6},{6,5},{7,4},{8,11},{9,10},{10,... | collective-permute-start | bytes 27656 | tf_op jit(solution)/shard_map/ppermute | solution.py:723
  10.4 32.0 %collective-permute-start.3 = (f32[3,768]{1,0:T(4,128)S(1)}, f32[3,768]{1,0:T(4,128)S(1)}, u32[]{:S(2)}, u32[]{:S(2)}) collective-permute-start(f32[3,768]{1,0:T(4,128)S(1)} %pad_maximum_fusion.10), channel_id=1, source_target_pairs={{0,2},{1,3},{2,0},{3,1},{4,6},{5,7},{6,4},{7,5},{8,10},{9,11},{10,... | collective-permute-start | bytes 27656 | tf_op jit(solution)/shard_map/ppermute | solution.py:723
  11.1 52.1 %collective-permute-start.5 = (bf16[768,3072]{1,0:T(8,128)(2,1)}, bf16[768,3072]{1,0:T(8,128)(2,1)}, u32[]{:S(2)}, u32[]{:S(2)}) collective-permute-start(bf16[768,3072]{1,0:T(8,128)(2,1)} %bitcast.178), channel_id=1, source_target_pairs={{0,1},{1,0},{2,3},{3,2},{4,5},{5,4},{6,7},{7,6},{8,9},{9,8},{10,11... | collective-permute-start | bytes 14155784 | tf_op jit(solution)/shard_map/ppermute | solution.py:723
  14.6 28.5 %collective-permute-start = (bf16[384,2304]{1,0:T(8,128)(2,1)}, bf16[384,2304]{1,0:T(8,128)(2,1)}, u32[]{:S(2)}, u32[]{:S(2)}) collective-permute-start(bf16[384,2304]{1,0:T(8,128)(2,1)} %get-tuple-element.570), channel_id=1, source_target_pairs={{0,2},{2,0},{4,6},{6,4},{8,10},{10,8},{12,14},{14,12},{16,18},{18,... | collective-permute-start | bytes 5308424 | tf_op jit(solution)/shard_map/ppermute | solution.py:723
  18.2 39.2 %collective-permute-start.1 = (bf16[384,2304]{1,0:T(8,128)(2,1)S(1)}, bf16[384,2304]{1,0:T(8,128)(2,1)}, u32[]{:S(2)}, u32[]{:S(2)}) collective-permute-start(bf16[384,2304]{1,0:T(8,128)(2,1)S(1)} %get-tuple-element.569), channel_id=1, source_target_pairs={{0,3},{2,1},{4,7},{6,5},{8,11},{10,9},{12,15},{14,13},{16,19},{18,... | collective-permute-start | bytes 5308424 | tf_op jit(solution)/shard_map/ppermute | solution.py:723
  70.3 18.1 %collective-permute-start.7 = (bf16[576,1536]{1,0:T(8,128)(2,1)S(1)}, bf16[576,1536]{1,0:T(8,128)(2,1)S(1)}, u32[]{:S(2)}, u32[]{:S(2)}) collective-permute-start(bf16[576,1536]{1,0:T(8,128)(2,1)S(1)} %slice.241), channel_id=1, source_target_pairs={{0,1},{1,0},{2,3},{3,2},{4,5},{5,4},{6,7},{7,6},{8,9},{9,8},{10,11... | collective-permute-start | bytes 5308424 | tf_op jit(solution)/shard_map/ppermute | solution.py:723
  71.6 16.8 %collective-permute-start.8 = (bf16[96,3072]{1,0:T(8,128)(2,1)S(1)}, bf16[96,3072]{1,0:T(8,128)(2,1)S(1)}, u32[]{:S(2)}, u32[]{:S(2)}) collective-permute-start(bf16[96,3072]{1,0:T(8,128)(2,1)S(1)} %copy-done.91), channel_id=1, source_target_pairs={{1,2},{3,0},{5,6},{7,4},{9,10},{11,8},{13,14},{15,12},{17,18},{19,... | collective-permute-start | bytes 1769480 | tf_op jit(solution)/shard_map/ppermute | solution.py:723
  73.6 35.4 %collective-permute-start.12 = (bf16[384,768]{1,0:T(8,128)(2,1)S(1)}, bf16[384,768]{1,0:T(8,128)(2,1)S(1)}, u32[]{:S(2)}, u32[]{:S(2)}) collective-permute-start(bf16[384,768]{1,0:T(8,128)(2,1)S(1)} %dynamic-slice_bitcast_fusion.8), channel_id=1, source_target_pairs={{0,2},{1,3},{2,0},{3,1},{4,6},{5,7},{6,4},{7,5},{8,10},{9,11},{10,... | collective-permute-start | bytes 1769480 | tf_op jit(solution)/shard_map/ppermute | solution.py:723
  88.5 20.5 %collective-permute-start.10 = (bf16[96,3072]{1,0:T(8,128)(2,1)S(1)}, bf16[96,3072]{1,0:T(8,128)(2,1)S(1)}, u32[]{:S(2)}, u32[]{:S(2)}) collective-permute-start(bf16[96,3072]{1,0:T(8,128)(2,1)S(1)} %broadcast_select_fusion.4.mine), channel_id=1, source_target_pairs={{0,4},{4,0},{8,12},{12,8},{16,20},{20,16},{24,28},{28,24},{1,5},{5... | collective-permute-start | bytes 1769480 | tf_op jit(solution)/shard_map/ppermute | solution.py:570
  90.3 18.8 %collective-permute-start.11 = (bf16[96,3072]{1,0:T(8,128)(2,1)S(1)}, bf16[96,3072]{1,0:T(8,128)(2,1)S(1)}, u32[]{:S(2)}, u32[]{:S(2)}) collective-permute-start(bf16[96,3072]{1,0:T(8,128)(2,1)S(1)} %broadcast_select_fusion.4.mine), channel_id=1, source_target_pairs={{0,8},{4,12},{8,0},{12,4},{16,24},{20,28},{24,16},{28,20},{1,9},{5... | collective-permute-start | bytes 1769480 | tf_op jit(solution)/shard_map/ppermute | solution.py:570
  91.8 38.4 %collective-permute-start.17 = (bf16[768,768]{1,0:T(8,128)(2,1)}, bf16[768,768]{1,0:T(8,128)(2,1)S(1)}, u32[]{:S(2)}, u32[]{:S(2)}) collective-permute-start(bf16[768,768]{1,0:T(8,128)(2,1)} %slice.306), channel_id=1, source_target_pairs={{0,2},{2,0},{4,6},{6,4},{8,10},{10,8},{12,14},{14,12},{16,18},{18,... | collective-permute-start | bytes 3538952 | tf_op jit(solution)/shard_map/ppermute | solution.py:723
  109.0 21.2 %collective-permute-start.15 = (bf16[384,768]{1,0:T(8,128)(2,1)S(1)}, bf16[384,768]{1,0:T(8,128)(2,1)S(1)}, u32[]{:S(2)}, u32[]{:S(2)}) collective-permute-start(bf16[384,768]{1,0:T(8,128)(2,1)S(1)} %collective-permute-done.12.mine), channel_id=1, source_target_pairs={{0,4},{4,0},{8,12},{12,8},{16,20},{20,16},{24,28},{28,24},{1,5},{5... | collective-permute-start | bytes 1769480 | tf_op jit(solution)/shard_map/ppermute | solution.py:570
  109.6 20.6 %collective-permute-start.16 = (bf16[384,768]{1,0:T(8,128)(2,1)S(1)}, bf16[384,768]{1,0:T(8,128)(2,1)S(1)}, u32[]{:S(2)}, u32[]{:S(2)}) collective-permute-start(bf16[384,768]{1,0:T(8,128)(2,1)S(1)} %collective-permute-done.12.mine), channel_id=1, source_target_pairs={{0,8},{4,12},{8,0},{12,4},{16,24},{20,28},{24,16},{28,20},{1,9},{5... | collective-permute-start | bytes 1769480 | tf_op jit(solution)/shard_map/ppermute | solution.py:570
  110.1 18.4 %collective-permute-start.13 = (bf16[48,3072]{1,0:T(8,128)(2,1)S(1)}, bf16[48,3072]{1,0:T(8,128)(2,1)S(1)}, u32[]{:S(2)}, u32[]{:S(2)}) collective-permute-start(bf16[48,3072]{1,0:T(8,128)(2,1)S(1)} %slice.242), channel_id=1, source_target_pairs={{0,4},{4,0},{8,12},{12,8},{16,20},{20,16},{24,28},{28,24},{1,5},{5... | collective-permute-start | bytes 884744 | tf_op jit(solution)/shard_map/ppermute | solution.py:570
  111.7 17.8 %collective-permute-start.14 = (bf16[48,3072]{1,0:T(8,128)(2,1)S(1)}, bf16[48,3072]{1,0:T(8,128)(2,1)S(1)}, u32[]{:S(2)}, u32[]{:S(2)}) collective-permute-start(bf16[48,3072]{1,0:T(8,128)(2,1)S(1)} %slice.243), channel_id=1, source_target_pairs={{0,8},{4,12},{8,0},{12,4},{16,24},{20,28},{24,16},{28,20},{1,9},{5... | collective-permute-start | bytes 884744 | tf_op jit(solution)/shard_map/ppermute | solution.py:570
  134.7 18.5 %collective-permute-start.20 = (bf16[1536,768]{1,0:T(8,128)(2,1)}, bf16[1536,768]{1,0:T(8,128)(2,1)S(1)}, u32[]{:S(2)}, u32[]{:S(2)}) collective-permute-start(bf16[1536,768]{1,0:T(8,128)(2,1)} %bitcast.192), channel_id=1, source_target_pairs={{0,1},{1,0},{2,3},{3,2},{4,5},{5,4},{6,7},{7,6},{8,9},{9,8},{10,11... | collective-permute-start | bytes 7077896 | tf_op jit(solution)/shard_map/ppermute | solution.py:723
  182.7 31.8 %collective-permute-start.25 = (bf16[576,768]{1,0:T(8,128)(2,1)S(1)}, bf16[576,768]{1,0:T(8,128)(2,1)S(1)}, u32[]{:S(2)}, u32[]{:S(2)}) collective-permute-start(bf16[576,768]{1,0:T(8,128)(2,1)S(1)} %copy-done.63), channel_id=1, source_target_pairs={{2,0},{3,1},{6,4},{7,5},{10,8},{11,9},{14,12},{15,13},{18,16},{19,... | collective-permute-start | bytes 2654216 | tf_op jit(solution)/shard_map/ppermute | solution.py:723
  184.0 47.3 %collective-permute-start.26 = (bf16[576,768]{1,0:T(8,128)(2,1)}, bf16[576,768]{1,0:T(8,128)(2,1)}, u32[]{:S(2)}, u32[]{:S(2)}) collective-permute-start(bf16[576,768]{1,0:T(8,128)(2,1)} %get-tuple-element.353), channel_id=1, source_target_pairs={{0,1},{1,0},{4,5},{5,4},{8,9},{9,8},{12,13},{13,12},{16,17},{17,16... | collective-permute-start | bytes 2654216 | tf_op jit(solution)/shard_map/ppermute | solution.py:723
  186.0 45.3 %collective-permute-start.27 = (bf16[576,768]{1,0:T(8,128)(2,1)}, bf16[576,768]{1,0:T(8,128)(2,1)}, u32[]{:S(2)}, u32[]{:S(2)}) collective-permute-start(bf16[576,768]{1,0:T(8,128)(2,1)} %get-tuple-element.353), channel_id=1, source_target_pairs={{3,0},{2,1},{7,4},{6,5},{11,8},{10,9},{15,12},{14,13},{19,16},{18,... | collective-permute-start | bytes 2654216 | tf_op jit(solution)/shard_map/ppermute | solution.py:723
  231.3 26.1 %collective-permute-start.28 = (bf16[576,768]{1,0:T(8,128)(2,1)}, bf16[576,768]{1,0:T(8,128)(2,1)S(1)}, u32[]{:S(2)}, u32[]{:S(2)}) collective-permute-start(bf16[576,768]{1,0:T(8,128)(2,1)} %get-tuple-element.507), channel_id=1, source_target_pairs={{0,2},{1,3},{4,6},{5,7},{8,10},{9,11},{12,14},{13,15},{16,18},{17,... | collective-permute-start | bytes 2654216 | tf_op jit(solution)/shard_map/ppermute | solution.py:723
  237.0 38.0 %collective-permute-start.29 = (bf16[576,768]{1,0:T(8,128)(2,1)}, bf16[576,768]{1,0:T(8,128)(2,1)S(1)}, u32[]{:S(2)}, u32[]{:S(2)}) collective-permute-start(bf16[576,768]{1,0:T(8,128)(2,1)} %get-tuple-element.375), channel_id=1, source_target_pairs={{2,3},{3,2},{6,7},{7,6},{10,11},{11,10},{14,15},{15,14},{18,19},{1... | collective-permute-start | bytes 2654216 | tf_op jit(solution)/shard_map/ppermute | solution.py:723
  237.7 37.7 %collective-permute-start.30 = (bf16[576,768]{1,0:T(8,128)(2,1)}, bf16[576,768]{1,0:T(8,128)(2,1)S(1)}, u32[]{:S(2)}, u32[]{:S(2)}) collective-permute-start(bf16[576,768]{1,0:T(8,128)(2,1)} %get-tuple-element.375), channel_id=1, source_target_pairs={{1,2},{0,3},{5,6},{4,7},{9,10},{8,11},{13,14},{12,15},{17,18},{16,... | collective-permute-start | bytes 2654216 | tf_op jit(solution)/shard_map/ppermute | solution.py:723
  275.4 18.4 %collective-permute-start.31 = (bf16[8,384,768]{2,1,0:T(8,128)(2,1)}, bf16[8,384,768]{2,1,0:T(8,128)(2,1)}, u32[]{:S(2)}, u32[]{:S(2)}) collective-permute-start(bf16[8,384,768]{2,1,0:T(8,128)(2,1)} %get-tuple-element.384), channel_id=1, source_target_pairs={{0,1},{1,0},{2,3},{3,2},{4,5},{5,4},{6,7},{7,6},{8,9},{9,8},{10,11... | collective-permute-start | bytes 14155784 | tf_op jit(solution)/shard_map/ppermute | solution.py:723
  299.6 173.9 %reduce-scatter.6.cloned.1.call-start = ((), (), s32[]{:S(2)}) async-start(), calls=%async_computation.4 | async-start | bytes 2654208 | tf_op jit(solution)/shard_map/reduce_scatter | solution.py:784
  299.7 18.4 %collective-permute-start.32 = (bf16[2,576,384]{2,1,0:T(8,128)(2,1)}, bf16[2,576,384]{2,1,0:T(8,128)(2,1)S(1)}, u32[]{:S(2)}, u32[]{:S(2)}) collective-permute-start(bf16[2,576,384]{2,1,0:T(8,128)(2,1)} %get-tuple-element.388), channel_id=1, source_target_pairs={{0,1},{1,0},{2,3},{3,2},{4,5},{5,4},{6,7},{7,6},{8,9},{9,8},{10,11... | collective-permute-start | bytes 2654216 | tf_op jit(solution)/shard_map/ppermute | solution.py:723
  338.0 27.9 %collective-permute-start.34 = (bf16[8,192,768]{2,1,0:T(8,128)(2,1)}, bf16[8,192,768]{2,1,0:T(8,128)(2,1)}, u32[]{:S(2)}, u32[]{:S(2)}) collective-permute-start(bf16[8,192,768]{2,1,0:T(8,128)(2,1)} %get-tuple-element.417), channel_id=1, source_target_pairs={{0,1},{1,0},{2,3},{3,2},{4,5},{5,4},{6,7},{7,6},{8,9},{9,8},{10,11... | collective-permute-start | bytes 7077896 | tf_op jit(solution)/shard_map/ppermute | solution.py:723
  339.7 26.2 %collective-permute-start.35 = (bf16[576,768]{1,0:T(8,128)(2,1)S(1)}, bf16[576,768]{1,0:T(8,128)(2,1)S(1)}, u32[]{:S(2)}, u32[]{:S(2)}) collective-permute-start(bf16[576,768]{1,0:T(8,128)(2,1)S(1)} %get-tuple-element.553), channel_id=1, source_target_pairs={{0,2},{1,3},{4,6},{5,7},{8,10},{9,11},{12,14},{13,15},{16,18},{17,... | collective-permute-start | bytes 2654216 | tf_op jit(solution)/shard_map/ppermute | solution.py:723
  343.7 43.1 %collective-permute-start.36 = (bf16[576,768]{1,0:T(8,128)(2,1)}, bf16[576,768]{1,0:T(8,128)(2,1)}, u32[]{:S(2)}, u32[]{:S(2)}) collective-permute-start(bf16[576,768]{1,0:T(8,128)(2,1)} %get-tuple-element.571), channel_id=1, source_target_pairs={{2,3},{3,2},{6,7},{7,6},{10,11},{11,10},{14,15},{15,14},{18,19},{1... | collective-permute-start | bytes 2654216 | tf_op jit(solution)/shard_map/ppermute | solution.py:723
  345.3 41.5 %collective-permute-start.37 = (bf16[576,768]{1,0:T(8,128)(2,1)}, bf16[576,768]{1,0:T(8,128)(2,1)}, u32[]{:S(2)}, u32[]{:S(2)}) collective-permute-start(bf16[576,768]{1,0:T(8,128)(2,1)} %get-tuple-element.571), channel_id=1, source_target_pairs={{1,2},{0,3},{5,6},{4,7},{9,10},{8,11},{13,14},{12,15},{17,18},{16,... | collective-permute-start | bytes 2654216 | tf_op jit(solution)/shard_map/ppermute | solution.py:723
  386.8 22.8 %collective-permute-start.38 = (bf16[8,384,768]{2,1,0:T(8,128)(2,1)}, bf16[8,384,768]{2,1,0:T(8,128)(2,1)}, u32[]{:S(2)}, u32[]{:S(2)}) collective-permute-start(bf16[8,384,768]{2,1,0:T(8,128)(2,1)} %get-tuple-element.437), channel_id=1, source_target_pairs={{0,1},{1,0},{2,3},{3,2},{4,5},{5,4},{6,7},{7,6},{8,9},{9,8},{10,11... | collective-permute-start | bytes 14155784 | tf_op jit(solution)/shard_map/ppermute | solution.py:723
  387.1 179.7 %reduce-scatter.8.cloned.1.call-start = ((), (), s32[]{:S(2)}) async-start(), calls=%async_computation.5 | async-start | bytes 2654208 | tf_op jit(solution)/shard_map/reduce_scatter | solution.py:784
  388.0 21.6 %collective-permute-start.39 = (bf16[576,768]{1,0:T(8,128)(2,1)S(1)}, bf16[576,768]{1,0:T(8,128)(2,1)S(1)}, u32[]{:S(2)}, u32[]{:S(2)}) collective-permute-start(bf16[576,768]{1,0:T(8,128)(2,1)S(1)} %copy-done.23), channel_id=1, source_target_pairs={{0,1},{4,5},{8,9},{12,13},{16,17},{20,21},{24,25},{28,29}} | collective-permute-start | bytes 2654216 | tf_op jit(solution)/shard_map/ppermute | solution.py:723
  390.1 19.5 %collective-permute-start.40 = (bf16[576,768]{1,0:T(8,128)(2,1)S(1)}, bf16[576,768]{1,0:T(8,128)(2,1)S(1)}, u32[]{:S(2)}, u32[]{:S(2)}) collective-permute-start(bf16[576,768]{1,0:T(8,128)(2,1)S(1)} %copy-done.23), channel_id=1, source_target_pairs={{3,1},{7,5},{11,9},{15,13},{19,17},{23,21},{27,25},{31,29}} | collective-permute-start | bytes 2654216 | tf_op jit(solution)/shard_map/ppermute | solution.py:723
  390.9 18.8 %collective-permute-start.41 = (bf16[576,768]{1,0:T(8,128)(2,1)S(1)}, bf16[576,768]{1,0:T(8,128)(2,1)S(1)}, u32[]{:S(2)}, u32[]{:S(2)}) collective-permute-start(bf16[576,768]{1,0:T(8,128)(2,1)S(1)} %copy-done.23), channel_id=1, source_target_pairs={{2,1},{6,5},{10,9},{14,13},{18,17},{22,21},{26,25},{30,29}} | collective-permute-start | bytes 2654216 | tf_op jit(solution)/shard_map/ppermute | solution.py:723
  415.6 30.7 %collective-permute-start.42 = (bf16[2,576,384]{2,1,0:T(8,128)(2,1)}, bf16[2,576,384]{2,1,0:T(8,128)(2,1)S(1)}, u32[]{:S(2)}, u32[]{:S(2)}) collective-permute-start(bf16[2,576,384]{2,1,0:T(8,128)(2,1)} %get-tuple-element.441), channel_id=1, source_target_pairs={{0,1},{1,0},{2,3},{3,2},{4,5},{5,4},{6,7},{7,6},{8,9},{9,8},{10,11... | collective-permute-start | bytes 2654216 | tf_op jit(solution)/shard_map/ppermute | solution.py:723
  419.3 25.4 %collective-permute-start.43 = (bf16[2,2,2,192,256]{4,3,2,1,0:T(8,128)(2,1)S(1)}, bf16[2,2,2,192,256]{4,3,2,1,0:T(8,128)(2,1)S(1)}, u32[]{:S(2)}, u32[]{:S(2)}) collective-permute-start(bf16[2,2,2,192,256]{4,3,2,1,0:T(8,128)(2,1)S(1)} %get-tuple-element.578), channel_id=1, source_target_pairs={{0,4},{4,0},{8,12},{12,8},{16,20},{20,16},{24,28},{28,24},{1,5},{5... | collective-permute-start | bytes 2359304 | tf_op jit(solution)/shard_map/ppermute | solution.py:761
  421.1 23.5 %collective-permute-start.44 = (bf16[2,2,2,192,256]{4,3,2,1,0:T(8,128)(2,1)}, bf16[2,2,2,192,256]{4,3,2,1,0:T(8,128)(2,1)S(1)}, u32[]{:S(2)}, u32[]{:S(2)}) collective-permute-start(bf16[2,2,2,192,256]{4,3,2,1,0:T(8,128)(2,1)} %get-tuple-element.576), channel_id=1, source_target_pairs={{0,2},{1,3},{2,0},{3,1},{4,6},{5,7},{6,4},{7,5},{8,10},{9,11},{10,... | collective-permute-start | bytes 2359304 | tf_op jit(solution)/shard_map/ppermute | solution.py:761
  422.4 23.9 %collective-permute-start.45 = (bf16[2,2,2,192,256]{4,3,2,1,0:T(8,128)(2,1)}, bf16[2,2,2,192,256]{4,3,2,1,0:T(8,128)(2,1)S(1)}, u32[]{:S(2)}, u32[]{:S(2)}) collective-permute-start(bf16[2,2,2,192,256]{4,3,2,1,0:T(8,128)(2,1)} %get-tuple-element.574), channel_id=1, source_target_pairs={{0,8},{4,12},{8,0},{12,4},{16,24},{20,28},{24,16},{28,20},{1,9},{5... | collective-permute-start | bytes 2359304 | tf_op jit(solution)/shard_map/ppermute | solution.py:761
  477.6 33.5 %collective-permute-start.53 = (bf16[576,768]{1,0:T(8,128)(2,1)}, bf16[576,768]{1,0:T(8,128)(2,1)}, u32[]{:S(2)}, u32[]{:S(2)}) collective-permute-start(bf16[576,768]{1,0:T(8,128)(2,1)} %get-tuple-element.538), channel_id=1, source_target_pairs={{2,0},{6,4},{10,8},{14,12},{18,16},{22,20},{26,24},{30,28}} | collective-permute-start | bytes 2654216 | tf_op jit(solution)/shard_map/ppermute | solution.py:723
  478.9 32.2 %collective-permute-start.54 = (bf16[576,768]{1,0:T(8,128)(2,1)}, bf16[576,768]{1,0:T(8,128)(2,1)}, u32[]{:S(2)}, u32[]{:S(2)}) collective-permute-start(bf16[576,768]{1,0:T(8,128)(2,1)} %get-tuple-element.538), channel_id=1, source_target_pairs={{3,0},{7,4},{11,8},{15,12},{19,16},{23,20},{27,24},{31,28}} | collective-permute-start | bytes 2654216 | tf_op jit(solution)/shard_map/ppermute | solution.py:723
  485.6 25.4 %collective-permute-start.52 = (bf16[288,768]{1,0:T(8,128)(2,1)S(1)}, bf16[288,768]{1,0:T(8,128)(2,1)S(1)}, u32[]{:S(2)}, u32[]{:S(2)}) collective-permute-start(bf16[288,768]{1,0:T(8,128)(2,1)S(1)} %pad_maximum_fusion.1), channel_id=1, source_target_pairs={{0,2},{1,3},{2,0},{3,1},{4,6},{5,7},{6,4},{7,5},{8,10},{9,11},{10,... | collective-permute-start | bytes 1327112 | tf_op jit(solution)/shard_map/ppermute | solution.py:723
  491.3 19.8 %collective-permute-start.55 = (bf16[2,192,256]{2,1,0:T(8,128)(2,1)}, bf16[2,192,256]{2,1,0:T(8,128)(2,1)}, u32[]{:S(2)}, u32[]{:S(2)}) collective-permute-start(bf16[2,192,256]{2,1,0:T(8,128)(2,1)} %get-tuple-element.601), channel_id=1, source_target_pairs={{0,8},{4,12},{8,0},{12,4},{16,24},{20,28},{24,16},{28,20},{1,9},{5... | collective-permute-start | bytes 589832 | tf_op jit(solution)/shard_map/ppermute | solution.py:761
  494.4 16.8 %collective-permute-start.56 = (bf16[2,192,256]{2,1,0:T(8,128)(2,1)}, bf16[2,192,256]{2,1,0:T(8,128)(2,1)}, u32[]{:S(2)}, u32[]{:S(2)}) collective-permute-start(bf16[2,192,256]{2,1,0:T(8,128)(2,1)} %get-tuple-element.599), channel_id=1, source_target_pairs={{0,4},{4,0},{8,12},{12,8},{16,20},{20,16},{24,28},{28,24},{1,5},{5... | collective-permute-start | bytes 589832 | tf_op jit(solution)/shard_map/ppermute | solution.py:761
  523.9 16.7 %collective-permute-start.63 = (bf16[192,768]{1,0:T(8,128)(2,1)S(1)}, bf16[192,768]{1,0:T(8,128)(2,1)S(1)}, u32[]{:S(2)}, u32[]{:S(2)}) collective-permute-start(bf16[192,768]{1,0:T(8,128)(2,1)S(1)} %get-tuple-element.596), channel_id=1, source_target_pairs={{1,2},{0,3},{5,6},{4,7},{9,10},{8,11},{13,14},{12,15},{17,18},{16,... | collective-permute-start | bytes 884744 | tf_op jit(solution)/shard_map/ppermute | solution.py:723
  527.2 16.5 %collective-permute-start.64 = (bf16[192,768]{1,0:T(8,128)(2,1)S(1)}, bf16[192,768]{1,0:T(8,128)(2,1)S(1)}, u32[]{:S(2)}, u32[]{:S(2)}) collective-permute-start(bf16[192,768]{1,0:T(8,128)(2,1)S(1)} %get-tuple-element.594), channel_id=1, source_target_pairs={{0,16},{4,20},{8,24},{12,28},{16,0},{20,4},{24,8},{28,12},{1,17},{... | collective-permute-start | bytes 884744 | tf_op jit(solution)/shard_map/ppermute | solution.py:761
  543.8 16.8 %collective-permute-start.67 = (f32[12336]{0:T(1024)S(1)}, f32[12336]{0:T(1024)S(1)}, u32[]{:S(2)}, u32[]{:S(2)}) collective-permute-start(f32[12336]{0:T(1024)S(1)} %add_add_fusion.1), channel_id=1, source_target_pairs={{0,12},{4,8},{8,4},{12,0},{16,28},{20,24},{24,20},{28,16},{1,13},{... | collective-permute-start | bytes 148040 | tf_op jit(solution)/shard_map/ppermute | solution.py:570
  547.4 19.4 %collective-permute-start.68 = (bf16[192,768]{1,0:T(8,128)(2,1)S(1)}, bf16[192,768]{1,0:T(8,128)(2,1)S(1)}, u32[]{:S(2)}, u32[]{:S(2)}) collective-permute-start(bf16[192,768]{1,0:T(8,128)(2,1)S(1)} %add.428), channel_id=1, source_target_pairs={{0,1},{4,5},{8,9},{12,13},{16,17},{20,21},{24,25},{28,29}} | collective-permute-start | bytes 884744 | tf_op jit(solution)/shard_map/ppermute | solution.py:723
  (147 other events, 1288.2 us)
Sparse Core Ops, SparseCore 0:
  299.7 95.5 reduce-scatter.3
  398.8 73.4 reduce-scatter.5
  484.1 73.5 reduce-scatter.7
